TPU v7x, 32 devices: a whole 2x2x4 slice. The times are simulated.
32 devices in a mesh: dom: 4 (over y, core), band: 8 (over z, x).
Axes of the slice: x: 2, y: 2, z: 4, core: 2. Of those that a mesh axis runs over, the one named last changes fastest.
Arguments:
- psi_in: float32 [4, 8, 20, 1600], P('dom', 'band'), may hold values from -6 to 6
- v_in: float32 [4, 40, 1600], P('dom'), may hold values from -3 to 3
- offsets: int32 [4, 3], replicated, may hold values from 0 to 32, as said below
Outputs:
- psi_out: float32 [4, 8, 20, 1600], P('dom', 'band')
Inputs may be any that keep to these rules, and one draw needn't show every extreme that they name: `offsets`: row d is the first corner of domain d's core in the global grid: its first two entries are 0 or 32, its third a multiple of 32 below 32; the 4 rows are distinct, so the cores tile the grid.
All inputs are finite; a program needn't handle non-finite values.
Results may differ from a plain program's by a relative error of at most 0.0003.
Values sent between devices are 32-bit elements; how exact they have to be, the bound alone decides.
No kernel may reach another device: no remote copies, remote signals or barrier semaphores. Data moves between devices by JAX's collectives and lax.ppermute only.
A program may use at most 64 MiB of HBM per device.

v0:
```python
import math

import jax
import jax.numpy as jnp
from jax import lax
from jax.sharding import PartitionSpec as P

CORE = 32
BUF = 4
DEG = 8


CENTER = 3.0
HALF_WIDTH = 4.5
FOUR_PI = 4.0 * math.pi
EXCHANGE_COEF = -((3.0 / math.pi) ** (1.0 / 3.0))
precise = lax.Precision.HIGHEST


def swapped(value, axis, distance):
    mask = 2**distance
    pairs = [(source, source ^ mask) for source in range(lax.axis_size(axis))]
    return lax.ppermute(value, axis, pairs)


def hamiltonian(values, potential, side_len):
    row_len = values.shape[1]
    zero_row = jnp.zeros((1, row_len), jnp.float32)
    prev_rows = jnp.concatenate([zero_row, values[:-1]], 0)
    next_rows = jnp.concatenate([values[1:], zero_row], 0)
    column = jnp.arange(row_len) % side_len
    prev_cols = jnp.where(column == 0, 0.0, jnp.roll(values, 1, 1))
    next_cols = jnp.where(column == side_len - 1, 0.0, jnp.roll(values, -1, 1))
    zero_block = jnp.zeros((values.shape[0], side_len), jnp.float32)
    prev_lines = jnp.concatenate([zero_block, values[:, :-side_len]], 1)
    next_lines = jnp.concatenate([values[:, side_len:], zero_block], 1)
    beside_all = prev_rows + next_rows + prev_lines + next_lines + prev_cols + next_cols
    return 0.5 * (6.0 * values - beside_all) + potential * values


def chebyshev(values, potential, side_len):

    def shifted(operand):
        return (hamiltonian(operand, potential, side_len) - CENTER * operand) / HALF_WIDTH

    previous = values
    current = shifted(values)
    for order_idx in range(DEG - 1):
        following = 2.0 * shifted(current) - previous
        previous, current = (current, following)
    return current


def phase_tables(positions, freqs, length):
    product = positions[..., None] * freqs % length
    angle = 2.0 * math.pi / length * product.astype(jnp.float32)
    return (jnp.cos(angle), jnp.sin(angle))


def poisson_factor(depth_waves, grid_z):
    wave_x = jnp.arange(2 * CORE, dtype=jnp.int32)
    eigen_x = 2.0 - 2.0 * jnp.cos(2.0 * math.pi * wave_x.astype(jnp.float32) / (2 * CORE))
    eigen_z = 2.0 - 2.0 * jnp.cos(2.0 * math.pi * depth_waves.astype(jnp.float32) / grid_z)
    eigen = eigen_z[:, None, None] + eigen_x[None, :, None] + eigen_x[None, None, :]
    zero_mode = (
        (depth_waves == 0)[:, None, None]
        & (wave_x == 0)[None, :, None]
        & (wave_x == 0)[None, None, :]
    )
    return jnp.where(zero_mode, 0.0, FOUR_PI / jnp.where(zero_mode, 1.0, eigen))


def plane_spectrum(own_parts, first_part, anchor):
    part_count = own_parts.shape[0]
    cell_ids = jnp.arange(CORE, dtype=jnp.int32)
    wave_ids = jnp.arange(2 * CORE, dtype=jnp.int32)
    cos_x, sin_x = phase_tables(anchor[0] + cell_ids, wave_ids, 2 * CORE)
    cos_y, sin_y = phase_tables(anchor[1] + cell_ids, wave_ids, 2 * CORE)
    with_cos = jnp.einsum("txy,yk->txk", own_parts, cos_y, precision=precise)
    with_sin = jnp.einsum("txy,yk->txk", own_parts, sin_y, precision=precise)
    real_part = jnp.einsum("xj,txk->tjk", cos_x, with_cos, precision=precise) - jnp.einsum(
        "xj,txk->tjk", sin_x, with_sin, precision=precise
    )
    imag_part = -(
        jnp.einsum("xj,txk->tjk", sin_x, with_cos, precision=precise)
        + jnp.einsum("xj,txk->tjk", cos_x, with_sin, precision=precise)
    )
    odd_part = ((first_part + jnp.arange(part_count, dtype=jnp.int32)) % 2 == 1)[:, None, None]
    return jnp.stack(
        [jnp.where(odd_part, -imag_part, real_part), jnp.where(odd_part, real_part, imag_part)], 1
    )


def field_planes(all_spectra, first_part, anchor, side_len, grid_z):
    part_count = all_spectra.shape[0]
    depth_waves = (first_part + jnp.arange(part_count, dtype=jnp.int32)) // 2
    factor = poisson_factor(depth_waves, grid_z)
    real_in = jnp.stack([all_spectra[:, 0], all_spectra[:, 0] * factor], 1)
    imag_in = jnp.stack([all_spectra[:, 1], all_spectra[:, 1] * factor], 1)
    wave_ids = jnp.arange(2 * CORE, dtype=jnp.int32)
    region_pos = jnp.arange(side_len, dtype=jnp.int32) - BUF
    cos_x, sin_x = phase_tables(anchor[0] + region_pos, wave_ids, 2 * CORE)
    cos_y, sin_y = phase_tables(anchor[1] + region_pos, wave_ids, 2 * CORE)
    first_re = jnp.einsum("tfjk,rj->tfrk", real_in, cos_x, precision=precise) - jnp.einsum(
        "tfjk,rj->tfrk", imag_in, sin_x, precision=precise
    )
    first_im = jnp.einsum("tfjk,rj->tfrk", real_in, sin_x, precision=precise) + jnp.einsum(
        "tfjk,rj->tfrk", imag_in, cos_x, precision=precise
    )
    plane_re = jnp.einsum("tfrk,sk->tfrs", first_re, cos_y, precision=precise) - jnp.einsum(
        "tfrk,sk->tfrs", first_im, sin_y, precision=precise
    )
    plane_im = jnp.einsum("tfrk,sk->tfrs", first_re, sin_y, precision=precise) + jnp.einsum(
        "tfrk,sk->tfrs", first_im, cos_y, precision=precise
    )
    return (plane_re, plane_im)


def depth_terms(plane_re, plane_im, anchor_z, side_len, grid_z):
    part_count = plane_re.shape[0]
    depth_waves = jnp.arange(part_count, dtype=jnp.int32) // 2
    region_pos = jnp.arange(side_len, dtype=jnp.int32) - BUF
    cos_z, sin_z = phase_tables(anchor_z + region_pos, depth_waves, grid_z)
    return jnp.einsum("tfxy,zt->fxyz", plane_re, cos_z, precision=precise) - jnp.einsum(
        "tfxy,zt->fxyz", plane_im, sin_z, precision=precise
    )


def local(psi_in, v_in, offsets):
    band_count = lax.axis_size("band")
    dom_count = lax.axis_size("dom")
    band_idx = lax.axis_index("band")
    dom_idx = lax.axis_index("dom")
    slab_idx = band_idx % 2
    lower_slab = slab_idx == 0
    side_len = v_in.shape[1]
    half_rows = side_len // 2
    grid_z = CORE * dom_count // 4
    cell_count = 4 * CORE * CORE * grid_z
    wavefunc = psi_in[0, 0]
    other_rows = swapped(wavefunc, "band", 0)
    start_field = jnp.where(
        lower_slab,
        jnp.concatenate([wavefunc, other_rows], 0),
        jnp.concatenate([other_rows, wavefunc], 0),
    )
    potential_in = v_in[0]
    filtered = chebyshev(start_field, potential_in, side_len)
    own_filtered = lax.dynamic_slice_in_dim(filtered, slab_idx * half_rows, half_rows, 0)
    anchor = lax.dynamic_slice_in_dim(offsets, dom_idx, 1, 0)[0]
    slab_cube = own_filtered.reshape(half_rows, side_len, side_len)
    core_rows = lax.dynamic_slice_in_dim(slab_cube, jnp.where(lower_slab, BUF, 0), CORE // 2, 0)
    squares = core_rows[:, BUF : BUF + CORE, BUF : BUF + CORE] ** 2 / (band_count // 2)
    density = lax.dynamic_update_slice_in_dim(
        jnp.zeros((CORE, CORE, CORE), jnp.float32), squares, slab_idx * (CORE // 2), 0
    )
    cos_z, sin_z = phase_tables(
        anchor[2] + jnp.arange(CORE, dtype=jnp.int32), jnp.arange(grid_z, dtype=jnp.int32), grid_z
    )
    z_table = jnp.stack([cos_z, -sin_z], 2).reshape(CORE, 2 * grid_z)
    zparts = jnp.einsum("xyz,zq->qxy", density, z_table, precision=precise)
    own_parts = lax.psum_scatter(zparts, "band", scatter_dimension=0, tiled=True)
    first_part = band_idx * own_parts.shape[0]
    spectrum = plane_spectrum(own_parts, first_part, anchor)
    all_spectra = lax.psum(spectrum, "dom")
    plane_re, plane_im = field_planes(all_spectra, first_part, anchor, side_len, grid_z)
    every_re, every_im = (
        lax.all_gather(plane_re, "band", axis=0, tiled=True),
        lax.all_gather(plane_im, "band", axis=0, tiled=True),
    )
    fields = depth_terms(every_re, every_im, anchor[2], side_len, grid_z)
    fields = fields / cell_count
    density_rows = fields[0].reshape(side_len, side_len * side_len)
    hartree_rows = fields[1].reshape(side_len, side_len * side_len)
    renewed = potential_in + hartree_rows + EXCHANGE_COEF * jnp.cbrt(density_rows)
    result = chebyshev(filtered, renewed, side_len)
    own_result = lax.dynamic_slice_in_dim(result, slab_idx * half_rows, half_rows, 0)
    return own_result[None, None]


def solution(mesh):
    in_specs = (P("dom", "band", None, None), P("dom", None, None), P())
    out_specs = P("dom", "band", None, None)
    return jax.shard_map(local, mesh=mesh, in_specs=in_specs, out_specs=out_specs, check_vma=False)
```

profile of v0, /device:TPU:0, one launch (start us, length us, event | category | flops | bytes accessed | tf_op | source)
XLA Modules:
  0.0 270.2 jit_solution(14124833167229604960)
XLA Ops:
  6.5 1.0 copy.73
  7.5 3.0 %collective-permute-start = (f32[20,1600]{1,0:T(8,128)S(1)}, f32[20,1600]{1,0:T(8,128)S(1)}, u32[]{:S(2)}, u32[]{:S(2)}) collective-permute-start(f32[20,1600]{1,0:T(8,128)S(1)} %bitcast.123), channel_id=1, source_target_pairs={{0,1},{1,0},{2,3},{3,2},{4,5},{5,4},{6,7},{7,6},{8,9},{9,8},{10,11... | collective-permute-start | bytes 384008 | tf_op jit(solution)/shard_map/ppermute | solution.py:23
  10.7 0.7 fusion.371
  12.7 0.7 fusion.252
  13.4 0.7 iota_add_fusion.1
  22.2 3.6 %fusion.374 = f32[64,32,32]{2,0,1:T(8,128)} fusion(f32[32,64,1]{0,1,2:T(8,128)S(1)} %bitcast.125, f32[32,32,32]{2,1,0:T(8,128)S(1)} %fusion.138), kind=kOutput, calls=%fused_computation.461 | convolution fusion | flops 25165824 | bytes 401408 | tf_op jit(solution)/shard_map/xyz,zq->qxy/dot_general | solution.py:161
  26.2 0.7 fusion.335
  27.0 63.4 %reduce-scatter.2.cloned.1.call-done = f32[8,32,32]{2,0,1:T(8,128)} async-done(((f32[64,32,32]{2,0,1:T(8,128)}), f32[8,32,32]{2,0,1:T(8,128)}) %reduce-scatter.2.cloned.1.call-update) | async-done | bytes 32784 | tf_op jit(solution)/shard_map/reduce_scatter | solution.py:162
  90.3 1.3 fusion.147
  92.9 1.3 fusion.145
  95.6 0.9 pad_maximum_fusion
  96.5 32.3 %all-reduce.66.cloned.1.call-done = f32[8,2,64,64]{2,3,0,1:T(8,128)} async-done(((f32[8,2,64,64]{2,3,0,1:T(8,128)}), f32[8,2,64,64]{2,3,0,1:T(8,128)}) %all-reduce.66.cloned.1.call-update) | async-done | bytes 262160 | tf_op jit(solution)/shard_map/psum | solution.py:165
  128.8 1.2 fusion.139
  130.1 1.7 fusion.13
  131.7 1.7 fusion.15
  133.4 1.7 fusion.7
  136.2 1.7 fusion.6
  139.0 54.7 %all_gather.7 = f32[64,2,40,40]{3,2,1,0:T(8,128)S(1)} all-gather(f32[8,2,40,40]{3,2,1,0:T(8,128)S(1)} %convolution_add_fusion), channel_id=1, replica_groups=mesh['dom'=4,'band'=8] {'band'}, dimensions={0}, use_global_device_ids=true | all-gather | bytes 921600 | tf_op jit(solution)/shard_map/all_gather | solution.py:169
  193.6 51.1 %all_gather.6 = f32[64,2,40,40]{3,2,1,0:T(8,128)S(1)} all-gather(f32[8,2,40,40]{3,2,1,0:T(8,128)S(1)} %convolution_subtract_fusion), channel_id=1, replica_groups=mesh['dom'=4,'band'=8] {'band'}, dimensions={0}, use_global_device_ids=true | all-gather | bytes 921600 | tf_op jit(solution)/shard_map/all_gather | solution.py:168
  244.7 4.6 %fusion = f32[2,40,40,40]{3,2,1,0:T(8,128)S(1)} fusion(f32[64,2,40,40]{3,2,1,0:T(8,128)S(1)} %all_gather.7, s32[64]{0:T(128)S(1)} %and_select_fusion.2, s32[40]{0:T(128)S(1)} %fusion.251), kind=kOutput, calls=%fused_computation | convolution fusion | flops 98339840 | bytes 1331616 | tf_op jit(solution)/shard_map/tfxy,zt->fxyz/dot_general | solution.py:124
  249.3 4.6 %subtract_multiply_fusion = f32[2,40,40,40]{3,2,1,0:T(8,128)S(1)} fusion(f32[2,40,40,40]{3,2,1,0:T(8,128)S(1)} %fusion, f32[64,2,40,40]{3,2,1,0:T(8,128)S(1)} %all_gather.6, s32[64]{0:T(128)S(1)} %and_select_fusion.2, s32[40]{0:T(128)S(1)} %fusion.251), kind=kOutput, calls=%fused_computation.4 | convolution fusion | flops 98595840 | bytes 1843616 | tf_op jit(solution)/shard_map/tfxy,zt->fxyz/dot_general | solution.py:124
  254.6 1.0 reshape_squeeze.4
  255.8 1.4 broadcast_multiply_fusion
  262.6 0.7 broadcast_in_dim.182
  (120 shorter events, 20.7 us)
Async XLA Ops:
  6.5 4.1 %copy-start = (s32[4,3]{1,0:T(4,128)S(1)}, s32[4,3]{1,0:T(4,128)}, u32[]{:S(2)}) copy-start(s32[4,3]{1,0:T(4,128)} %param.5) | copy-start | bytes 148
  6.5 9.6 %copy-start.1 = (f32[1,40,1600]{2,1,0:T(8,128)S(1)}, f32[1,40,1600]{2,1,0:T(8,128)}, u32[]{:S(2)}) copy-start(f32[1,40,1600]{2,1,0:T(8,128)} %param.4) | copy-start | bytes 768004
  6.5 83.8 %reduce-scatter.2.cloned.1.call-start = ((), (), s32[]{:S(2)}) async-start(), calls=%async_computation.1 | async-start | bytes 1179648 | tf_op jit(solution)/shard_map/reduce_scatter | solution.py:162
  7.5 8.1 %collective-permute-start = (f32[20,1600]{1,0:T(8,128)S(1)}, f32[20,1600]{1,0:T(8,128)S(1)}, u32[]{:S(2)}, u32[]{:S(2)}) collective-permute-start(f32[20,1600]{1,0:T(8,128)S(1)} %bitcast.123), channel_id=1, source_target_pairs={{0,1},{1,0},{2,3},{3,2},{4,5},{5,4},{6,7},{7,6},{8,9},{9,8},{10,11... | collective-permute-start | bytes 384008 | tf_op jit(solution)/shard_map/ppermute | solution.py:23
  25.9 103.0 %all-reduce.66.cloned.1.call-start = ((), (), s32[]{:S(2)}) async-start(), calls=%async_computation.2 | async-start | bytes 1048576 | tf_op jit(solution)/shard_map/psum | solution.py:165
Sparse Core Ops, SparseCore 0:
  26.0 64.3 reduce-scatter.1
  96.6 32.2 all-reduce.65
where the time goes:
time: 270 us
  blocking collectives  106 us (39%)
  waiting for transfers between devices  95.7 us (35%)
  matrix products  26.9 us (10%)
  between operations  14.1 us (5%)
  other arithmetic  13.8 us (5%)
  local copies, waits for them, and re-layouts  10.8 us (4%)
  starting transfers between devices  3.23 us (1%)
    reduce_scatter x1, waiting for transfers between devices, local(): lax.psum_scatter(zparts, 'band', scatter_dimension=0, tiled=True)  63.4 us
    all_gather x1, blocking collectives, local(): lax.all_gather(plane_im, 'band', axis=0, tiled=True)  54.7 us
    all_gather x1, blocking collectives, local(): lax.all_gather(plane_re, 'band', axis=0, tiled=True)  51.1 us
    psum x1, waiting for transfers between devices, local(): all_spectra = lax.psum(spectrum, 'dom')  32.3 us
  transfers between devices with their start and end apart: 3, of which 2 were waited for; matrix products, arithmetic and copies ran while one was open for 2% of the time, Pallas kernels for 0%

commit v1 on v0

v1 whole, which is shorter than its diff:
```python
import functools
import math

import jax
import jax.numpy as jnp
import numpy as np
from jax import lax
from jax.experimental import pallas as pl
from jax.experimental.pallas import tpu as pltpu
from jax.sharding import PartitionSpec as P

CORE = 32
BUF = 4
DEG = 8

HALF_WIDTH = 4.5
FOUR_PI = 4.0 * math.pi
EXCHANGE_COEF = -((3.0 / math.pi) ** (1.0 / 3.0))
precise = lax.Precision.HIGHEST


def swapped(value, axis, mask):
    pairs = [(source, source ^ mask) for source in range(lax.axis_size(axis))]
    return lax.ppermute(value, axis, pairs)


def wave_basis(length):
    cells = np.arange(length)
    rows, waves = [], []
    for wave in range(length // 2 + 1):
        angle = 2.0 * np.pi * ((wave * cells) % length) / length
        if wave in (0, length // 2):
            rows.append(np.cos(angle) / np.sqrt(length))
            waves.append(wave)
        else:
            rows.append(np.cos(angle) * np.sqrt(2.0 / length))
            rows.append(np.sin(angle) * np.sqrt(2.0 / length))
            waves += [wave, wave]
    return np.array(rows), np.array(waves)


def parity_basis():
    rows, waves = wave_basis(2 * CORE)
    return np.stack([rows[waves % 2 == 0], rows[waves % 2 == 1]]), np.stack(
        [waves[waves % 2 == 0], waves[waves % 2 == 1]]
    )


def eigenvalue(waves, length):
    return 2.0 - 2.0 * np.cos(2.0 * np.pi * waves / length)


def padded(length, unit):
    return -(-length // unit) * unit


def place(is_lower, own, halo, field_ref, half, side):
    cells = side * side
    field_ref[...] = jnp.zeros(field_ref.shape, jnp.float32)

    @pl.when(is_lower)
    def _():
        field_ref[0:half, 0:cells] = own
        field_ref[half : half + DEG, 0:cells] = halo

    @pl.when(jnp.logical_not(is_lower))
    def _():
        field_ref[0:DEG, 0:cells] = halo
        field_ref[DEG : DEG + half, 0:cells] = own


def filtered_field(field, scaled_potential, half, side):
    rows, lanes = field.shape
    row_id = lax.broadcasted_iota(jnp.int32, (rows, lanes), 0)
    lane_id = lax.broadcasted_iota(jnp.int32, (rows, lanes), 1)
    inside = (row_id < half + DEG) & (lane_id < side * side)
    weight = jnp.where(inside, 1.0 / HALF_WIDTH, 0.0)
    column = lane_id % side
    not_first = column != 0
    not_last = column != side - 1

    def beside(values):
        total = pltpu.roll(values, 1, 0) + pltpu.roll(values, rows - 1, 0)
        total = total + pltpu.roll(values, side, 1) + pltpu.roll(values, lanes - side, 1)
        total = total + jnp.where(not_first, pltpu.roll(values, 1, 1), 0.0)
        return total + jnp.where(not_last, pltpu.roll(values, lanes - 1, 1), 0.0)

    previous = field
    current = 0.5 * (scaled_potential * field - weight * beside(field))
    for _ in range(DEG - 1):
        following = scaled_potential * current - weight * beside(current) - previous
        previous, current = current, following
    return current


def own_rows(is_lower, values, half):
    return jnp.where(is_lower, values[0:half], values[DEG : DEG + half])


def first_kernel(bands, slab_ref, psi_ref, halo_ref, pot_ref, filt_ref, dens_ref, field_ref, coef_ref):
    half, cells = psi_ref.shape
    side = 2 * half
    is_lower = slab_ref[0] == 0
    place(is_lower, psi_ref[...], halo_ref[...], field_ref, half, side)
    coef_ref[...] = jnp.zeros(coef_ref.shape, jnp.float32)

    @pl.when(is_lower)
    def _():
        coef_ref[0 : half + DEG, 0:cells] = pot_ref[0 : half + DEG] * (2.0 / HALF_WIDTH)

    @pl.when(jnp.logical_not(is_lower))
    def _():
        coef_ref[0 : half + DEG, 0:cells] = pot_ref[half - DEG : side] * (2.0 / HALF_WIDTH)

    result = filtered_field(field_ref[...], coef_ref[...], half, side)
    filt_ref[...] = own_rows(is_lower, result, half)[:, 0:cells]
    slab = CORE // 2
    core_rows = jnp.where(is_lower, result[BUF : BUF + slab], result[DEG : DEG + slab])
    squares = core_rows * core_rows * (1.0 / bands)
    per_tile = 128 // CORE
    for tile in range(CORE // per_tile):
        pieces = []
        for line in range(tile * per_tile, (tile + 1) * per_tile):
            start = (line + BUF) * side + BUF
            pieces.append(squares[:, start : start + CORE])
        dens_ref[:, tile * 128 : (tile + 1) * 128] = jnp.concatenate(pieces, 1)


def second_kernel(slab_ref, filt_ref, halo_ref, pot_ref, out_ref, field_ref, coef_ref):
    half, cells = filt_ref.shape
    side = 2 * half
    is_lower = slab_ref[0] == 0
    place(is_lower, filt_ref[...], halo_ref[...], field_ref, half, side)
    coef_ref[...] = jnp.zeros(coef_ref.shape, jnp.float32)

    @pl.when(is_lower)
    def _():
        coef_ref[0 : half + DEG, 0:cells] = pot_ref[0 : half + DEG] * (2.0 / HALF_WIDTH)

    @pl.when(jnp.logical_not(is_lower))
    def _():
        coef_ref[0 : half + DEG, 0:cells] = pot_ref[half - DEG : side] * (2.0 / HALF_WIDTH)

    result = filtered_field(field_ref[...], coef_ref[...], half, side)
    out_ref[...] = own_rows(is_lower, result, half)[:, 0:cells]


def field_scratch(half):
    shape = (padded(half + DEG, 8), padded(4 * half * half, 128))
    return [pltpu.VMEM(shape, jnp.float32)] * 2


SMEM = pl.BlockSpec(memory_space=pltpu.SMEM)
VMEM = pl.BlockSpec(memory_space=pltpu.VMEM)
params = pltpu.CompilerParams(vmem_limit_bytes=40 * 1024 * 1024)


def local(psi_in, v_in, offsets):
    band_count = lax.axis_size("band")
    dom_count = lax.axis_size("dom")
    dom_idx = lax.axis_index("dom")
    slab_idx = lax.axis_index("band") % 2
    is_lower = slab_idx == 0
    slab_scalar = slab_idx.astype(jnp.int32).reshape(1)
    side = v_in.shape[1]
    half = side // 2
    cells = side * side
    bands = band_count // 2
    grid_z = CORE * dom_count // 4

    wavefunc = psi_in[0, 0]
    potential = v_in[0]

    def halo_of(rows):
        edge = jnp.where(is_lower, rows[half - DEG : half], rows[0:DEG])
        return swapped(edge, "band", 1)

    filt, dens = pl.pallas_call(
        functools.partial(first_kernel, bands),
        out_shape=(
            jax.ShapeDtypeStruct((half, cells), jnp.float32),
            jax.ShapeDtypeStruct((CORE // 2, CORE * CORE), jnp.float32),
        ),
        in_specs=[SMEM, VMEM, VMEM, VMEM],
        out_specs=(VMEM, VMEM),
        scratch_shapes=field_scratch(half),
        compiler_params=params,
    )(slab_scalar, wavefunc, halo_of(wavefunc), potential)

    mask = 2
    while mask < band_count:
        dens = dens + swapped(dens, "band", mask)
        mask *= 2
    filt_edge, dens = lax.optimization_barrier((filt, dens))
    halo = halo_of(filt_edge)
    beside = swapped(dens, "band", 1)
    cube = jnp.concatenate([jnp.where(is_lower, dens, beside), jnp.where(is_lower, beside, dens)], 0)
    cubes = cube[None]
    masks = [0]
    bit = dom_count // 2
    while bit:
        cubes = jnp.concatenate([cubes, swapped(cubes, "dom", bit)], 0)
        masks = masks + [one | bit for one in masks]
        bit //= 2

    anchor = lax.dynamic_slice_in_dim(offsets, dom_idx, 1, 0)[0]
    others = jnp.take(offsets, dom_idx ^ jnp.array(masks, jnp.int32), axis=0)
    shift = (others - anchor) // CORE
    shift = jnp.stack([shift[:, 0] % 2, shift[:, 1] % 2, shift[:, 2] % (grid_z // CORE)], 1)
    basis, waves = parity_basis()
    z_basis, z_waves = wave_basis(grid_z)
    parity = jnp.arange(2)
    sign_x = 1.0 - 2.0 * ((shift[:, 0:1] * parity) % 2).astype(jnp.float32)
    sign_y = 1.0 - 2.0 * ((shift[:, 1:2] * parity) % 2).astype(jnp.float32)
    z_tables = z_basis.T.reshape(grid_z // CORE, CORE, grid_z).astype(np.float32)
    into_z = jnp.take(jnp.asarray(z_tables), shift[:, 2], axis=0)
    into_z = sign_x[:, :, None, None, None] * sign_y[:, None, :, None, None] * into_z[:, None, None]
    region = np.arange(side) - BUF
    inner = basis[:, :, :CORE].astype(np.float32)
    outer = basis[:, :, region % (2 * CORE)].astype(np.float32)
    outer_z = z_basis[:, region % grid_z].astype(np.float32)
    eigen = eigenvalue(waves, 2 * CORE)
    lam = (
        eigen[:, None, :, None, None]
        + eigen[None, :, None, :, None]
        + eigenvalue(z_waves, grid_z)[None, None, None, None, :]
    )
    lam[0, 0, 0, 0, 0] = np.inf
    factor = (FOUR_PI / lam).astype(np.float32)
    grid_cubes = cubes.reshape(dom_count, CORE, CORE, CORE)
    spec = jnp.einsum("jxyz,jpqzk->pqxyk", grid_cubes, into_z, precision=precise)
    spec = jnp.einsum("pqxyk,pax->pqayk", spec, inner, precision=precise)
    spec = jnp.einsum("pqayk,qby->pqabk", spec, inner, precision=precise)
    spec = spec * factor
    field = jnp.einsum("pqabk,pax->qxbk", spec, outer, precision=precise)
    field = jnp.einsum("qxbk,qby->xyk", field, outer, precision=precise)
    hartree = jnp.einsum("xyk,kz->xyz", field, outer_z, precision=precise)
    place_of = (shift[:, 2] * 2 + shift[:, 1]) * 2 + shift[:, 0]
    by_place = jnp.zeros_like(grid_cubes).at[place_of].set(grid_cubes)
    by_place = by_place.reshape(grid_z // CORE, 2, 2, CORE, CORE, CORE)
    density = jnp.transpose(by_place, (2, 3, 1, 4, 0, 5)).reshape(2 * CORE, 2 * CORE, grid_z)
    density = jnp.concatenate([density[-BUF:], density[: CORE + BUF]], 0)
    density = jnp.concatenate([density[:, -BUF:], density[:, : CORE + BUF]], 1)
    z_index = region % grid_z
    density = jnp.take(density, jnp.asarray(z_index), axis=2)
    renewed = potential + hartree.reshape(side, cells) + EXCHANGE_COEF * jnp.cbrt(density.reshape(side, cells))

    result = pl.pallas_call(
        second_kernel,
        out_shape=jax.ShapeDtypeStruct((half, cells), jnp.float32),
        in_specs=[SMEM, VMEM, VMEM, VMEM],
        out_specs=VMEM,
        scratch_shapes=field_scratch(half),
        compiler_params=params,
    )(slab_scalar, filt, halo, renewed)
    return result[None, None]


def solution(mesh):
    in_specs = (P("dom", "band", None, None), P("dom", None, None), P())
    out_specs = P("dom", "band", None, None)
    return jax.shard_map(local, mesh=mesh, in_specs=in_specs, out_specs=out_specs, check_vma=False)
```

time: 270 us -> 81.9 us (0.30)
  blocking collectives: 106 us -> 0 us
  waiting for transfers between devices: 95.7 us -> 9.72 us
  local copies, waits for them, and re-layouts: 10.8 us -> 30.2 us
  between operations: 14.1 us -> 0.35 us
  other arithmetic: 13.8 us -> 2.58 us
  starting transfers between devices: 3.23 us -> 14 us
  matrix products: 26.9 us -> 20.2 us
  Pallas kernels: 0 us -> 4.58 us
    all_gather x2 -> x0, blocking collectives: 106 us -> none  [the longest x1 54.7 us: local(): lax.all_gather(plane_im, 'band', axis=0, tiled=True)]
    reduce_scatter x1 -> x0, waiting for transfers between devices: 63.4 us -> none  [local(): lax.psum_scatter(zparts, 'band', scatter_dimension=0, tiled=True)]
    psum x1 -> x0, waiting for transfers between devices: 32.3 us -> none  [local(): all_spectra = lax.psum(spectrum, 'dom')]
    ppermute x1 -> x7, starting transfers between devices: 3 us -> 14 us  [swapped(): return lax.ppermute(value, axis, pairs)]
    ppermute x1 -> x7, waiting for transfers between devices: 0.01 us -> 9.72 us  [swapped(): return lax.ppermute(value, axis, pairs)]
    transpose x0 -> x3, local copies, waits for them, and re-layouts: none -> 8.95 us  [the longest x1 3.25 us: local(): spec = jnp.einsum('pqxyk,pax->pqayk', spec, inner, precision=precise)]
    dot_general x17 -> x6, matrix products: 26.9 us -> 20.2 us  [the longest x1 7.31 us: local(): jnp.einsum('jxyz,jpqzk->pqxyk', grid_cubes, into_z, precision=precise)]
    slice x65 -> x3, local copies, waits for them, and re-layouts: 7.44 us -> 1.58 us  [the longest x1 0.88 us: halo_of(): edge = jnp.where(is_lower, rows[half - DEG:half], rows[0:DEG])]
  transfers between devices with their start and end apart: 3 -> 7, of which waited for: 2 -> 4; matrix products, arithmetic and copies ran while one was open for 2% -> 61% of each run, Pallas kernels for 0% -> 0%
where the time goes in v1:
time: 81.9 us; the launch traced here: 81.5 us
  local copies, waits for them, and re-layouts  30.2 us (37%)
  matrix products  20.2 us (25%)
  starting transfers between devices  14 us (17%)
  waiting for transfers between devices  9.72 us (12%)
  Pallas kernels  4.58 us (6%)
  other arithmetic  2.58 us (3%)
    ppermute x7, starting transfers between devices, swapped(): return lax.ppermute(value, axis, pairs)  14 us
    ppermute x7, waiting for transfers between devices, swapped(): return lax.ppermute(value, axis, pairs)  9.72 us
    dot_general x1, matrix products, local(): jnp.einsum('jxyz,jpqzk->pqxyk', grid_cubes, into_z, precision=precise)  7.31 us
    reshape x2, local copies, waits for them, and re-layouts, local(): jnp.transpose(by_place, (2, 3, 1, 4, 0, 5))  5.66 us
    dot_general x1, matrix products, local(): spec = jnp.einsum('pqayk,qby->pqabk', spec, inner, precision=precise)  4.18 us
    mul x1, local copies, waits for them, and re-layouts, local(): spec = spec * factor  3.51 us
    transpose x1, local copies, waits for them, and re-layouts, local(): spec = jnp.einsum('pqxyk,pax->pqayk', spec, inner, precision=precise)  3.25 us
    transpose x1, local copies, waits for them, and re-layouts, local(): jnp.einsum('jxyz,jpqzk->pqxyk', grid_cubes, into_z, precision=precise)  3.25 us
  transfers between devices with their start and end apart: 7, of which 4 were waited for; matrix products, arithmetic and copies ran while one was open for 61% of the time, Pallas kernels for 0%

profile of v1, /device:TPU:0, one launch (start us, length us, event | category | flops | bytes accessed | tf_op | source)
XLA Modules:
  0.0 81.5 jit_solution(7560990516581358359)
XLA Ops:
  0.9 3.0 %collective-permute-start = (f32[8,1600]{1,0:T(8,128)S(1)}, f32[8,1600]{1,0:T(8,128)S(1)}, u32[]{:S(2)}, u32[]{:S(2)}) collective-permute-start(f32[8,1600]{1,0:T(8,128)S(1)} %fusion.10), channel_id=1, source_target_pairs={{0,1},{1,0},{2,3},{3,2},{4,5},{5,4},{6,7},{7,6},{8,9},{9,8},{10,11... | collective-permute-start | bytes 153608 | tf_op jit(solution)/shard_map/ppermute | solution.py:24
  7.1 2.4 %shard_map.118 = (f32[20,1600]{1,0:T(8,128)S(1)}, f32[16,1024]{1,0:T(8,128)S(1)}) custom-call(s32[1]{0:T(128)} %bitcast.slab_ref, f32[20,1600]{1,0:T(8,128)S(1)} %bitcast.72, f32[8,1600]{1,0:T(8,128)S(1)} %collective-permute-done.halo_ref, f32[40,1600]{1,0:T(8,128)S(1)} %bitcast.71), custom_call_target="tpu_custom_call" | custom-call | tf_op jit(solution)/shard_map/pallas_call | solution.py:178
  9.4 2.1 %collective-permute-start.1 = (f32[16,1024]{1,0:T(8,128)S(1)}, f32[16,1024]{1,0:T(8,128)S(1)}, u32[]{:S(2)}, u32[]{:S(2)}) collective-permute-start(f32[16,1024]{1,0:T(8,128)S(1)} %get-tuple-element.10), channel_id=1, source_target_pairs={{0,2},{1,3},{2,0},{3,1},{4,6},{5,7},{6,4},{7,5},{8,10},{9,11},{10,... | collective-permute-start | bytes 196616 | tf_op jit(solution)/shard_map/ppermute | solution.py:24
  11.6 2.2 %collective-permute-done.1 = f32[16,1024]{1,0:T(8,128)S(1)} collective-permute-done((f32[16,1024]{1,0:T(8,128)S(1)}, f32[16,1024]{1,0:T(8,128)S(1)}, u32[]{:S(2)}, u32[]{:S(2)}) %collective-permute-start.1) | collective-permute-done | bytes 65568 | tf_op jit(solution)/shard_map/ppermute | solution.py:24
  13.8 3.1 %collective-permute-start.2 = (f32[16,1024]{1,0:T(8,128)S(1)}, f32[16,1024]{1,0:T(8,128)S(1)}, u32[]{:S(2)}, u32[]{:S(2)}) collective-permute-start(f32[16,1024]{1,0:T(8,128)S(1)} %add.85), channel_id=1, source_target_pairs={{0,4},{1,5},{2,6},{3,7},{4,0},{5,1},{6,2},{7,3},{8,12},{9,13},{10,... | collective-permute-start | bytes 196616 | tf_op jit(solution)/shard_map/ppermute | solution.py:24
  17.1 2.0 %collective-permute-done.2 = f32[16,1024]{1,0:T(8,128)S(1)} collective-permute-done((f32[16,1024]{1,0:T(8,128)S(1)}, f32[16,1024]{1,0:T(8,128)S(1)}, u32[]{:S(2)}, u32[]{:S(2)}) %collective-permute-start.2) | collective-permute-done | bytes 65568 | tf_op jit(solution)/shard_map/ppermute | solution.py:24
  19.1 1.9 %collective-permute-start.4 = (f32[16,1024]{1,0:T(8,128)S(1)}, f32[16,1024]{1,0:T(8,128)S(1)}, u32[]{:S(2)}, u32[]{:S(2)}) collective-permute-start(f32[16,1024]{1,0:T(8,128)S(1)} %add.86), channel_id=1, source_target_pairs={{0,1},{1,0},{2,3},{3,2},{4,5},{5,4},{6,7},{7,6},{8,9},{9,8},{10,11... | collective-permute-start | bytes 196616 | tf_op jit(solution)/shard_map/ppermute | solution.py:24
  21.0 2.4 %collective-permute-done.4 = f32[16,1024]{1,0:T(8,128)S(1)} collective-permute-done((f32[16,1024]{1,0:T(8,128)S(1)}, f32[16,1024]{1,0:T(8,128)S(1)}, u32[]{:S(2)}, u32[]{:S(2)}) %collective-permute-start.4) | collective-permute-done | bytes 65568 | tf_op jit(solution)/shard_map/ppermute | solution.py:24
  23.5 1.9 %collective-permute-start.5 = (f32[1,32,1024]{2,1,0:T(8,128)S(1)}, f32[1,32,1024]{2,1,0:T(8,128)S(1)}, u32[]{:S(2)}, u32[]{:S(2)}) collective-permute-start(f32[1,32,1024]{2,1,0:T(8,128)S(1)} %get-tuple-element.21), channel_id=1, source_target_pairs={{0,16},{8,24},{16,0},{24,8},{1,17},{9,25},{17,1},{25,9},{2,18},{10... | collective-permute-start | bytes 393224 | tf_op jit(solution)/shard_map/ppermute | solution.py:24
  25.4 3.1 %collective-permute-done.5 = f32[1,32,1024]{2,1,0:T(8,128)S(1)} collective-permute-done((f32[1,32,1024]{2,1,0:T(8,128)S(1)}, f32[1,32,1024]{2,1,0:T(8,128)S(1)}, u32[]{:S(2)}, u32[]{:S(2)}) %collective-permute-start.5) | collective-permute-done | bytes 131104 | tf_op jit(solution)/shard_map/ppermute | solution.py:24
  28.7 1.9 %collective-permute-start.3 = (f32[8,1600]{1,0:T(8,128)S(1)}, f32[8,1600]{1,0:T(8,128)S(1)}, u32[]{:S(2)}, u32[]{:S(2)}) collective-permute-start(f32[8,1600]{1,0:T(8,128)S(1)} %slice_select_fusion), channel_id=1, source_target_pairs={{0,1},{1,0},{2,3},{3,2},{4,5},{5,4},{6,7},{7,6},{8,9},{9,8},{10,11... | collective-permute-start | bytes 153608 | tf_op jit(solution)/shard_map/ppermute | solution.py:24
  32.2 1.5 %copy.45 = f32[4,32,32,32]{3,2,1,0:T(8,128)} copy(f32[4,32,32,32]{3,2,0,1:T(8,128)S(1)} %pad_maximum_fusion) | data formatting | bytes 1048576 | tf_op jit(solution)/shard_map/concatenate | solution.py:202
  34.0 2.6 %scatter_fusion = f32[4,32,32,32]{3,2,1,0:T(8,128)S(1)} fusion(f32[4,32,32,32]{3,2,1,0:T(8,128)S(1)} %broadcast_in_dim.51, s32[4]{0:T(128)S(1)} %get-tuple-element.14, f32[4,32,32,32]{3,2,1,0:T(8,128)} %copy.45), kind=kCustom, calls=%fused_computation.2 | custom fusion | bytes 1572880 | tf_op jit(solution)/shard_map/scatter | solution.py:239
  36.6 3.0 %copy.58 = f32[2,32,2,32,1,32]{3,2,1,0,5,4:T(2,128)} copy(f32[2,32,2,32,1,32]{5,3,1,0,2,4:T(8,128)S(1)} %bitcast.74) | data formatting | bytes 1048576 | tf_op jit(solution)/shard_map/reshape | solution.py:241
  39.6 2.7 %reshape.159 = f32[64,64,32]{1,0,2:T(8,128)S(1)} reshape(f32[2,32,2,32,1,32]{3,2,1,0,5,4:T(2,128)} %copy.58) | data formatting | bytes 1048576 | tf_op jit(solution)/shard_map/reshape | solution.py:241
  43.0 7.3 %fusion.2 = f32[2,2,32,32,32]{3,4,2,1,0:T(8,128)} fusion(f32[32,32]{0,1:T(8,128)} %constant.151, f32[4,2,2]{0,2,1:T(2,128)S(1)} %broadcast_multiply_fusion, f32[1,32,32,32]{3,2,0,1:T(8,128)} %bitcast.78, f32[1,32,32,32]{3,2,0,1:T(8,128)S(1)} %bitcast.76, f32[2,32,32,32]{3,2,1,0:T(8,128)S(1)} %copy-done.4), kind=kOutput, calls=%fused_computation.8 | convolution fusion | flops 201605120 | bytes 1052736 | tf_op jit(solution)/shard_map/jxyz,jpqzk->pqxyk/dot_general | solution.py:231
  50.3 3.2 %copy.41 = f32[2,2,32,32,32]{2,4,3,1,0:T(8,128)S(1)} copy(f32[2,2,32,32,32]{3,4,2,1,0:T(8,128)} %fusion.2) | data formatting | bytes 1048576 | tf_op jit(solution)/shard_map/jxyz,jpqzk->pqxyk/transpose | solution.py:231
  53.6 3.2 %convolution_bitcast_fusion = f32[2,2,32,32,32]{2,4,3,1,0:T(8,128)} fusion(f32[2,2,32,32,32]{2,4,3,1,0:T(8,128)S(1)} %copy.41, f32[2,32,32,1,1]{2,1,4,3,0:T(8,128)S(1)} %copy-done.7), kind=kOutput, calls=%fused_computation.7 | convolution fusion | flops 50331648 | bytes 1056768 | tf_op jit(solution)/shard_map/pqxyk,pax->pqayk/dot_general | solution.py:232
  56.8 3.3 %copy.42 = f32[2,2,32,32,32]{3,4,2,0,1:T(8,128)S(1)} copy(f32[2,2,32,32,32]{2,4,3,1,0:T(8,128)} %convolution_bitcast_fusion) | data formatting | bytes 1048576 | tf_op jit(solution)/shard_map/pqxyk,pax->pqayk/transpose | solution.py:232
  60.1 4.2 %multiply_bitcast_fusion = f32[2,2,32,32,32]{3,4,2,0,1:T(8,128)} fusion(f32[2,2,32,32,32]{4,3,2,1,0:T(8,128)} %constant.160, f32[2,2,32,32,32]{3,4,2,0,1:T(8,128)S(1)} %copy.42, f32[2,32,32,1,1]{2,1,4,3,0:T(8,128)S(1)} %copy-done.7), kind=kOutput, calls=%fused_computation.6 | convolution fusion | flops 50462720 | bytes 1581056 | tf_op jit(solution)/shard_map/pqayk,qby->pqabk/dot_general | solution.py:233
  64.3 3.5 %copy.43 = f32[2,2,32,32,32]{2,4,0,3,1:T(8,128)S(1)} copy(f32[2,2,32,32,32]{3,4,2,0,1:T(8,128)} %multiply_bitcast_fusion) | data formatting | bytes 1048576 | tf_op jit(solution)/shard_map/mul | solution.py:234
  67.8 2.8 %convolution_bitcast_fusion.1 = f32[2,40,32,32]{1,3,2,0:T(8,128)} fusion(f32[2,2,32,32,32]{2,4,0,3,1:T(8,128)S(1)} %copy.43, f32[2,32,40,1,1]{2,1,0,4,3:T(8,128)S(1)} %copy-done.9), kind=kOutput, calls=%fused_computation.9 | convolution fusion | flops 62914560 | bytes 862208 | tf_op jit(solution)/shard_map/pqabk,pax->qxbk/dot_general | solution.py:235
  70.6 2.4 %copy.44 = f32[2,40,32,32]{2,3,0,1:T(8,128)S(1)} copy(f32[2,40,32,32]{1,3,2,0:T(8,128)} %convolution_bitcast_fusion.1) | data formatting | bytes 655360 | tf_op jit(solution)/shard_map/pqabk,pax->qxbk/transpose | solution.py:235
  78.5 2.2 %shard_map.119 = f32[20,1600]{1,0:T(8,128)S(1)} custom-call(s32[1]{0:T(128)} %bitcast.slab_ref, f32[20,1600]{1,0:T(8,128)S(1)} %get-tuple-element.11.filt_ref, f32[8,1600]{1,0:T(8,128)S(1)} %collective-permute-done.3.halo_ref, f32[40,1600]{1,0:T(8,128)S(1)} %add_add_fusion.pot_ref), custom_call_target="tpu_custom_call" | custom-call | tf_op jit(solution)/shard_map/pallas_call | solution.py:248
  (64 shorter events, 13.3 us)
Async XLA Ops:
  0.0 4.6 %copy-start = (s32[4,3]{1,0:T(4,128)S(1)}, s32[4,3]{1,0:T(4,128)}, u32[]{:S(2)}) copy-start(s32[4,3]{1,0:T(4,128)} %param.14) | copy-start | bytes 148
  0.0 25.4 %copy-start.11 = (s32[40]{0:T(128)S(1)}, s32[40]{0:T(128)}, u32[]{:S(2)}) copy-start(s32[40]{0:T(128)} %constant.161) | copy-start | bytes 484
  0.9 5.2 %collective-permute-start = (f32[8,1600]{1,0:T(8,128)S(1)}, f32[8,1600]{1,0:T(8,128)S(1)}, u32[]{:S(2)}, u32[]{:S(2)}) collective-permute-start(f32[8,1600]{1,0:T(8,128)S(1)} %fusion.10), channel_id=1, source_target_pairs={{0,1},{1,0},{2,3},{3,2},{4,5},{5,4},{6,7},{7,6},{8,9},{9,8},{10,11... | collective-permute-start | bytes 153608 | tf_op jit(solution)/shard_map/ppermute | solution.py:24
  6.1 1.0 %copy-start.1 = (f32[1,40,1600]{2,1,0:T(8,128)S(1)}, f32[1,40,1600]{2,1,0:T(8,128)}, u32[]{:S(2)}) copy-start(f32[1,40,1600]{2,1,0:T(8,128)} %param.13) | copy-start | bytes 768004
  9.4 4.3 %collective-permute-start.1 = (f32[16,1024]{1,0:T(8,128)S(1)}, f32[16,1024]{1,0:T(8,128)S(1)}, u32[]{:S(2)}, u32[]{:S(2)}) collective-permute-start(f32[16,1024]{1,0:T(8,128)S(1)} %get-tuple-element.10), channel_id=1, source_target_pairs={{0,2},{1,3},{2,0},{3,1},{4,6},{5,7},{6,4},{7,5},{8,10},{9,11},{10,... | collective-permute-start | bytes 196616 | tf_op jit(solution)/shard_map/ppermute | solution.py:24
  13.8 5.3 %collective-permute-start.2 = (f32[16,1024]{1,0:T(8,128)S(1)}, f32[16,1024]{1,0:T(8,128)S(1)}, u32[]{:S(2)}, u32[]{:S(2)}) collective-permute-start(f32[16,1024]{1,0:T(8,128)S(1)} %add.85), channel_id=1, source_target_pairs={{0,4},{1,5},{2,6},{3,7},{4,0},{5,1},{6,2},{7,3},{8,12},{9,13},{10,... | collective-permute-start | bytes 196616 | tf_op jit(solution)/shard_map/ppermute | solution.py:24
  19.1 4.3 %collective-permute-start.4 = (f32[16,1024]{1,0:T(8,128)S(1)}, f32[16,1024]{1,0:T(8,128)S(1)}, u32[]{:S(2)}, u32[]{:S(2)}) collective-permute-start(f32[16,1024]{1,0:T(8,128)S(1)} %add.86), channel_id=1, source_target_pairs={{0,1},{1,0},{2,3},{3,2},{4,5},{5,4},{6,7},{7,6},{8,9},{9,8},{10,11... | collective-permute-start | bytes 196616 | tf_op jit(solution)/shard_map/ppermute | solution.py:24
  23.5 5.0 %collective-permute-start.5 = (f32[1,32,1024]{2,1,0:T(8,128)S(1)}, f32[1,32,1024]{2,1,0:T(8,128)S(1)}, u32[]{:S(2)}, u32[]{:S(2)}) collective-permute-start(f32[1,32,1024]{2,1,0:T(8,128)S(1)} %get-tuple-element.21), channel_id=1, source_target_pairs={{0,16},{8,24},{16,0},{24,8},{1,17},{9,25},{17,1},{25,9},{2,18},{10... | collective-permute-start | bytes 393224 | tf_op jit(solution)/shard_map/ppermute | solution.py:24
  28.6 2.3 %collective-permute-start.6 = (f32[2,32,1024]{2,1,0:T(8,128)S(1)}, f32[2,32,1024]{2,1,0:T(8,128)S(1)}, u32[]{:S(2)}, u32[]{:S(2)}) collective-permute-start(f32[2,32,1024]{2,1,0:T(8,128)S(1)} %pad_maximum_fusion.2), channel_id=1, source_target_pairs={{0,8},{8,0},{16,24},{24,16},{1,9},{9,1},{17,25},{25,17},{2,10},{10... | collective-permute-start | bytes 786440 | tf_op jit(solution)/shard_map/ppermute | solution.py:24
  28.7 49.9 %collective-permute-start.3 = (f32[8,1600]{1,0:T(8,128)S(1)}, f32[8,1600]{1,0:T(8,128)S(1)}, u32[]{:S(2)}, u32[]{:S(2)}) collective-permute-start(f32[8,1600]{1,0:T(8,128)S(1)} %slice_select_fusion), channel_id=1, source_target_pairs={{0,1},{1,0},{2,3},{3,2},{4,5},{5,4},{6,7},{7,6},{8,9},{9,8},{10,11... | collective-permute-start | bytes 153608 | tf_op jit(solution)/shard_map/ppermute | solution.py:24
  30.9 0.8 copy-start.5
  31.3 1.0 %copy-start.3 = (f32[2,32,32,32]{3,2,1,0:T(8,128)}, f32[2,32,32,32]{3,2,1,0:T(8,128)S(1)}, u32[]{:S(2)}) copy-start(f32[2,32,32,32]{3,2,1,0:T(8,128)S(1)} %concatenate.27) | copy-start | bytes 786436
  39.6 3.4 %copy-start.4 = (f32[2,32,32,32]{3,2,1,0:T(8,128)S(1)}, f32[2,32,32,32]{3,2,1,0:T(8,128)}, u32[]{:S(2)}) copy-start(f32[2,32,32,32]{3,2,1,0:T(8,128)} %copy-done.3) | copy-start | bytes 786436
  50.3 3.3 %copy-start.7 = (f32[2,32,32,1,1]{2,1,4,3,0:T(8,128)S(1)}, f32[2,32,32,1,1]{2,1,4,3,0:T(8,128)}, u32[]{:S(2)}) copy-start(f32[2,32,32,1,1]{2,1,4,3,0:T(8,128)} %constant.162) | copy-start | bytes 24580
  64.3 3.5 %copy-start.9 = (f32[2,32,40,1,1]{2,1,0,4,3:T(8,128)S(1)}, f32[2,32,40,1,1]{2,1,0,4,3:T(8,128)}, u32[]{:S(2)}) copy-start(f32[2,32,40,1,1]{2,1,0,4,3:T(8,128)} %constant.163) | copy-start | bytes 30724
  67.8 5.3 %copy-start.8 = (f32[2,32,40,1]{2,1,0,3:T(8,128)S(1)}, f32[2,32,40,1]{2,1,0,3:T(8,128)}, u32[]{:S(2)}) copy-start(f32[2,32,40,1]{2,1,0,3:T(8,128)} %constant.164) | copy-start | bytes 30724
  70.6 3.7 %copy-start.10 = (f32[32,40,1]{1,0,2:T(8,128)S(1)}, f32[32,40,1]{1,0,2:T(8,128)}, u32[]{:S(2)}) copy-start(f32[32,40,1]{1,0,2:T(8,128)} %constant.165) | copy-start | bytes 15364
  73.1 3.0 %copy-start.6 = (f32[4,64,32]{1,0,2:T(4,128)S(1)}, f32[4,64,32]{1,0,2:T(4,128)}, u32[]{:S(2)}) copy-start(f32[4,64,32]{1,0,2:T(4,128)} %slice.47) | copy-start | bytes 98308
  77.2 1.2 %copy-start.2 = (f32[1,40,1600]{2,1,0:T(8,128)S(1)}, f32[1,40,1600]{2,1,0:T(8,128)}, u32[]{:S(2)}) copy-start(f32[1,40,1600]{2,1,0:T(8,128)} %param.13) | copy-start | bytes 768004

commit v2 on v1

--- a/solution.py
+++ b/solution.py
@@ -3,6 +3,7 @@
 
 import jax
 import jax.numpy as jnp
+import ml_dtypes
 import numpy as np
 from jax import lax
 from jax.experimental import pallas as pl
@@ -16,7 +17,6 @@
 HALF_WIDTH = 4.5
 FOUR_PI = 4.0 * math.pi
 EXCHANGE_COEF = -((3.0 / math.pi) ** (1.0 / 3.0))
-precise = lax.Precision.HIGHEST
 
 
 def swapped(value, axis, mask):
@@ -126,28 +126,238 @@
         dens_ref[:, tile * 128 : (tile + 1) * 128] = jnp.concatenate(pieces, 1)
 
 
-def second_kernel(slab_ref, filt_ref, halo_ref, pot_ref, out_ref, field_ref, coef_ref):
+def split2(values):
+    high = values.astype(jnp.bfloat16)
+    return high, (values - high.astype(jnp.float32)).astype(jnp.bfloat16)
+
+
+def split3(values):
+    high = values.astype(jnp.bfloat16)
+    rest = values - high.astype(jnp.float32)
+    middle = rest.astype(jnp.bfloat16)
+    return high, middle, (rest - middle.astype(jnp.float32)).astype(jnp.bfloat16)
+
+
+def dot(left, right):
+    return jnp.dot(left, right, preferred_element_type=jnp.float32)
+
+
+def table_parts(table):
+    high = table.astype(ml_dtypes.bfloat16)
+    return high, (table - high.astype(np.float64)).astype(ml_dtypes.bfloat16)
+
+
+def left_table(table):
+    high, low = table_parts(table)
+    return np.concatenate([high, low, high], -1)
+
+
+def stacked(values):
+    high, low = split2(values)
+    return jnp.concatenate([high, high, low], 0)
+
+
+@functools.lru_cache(maxsize=None)
+def solver_tables(side, grid_z):
+    half = side // 2
+    blocks_z = grid_z // CORE
+    basis, waves = parity_basis()
+    z_basis, z_waves = wave_basis(grid_z)
+    lines = 128 // CORE
+    into = []
+    for place_z in range(blocks_z):
+        along_z = z_basis[:, place_z * CORE : (place_z + 1) * CORE].T
+        for place_y in range(2):
+            for place_x in range(2):
+                signs = [(-1.0) ** (px * place_x + py * place_y) for px in range(2) for py in range(2)]
+                table = np.kron(np.eye(lines), np.concatenate([sign * along_z for sign in signs], 1))
+                high, low = table_parts(table)
+                into += [high, high, low]
+    into = np.concatenate(into, 0)
+    forward = left_table(np.concatenate([basis[0, :, :CORE], basis[1, :, :CORE]], 0))
+    region = np.arange(side) - BUF
+    outer = basis[:, :, region % (2 * CORE)]
+    back_y = left_table(np.concatenate([outer[0].T, outer[1].T], 0))
+    back_x = []
+    for first_row in (0, half - DEG):
+        rows = outer[:, :, first_row : first_row + half + DEG]
+        rows = np.pad(rows, ((0, 0), (0, 0), (0, padded(half + DEG, 8) - half - DEG)))
+        back_x.append(left_table(np.concatenate([rows[0].T, rows[1].T], 0)))
+    back_x = np.stack(back_x)
+    outer_z = np.zeros((4, grid_z, 128))
+    outer_z[:, :, :side] = z_basis[:, region % grid_z]
+    high, low = table_parts(outer_z.reshape(4 * grid_z, 128))
+    back_z = np.block([[high, low], [high, np.zeros_like(low)]])
+    eigen = eigenvalue(waves, 2 * CORE)
+    lam = (
+        eigen.T[:, None, :, None, None]
+        + eigen.T[None, :, None, :, None]
+        + eigenvalue(z_waves, grid_z)[None, None, None, None, :]
+    )
+    lam[0, 0, 0, 0, 0] = np.inf
+    factor = (FOUR_PI / lam).reshape(CORE * CORE, 4 * grid_z).astype(np.float32)
+    spread = np.zeros((blocks_z, 3, CORE, side))
+    for cell, pos in enumerate(region % grid_z):
+        spread[pos // CORE, :, pos % CORE, cell] = 1.0
+    spread = np.concatenate(
+        [np.kron(np.eye(lines), spread[block, part]) for block in range(blocks_z) for part in range(3)], 0
+    ).astype(ml_dtypes.bfloat16)
+    return dict(
+        into=into, forward=forward, back_y=back_y, back_x=back_x, back_z=back_z, factor=factor, spread=spread
+    )
+
+
+def cube_root(values):
+    positive = values > 0.0
+    safe = jnp.where(positive, values, 1.0)
+    root = jnp.exp(jnp.log(safe) * (1.0 / 3.0))
+    root = root - (root - safe / (root * root)) * (1.0 / 3.0)
+    return jnp.where(positive, root, 0.0)
+
+
+def second_kernel(
+    masks, index_ref, offsets_ref, cubes_ref, filt_ref, halo_ref, pot_ref,
+    into_ref, forward_ref, back_y_ref, back_x_ref, back_z_ref, factor_ref, spread_ref,
+    out_ref, field_ref, coef_ref, dens_ref, left_ref, rows_ref, waves_ref, mixed_ref, flat_ref,
+):
     half, cells = filt_ref.shape
     side = 2 * half
-    is_lower = slab_ref[0] == 0
+    slab, dom = index_ref[0], index_ref[1]
+    is_lower = slab == 0
+    dom_count = len(masks)
+    blocks_z = dom_count // 4
+    grid_z = CORE * blocks_z
+    lanes = 4 * grid_z
+    columns = lanes // 128
+    tiles = CORE * CORE // 128
+    lines = 128 // CORE
+    field_rows = field_ref.shape[0]
+
+    place_of = []
+    for mask in masks:
+        other = dom ^ mask
+        at_x = (offsets_ref[other, 0] != offsets_ref[dom, 0]).astype(jnp.int32)
+        at_y = (offsets_ref[other, 1] != offsets_ref[dom, 1]).astype(jnp.int32)
+        at_z = (offsets_ref[other, 2] - offsets_ref[dom, 2]) // CORE
+        at_z = jnp.where(at_z < 0, at_z + blocks_z, at_z)
+        place_of.append((at_z * 2 + at_y) * 2 + at_x)
+    cube_at = []
+    for where in range(dom_count):
+        found = jnp.int32(0)
+        for idx in range(dom_count):
+            found = found + jnp.where(place_of[idx] == where, idx, 0)
+        cube_at.append(found)
+
+    mean = jnp.sum(cubes_ref[...]) * (1.0 / (dom_count * CORE * CORE * CORE))
+
+    for where in range(dom_count):
+        for tile in range(tiles):
+            part = cubes_ref[cube_at[where], :, tile * 128 : (tile + 1) * 128] - mean
+            high, low = split2(part)
+            rows = slice(tile * CORE, (tile + 1) * CORE)
+            for idx, piece in enumerate((high, low, high)):
+                left_ref[rows, (where * 3 + idx) * 128 : (where * 3 + idx + 1) * 128] = piece
+    product = dot(left_ref[...], into_ref[...])
+    for tile in range(tiles):
+        for line in range(lines):
+            y = tile * lines + line
+            for col in range(columns):
+                start = line * lanes + col * 128
+                rows_ref[col, y * CORE : (y + 1) * CORE, :] = product[
+                    tile * CORE : (tile + 1) * CORE, start : start + 128
+                ]
+
+    group = max(1, 256 // lanes)
+    lane_id = lax.broadcasted_iota(jnp.int32, (1, group * lanes), 1) % lanes
+    even_x = lane_id < 2 * grid_z
+    even_y = (lane_id // grid_z) % 2 == 0
+
+    def side_by_side(ref, starts, stride, count):
+        pieces = []
+        for start in starts:
+            for col in range(columns):
+                if stride == 1:
+                    pieces.append(ref[col, pl.ds(start, count), :])
+                else:
+                    pieces.append(ref[col, pl.ds(start, count, stride=stride), :])
+        return jnp.concatenate(pieces, 1)
+
+    def scatter(ref, starts, values, count):
+        for idx, start in enumerate(starts):
+            for col in range(columns):
+                at = (idx * columns + col) * 128
+                ref[col, start : start + count, :] = values[:, at : at + 128]
+
+    forward = forward_ref[...]
+    for first in range(0, CORE, group):
+        starts = [y * CORE for y in range(first, first + group)]
+        both = dot(forward, stacked(side_by_side(rows_ref, starts, 1, CORE)))
+        scatter(waves_ref, starts, jnp.where(even_x, both[:CORE], both[CORE:]), CORE)
+
+    back_y = back_y_ref[...]
+    for first in range(0, CORE, group):
+        waves_x = list(range(first, first + group))
+        both = dot(forward, stacked(side_by_side(waves_ref, waves_x, CORE, CORE)))
+        modes = jnp.where(even_y, both[:CORE], both[CORE:])
+        scale = jnp.concatenate([factor_ref[wave * CORE : (wave + 1) * CORE] for wave in waves_x], 1)
+        both = dot(back_y, stacked(modes * scale))
+        scatter(mixed_ref, [wave * side for wave in waves_x], jnp.where(even_y, both[:side], both[side:]), side)
+
+    back_x = back_x_ref[slab]
+    for first in range(0, side, group):
+        both = dot(back_x, stacked(side_by_side(mixed_ref, list(range(first, first + group)), side, CORE)))
+        high, low = split2(jnp.where(even_x, both[:field_rows], both[field_rows:]))
+        for idx in range(group):
+            rows = slice((first + idx) * field_rows, (first + idx + 1) * field_rows)
+            flat_ref[rows, 0:lanes] = high[:, idx * lanes : (idx + 1) * lanes]
+            flat_ref[rows, lanes : 2 * lanes] = low[:, idx * lanes : (idx + 1) * lanes]
+
+    product = dot(flat_ref[...], back_z_ref[...])
+    hartree = product[:, 0:128] + product[:, 128:256]
+    coef_ref[...] = jnp.zeros(coef_ref.shape, jnp.float32)
+    for y in range(side):
+        coef_ref[:, y * side : (y + 1) * side] = hartree[y * field_rows : (y + 1) * field_rows, 0:side]
+
+    dens_ref[...] = jnp.zeros(dens_ref.shape, jnp.float32)
+    ahead = half + DEG - BUF
+    width = lines * side
+    for tile in range(-1, tiles + 1):
+        at_y = 0 if 0 <= tile < tiles else 1
+        src = tile % tiles
+        pieces = []
+        for at_z in range(blocks_z):
+            cols = slice(src * 128, (src + 1) * 128)
+            own = cubes_ref[cube_at[(at_z * 2 + at_y) * 2], :, cols]
+            beside = cubes_ref[cube_at[(at_z * 2 + at_y) * 2 + 1], :, cols]
+            lower = jnp.concatenate([beside[CORE - BUF :], own[:ahead]], 0)
+            upper = jnp.concatenate([own[CORE - ahead :], beside[:BUF]], 0)
+            rows = jnp.where(is_lower, lower, upper)
+            rows = jnp.concatenate([rows, jnp.zeros((field_rows - half - DEG, 128), jnp.float32)], 0)
+            pieces += split3(rows)
+        spread = dot(jnp.concatenate(pieces, 1), spread_ref[...])
+        start = (tile + 1) * width
+        dens_ref[:, start : start + width] = spread
+    hartree_exchange = coef_ref[...] + EXCHANGE_COEF * cube_root(dens_ref[...])
+
+    field_ref[...] = jnp.zeros(field_ref.shape, jnp.float32)
+
+    @pl.when(is_lower)
+    def _():
+        field_ref[0 : half + DEG, 0:cells] = pot_ref[0 : half + DEG]
+
+    @pl.when(jnp.logical_not(is_lower))
+    def _():
+        field_ref[0 : half + DEG, 0:cells] = pot_ref[half - DEG : side]
+
+    coef_ref[...] = (field_ref[...] + hartree_exchange) * (2.0 / HALF_WIDTH)
     place(is_lower, filt_ref[...], halo_ref[...], field_ref, half, side)
-    coef_ref[...] = jnp.zeros(coef_ref.shape, jnp.float32)
-
-    @pl.when(is_lower)
-    def _():
-        coef_ref[0 : half + DEG, 0:cells] = pot_ref[0 : half + DEG] * (2.0 / HALF_WIDTH)
-
-    @pl.when(jnp.logical_not(is_lower))
-    def _():
-        coef_ref[0 : half + DEG, 0:cells] = pot_ref[half - DEG : side] * (2.0 / HALF_WIDTH)
-
     result = filtered_field(field_ref[...], coef_ref[...], half, side)
     out_ref[...] = own_rows(is_lower, result, half)[:, 0:cells]
 
 
-def field_scratch(half):
+def field_scratch(half, count):
     shape = (padded(half + DEG, 8), padded(4 * half * half, 128))
-    return [pltpu.VMEM(shape, jnp.float32)] * 2
+    return [pltpu.VMEM(shape, jnp.float32)] * count
 
 
 SMEM = pl.BlockSpec(memory_space=pltpu.SMEM)
@@ -183,7 +393,7 @@
         ),
         in_specs=[SMEM, VMEM, VMEM, VMEM],
         out_specs=(VMEM, VMEM),
-        scratch_shapes=field_scratch(half),
+        scratch_shapes=field_scratch(half, 2),
         compiler_params=params,
     )(slab_scalar, wavefunc, halo_of(wavefunc), potential)
 
@@ -203,56 +413,27 @@
         masks = masks + [one | bit for one in masks]
         bit //= 2
 
-    anchor = lax.dynamic_slice_in_dim(offsets, dom_idx, 1, 0)[0]
-    others = jnp.take(offsets, dom_idx ^ jnp.array(masks, jnp.int32), axis=0)
-    shift = (others - anchor) // CORE
-    shift = jnp.stack([shift[:, 0] % 2, shift[:, 1] % 2, shift[:, 2] % (grid_z // CORE)], 1)
-    basis, waves = parity_basis()
-    z_basis, z_waves = wave_basis(grid_z)
-    parity = jnp.arange(2)
-    sign_x = 1.0 - 2.0 * ((shift[:, 0:1] * parity) % 2).astype(jnp.float32)
-    sign_y = 1.0 - 2.0 * ((shift[:, 1:2] * parity) % 2).astype(jnp.float32)
-    z_tables = z_basis.T.reshape(grid_z // CORE, CORE, grid_z).astype(np.float32)
-    into_z = jnp.take(jnp.asarray(z_tables), shift[:, 2], axis=0)
-    into_z = sign_x[:, :, None, None, None] * sign_y[:, None, :, None, None] * into_z[:, None, None]
-    region = np.arange(side) - BUF
-    inner = basis[:, :, :CORE].astype(np.float32)
-    outer = basis[:, :, region % (2 * CORE)].astype(np.float32)
-    outer_z = z_basis[:, region % grid_z].astype(np.float32)
-    eigen = eigenvalue(waves, 2 * CORE)
-    lam = (
-        eigen[:, None, :, None, None]
-        + eigen[None, :, None, :, None]
-        + eigenvalue(z_waves, grid_z)[None, None, None, None, :]
-    )
-    lam[0, 0, 0, 0, 0] = np.inf
-    factor = (FOUR_PI / lam).astype(np.float32)
-    grid_cubes = cubes.reshape(dom_count, CORE, CORE, CORE)
-    spec = jnp.einsum("jxyz,jpqzk->pqxyk", grid_cubes, into_z, precision=precise)
-    spec = jnp.einsum("pqxyk,pax->pqayk", spec, inner, precision=precise)
-    spec = jnp.einsum("pqayk,qby->pqabk", spec, inner, precision=precise)
-    spec = spec * factor
-    field = jnp.einsum("pqabk,pax->qxbk", spec, outer, precision=precise)
-    field = jnp.einsum("qxbk,qby->xyk", field, outer, precision=precise)
-    hartree = jnp.einsum("xyk,kz->xyz", field, outer_z, precision=precise)
-    place_of = (shift[:, 2] * 2 + shift[:, 1]) * 2 + shift[:, 0]
-    by_place = jnp.zeros_like(grid_cubes).at[place_of].set(grid_cubes)
-    by_place = by_place.reshape(grid_z // CORE, 2, 2, CORE, CORE, CORE)
-    density = jnp.transpose(by_place, (2, 3, 1, 4, 0, 5)).reshape(2 * CORE, 2 * CORE, grid_z)
-    density = jnp.concatenate([density[-BUF:], density[: CORE + BUF]], 0)
-    density = jnp.concatenate([density[:, -BUF:], density[:, : CORE + BUF]], 1)
-    z_index = region % grid_z
-    density = jnp.take(density, jnp.asarray(z_index), axis=2)
-    renewed = potential + hartree.reshape(side, cells) + EXCHANGE_COEF * jnp.cbrt(density.reshape(side, cells))
-
+    tables = solver_tables(side, grid_z)
+    names = ("into", "forward", "back_y", "back_x", "back_z", "factor", "spread")
+    index = jnp.stack([slab_idx, dom_idx]).astype(jnp.int32)
+    lanes = 4 * grid_z
+    field_rows = padded(half + DEG, 8)
+    f32, bf16 = jnp.float32, jnp.bfloat16
     result = pl.pallas_call(
-        second_kernel,
-        out_shape=jax.ShapeDtypeStruct((half, cells), jnp.float32),
-        in_specs=[SMEM, VMEM, VMEM, VMEM],
+        functools.partial(second_kernel, masks),
+        out_shape=jax.ShapeDtypeStruct((half, cells), f32),
+        in_specs=[SMEM, SMEM] + [VMEM] * (4 + len(names)),
         out_specs=VMEM,
-        scratch_shapes=field_scratch(half),
+        scratch_shapes=field_scratch(half, 3)
+        + [
+            pltpu.VMEM((CORE * CORE * CORE // 128, dom_count * 3 * 128), bf16),
+            pltpu.VMEM((lanes // 128, CORE * CORE, 128), f32),
+            pltpu.VMEM((lanes // 128, CORE * CORE, 128), f32),
+            pltpu.VMEM((lanes // 128, CORE * side, 128), f32),
+            pltpu.VMEM((side * field_rows, 2 * lanes), bf16),
+        ],
         compiler_params=params,
-    )(slab_scalar, filt, halo, renewed)
+    )(index, offsets, cubes, filt, halo, potential, *[jnp.asarray(tables[name]) for name in names])
     return result[None, None]
 
 

time: 81.9 us -> 40.5 us (0.49)
  local copies, waits for them, and re-layouts: 30.2 us -> 3.56 us
  matrix products: 20.2 us -> 0 us
  Pallas kernels: 4.58 us -> 8.67 us
  waiting for transfers between devices: 9.72 us -> 13.6 us
  other arithmetic: 2.58 us -> 0.19 us
    dot_general x6 -> x0, matrix products: 20.2 us -> none  [the longest x1 7.31 us: local(): jnp.einsum('jxyz,jpqzk->pqxyk', grid_cubes, into_z, precision=precise)]
    transpose x3 -> x0, local copies, waits for them, and re-layouts: 8.95 us -> none  [the longest x1 3.25 us: local(): spec = jnp.einsum('pqxyk,pax->pqayk', spec, inner, precision=precise)]
    reshape x3 -> x0, local copies, waits for them, and re-layouts: 5.92 us -> none  [the longest x2 5.66 us: local(): jnp.transpose(by_place, (2, 3, 1, 4, 0, 5))]
    pallas_call x1, Pallas kernels: 2.22 us -> 6.3 us  [local(): pl.pallas_call(functools.partial(second_kernel, masks), out_shape=jax.Sha...]
    mul x3 -> x0, local copies, waits for them, and re-layouts: 4.06 us -> none  [the longest x1 3.51 us: local(): spec = spec * factor]
    ppermute x7, waiting for transfers between devices: 9.72 us -> 13.6 us  [swapped(): return lax.ppermute(value, axis, pairs)]
    scatter x1 -> x0, local copies, waits for them, and re-layouts: 2.62 us -> none  [local(): by_place = jnp.zeros_like(grid_cubes).at[place_of].set(grid_cubes)]
    concatenate x4 -> x0, local copies, waits for them, and re-layouts: 2.18 us -> none  [local(): cubes = jnp.concatenate([cubes, swapped(cubes, 'dom', bit)], 0)]
  transfers between devices with their start and end apart: 7 -> 7, of which waited for: 4 -> 6; matrix products, arithmetic and copies ran while one was open for 61% -> 3% of each run, Pallas kernels for 0% -> 0%
where the time goes in v2:
time: 40.5 us; the launch traced here: 40.3 us
  starting transfers between devices  14 us (35%)
  waiting for transfers between devices  13.6 us (34%)
  Pallas kernels  8.67 us (21%)
  local copies, waits for them, and re-layouts  3.56 us (9%)
    ppermute x7, starting transfers between devices, swapped(): return lax.ppermute(value, axis, pairs)  14 us
    ppermute x7, waiting for transfers between devices, swapped(): return lax.ppermute(value, axis, pairs)  13.6 us
    pallas_call x1, Pallas kernels, local(): pl.pallas_call(functools.partial(second_kernel, masks), out_shape=jax.Sha...  6.3 us
    pallas_call x1, Pallas kernels, local(): pl.pallas_call(functools.partial(first_kernel, bands), out_shape=(jax.Sha...  2.37 us
    unnamed x21, local copies, waits for them, and re-layouts  1.92 us
    slice x1, local copies, waits for them, and re-layouts, halo_of(): edge = jnp.where(is_lower, rows[half - DEG:half], rows[0:DEG])  0.85 us
  transfers between devices with their start and end apart: 7, of which 6 were waited for; matrix products, arithmetic and copies ran while one was open for 3% of the time, Pallas kernels for 0%

profile of v2, /device:TPU:0, one launch (start us, length us, event | category | flops | bytes accessed | tf_op | source)
XLA Modules:
  0.0 40.3 jit_solution(1094969241155396510)
XLA Ops:
  0.0 0.9 %fusion.1 = (f32[1,1,8,1600]{3,1,2,0:T(1,128)S(1)}, f32[1,1,8,1600]{3,1,2,0:T(1,128)S(1)}) fusion(f32[1,1,20,1600]{3,1,2,0:T(1,128)} %param.10), kind=kLoop, calls=%fused_computation.10 | loop fusion | bytes 204800 | tf_op jit(solution)/shard_map/slice | solution.py:385
  0.9 3.0 %collective-permute-start = (f32[8,1600]{1,0:T(8,128)S(1)}, f32[8,1600]{1,0:T(8,128)S(1)}, u32[]{:S(2)}, u32[]{:S(2)}) collective-permute-start(f32[8,1600]{1,0:T(8,128)S(1)} %fusion), channel_id=1, source_target_pairs={{0,1},{1,0},{2,3},{3,2},{4,5},{5,4},{6,7},{7,6},{8,9},{9,8},{10,11... | collective-permute-start | bytes 153608 | tf_op jit(solution)/shard_map/ppermute | solution.py:24
  3.9 0.9 %copy.22 = f32[1,1,20,1600]{3,2,1,0:T(8,128)S(1)} copy(f32[1,1,20,1600]{3,1,2,0:T(1,128)} %param.10) | data formatting | bytes 256000
  4.8 1.2 %collective-permute-done.halo_ref = f32[8,1600]{1,0:T(8,128)S(1)} collective-permute-done((f32[8,1600]{1,0:T(8,128)S(1)}, f32[8,1600]{1,0:T(8,128)S(1)}, u32[]{:S(2)}, u32[]{:S(2)}) %collective-permute-start) | collective-permute-done | bytes 51232 | tf_op jit(solution)/shard_map/ppermute | solution.py:24
  6.0 0.9 %copy-done.1 = f32[1,40,1600]{2,1,0:T(8,128)S(1)} copy-done((f32[1,40,1600]{2,1,0:T(8,128)S(1)}, f32[1,40,1600]{2,1,0:T(8,128)}, u32[]{:S(2)}) %copy-start.1) | copy-done | bytes 256024
  7.0 0.0 copy-start.5
  7.0 0.0 copy-start.6
  7.0 0.0 copy-start.7
  7.0 0.0 copy-start.8
  7.0 2.4 %shard_map.100 = (f32[20,1600]{1,0:T(8,128)S(1)}, f32[16,1024]{1,0:T(8,128)S(1)}) custom-call(s32[1]{0:T(128)} %bitcast.slab_ref, f32[20,1600]{1,0:T(8,128)S(1)} %bitcast.14, f32[8,1600]{1,0:T(8,128)S(1)} %collective-permute-done.halo_ref, f32[40,1600]{1,0:T(8,128)S(1)} %bitcast.11), custom_call_target="tpu_custom_call" | custom-call | tf_op jit(solution)/shard_map/pallas_call | solution.py:388
  9.4 2.2 %collective-permute-start.1 = (f32[16,1024]{1,0:T(8,128)S(1)}, f32[16,1024]{1,0:T(8,128)S(1)}, u32[]{:S(2)}, u32[]{:S(2)}) collective-permute-start(f32[16,1024]{1,0:T(8,128)S(1)} %get-tuple-element.10), channel_id=1, source_target_pairs={{0,2},{1,3},{2,0},{3,1},{4,6},{5,7},{6,4},{7,5},{8,10},{9,11},{10,... | collective-permute-start | bytes 196616 | tf_op jit(solution)/shard_map/ppermute | solution.py:24
  11.6 2.2 %collective-permute-done.1 = f32[16,1024]{1,0:T(8,128)S(1)} collective-permute-done((f32[16,1024]{1,0:T(8,128)S(1)}, f32[16,1024]{1,0:T(8,128)S(1)}, u32[]{:S(2)}, u32[]{:S(2)}) %collective-permute-start.1) | collective-permute-done | bytes 65568 | tf_op jit(solution)/shard_map/ppermute | solution.py:24
  13.8 3.1 %collective-permute-start.2 = (f32[16,1024]{1,0:T(8,128)S(1)}, f32[16,1024]{1,0:T(8,128)S(1)}, u32[]{:S(2)}, u32[]{:S(2)}) collective-permute-start(f32[16,1024]{1,0:T(8,128)S(1)} %add.11), channel_id=1, source_target_pairs={{0,4},{1,5},{2,6},{3,7},{4,0},{5,1},{6,2},{7,3},{8,12},{9,13},{10,... | collective-permute-start | bytes 196616 | tf_op jit(solution)/shard_map/ppermute | solution.py:24
  16.9 2.2 %collective-permute-done.2 = f32[16,1024]{1,0:T(8,128)S(1)} collective-permute-done((f32[16,1024]{1,0:T(8,128)S(1)}, f32[16,1024]{1,0:T(8,128)S(1)}, u32[]{:S(2)}, u32[]{:S(2)}) %collective-permute-start.2) | collective-permute-done | bytes 65568 | tf_op jit(solution)/shard_map/ppermute | solution.py:24
  19.2 1.9 %collective-permute-start.3 = (f32[16,1024]{1,0:T(8,128)S(1)}, f32[16,1024]{1,0:T(8,128)S(1)}, u32[]{:S(2)}, u32[]{:S(2)}) collective-permute-start(f32[16,1024]{1,0:T(8,128)S(1)} %add.12), channel_id=1, source_target_pairs={{0,1},{1,0},{2,3},{3,2},{4,5},{5,4},{6,7},{7,6},{8,9},{9,8},{10,11... | collective-permute-start | bytes 196616 | tf_op jit(solution)/shard_map/ppermute | solution.py:24
  21.1 2.4 %collective-permute-done.3 = f32[16,1024]{1,0:T(8,128)S(1)} collective-permute-done((f32[16,1024]{1,0:T(8,128)S(1)}, f32[16,1024]{1,0:T(8,128)S(1)}, u32[]{:S(2)}, u32[]{:S(2)}) %collective-permute-start.3) | collective-permute-done | bytes 65568 | tf_op jit(solution)/shard_map/ppermute | solution.py:24
  23.6 1.9 %collective-permute-start.4 = (f32[1,32,1024]{2,1,0:T(8,128)S(1)}, f32[1,32,1024]{2,1,0:T(8,128)S(1)}, u32[]{:S(2)}, u32[]{:S(2)}) collective-permute-start(f32[1,32,1024]{2,1,0:T(8,128)S(1)} %maximum_bitcast_fusion), channel_id=1, source_target_pairs={{0,16},{8,24},{16,0},{24,8},{1,17},{9,25},{17,1},{25,9},{2,18},{10... | collective-permute-start | bytes 393224 | tf_op jit(solution)/shard_map/ppermute | solution.py:24
  25.5 0.1 pad_add_fusion.index_ref
  25.5 3.0 %collective-permute-done.4 = f32[1,32,1024]{2,1,0:T(8,128)S(1)} collective-permute-done((f32[1,32,1024]{2,1,0:T(8,128)S(1)}, f32[1,32,1024]{2,1,0:T(8,128)S(1)}, u32[]{:S(2)}, u32[]{:S(2)}) %collective-permute-start.4) | collective-permute-done | bytes 131104 | tf_op jit(solution)/shard_map/ppermute | solution.py:24
  28.6 0.1 collective-permute-start.5
  28.7 1.9 %collective-permute-start.6 = (f32[8,1600]{1,0:T(8,128)S(1)}, f32[8,1600]{1,0:T(8,128)S(1)}, u32[]{:S(2)}, u32[]{:S(2)}) collective-permute-start(f32[8,1600]{1,0:T(8,128)S(1)} %slice_select_fusion), channel_id=1, source_target_pairs={{0,1},{1,0},{2,3},{3,2},{4,5},{5,4},{6,7},{7,6},{8,9},{9,8},{10,11... | collective-permute-start | bytes 153608 | tf_op jit(solution)/shard_map/ppermute | solution.py:24
  30.6 2.4 %collective-permute-done.6.halo_ref = f32[8,1600]{1,0:T(8,128)S(1)} collective-permute-done((f32[8,1600]{1,0:T(8,128)S(1)}, f32[8,1600]{1,0:T(8,128)S(1)}, u32[]{:S(2)}, u32[]{:S(2)}) %collective-permute-start.6) | collective-permute-done | bytes 51232 | tf_op jit(solution)/shard_map/ppermute | solution.py:24
  33.2 6.3 %shard_map.101 = f32[20,1600]{1,0:T(8,128)S(1)} custom-call(s32[2]{0:T(128)S(1)} %pad_add_fusion.index_ref, s32[4,3]{1,0:T(4,128)S(1)} %copy-done.9, f32[4,32,1024]{2,1,0:T(8,128)S(1)} %pad_maximum_fusion.cubes_ref, f32[20,1600]{1,0:T(8,128)S(1)} %get-tuple-element.12.filt_ref, f32[8,1600]{1,0:T(8,128)S(1)} %collective-permute-done.6.halo_ref, ...), custom_call_target="tpu_custom_call" | custom-call | tf_op jit(solution)/shard_map/pallas_call | solution.py:422
  39.5 0.8 %copy.13 = f32[1,1,20,1600]{3,1,2,0:T(1,128)} copy(f32[1,1,20,1600]{3,2,1,0:T(8,128)S(1)} %bitcast.13) | data formatting | bytes 256000 | tf_op jit(solution)/shard_map/broadcast_in_dim | solution.py:437
  (24 shorter events, 0.2 us)
Async XLA Ops:
  0.9 5.1 %collective-permute-start = (f32[8,1600]{1,0:T(8,128)S(1)}, f32[8,1600]{1,0:T(8,128)S(1)}, u32[]{:S(2)}, u32[]{:S(2)}) collective-permute-start(f32[8,1600]{1,0:T(8,128)S(1)} %fusion), channel_id=1, source_target_pairs={{0,1},{1,0},{2,3},{3,2},{4,5},{5,4},{6,7},{7,6},{8,9},{9,8},{10,11... | collective-permute-start | bytes 153608 | tf_op jit(solution)/shard_map/ppermute | solution.py:24
  6.0 1.0 %copy-start.1 = (f32[1,40,1600]{2,1,0:T(8,128)S(1)}, f32[1,40,1600]{2,1,0:T(8,128)}, u32[]{:S(2)}) copy-start(f32[1,40,1600]{2,1,0:T(8,128)} %param.11) | copy-start | bytes 768004
  7.0 26.1 %copy-start = (bf16[1536,512]{1,0:T(8,128)(2,1)S(1)}, bf16[1536,512]{1,0:T(8,128)(2,1)}, u32[]{:S(2)}) copy-start(bf16[1536,512]{1,0:T(8,128)(2,1)} %constant.36.clone.into_ref) | copy-start | bytes 4718596
  7.0 26.1 %copy-start.2 = (f32[1,40,1600]{2,1,0:T(8,128)S(1)}, f32[1,40,1600]{2,1,0:T(8,128)}, u32[]{:S(2)}) copy-start(f32[1,40,1600]{2,1,0:T(8,128)} %param.11) | copy-start | bytes 768004
  7.0 26.1 %copy-start.3 = (f32[1024,128]{1,0:T(8,128)S(1)}, f32[1024,128]{1,0:T(8,128)}, u32[]{:S(2)}) copy-start(f32[1024,128]{1,0:T(8,128)} %constant.41.clone.factor_ref) | copy-start | bytes 1572868
  7.0 26.1 %copy-start.4 = (bf16[384,160]{1,0:T(8,128)(2,1)S(1)}, bf16[384,160]{1,0:T(8,128)(2,1)}, u32[]{:S(2)}) copy-start(bf16[384,160]{1,0:T(8,128)(2,1)} %constant.42.clone.spread_ref) | copy-start | bytes 368644
  7.0 26.2 %copy-start.5 = (bf16[256,256]{1,0:T(8,128)(2,1)S(1)}, bf16[256,256]{1,0:T(8,128)(2,1)}, u32[]{:S(2)}) copy-start(bf16[256,256]{1,0:T(8,128)(2,1)} %constant.40.clone.back_z_ref) | copy-start | bytes 393220
  7.0 26.1 %copy-start.6 = (bf16[2,64,96]{2,1,0:T(8,128)(2,1)S(1)}, bf16[2,64,96]{2,1,0:T(8,128)(2,1)}, u32[]{:S(2)}) copy-start(bf16[2,64,96]{2,1,0:T(8,128)(2,1)} %constant.39.clone.back_x_ref) | copy-start | bytes 73732
  7.0 26.1 %copy-start.7 = (bf16[80,96]{1,0:T(8,128)(2,1)S(1)}, bf16[80,96]{1,0:T(8,128)(2,1)}, u32[]{:S(2)}) copy-start(bf16[80,96]{1,0:T(8,128)(2,1)} %constant.38.clone.back_y_ref) | copy-start | bytes 46084
  7.0 26.1 %copy-start.8 = (bf16[64,96]{1,0:T(8,128)(2,1)S(1)}, bf16[64,96]{1,0:T(8,128)(2,1)}, u32[]{:S(2)}) copy-start(bf16[64,96]{1,0:T(8,128)(2,1)} %constant.37.clone.forward_ref) | copy-start | bytes 36868
  7.0 26.1 %copy-start.9 = (s32[4,3]{1,0:T(4,128)S(1)}, s32[4,3]{1,0:T(4,128)}, u32[]{:S(2)}) copy-start(s32[4,3]{1,0:T(4,128)} %offsets_ref.1) | copy-start | bytes 148
  9.4 4.4 %collective-permute-start.1 = (f32[16,1024]{1,0:T(8,128)S(1)}, f32[16,1024]{1,0:T(8,128)S(1)}, u32[]{:S(2)}, u32[]{:S(2)}) collective-permute-start(f32[16,1024]{1,0:T(8,128)S(1)} %get-tuple-element.10), channel_id=1, source_target_pairs={{0,2},{1,3},{2,0},{3,1},{4,6},{5,7},{6,4},{7,5},{8,10},{9,11},{10,... | collective-permute-start | bytes 196616 | tf_op jit(solution)/shard_map/ppermute | solution.py:24
  13.8 5.3 %collective-permute-start.2 = (f32[16,1024]{1,0:T(8,128)S(1)}, f32[16,1024]{1,0:T(8,128)S(1)}, u32[]{:S(2)}, u32[]{:S(2)}) collective-permute-start(f32[16,1024]{1,0:T(8,128)S(1)} %add.11), channel_id=1, source_target_pairs={{0,4},{1,5},{2,6},{3,7},{4,0},{5,1},{6,2},{7,3},{8,12},{9,13},{10,... | collective-permute-start | bytes 196616 | tf_op jit(solution)/shard_map/ppermute | solution.py:24
  19.2 4.3 %collective-permute-start.3 = (f32[16,1024]{1,0:T(8,128)S(1)}, f32[16,1024]{1,0:T(8,128)S(1)}, u32[]{:S(2)}, u32[]{:S(2)}) collective-permute-start(f32[16,1024]{1,0:T(8,128)S(1)} %add.12), channel_id=1, source_target_pairs={{0,1},{1,0},{2,3},{3,2},{4,5},{5,4},{6,7},{7,6},{8,9},{9,8},{10,11... | collective-permute-start | bytes 196616 | tf_op jit(solution)/shard_map/ppermute | solution.py:24
  23.6 5.0 %collective-permute-start.4 = (f32[1,32,1024]{2,1,0:T(8,128)S(1)}, f32[1,32,1024]{2,1,0:T(8,128)S(1)}, u32[]{:S(2)}, u32[]{:S(2)}) collective-permute-start(f32[1,32,1024]{2,1,0:T(8,128)S(1)} %maximum_bitcast_fusion), channel_id=1, source_target_pairs={{0,16},{8,24},{16,0},{24,8},{1,17},{9,25},{17,1},{25,9},{2,18},{10... | collective-permute-start | bytes 393224 | tf_op jit(solution)/shard_map/ppermute | solution.py:24
  28.6 2.0 %collective-permute-start.5 = (f32[2,32,1024]{2,1,0:T(8,128)S(1)}, f32[2,32,1024]{2,1,0:T(8,128)S(1)}, u32[]{:S(2)}, u32[]{:S(2)}) collective-permute-start(f32[2,32,1024]{2,1,0:T(8,128)S(1)} %pad_maximum_fusion.1), channel_id=1, source_target_pairs={{0,8},{8,0},{16,24},{24,16},{1,9},{9,1},{17,25},{25,17},{2,10},{10... | collective-permute-start | bytes 786440 | tf_op jit(solution)/shard_map/ppermute | solution.py:24
  28.7 4.4 %collective-permute-start.6 = (f32[8,1600]{1,0:T(8,128)S(1)}, f32[8,1600]{1,0:T(8,128)S(1)}, u32[]{:S(2)}, u32[]{:S(2)}) collective-permute-start(f32[8,1600]{1,0:T(8,128)S(1)} %slice_select_fusion), channel_id=1, source_target_pairs={{0,1},{1,0},{2,3},{3,2},{4,5},{5,4},{6,7},{7,6},{8,9},{9,8},{10,11... | collective-permute-start | bytes 153608 | tf_op jit(solution)/shard_map/ppermute | solution.py:24

commit v3 on v2

--- a/solution.py
+++ b/solution.py
@@ -54,19 +54,53 @@
     return -(-length // unit) * unit
 
 
-def place(is_lower, own, halo, field_ref, half, side):
-    cells = side * side
+def set_halo(is_lower, halo, field_ref, half):
+    cells = halo.shape[1]
+
+    @pl.when(is_lower)
+    def _():
+        field_ref[half : half + DEG, 0:cells] = halo
+
+    @pl.when(jnp.logical_not(is_lower))
+    def _():
+        field_ref[0:DEG, 0:cells] = halo
+
+
+def edge_rows(is_lower, own, half):
+    return jnp.where(is_lower, own[half - DEG : half], own[0:DEG])
+
+
+def start_kernel(slab_ref, psi_ref, pot_ref, edge_ref, field_ref, coef_ref, own_ref, all_ref, sems):
+    half, _, cells = psi_ref.shape
+    side = 2 * half
+    is_lower = slab_ref[0] == 0
+    rows_copy = pltpu.make_async_copy(psi_ref, own_ref, sems.at[0])
+    pot_copy = pltpu.make_async_copy(pot_ref, all_ref, sems.at[1])
+    rows_copy.start()
+    pot_copy.start()
     field_ref[...] = jnp.zeros(field_ref.shape, jnp.float32)
+    coef_ref[...] = jnp.zeros(coef_ref.shape, jnp.float32)
+    rows_copy.wait()
+    own = own_ref[:, 0, :]
+    edge_ref[...] = edge_rows(is_lower, own, half)
 
     @pl.when(is_lower)
     def _():
         field_ref[0:half, 0:cells] = own
-        field_ref[half : half + DEG, 0:cells] = halo
 
     @pl.when(jnp.logical_not(is_lower))
     def _():
-        field_ref[0:DEG, 0:cells] = halo
         field_ref[DEG : DEG + half, 0:cells] = own
+
+    pot_copy.wait()
+
+    @pl.when(is_lower)
+    def _():
+        coef_ref[0 : half + DEG, 0:cells] = all_ref[0 : half + DEG] * (2.0 / HALF_WIDTH)
+
+    @pl.when(jnp.logical_not(is_lower))
+    def _():
+        coef_ref[0 : half + DEG, 0:cells] = all_ref[half - DEG : side] * (2.0 / HALF_WIDTH)
 
 
 def filtered_field(field, scaled_potential, half, side):
@@ -97,23 +131,15 @@
     return jnp.where(is_lower, values[0:half], values[DEG : DEG + half])
 
 
-def first_kernel(bands, slab_ref, psi_ref, halo_ref, pot_ref, filt_ref, dens_ref, field_ref, coef_ref):
-    half, cells = psi_ref.shape
-    side = 2 * half
+def first_kernel(bands, side, slab_ref, start_ref, halo_ref, coef_ref, filt_ref, edge_ref, dens_ref, field_ref):
+    half = side // 2
+    cells = side * side
     is_lower = slab_ref[0] == 0
-    place(is_lower, psi_ref[...], halo_ref[...], field_ref, half, side)
-    coef_ref[...] = jnp.zeros(coef_ref.shape, jnp.float32)
-
-    @pl.when(is_lower)
-    def _():
-        coef_ref[0 : half + DEG, 0:cells] = pot_ref[0 : half + DEG] * (2.0 / HALF_WIDTH)
-
-    @pl.when(jnp.logical_not(is_lower))
-    def _():
-        coef_ref[0 : half + DEG, 0:cells] = pot_ref[half - DEG : side] * (2.0 / HALF_WIDTH)
-
+    field_ref[...] = start_ref[...]
+    set_halo(is_lower, halo_ref[...], field_ref, half)
     result = filtered_field(field_ref[...], coef_ref[...], half, side)
-    filt_ref[...] = own_rows(is_lower, result, half)[:, 0:cells]
+    filt_ref[...] = result
+    edge_ref[...] = edge_rows(is_lower, own_rows(is_lower, result, half), half)[:, 0:cells]
     slab = CORE // 2
     core_rows = jnp.where(is_lower, result[BUF : BUF + slab], result[DEG : DEG + slab])
     squares = core_rows * core_rows * (1.0 / bands)
@@ -216,11 +242,11 @@
 
 
 def second_kernel(
-    masks, index_ref, offsets_ref, cubes_ref, filt_ref, halo_ref, pot_ref,
+    masks, index_ref, offsets_ref, cubes_ref, filt_ref, halo_ref, start_coef_ref,
     into_ref, forward_ref, back_y_ref, back_x_ref, back_z_ref, factor_ref, spread_ref,
     out_ref, field_ref, coef_ref, dens_ref, left_ref, rows_ref, waves_ref, mixed_ref, flat_ref,
 ):
-    half, cells = filt_ref.shape
+    half, _, cells = out_ref.shape
     side = 2 * half
     slab, dom = index_ref[0], index_ref[1]
     is_lower = slab == 0
@@ -339,29 +365,16 @@
         dens_ref[:, start : start + width] = spread
     hartree_exchange = coef_ref[...] + EXCHANGE_COEF * cube_root(dens_ref[...])
 
-    field_ref[...] = jnp.zeros(field_ref.shape, jnp.float32)
-
-    @pl.when(is_lower)
-    def _():
-        field_ref[0 : half + DEG, 0:cells] = pot_ref[0 : half + DEG]
-
-    @pl.when(jnp.logical_not(is_lower))
-    def _():
-        field_ref[0 : half + DEG, 0:cells] = pot_ref[half - DEG : side]
-
-    coef_ref[...] = (field_ref[...] + hartree_exchange) * (2.0 / HALF_WIDTH)
-    place(is_lower, filt_ref[...], halo_ref[...], field_ref, half, side)
+    coef_ref[...] = start_coef_ref[...] + hartree_exchange * (2.0 / HALF_WIDTH)
+    field_ref[...] = filt_ref[...]
+    set_halo(is_lower, halo_ref[...], field_ref, half)
     result = filtered_field(field_ref[...], coef_ref[...], half, side)
-    out_ref[...] = own_rows(is_lower, result, half)[:, 0:cells]
-
-
-def field_scratch(half, count):
-    shape = (padded(half + DEG, 8), padded(4 * half * half, 128))
-    return [pltpu.VMEM(shape, jnp.float32)] * count
+    out_ref[:, 0, :] = own_rows(is_lower, result, half)[:, 0:cells]
 
 
 SMEM = pl.BlockSpec(memory_space=pltpu.SMEM)
 VMEM = pl.BlockSpec(memory_space=pltpu.VMEM)
+HBM = pl.BlockSpec(memory_space=pltpu.HBM)
 params = pltpu.CompilerParams(vmem_limit_bytes=40 * 1024 * 1024)
 
 
@@ -378,36 +391,61 @@
     bands = band_count // 2
     grid_z = CORE * dom_count // 4
 
-    wavefunc = psi_in[0, 0]
-    potential = v_in[0]
-
-    def halo_of(rows):
-        edge = jnp.where(is_lower, rows[half - DEG : half], rows[0:DEG])
-        return swapped(edge, "band", 1)
-
-    filt, dens = pl.pallas_call(
-        functools.partial(first_kernel, bands),
-        out_shape=(
-            jax.ShapeDtypeStruct((half, cells), jnp.float32),
-            jax.ShapeDtypeStruct((CORE // 2, CORE * CORE), jnp.float32),
-        ),
+    f32, bf16 = jnp.float32, jnp.bfloat16
+    field_rows = padded(half + DEG, 8)
+    field_shape = (field_rows, padded(cells, 128))
+    field_type = jax.ShapeDtypeStruct(field_shape, f32)
+    edge_type = jax.ShapeDtypeStruct((DEG, cells), f32)
+
+    edge, start, coef = pl.pallas_call(
+        start_kernel,
+        out_shape=(edge_type, field_type, field_type),
+        in_specs=[SMEM, HBM, HBM],
+        out_specs=(VMEM, VMEM, VMEM),
+        scratch_shapes=[
+            pltpu.VMEM((half, 1, cells), f32),
+            pltpu.VMEM((side, cells), f32),
+            pltpu.SemaphoreType.DMA((2,)),
+        ],
+        compiler_params=params,
+    )(slab_scalar, psi_in.reshape(half, 1, cells), v_in[0])
+
+    filt, edge, dens = pl.pallas_call(
+        functools.partial(first_kernel, bands, side),
+        out_shape=(field_type, edge_type, jax.ShapeDtypeStruct((CORE // 2, CORE * CORE), f32)),
         in_specs=[SMEM, VMEM, VMEM, VMEM],
-        out_specs=(VMEM, VMEM),
-        scratch_shapes=field_scratch(half, 2),
+        out_specs=(VMEM, VMEM, VMEM),
+        scratch_shapes=[pltpu.VMEM(field_shape, f32)],
         compiler_params=params,
-    )(slab_scalar, wavefunc, halo_of(wavefunc), potential)
+    )(slab_scalar, start, swapped(edge, "band", 1), coef)
 
     mask = 2
     while mask < band_count:
-        dens = dens + swapped(dens, "band", mask)
+        received = swapped(dens, "band", mask)
         mask *= 2
-    filt_edge, dens = lax.optimization_barrier((filt, dens))
-    halo = halo_of(filt_edge)
-    beside = swapped(dens, "band", 1)
-    cube = jnp.concatenate([jnp.where(is_lower, dens, beside), jnp.where(is_lower, beside, dens)], 0)
-    cubes = cube[None]
-    masks = [0]
-    bit = dom_count // 2
+        if mask >= band_count:
+            edge, _ = lax.optimization_barrier((edge, dens))
+            halo = swapped(edge, "band", 1)
+            received, halo = lax.optimization_barrier((received, halo))
+        dens = dens + received
+
+    far = dom_count // 2
+    both = ("dom", "band")
+    count = dom_count * band_count
+
+    def crossed(value, mask):
+        return lax.ppermute(value, both, [(source, source ^ mask) for source in range(count)])
+
+    beside = crossed(dens, 1)
+    across = crossed(dens, far * band_count)
+    diagonal = crossed(dens, far * band_count + 1)
+
+    def cube_of(own, other):
+        return jnp.concatenate([jnp.where(is_lower, own, other), jnp.where(is_lower, other, own)], 0)
+
+    cubes = jnp.stack([cube_of(dens, beside), cube_of(across, diagonal)])
+    masks = [0, far]
+    bit = far // 2
     while bit:
         cubes = jnp.concatenate([cubes, swapped(cubes, "dom", bit)], 0)
         masks = masks + [one | bit for one in masks]
@@ -417,14 +455,12 @@
     names = ("into", "forward", "back_y", "back_x", "back_z", "factor", "spread")
     index = jnp.stack([slab_idx, dom_idx]).astype(jnp.int32)
     lanes = 4 * grid_z
-    field_rows = padded(half + DEG, 8)
-    f32, bf16 = jnp.float32, jnp.bfloat16
     result = pl.pallas_call(
         functools.partial(second_kernel, masks),
-        out_shape=jax.ShapeDtypeStruct((half, cells), f32),
+        out_shape=jax.ShapeDtypeStruct((half, 1, cells), f32),
         in_specs=[SMEM, SMEM] + [VMEM] * (4 + len(names)),
         out_specs=VMEM,
-        scratch_shapes=field_scratch(half, 3)
+        scratch_shapes=[pltpu.VMEM(field_shape, f32)] * 3
         + [
             pltpu.VMEM((CORE * CORE * CORE // 128, dom_count * 3 * 128), bf16),
             pltpu.VMEM((lanes // 128, CORE * CORE, 128), f32),
@@ -433,8 +469,8 @@
             pltpu.VMEM((side * field_rows, 2 * lanes), bf16),
         ],
         compiler_params=params,
-    )(index, offsets, cubes, filt, halo, potential, *[jnp.asarray(tables[name]) for name in names])
-    return result[None, None]
+    )(index, offsets, cubes, filt, halo, coef, *[jnp.asarray(tables[name]) for name in names])
+    return result.reshape(1, 1, half, cells)
 
 
 def solution(mesh):

time: 40.5 us -> 39.7 us (0.980)
  local copies, waits for them, and re-layouts: 3.56 us -> 1.91 us
  other arithmetic: 0.19 us -> 1.15 us
  Pallas kernels: 8.67 us -> 9.52 us
  starting transfers between devices: 14 us -> 13.4 us
    ppermute x7 -> x5, waiting for transfers between devices: 13.6 us -> 8.63 us  [swapped(): return lax.ppermute(value, axis, pairs)]
    ppermute x0 -> x3, waiting for transfers between devices: none -> 4.68 us  [crossed(): lax.ppermute(value, both, [(source, source ^ mask) for source in range(co...]
    ppermute x7 -> x5, starting transfers between devices: 14 us -> 9.84 us  [swapped(): return lax.ppermute(value, axis, pairs)]
    ppermute x0 -> x3, starting transfers between devices: none -> 3.55 us  [crossed(): lax.ppermute(value, both, [(source, source ^ mask) for source in range(co...]
    concatenate x2 -> x1, other arithmetic: 0.05 us -> 0.99 us  [local(): cubes = jnp.concatenate([cubes, swapped(cubes, 'dom', bit)], 0)]
    slice x1 -> x0, local copies, waits for them, and re-layouts: 0.85 us -> none  [halo_of(): edge = jnp.where(is_lower, rows[half - DEG:half], rows[0:DEG])]
    broadcast_in_dim x1 -> x0, local copies, waits for them, and re-layouts: 0.79 us -> none  [local(): return result[None, None]]
    pallas_call x1, Pallas kernels: 6.3 us -> 6.91 us  [local(): pl.pallas_call(functools.partial(second_kernel, masks), out_shape=jax.Sha...]
  transfers between devices with their start and end apart: 7 -> 8, of which waited for: 6 -> 7; matrix products, arithmetic and copies ran while one was open for 3% -> 0% of each run, Pallas kernels for 0% -> 0%
where the time goes in v3:
time: 39.7 us; the launch traced here: 39.5 us
  starting transfers between devices  13.4 us (34%)
  waiting for transfers between devices  13.3 us (34%)
  Pallas kernels  9.52 us (24%)
  local copies, waits for them, and re-layouts  1.91 us (5%)
  other arithmetic  1.15 us (3%)
    ppermute x5, starting transfers between devices, swapped(): return lax.ppermute(value, axis, pairs)  9.84 us
    ppermute x5, waiting for transfers between devices, swapped(): return lax.ppermute(value, axis, pairs)  8.63 us
    pallas_call x1, Pallas kernels, local(): pl.pallas_call(functools.partial(second_kernel, masks), out_shape=jax.Sha...  6.91 us
    ppermute x3, waiting for transfers between devices, crossed(): lax.ppermute(value, both, [(source, source ^ mask) for source in range(co...  4.68 us
    ppermute x3, starting transfers between devices, crossed(): lax.ppermute(value, both, [(source, source ^ mask) for source in range(co...  3.55 us
    pallas_call x1, Pallas kernels, local(): pl.pallas_call(functools.partial(first_kernel, bands, side), out_shape=(f...  2.34 us
    unnamed x20, local copies, waits for them, and re-layouts  1.91 us
    concatenate x1, other arithmetic, local(): cubes = jnp.concatenate([cubes, swapped(cubes, 'dom', bit)], 0)  0.99 us
  transfers between devices with their start and end apart: 8, of which 7 were waited for; matrix products, arithmetic and copies ran while one was open for 0% of the time, Pallas kernels for 0%

profile of v3, /device:TPU:0, one launch (start us, length us, event | category | flops | bytes accessed | tf_op | source)
XLA Modules:
  0.0 39.5 jit_solution(6356249207632076007)
XLA Ops:
  0.0 0.9 %copy-done.2 = f32[1,40,1600]{2,1,0:T(8,128)S(1)} copy-done((f32[1,40,1600]{2,1,0:T(8,128)S(1)}, f32[1,40,1600]{2,1,0:T(8,128)}, u32[]{:S(2)}) %copy-start.2) | copy-done | bytes 256024
  1.0 0.9 %copy-done.4 = f32[1,1,20,1600]{3,1,2,0:T(1,128)S(1)} copy-done((f32[1,1,20,1600]{3,1,2,0:T(1,128)S(1)}, f32[1,1,20,1600]{3,1,2,0:T(1,128)}, u32[]{:S(2)}) %copy-start.4) | copy-done | bytes 128024
  1.9 0.3 shard_map.100
  2.1 3.0 %collective-permute-start = (f32[8,1600]{1,0:T(8,128)S(1)}, f32[8,1600]{1,0:T(8,128)S(1)}, u32[]{:S(2)}, u32[]{:S(2)}) collective-permute-start(f32[8,1600]{1,0:T(8,128)S(1)} %get-tuple-element.15), channel_id=1, source_target_pairs={{0,1},{1,0},{2,3},{3,2},{4,5},{5,4},{6,7},{7,6},{8,9},{9,8},{10,11... | collective-permute-start | bytes 153608 | tf_op jit(solution)/shard_map/ppermute | solution.py:24
  5.2 2.1 %collective-permute-done.halo_ref = f32[8,1600]{1,0:T(8,128)S(1)} collective-permute-done((f32[8,1600]{1,0:T(8,128)S(1)}, f32[8,1600]{1,0:T(8,128)S(1)}, u32[]{:S(2)}, u32[]{:S(2)}) %collective-permute-start) | collective-permute-done | bytes 51232 | tf_op jit(solution)/shard_map/ppermute | solution.py:24
  7.3 2.3 %shard_map.101 = (f32[32,1664]{1,0:T(8,128)S(1)}, f32[8,1600]{1,0:T(8,128)S(1)}, f32[16,1024]{1,0:T(8,128)S(1)}) custom-call(s32[1]{0:T(128)} %bitcast.slab_ref, f32[32,1664]{1,0:T(8,128)S(1)} %get-tuple-element.14.start_ref, f32[8,1600]{1,0:T(8,128)S(1)} %collective-permute-done.halo_ref, f32[32,1664]{1,0:T(8,128)S(1)} %get-tuple-element.16.coef_ref.start_coef_ref), custom_call_target="tpu_custom_call" | custom-call | tf_op jit(solution)/shard_map/pallas_call | solution.py:413
  9.6 0.0 copy-start
  9.6 0.0 copy-start.1
  9.7 2.2 %collective-permute-start.1 = (f32[16,1024]{1,0:T(8,128)S(1)}, f32[16,1024]{1,0:T(8,128)S(1)}, u32[]{:S(2)}, u32[]{:S(2)}) collective-permute-start(f32[16,1024]{1,0:T(8,128)S(1)} %get-tuple-element.17), channel_id=1, source_target_pairs={{0,2},{1,3},{2,0},{3,1},{4,6},{5,7},{6,4},{7,5},{8,10},{9,11},{10,... | collective-permute-start | bytes 196616 | tf_op jit(solution)/shard_map/ppermute | solution.py:24
  11.9 2.2 %collective-permute-done.1 = f32[16,1024]{1,0:T(8,128)S(1)} collective-permute-done((f32[16,1024]{1,0:T(8,128)S(1)}, f32[16,1024]{1,0:T(8,128)S(1)}, u32[]{:S(2)}, u32[]{:S(2)}) %collective-permute-start.1) | collective-permute-done | bytes 65568 | tf_op jit(solution)/shard_map/ppermute | solution.py:24
  14.1 3.1 %collective-permute-start.2 = (f32[16,1024]{1,0:T(8,128)S(1)}, f32[16,1024]{1,0:T(8,128)S(1)}, u32[]{:S(2)}, u32[]{:S(2)}) collective-permute-start(f32[16,1024]{1,0:T(8,128)S(1)} %add.11), channel_id=1, source_target_pairs={{0,4},{1,5},{2,6},{3,7},{4,0},{5,1},{6,2},{7,3},{8,12},{9,13},{10,... | collective-permute-start | bytes 196616 | tf_op jit(solution)/shard_map/ppermute | solution.py:24
  17.2 1.5 %collective-permute-start.3 = (f32[8,1600]{1,0:T(8,128)S(1)}, f32[8,1600]{1,0:T(8,128)S(1)}, u32[]{:S(2)}, u32[]{:S(2)}) collective-permute-start(f32[8,1600]{1,0:T(8,128)S(1)} %get-tuple-element.19), channel_id=1, source_target_pairs={{0,1},{1,0},{2,3},{3,2},{4,5},{5,4},{6,7},{7,6},{8,9},{9,8},{10,11... | collective-permute-start | bytes 153608 | tf_op jit(solution)/shard_map/ppermute | solution.py:24
  18.7 2.7 %collective-permute-done.3.halo_ref = f32[8,1600]{1,0:T(8,128)S(1)} collective-permute-done((f32[8,1600]{1,0:T(8,128)S(1)}, f32[8,1600]{1,0:T(8,128)S(1)}, u32[]{:S(2)}, u32[]{:S(2)}) %collective-permute-start.3) | collective-permute-done | bytes 51232 | tf_op jit(solution)/shard_map/ppermute | solution.py:24
  21.4 1.6 %collective-permute-start.4 = (f32[16,1024]{1,0:T(8,128)S(1)}, f32[16,1024]{1,0:T(8,128)S(1)}, u32[]{:S(2)}, u32[]{:S(2)}) collective-permute-start(f32[16,1024]{1,0:T(8,128)S(1)} %add.12), channel_id=1, source_target_pairs={{0,1},{1,0},{2,3},{3,2},{4,5},{5,4},{6,7},{7,6},{8,9},{9,8},{10,11... | collective-permute-start | bytes 196616 | tf_op jit(solution)/shard_map/ppermute | solution.py:437
  23.0 1.5 %collective-permute-start.5 = (f32[16,1024]{1,0:T(8,128)S(1)}, f32[16,1024]{1,0:T(8,128)S(1)}, u32[]{:S(2)}, u32[]{:S(2)}) collective-permute-start(f32[16,1024]{1,0:T(8,128)S(1)} %add.12), channel_id=1, source_target_pairs={{0,16},{1,17},{2,18},{3,19},{4,20},{5,21},{6,22},{7,23},{8,24},{9,... | collective-permute-start | bytes 196616 | tf_op jit(solution)/shard_map/ppermute | solution.py:437
  24.5 0.5 %collective-permute-start.6 = (f32[16,1024]{1,0:T(8,128)S(1)}, f32[16,1024]{1,0:T(8,128)S(1)}, u32[]{:S(2)}, u32[]{:S(2)}) collective-permute-start(f32[16,1024]{1,0:T(8,128)S(1)} %add.12), channel_id=1, source_target_pairs={{0,17},{1,16},{2,19},{3,18},{4,21},{5,20},{6,23},{7,22},{8,25},{9,... | collective-permute-start | bytes 196616 | tf_op jit(solution)/shard_map/ppermute | solution.py:437
  25.0 0.8 %collective-permute-done.4 = f32[16,1024]{1,0:T(8,128)S(1)} collective-permute-done((f32[16,1024]{1,0:T(8,128)S(1)}, f32[16,1024]{1,0:T(8,128)S(1)}, u32[]{:S(2)}, u32[]{:S(2)}) %collective-permute-start.4) | collective-permute-done | bytes 65568 | tf_op jit(solution)/shard_map/ppermute | solution.py:437
  25.8 1.5 %collective-permute-done.5 = f32[16,1024]{1,0:T(8,128)S(1)} collective-permute-done((f32[16,1024]{1,0:T(8,128)S(1)}, f32[16,1024]{1,0:T(8,128)S(1)}, u32[]{:S(2)}, u32[]{:S(2)}) %collective-permute-start.5) | collective-permute-done | bytes 65568 | tf_op jit(solution)/shard_map/ppermute | solution.py:437
  27.3 2.4 %collective-permute-done.6 = f32[16,1024]{1,0:T(8,128)S(1)} collective-permute-done((f32[16,1024]{1,0:T(8,128)S(1)}, f32[16,1024]{1,0:T(8,128)S(1)}, u32[]{:S(2)}, u32[]{:S(2)}) %collective-permute-start.6) | collective-permute-done | bytes 65568 | tf_op jit(solution)/shard_map/ppermute | solution.py:437
  29.8 0.1 collective-permute-start.7
  29.8 0.1 pad_add_fusion.index_ref
  29.9 1.6 %collective-permute-done.7 = f32[2,32,1024]{2,1,0:T(8,128)} collective-permute-done((f32[2,32,1024]{2,1,0:T(8,128)S(1)}, f32[2,32,1024]{2,1,0:T(8,128)}, u32[]{:S(2)}, u32[]{:S(2)}) %collective-permute-start.7) | collective-permute-done | bytes 262176 | tf_op jit(solution)/shard_map/ppermute | solution.py:24
  31.5 1.0 %pad_maximum_fusion.cubes_ref = f32[4,32,1024]{2,1,0:T(8,128)S(1)} fusion(f32[2,32,1024]{2,1,0:T(8,128)} %collective-permute-done.7, f32[1,32,1024]{2,1,0:T(8,128)S(1)} %get-tuple-element.28, f32[1,32,1024]{2,1,0:T(8,128)S(1)} %get-tuple-element.27), kind=kLoop, calls=%fused_computation | loop fusion | flops 262144 | bytes 1048576 | tf_op jit(solution)/shard_map/concatenate | solution.py:450
  32.6 6.9 %shard_map.102 = f32[20,1,1600]{2,1,0:T(1,128)} custom-call(s32[2]{0:T(128)S(1)} %pad_add_fusion.index_ref, s32[4,3]{1,0:T(4,128)S(1)} %copy-done.9, f32[4,32,1024]{2,1,0:T(8,128)S(1)} %pad_maximum_fusion.cubes_ref, f32[32,1664]{1,0:T(8,128)S(1)} %get-tuple-element.21.filt_ref, f32[8,1600]{1,0:T(8,128)S(1)} %collective-permute-done.3.halo_ref, ...), custom_call_target="tpu_custom_call" | custom-call | tf_op jit(solution)/shard_map/pallas_call | solution.py:458
  (23 shorter events, 0.1 us)
Async XLA Ops:
  0.0 1.0 %copy-start.2 = (f32[1,40,1600]{2,1,0:T(8,128)S(1)}, f32[1,40,1600]{2,1,0:T(8,128)}, u32[]{:S(2)}) copy-start(f32[1,40,1600]{2,1,0:T(8,128)} %param.11) | copy-start | bytes 768004
  1.0 0.9 %copy-start.4 = (f32[1,1,20,1600]{3,1,2,0:T(1,128)S(1)}, f32[1,1,20,1600]{3,1,2,0:T(1,128)}, u32[]{:S(2)}) copy-start(f32[1,1,20,1600]{3,1,2,0:T(1,128)} %param.10) | copy-start | bytes 384004
  2.1 5.1 %collective-permute-start = (f32[8,1600]{1,0:T(8,128)S(1)}, f32[8,1600]{1,0:T(8,128)S(1)}, u32[]{:S(2)}, u32[]{:S(2)}) collective-permute-start(f32[8,1600]{1,0:T(8,128)S(1)} %get-tuple-element.15), channel_id=1, source_target_pairs={{0,1},{1,0},{2,3},{3,2},{4,5},{5,4},{6,7},{7,6},{8,9},{9,8},{10,11... | collective-permute-start | bytes 153608 | tf_op jit(solution)/shard_map/ppermute | solution.py:24
  9.6 22.9 %copy-start = (bf16[1536,512]{1,0:T(8,128)(2,1)S(1)}, bf16[1536,512]{1,0:T(8,128)(2,1)}, u32[]{:S(2)}) copy-start(bf16[1536,512]{1,0:T(8,128)(2,1)} %constant.36.clone.into_ref) | copy-start | bytes 4718596
  9.6 22.9 %copy-start.1 = (f32[1024,128]{1,0:T(8,128)S(1)}, f32[1024,128]{1,0:T(8,128)}, u32[]{:S(2)}) copy-start(f32[1024,128]{1,0:T(8,128)} %constant.41.clone.factor_ref) | copy-start | bytes 1572868
  9.6 22.9 %copy-start.3 = (bf16[384,160]{1,0:T(8,128)(2,1)S(1)}, bf16[384,160]{1,0:T(8,128)(2,1)}, u32[]{:S(2)}) copy-start(bf16[384,160]{1,0:T(8,128)(2,1)} %constant.42.clone.spread_ref) | copy-start | bytes 368644
  9.6 22.9 %copy-start.5 = (bf16[256,256]{1,0:T(8,128)(2,1)S(1)}, bf16[256,256]{1,0:T(8,128)(2,1)}, u32[]{:S(2)}) copy-start(bf16[256,256]{1,0:T(8,128)(2,1)} %constant.40.clone.back_z_ref) | copy-start | bytes 393220
  9.7 22.9 %copy-start.6 = (bf16[2,64,96]{2,1,0:T(8,128)(2,1)S(1)}, bf16[2,64,96]{2,1,0:T(8,128)(2,1)}, u32[]{:S(2)}) copy-start(bf16[2,64,96]{2,1,0:T(8,128)(2,1)} %constant.39.clone.back_x_ref) | copy-start | bytes 73732
  9.7 22.9 %copy-start.7 = (bf16[80,96]{1,0:T(8,128)(2,1)S(1)}, bf16[80,96]{1,0:T(8,128)(2,1)}, u32[]{:S(2)}) copy-start(bf16[80,96]{1,0:T(8,128)(2,1)} %constant.38.clone.back_y_ref) | copy-start | bytes 46084
  9.7 22.9 %copy-start.8 = (bf16[64,96]{1,0:T(8,128)(2,1)S(1)}, bf16[64,96]{1,0:T(8,128)(2,1)}, u32[]{:S(2)}) copy-start(bf16[64,96]{1,0:T(8,128)(2,1)} %constant.37.clone.forward_ref) | copy-start | bytes 36868
  9.7 22.9 %copy-start.9 = (s32[4,3]{1,0:T(4,128)S(1)}, s32[4,3]{1,0:T(4,128)}, u32[]{:S(2)}) copy-start(s32[4,3]{1,0:T(4,128)} %offsets_ref.1) | copy-start | bytes 148
  9.7 4.4 %collective-permute-start.1 = (f32[16,1024]{1,0:T(8,128)S(1)}, f32[16,1024]{1,0:T(8,128)S(1)}, u32[]{:S(2)}, u32[]{:S(2)}) collective-permute-start(f32[16,1024]{1,0:T(8,128)S(1)} %get-tuple-element.17), channel_id=1, source_target_pairs={{0,2},{1,3},{2,0},{3,1},{4,6},{5,7},{6,4},{7,5},{8,10},{9,11},{10,... | collective-permute-start | bytes 196616 | tf_op jit(solution)/shard_map/ppermute | solution.py:24
  14.1 7.3 %collective-permute-start.2 = (f32[16,1024]{1,0:T(8,128)S(1)}, f32[16,1024]{1,0:T(8,128)S(1)}, u32[]{:S(2)}, u32[]{:S(2)}) collective-permute-start(f32[16,1024]{1,0:T(8,128)S(1)} %add.11), channel_id=1, source_target_pairs={{0,4},{1,5},{2,6},{3,7},{4,0},{5,1},{6,2},{7,3},{8,12},{9,13},{10,... | collective-permute-start | bytes 196616 | tf_op jit(solution)/shard_map/ppermute | solution.py:24
  17.2 4.2 %collective-permute-start.3 = (f32[8,1600]{1,0:T(8,128)S(1)}, f32[8,1600]{1,0:T(8,128)S(1)}, u32[]{:S(2)}, u32[]{:S(2)}) collective-permute-start(f32[8,1600]{1,0:T(8,128)S(1)} %get-tuple-element.19), channel_id=1, source_target_pairs={{0,1},{1,0},{2,3},{3,2},{4,5},{5,4},{6,7},{7,6},{8,9},{9,8},{10,11... | collective-permute-start | bytes 153608 | tf_op jit(solution)/shard_map/ppermute | solution.py:24
  21.4 4.3 %collective-permute-start.4 = (f32[16,1024]{1,0:T(8,128)S(1)}, f32[16,1024]{1,0:T(8,128)S(1)}, u32[]{:S(2)}, u32[]{:S(2)}) collective-permute-start(f32[16,1024]{1,0:T(8,128)S(1)} %add.12), channel_id=1, source_target_pairs={{0,1},{1,0},{2,3},{3,2},{4,5},{5,4},{6,7},{7,6},{8,9},{9,8},{10,11... | collective-permute-start | bytes 196616 | tf_op jit(solution)/shard_map/ppermute | solution.py:437
  23.0 4.3 %collective-permute-start.5 = (f32[16,1024]{1,0:T(8,128)S(1)}, f32[16,1024]{1,0:T(8,128)S(1)}, u32[]{:S(2)}, u32[]{:S(2)}) collective-permute-start(f32[16,1024]{1,0:T(8,128)S(1)} %add.12), channel_id=1, source_target_pairs={{0,16},{1,17},{2,18},{3,19},{4,20},{5,21},{6,22},{7,23},{8,24},{9,... | collective-permute-start | bytes 196616 | tf_op jit(solution)/shard_map/ppermute | solution.py:437
  24.5 5.2 %collective-permute-start.6 = (f32[16,1024]{1,0:T(8,128)S(1)}, f32[16,1024]{1,0:T(8,128)S(1)}, u32[]{:S(2)}, u32[]{:S(2)}) collective-permute-start(f32[16,1024]{1,0:T(8,128)S(1)} %add.12), channel_id=1, source_target_pairs={{0,17},{1,16},{2,19},{3,18},{4,21},{5,20},{6,23},{7,22},{8,25},{9,... | collective-permute-start | bytes 196616 | tf_op jit(solution)/shard_map/ppermute | solution.py:437
  29.8 1.7 %collective-permute-start.7 = (f32[2,32,1024]{2,1,0:T(8,128)S(1)}, f32[2,32,1024]{2,1,0:T(8,128)}, u32[]{:S(2)}, u32[]{:S(2)}) collective-permute-start(f32[2,32,1024]{2,1,0:T(8,128)S(1)} %pad_maximum_fusion.1), channel_id=1, source_target_pairs={{0,8},{8,0},{16,24},{24,16},{1,9},{9,1},{17,25},{25,17},{2,10},{10... | collective-permute-start | bytes 786440 | tf_op jit(solution)/shard_map/ppermute | solution.py:24

commit v4 on v3

--- a/solution.py
+++ b/solution.py
@@ -70,37 +70,23 @@
     return jnp.where(is_lower, own[half - DEG : half], own[0:DEG])
 
 
-def start_kernel(slab_ref, psi_ref, pot_ref, edge_ref, field_ref, coef_ref, own_ref, all_ref, sems):
+def start_kernel(slab_ref, psi_ref, pot_ref, field_ref, coef_ref):
     half, _, cells = psi_ref.shape
     side = 2 * half
     is_lower = slab_ref[0] == 0
-    rows_copy = pltpu.make_async_copy(psi_ref, own_ref, sems.at[0])
-    pot_copy = pltpu.make_async_copy(pot_ref, all_ref, sems.at[1])
-    rows_copy.start()
-    pot_copy.start()
     field_ref[...] = jnp.zeros(field_ref.shape, jnp.float32)
     coef_ref[...] = jnp.zeros(coef_ref.shape, jnp.float32)
-    rows_copy.wait()
-    own = own_ref[:, 0, :]
-    edge_ref[...] = edge_rows(is_lower, own, half)
+    own = psi_ref[:, 0, :]
 
     @pl.when(is_lower)
     def _():
         field_ref[0:half, 0:cells] = own
+        coef_ref[0 : half + DEG, 0:cells] = pot_ref[0 : half + DEG] * (2.0 / HALF_WIDTH)
 
     @pl.when(jnp.logical_not(is_lower))
     def _():
         field_ref[DEG : DEG + half, 0:cells] = own
-
-    pot_copy.wait()
-
-    @pl.when(is_lower)
-    def _():
-        coef_ref[0 : half + DEG, 0:cells] = all_ref[0 : half + DEG] * (2.0 / HALF_WIDTH)
-
-    @pl.when(jnp.logical_not(is_lower))
-    def _():
-        coef_ref[0 : half + DEG, 0:cells] = all_ref[half - DEG : side] * (2.0 / HALF_WIDTH)
+        coef_ref[0 : half + DEG, 0:cells] = pot_ref[half - DEG : side] * (2.0 / HALF_WIDTH)
 
 
 def filtered_field(field, scaled_potential, half, side):
@@ -133,13 +119,16 @@
 
 def first_kernel(bands, side, slab_ref, start_ref, halo_ref, coef_ref, filt_ref, edge_ref, dens_ref, field_ref):
     half = side // 2
-    cells = side * side
     is_lower = slab_ref[0] == 0
     field_ref[...] = start_ref[...]
-    set_halo(is_lower, halo_ref[...], field_ref, half)
+    set_halo(is_lower, halo_ref[:, 0, :], field_ref, half)
     result = filtered_field(field_ref[...], coef_ref[...], half, side)
     filt_ref[...] = result
-    edge_ref[...] = edge_rows(is_lower, own_rows(is_lower, result, half), half)[:, 0:cells]
+    edge = edge_rows(is_lower, own_rows(is_lower, result, half), half)
+    width = edge_ref.shape[1]
+    edge_ref[0:DEG] = edge[:, 0:width]
+    edge_ref[DEG : 2 * DEG] = jnp.zeros((DEG, width), jnp.float32)
+    edge_ref[DEG : 2 * DEG, 0 : edge.shape[1] - width] = edge[:, width:]
     slab = CORE // 2
     core_rows = jnp.where(is_lower, result[BUF : BUF + slab], result[DEG : DEG + slab])
     squares = core_rows * core_rows * (1.0 / bands)
@@ -242,9 +231,9 @@
 
 
 def second_kernel(
-    masks, index_ref, offsets_ref, cubes_ref, filt_ref, halo_ref, start_coef_ref,
+    masks, index_ref, offsets_ref, near_ref, across_ref, filt_ref, beside_ref, start_coef_ref,
     into_ref, forward_ref, back_y_ref, back_x_ref, back_z_ref, factor_ref, spread_ref,
-    out_ref, field_ref, coef_ref, dens_ref, left_ref, rows_ref, waves_ref, mixed_ref, flat_ref,
+    out_ref, cubes_ref, field_ref, coef_ref, dens_ref, left_ref, rows_ref, waves_ref, mixed_ref, flat_ref,
 ):
     half, _, cells = out_ref.shape
     side = 2 * half
@@ -274,6 +263,8 @@
             found = found + jnp.where(place_of[idx] == where, idx, 0)
         cube_at.append(found)
 
+    cubes_ref[0 : dom_count // 2] = near_ref[...]
+    cubes_ref[dom_count // 2 : dom_count] = across_ref[...]
     mean = jnp.sum(cubes_ref[...]) * (1.0 / (dom_count * CORE * CORE * CORE))
 
     for where in range(dom_count):
@@ -367,15 +358,16 @@
 
     coef_ref[...] = start_coef_ref[...] + hartree_exchange * (2.0 / HALF_WIDTH)
     field_ref[...] = filt_ref[...]
-    set_halo(is_lower, halo_ref[...], field_ref, half)
+    packed = beside_ref[CORE // 2 :]
+    halo = jnp.concatenate([packed[0:DEG], packed[DEG : 2 * DEG]], 1)[:, 0:cells]
+    set_halo(is_lower, halo, field_ref, half)
     result = filtered_field(field_ref[...], coef_ref[...], half, side)
     out_ref[:, 0, :] = own_rows(is_lower, result, half)[:, 0:cells]
 
 
 SMEM = pl.BlockSpec(memory_space=pltpu.SMEM)
 VMEM = pl.BlockSpec(memory_space=pltpu.VMEM)
-HBM = pl.BlockSpec(memory_space=pltpu.HBM)
-params = pltpu.CompilerParams(vmem_limit_bytes=40 * 1024 * 1024)
+params = pltpu.CompilerParams(vmem_limit_bytes=32 * 1024 * 1024)
 
 
 def local(psi_in, v_in, offsets):
@@ -395,39 +387,33 @@
     field_rows = padded(half + DEG, 8)
     field_shape = (field_rows, padded(cells, 128))
     field_type = jax.ShapeDtypeStruct(field_shape, f32)
-    edge_type = jax.ShapeDtypeStruct((DEG, cells), f32)
-
-    edge, start, coef = pl.pallas_call(
+    rows = psi_in.reshape(half, 1, cells)
+    halo = swapped(lax.dynamic_slice_in_dim(rows, jnp.where(is_lower, half - DEG, 0), DEG, 0), "band", 1)
+    start, coef = pl.pallas_call(
         start_kernel,
-        out_shape=(edge_type, field_type, field_type),
-        in_specs=[SMEM, HBM, HBM],
-        out_specs=(VMEM, VMEM, VMEM),
-        scratch_shapes=[
-            pltpu.VMEM((half, 1, cells), f32),
-            pltpu.VMEM((side, cells), f32),
-            pltpu.SemaphoreType.DMA((2,)),
-        ],
+        out_shape=(field_type, field_type),
+        in_specs=[SMEM, VMEM, VMEM],
+        out_specs=(VMEM, VMEM),
         compiler_params=params,
-    )(slab_scalar, psi_in.reshape(half, 1, cells), v_in[0])
+    )(slab_scalar, rows, v_in[0])
 
     filt, edge, dens = pl.pallas_call(
         functools.partial(first_kernel, bands, side),
-        out_shape=(field_type, edge_type, jax.ShapeDtypeStruct((CORE // 2, CORE * CORE), f32)),
+        out_shape=(
+            field_type,
+            jax.ShapeDtypeStruct((2 * DEG, CORE * CORE), f32),
+            jax.ShapeDtypeStruct((CORE // 2, CORE * CORE), f32),
+        ),
         in_specs=[SMEM, VMEM, VMEM, VMEM],
         out_specs=(VMEM, VMEM, VMEM),
         scratch_shapes=[pltpu.VMEM(field_shape, f32)],
         compiler_params=params,
-    )(slab_scalar, start, swapped(edge, "band", 1), coef)
+    )(slab_scalar, start, halo, coef)
 
     mask = 2
     while mask < band_count:
-        received = swapped(dens, "band", mask)
+        dens = dens + swapped(dens, "band", mask)
         mask *= 2
-        if mask >= band_count:
-            edge, _ = lax.optimization_barrier((edge, dens))
-            halo = swapped(edge, "band", 1)
-            received, halo = lax.optimization_barrier((received, halo))
-        dens = dens + received
 
     far = dom_count // 2
     both = ("dom", "band")
@@ -436,7 +422,8 @@
     def crossed(value, mask):
         return lax.ppermute(value, both, [(source, source ^ mask) for source in range(count)])
 
-    beside = crossed(dens, 1)
+    beside_all = crossed(jnp.concatenate([dens, edge], 0), 1)
+    beside = beside_all[: CORE // 2]
     across = crossed(dens, far * band_count)
     diagonal = crossed(dens, far * band_count + 1)
 
@@ -447,9 +434,11 @@
     masks = [0, far]
     bit = far // 2
     while bit:
-        cubes = jnp.concatenate([cubes, swapped(cubes, "dom", bit)], 0)
+        if bit > 1:
+            cubes = jnp.concatenate([cubes, swapped(cubes, "dom", bit)], 0)
         masks = masks + [one | bit for one in masks]
         bit //= 2
+    cubes_across = swapped(cubes, "dom", 1)
 
     tables = solver_tables(side, grid_z)
     names = ("into", "forward", "back_y", "back_x", "back_z", "factor", "spread")
@@ -458,9 +447,10 @@
     result = pl.pallas_call(
         functools.partial(second_kernel, masks),
         out_shape=jax.ShapeDtypeStruct((half, 1, cells), f32),
-        in_specs=[SMEM, SMEM] + [VMEM] * (4 + len(names)),
+        in_specs=[SMEM, SMEM] + [VMEM] * (5 + len(names)),
         out_specs=VMEM,
-        scratch_shapes=[pltpu.VMEM(field_shape, f32)] * 3
+        scratch_shapes=[pltpu.VMEM((dom_count, CORE, CORE * CORE), f32)]
+        + [pltpu.VMEM(field_shape, f32)] * 3
         + [
             pltpu.VMEM((CORE * CORE * CORE // 128, dom_count * 3 * 128), bf16),
             pltpu.VMEM((lanes // 128, CORE * CORE, 128), f32),
@@ -469,7 +459,7 @@
             pltpu.VMEM((side * field_rows, 2 * lanes), bf16),
         ],
         compiler_params=params,
-    )(index, offsets, cubes, filt, halo, coef, *[jnp.asarray(tables[name]) for name in names])
+    )(index, offsets, cubes, cubes_across, filt, beside_all, coef, *[jnp.asarray(tables[name]) for name in names])
     return result.reshape(1, 1, half, cells)
 
 

time: 39.7 us -> 36.8 us (0.927)
  waiting for transfers between devices: 13.3 us -> 10.8 us
  local copies, waits for them, and re-layouts: 1.91 us -> 4.11 us
  starting transfers between devices: 13.4 us -> 12 us
  other arithmetic: 1.15 us -> 0.17 us
    ppermute x5 -> x4, waiting for transfers between devices: 8.63 us -> 6.1 us  [swapped(): return lax.ppermute(value, axis, pairs)]
    ppermute x5 -> x4, starting transfers between devices: 9.84 us -> 8.34 us  [swapped(): return lax.ppermute(value, axis, pairs)]
    unnamed x20, local copies, waits for them, and re-layouts: 1.91 us -> 3.28 us
    concatenate x1, other arithmetic: 0.99 us -> 0.01 us  [local(): beside_all = crossed(jnp.concatenate([dens, edge], 0), 1)]
    dynamic_slice x0 -> x1, local copies, waits for them, and re-layouts: none -> 0.82 us  [local(): lax.dynamic_slice_in_dim(rows, jnp.where(is_lower, half - DEG, 0), DEG, 0)]
  transfers between devices with their start and end apart: 8 -> 7, of which waited for: 7 -> 7; matrix products, arithmetic and copies ran while one was open for 0% -> 0% of each run, Pallas kernels for 0% -> 0%
where the time goes in v4:
time: 36.8 us; the launch traced here: 36.5 us
  starting transfers between devices  12 us (33%)
  waiting for transfers between devices  10.8 us (29%)
  Pallas kernels  9.32 us (25%)
  local copies, waits for them, and re-layouts  4.11 us (11%)
    ppermute x4, starting transfers between devices, swapped(): return lax.ppermute(value, axis, pairs)  8.34 us
    pallas_call x1, Pallas kernels, local(): pl.pallas_call(functools.partial(second_kernel, masks), out_shape=jax.Sha...  6.9 us
    ppermute x4, waiting for transfers between devices, swapped(): return lax.ppermute(value, axis, pairs)  6.1 us
    ppermute x3, waiting for transfers between devices, crossed(): lax.ppermute(value, both, [(source, source ^ mask) for source in range(co...  4.73 us
    ppermute x3, starting transfers between devices, crossed(): lax.ppermute(value, both, [(source, source ^ mask) for source in range(co...  3.62 us
    unnamed x20, local copies, waits for them, and re-layouts  3.28 us
    pallas_call x1, Pallas kernels, local(): pl.pallas_call(functools.partial(first_kernel, bands, side), out_shape=(f...  2.35 us
    dynamic_slice x1, local copies, waits for them, and re-layouts, local(): lax.dynamic_slice_in_dim(rows, jnp.where(is_lower, half - DEG, 0), DEG, 0)  0.82 us
  transfers between devices with their start and end apart: 7, of which 7 were waited for; matrix products, arithmetic and copies ran while one was open for 0% of the time, Pallas kernels for 0%

profile of v4, /device:TPU:0, one launch (start us, length us, event | category | flops | bytes accessed | tf_op | source)
XLA Modules:
  0.0 36.5 jit_solution(8211466659970638573)
XLA Ops:
  0.0 0.8 %dynamic-slice_bitcast_fusion = f32[8,1,1600]{2,1,0:T(1,128)S(1)} fusion(f32[1,1,20,1600]{3,1,2,0:T(1,128)} %param.10, s32[]{:T(128)S(6)} %select_n.34), kind=kLoop, calls=%fused_computation.6 | loop fusion | bytes 102404 | tf_op jit(solution)/shard_map/dynamic_slice | solution.py:391
  0.8 0.0 copy-start.1
  0.8 3.0 %collective-permute-start = (f32[8,1,1600]{2,1,0:T(1,128)S(1)}, f32[8,1,1600]{2,1,0:T(1,128)S(1)}, u32[]{:S(2)}, u32[]{:S(2)}) collective-permute-start(f32[8,1,1600]{2,1,0:T(1,128)S(1)} %dynamic-slice_bitcast_fusion), channel_id=1, source_target_pairs={{0,1},{1,0},{2,3},{3,2},{4,5},{5,4},{6,7},{7,6},{8,9},{9,8},{10,11... | collective-permute-start | bytes 153608 | tf_op jit(solution)/shard_map/ppermute | solution.py:24
  3.9 0.9 %copy-done.2 = f32[1,40,1600]{2,1,0:T(8,128)S(1)} copy-done((f32[1,40,1600]{2,1,0:T(8,128)S(1)}, f32[1,40,1600]{2,1,0:T(8,128)}, u32[]{:S(2)}) %copy-start.2) | copy-done | bytes 256024
  4.8 0.9 %copy-done.3 = f32[1,1,20,1600]{3,1,2,0:T(1,128)S(1)} copy-done((f32[1,1,20,1600]{3,1,2,0:T(1,128)S(1)}, f32[1,1,20,1600]{3,1,2,0:T(1,128)}, u32[]{:S(2)}) %copy-start.3) | copy-done | bytes 128024
  5.7 0.1 shard_map.100
  5.8 0.2 collective-permute-done.halo_ref
  6.0 2.3 %shard_map.101 = (f32[32,1664]{1,0:T(8,128)S(1)}, f32[16,1024]{1,0:T(8,128)S(1)}, f32[16,1024]{1,0:T(8,128)S(1)}) custom-call(s32[1]{0:T(128)} %bitcast.slab_ref, f32[32,1664]{1,0:T(8,128)S(1)} %get-tuple-element.10.start_ref, f32[8,1,1600]{2,1,0:T(1,128)S(1)} %collective-permute-done.halo_ref, f32[32,1664]{1,0:T(8,128)S(1)} %get-tuple-element.11.coef_ref.start_coef_ref), custom_call_target="tpu_custom_call" | custom-call | tf_op jit(solution)/shard_map/pallas_call | solution.py:400
  8.3 2.2 %collective-permute-start.1 = (f32[16,1024]{1,0:T(8,128)S(1)}, f32[16,1024]{1,0:T(8,128)S(1)}, u32[]{:S(2)}, u32[]{:S(2)}) collective-permute-start(f32[16,1024]{1,0:T(8,128)S(1)} %get-tuple-element.12), channel_id=1, source_target_pairs={{0,2},{1,3},{2,0},{3,1},{4,6},{5,7},{6,4},{7,5},{8,10},{9,11},{10,... | collective-permute-start | bytes 196616 | tf_op jit(solution)/shard_map/ppermute | solution.py:24
  10.5 2.2 %collective-permute-done.1 = f32[16,1024]{1,0:T(8,128)S(1)} collective-permute-done((f32[16,1024]{1,0:T(8,128)S(1)}, f32[16,1024]{1,0:T(8,128)S(1)}, u32[]{:S(2)}, u32[]{:S(2)}) %collective-permute-start.1) | collective-permute-done | bytes 65568 | tf_op jit(solution)/shard_map/ppermute | solution.py:24
  12.8 3.1 %collective-permute-start.2 = (f32[16,1024]{1,0:T(8,128)S(1)}, f32[16,1024]{1,0:T(8,128)S(1)}, u32[]{:S(2)}, u32[]{:S(2)}) collective-permute-start(f32[16,1024]{1,0:T(8,128)S(1)} %add.12), channel_id=1, source_target_pairs={{0,4},{1,5},{2,6},{3,7},{4,0},{5,1},{6,2},{7,3},{8,12},{9,13},{10,... | collective-permute-start | bytes 196616 | tf_op jit(solution)/shard_map/ppermute | solution.py:24
  15.8 2.2 %collective-permute-done.2 = f32[16,1024]{1,0:T(8,128)S(1)} collective-permute-done((f32[16,1024]{1,0:T(8,128)S(1)}, f32[16,1024]{1,0:T(8,128)S(1)}, u32[]{:S(2)}, u32[]{:S(2)}) %collective-permute-start.2) | collective-permute-done | bytes 65568 | tf_op jit(solution)/shard_map/ppermute | solution.py:24
  18.1 1.9 %collective-permute-start.4 = (f32[16,1024]{1,0:T(8,128)S(1)}, f32[16,1024]{1,0:T(8,128)S(1)}, u32[]{:S(2)}, u32[]{:S(2)}) collective-permute-start(f32[16,1024]{1,0:T(8,128)S(1)} %add.13), channel_id=1, source_target_pairs={{0,16},{1,17},{2,18},{3,19},{4,20},{5,21},{6,22},{7,23},{8,24},{9,... | collective-permute-start | bytes 196616 | tf_op jit(solution)/shard_map/ppermute | solution.py:423
  20.0 1.4 %collective-permute-start.5 = (f32[16,1024]{1,0:T(8,128)S(1)}, f32[16,1024]{1,0:T(8,128)S(1)}, u32[]{:S(2)}, u32[]{:S(2)}) collective-permute-start(f32[16,1024]{1,0:T(8,128)S(1)} %add.13), channel_id=1, source_target_pairs={{0,17},{1,16},{2,19},{3,18},{4,21},{5,20},{6,23},{7,22},{8,25},{9,... | collective-permute-start | bytes 196616 | tf_op jit(solution)/shard_map/ppermute | solution.py:423
  21.5 0.3 collective-permute-start.3
  21.7 0.7 %collective-permute-done.4 = f32[16,1024]{1,0:T(8,128)S(1)} collective-permute-done((f32[16,1024]{1,0:T(8,128)S(1)}, f32[16,1024]{1,0:T(8,128)S(1)}, u32[]{:S(2)}, u32[]{:S(2)}) %collective-permute-start.4) | collective-permute-done | bytes 65568 | tf_op jit(solution)/shard_map/ppermute | solution.py:423
  22.4 2.7 %collective-permute-done.5 = f32[16,1024]{1,0:T(8,128)S(1)} collective-permute-done((f32[16,1024]{1,0:T(8,128)S(1)}, f32[16,1024]{1,0:T(8,128)S(1)}, u32[]{:S(2)}, u32[]{:S(2)}) %collective-permute-start.5) | collective-permute-done | bytes 65568 | tf_op jit(solution)/shard_map/ppermute | solution.py:423
  25.2 1.3 %collective-permute-done.3.beside_ref = f32[32,1024]{1,0:T(8,128)S(1)} collective-permute-done((f32[32,1024]{1,0:T(8,128)S(1)}, f32[32,1024]{1,0:T(8,128)S(1)}, u32[]{:S(2)}, u32[]{:S(2)}) %collective-permute-start.3) | collective-permute-done | bytes 131104 | tf_op jit(solution)/shard_map/ppermute | solution.py:423
  26.6 0.1 collective-permute-start.6
  26.7 0.1 pad_add_fusion.index_ref
  26.7 1.4 %collective-permute-done.6.across_ref = f32[2,32,1024]{2,1,0:T(8,128)S(1)} collective-permute-done((f32[2,32,1024]{2,1,0:T(8,128)S(1)}, f32[2,32,1024]{2,1,0:T(8,128)S(1)}, u32[]{:S(2)}, u32[]{:S(2)}) %collective-permute-start.6) | collective-permute-done | bytes 262176 | tf_op jit(solution)/shard_map/ppermute | solution.py:24
  28.2 0.7 %copy-done.7 = bf16[80,96]{1,0:T(8,128)(2,1)S(1)} copy-done((bf16[80,96]{1,0:T(8,128)(2,1)S(1)}, bf16[80,96]{1,0:T(8,128)(2,1)}, u32[]{:S(2)}) %copy-start.7) | copy-done | bytes 15384
  28.9 0.7 %copy-done.9 = s32[4,3]{1,0:T(4,128)S(1)} copy-done((s32[4,3]{1,0:T(4,128)S(1)}, s32[4,3]{1,0:T(4,128)}, u32[]{:S(2)}) %copy-start.9) | copy-done | bytes 72
  29.6 6.9 %shard_map.102 = f32[20,1,1600]{2,1,0:T(1,128)} custom-call(s32[2]{0:T(128)S(1)} %pad_add_fusion.index_ref, s32[4,3]{1,0:T(4,128)S(1)} %copy-done.9, f32[2,32,1024]{2,1,0:T(8,128)S(1)} %pad_maximum_fusion.near_ref, f32[2,32,1024]{2,1,0:T(8,128)S(1)} %collective-permute-done.6.across_ref, f32[32,1664]{1,0:T(8,128)S(1)} %get-tuple-element.14.filt_ref, ...), custom_call_target="tpu_custom_call" | custom-call | tf_op jit(solution)/shard_map/pallas_call | solution.py:447
  (23 shorter events, 0.1 us)
Async XLA Ops:
  0.0 28.2 %copy-start.6 = (bf16[2,64,96]{2,1,0:T(8,128)(2,1)S(1)}, bf16[2,64,96]{2,1,0:T(8,128)(2,1)}, u32[]{:S(2)}) copy-start(bf16[2,64,96]{2,1,0:T(8,128)(2,1)} %constant.44.clone.back_x_ref) | copy-start | bytes 73732
  0.0 28.2 %copy-start.8 = (bf16[64,96]{1,0:T(8,128)(2,1)S(1)}, bf16[64,96]{1,0:T(8,128)(2,1)}, u32[]{:S(2)}) copy-start(bf16[64,96]{1,0:T(8,128)(2,1)} %constant.42.clone.forward_ref) | copy-start | bytes 36868
  0.8 27.3 %copy-start = (bf16[1536,512]{1,0:T(8,128)(2,1)S(1)}, bf16[1536,512]{1,0:T(8,128)(2,1)}, u32[]{:S(2)}) copy-start(bf16[1536,512]{1,0:T(8,128)(2,1)} %constant.41.clone.into_ref) | copy-start | bytes 4718596
  0.8 27.3 %copy-start.1 = (f32[1024,128]{1,0:T(8,128)S(1)}, f32[1024,128]{1,0:T(8,128)}, u32[]{:S(2)}) copy-start(f32[1024,128]{1,0:T(8,128)} %constant.46.clone.factor_ref) | copy-start | bytes 1572868
  0.8 5.1 %collective-permute-start = (f32[8,1,1600]{2,1,0:T(1,128)S(1)}, f32[8,1,1600]{2,1,0:T(1,128)S(1)}, u32[]{:S(2)}, u32[]{:S(2)}) collective-permute-start(f32[8,1,1600]{2,1,0:T(1,128)S(1)} %dynamic-slice_bitcast_fusion), channel_id=1, source_target_pairs={{0,1},{1,0},{2,3},{3,2},{4,5},{5,4},{6,7},{7,6},{8,9},{9,8},{10,11... | collective-permute-start | bytes 153608 | tf_op jit(solution)/shard_map/ppermute | solution.py:24
  3.9 1.0 %copy-start.2 = (f32[1,40,1600]{2,1,0:T(8,128)S(1)}, f32[1,40,1600]{2,1,0:T(8,128)}, u32[]{:S(2)}) copy-start(f32[1,40,1600]{2,1,0:T(8,128)} %param.11) | copy-start | bytes 768004
  4.8 0.9 %copy-start.3 = (f32[1,1,20,1600]{3,1,2,0:T(1,128)S(1)}, f32[1,1,20,1600]{3,1,2,0:T(1,128)}, u32[]{:S(2)}) copy-start(f32[1,1,20,1600]{3,1,2,0:T(1,128)} %param.10) | copy-start | bytes 384004
  5.7 22.5 %copy-start.4 = (bf16[384,160]{1,0:T(8,128)(2,1)S(1)}, bf16[384,160]{1,0:T(8,128)(2,1)}, u32[]{:S(2)}) copy-start(bf16[384,160]{1,0:T(8,128)(2,1)} %constant.47.clone.spread_ref) | copy-start | bytes 368644
  5.7 22.5 %copy-start.5 = (bf16[256,256]{1,0:T(8,128)(2,1)S(1)}, bf16[256,256]{1,0:T(8,128)(2,1)}, u32[]{:S(2)}) copy-start(bf16[256,256]{1,0:T(8,128)(2,1)} %constant.45.clone.back_z_ref) | copy-start | bytes 393220
  8.3 4.4 %collective-permute-start.1 = (f32[16,1024]{1,0:T(8,128)S(1)}, f32[16,1024]{1,0:T(8,128)S(1)}, u32[]{:S(2)}, u32[]{:S(2)}) collective-permute-start(f32[16,1024]{1,0:T(8,128)S(1)} %get-tuple-element.12), channel_id=1, source_target_pairs={{0,2},{1,3},{2,0},{3,1},{4,6},{5,7},{6,4},{7,5},{8,10},{9,11},{10,... | collective-permute-start | bytes 196616 | tf_op jit(solution)/shard_map/ppermute | solution.py:24
  12.8 5.3 %collective-permute-start.2 = (f32[16,1024]{1,0:T(8,128)S(1)}, f32[16,1024]{1,0:T(8,128)S(1)}, u32[]{:S(2)}, u32[]{:S(2)}) collective-permute-start(f32[16,1024]{1,0:T(8,128)S(1)} %add.12), channel_id=1, source_target_pairs={{0,4},{1,5},{2,6},{3,7},{4,0},{5,1},{6,2},{7,3},{8,12},{9,13},{10,... | collective-permute-start | bytes 196616 | tf_op jit(solution)/shard_map/ppermute | solution.py:24
  18.1 4.3 %collective-permute-start.4 = (f32[16,1024]{1,0:T(8,128)S(1)}, f32[16,1024]{1,0:T(8,128)S(1)}, u32[]{:S(2)}, u32[]{:S(2)}) collective-permute-start(f32[16,1024]{1,0:T(8,128)S(1)} %add.13), channel_id=1, source_target_pairs={{0,16},{1,17},{2,18},{3,19},{4,20},{5,21},{6,22},{7,23},{8,24},{9,... | collective-permute-start | bytes 196616 | tf_op jit(solution)/shard_map/ppermute | solution.py:423
  20.0 5.2 %collective-permute-start.5 = (f32[16,1024]{1,0:T(8,128)S(1)}, f32[16,1024]{1,0:T(8,128)S(1)}, u32[]{:S(2)}, u32[]{:S(2)}) collective-permute-start(f32[16,1024]{1,0:T(8,128)S(1)} %add.13), channel_id=1, source_target_pairs={{0,17},{1,16},{2,19},{3,18},{4,21},{5,20},{6,23},{7,22},{8,25},{9,... | collective-permute-start | bytes 196616 | tf_op jit(solution)/shard_map/ppermute | solution.py:423
  21.5 5.0 %collective-permute-start.3 = (f32[32,1024]{1,0:T(8,128)S(1)}, f32[32,1024]{1,0:T(8,128)S(1)}, u32[]{:S(2)}, u32[]{:S(2)}) collective-permute-start(f32[32,1024]{1,0:T(8,128)S(1)} %pad_maximum_fusion.1), channel_id=1, source_target_pairs={{0,1},{1,0},{2,3},{3,2},{4,5},{5,4},{6,7},{7,6},{8,9},{9,8},{10,11... | collective-permute-start | bytes 393224 | tf_op jit(solution)/shard_map/ppermute | solution.py:423
  26.6 1.6 %collective-permute-start.6 = (f32[2,32,1024]{2,1,0:T(8,128)S(1)}, f32[2,32,1024]{2,1,0:T(8,128)S(1)}, u32[]{:S(2)}, u32[]{:S(2)}) collective-permute-start(f32[2,32,1024]{2,1,0:T(8,128)S(1)} %pad_maximum_fusion.near_ref), channel_id=1, source_target_pairs={{0,8},{8,0},{16,24},{24,16},{1,9},{9,1},{17,25},{25,17},{2,10},{10... | collective-permute-start | bytes 786440 | tf_op jit(solution)/shard_map/ppermute | solution.py:24
  28.2 0.7 %copy-start.7 = (bf16[80,96]{1,0:T(8,128)(2,1)S(1)}, bf16[80,96]{1,0:T(8,128)(2,1)}, u32[]{:S(2)}) copy-start(bf16[80,96]{1,0:T(8,128)(2,1)} %constant.43.clone.back_y_ref) | copy-start | bytes 46084
  28.9 0.7 %copy-start.9 = (s32[4,3]{1,0:T(4,128)S(1)}, s32[4,3]{1,0:T(4,128)}, u32[]{:S(2)}) copy-start(s32[4,3]{1,0:T(4,128)} %offsets_ref.1) | copy-start | bytes 148

commit v5 on v4

v5 whole, which is shorter than its diff:
```python
import functools
import math

import jax
import jax.numpy as jnp
import ml_dtypes
import numpy as np
from jax import lax
from jax.experimental import pallas as pl
from jax.experimental.pallas import tpu as pltpu
from jax.sharding import PartitionSpec as P

CORE = 32
BUF = 4
DEG = 8

HALF_WIDTH = 4.5
FOUR_PI = 4.0 * math.pi
EXCHANGE_COEF = -((3.0 / math.pi) ** (1.0 / 3.0))


def swapped(value, axis, mask):
    pairs = [(source, source ^ mask) for source in range(lax.axis_size(axis))]
    return lax.ppermute(value, axis, pairs)


def wave_basis(length):
    cells = np.arange(length)
    rows, waves = [], []
    for wave in range(length // 2 + 1):
        angle = 2.0 * np.pi * ((wave * cells) % length) / length
        if wave in (0, length // 2):
            rows.append(np.cos(angle) / np.sqrt(length))
            waves.append(wave)
        else:
            rows.append(np.cos(angle) * np.sqrt(2.0 / length))
            rows.append(np.sin(angle) * np.sqrt(2.0 / length))
            waves += [wave, wave]
    return np.array(rows), np.array(waves)


def parity_basis():
    rows, waves = wave_basis(2 * CORE)
    return np.stack([rows[waves % 2 == 0], rows[waves % 2 == 1]]), np.stack(
        [waves[waves % 2 == 0], waves[waves % 2 == 1]]
    )


def eigenvalue(waves, length):
    return 2.0 - 2.0 * np.cos(2.0 * np.pi * waves / length)


def padded(length, unit):
    return -(-length // unit) * unit


class Packing:
    def __init__(self, side):
        self.side = side
        self.half = side // 2
        self.rows = self.half + DEG
        self.blocks = 128 // (side + 1)
        self.span = 128 // self.blocks
        self.depth = -(-self.rows // self.blocks)
        self.shape = (self.depth, side, 128)
        self.padded_shape = (self.depth, side + 16, 128)
        self.edge_groups = -(-DEG // self.blocks)
        self.pitch = padded(self.rows, 16) + 8

    def where(self, row):
        return row // self.depth, row % self.depth


def lanes_of(shape):
    return lax.broadcasted_iota(jnp.int32, shape, len(shape) - 1)


def roll(values, shift):
    return values if isinstance(shift, int) and shift % 128 == 0 else pltpu.roll(values, shift % 128, 1)


def pack(pk, flat, pitched_ref, field_ref):
    count = flat.shape[0]
    pitched_ref[...] = jnp.zeros(pitched_ref.shape, jnp.float32)
    for y in range(pk.side):
        pitched_ref[y * pk.pitch : y * pk.pitch + count, 0 : pk.side] = flat[:, y * pk.side : (y + 1) * pk.side]
    for level in range(pk.depth):
        total = None
        for block in range(pk.blocks):
            row = block * pk.depth + level
            if row < pk.rows:
                part = roll(pitched_ref[pl.ds(row, pk.side, stride=pk.pitch), :], block * pk.span)
                total = part if total is None else total + part
        field_ref[level] = total


def start_kernel(pk, slab_ref, psi_ref, pot_ref, field_ref, coef_ref, flat_ref, pitched_ref):
    half, side = pk.half, pk.side
    cells = side * side
    is_lower = slab_ref[0] == 0
    flat_ref[...] = jnp.zeros(flat_ref.shape, jnp.float32)
    own = psi_ref[:, 0, :]

    @pl.when(is_lower)
    def _():
        flat_ref[0:half] = own

    @pl.when(jnp.logical_not(is_lower))
    def _():
        flat_ref[DEG : DEG + half] = own

    pack(pk, flat_ref[...], pitched_ref, field_ref)

    @pl.when(is_lower)
    def _():
        flat_ref[0 : pk.rows] = pot_ref[0 : pk.rows] * (2.0 / HALF_WIDTH)

    @pl.when(jnp.logical_not(is_lower))
    def _():
        flat_ref[0 : pk.rows] = pot_ref[side - pk.rows : side] * (2.0 / HALF_WIDTH)

    pack(pk, flat_ref[...], pitched_ref, coef_ref)


def filtered_field(pk, first_ref, second_ref, coef_ref):
    lane = lanes_of((8, 128))
    is_cell = (lane % pk.span < pk.side) & (lane < pk.blocks * pk.span)
    full_weight = jnp.where(is_cell, 1.0 / HALF_WIDTH, 0.0)
    part_weight = jnp.where(is_cell & (lane < (pk.blocks - 1) * pk.span), 1.0 / HALF_WIDTH, 0.0)
    after_first = lane >= pk.span
    before_last = lane < (pk.blocks - 1) * pk.span
    current_ref, other_ref = first_ref, second_ref
    for order in range(DEG):
        for tile in range(pk.side // 8):
            at = 8 + 8 * tile
            values = [current_ref[level, at : at + 8, :] for level in range(pk.depth)]
            before = jnp.where(after_first, roll(values[-1], pk.span), 0.0)
            after = jnp.where(before_last, roll(values[0], -pk.span), 0.0)
            around = [before] + values + [after]
            for level in range(pk.depth):
                value = values[level]
                total = around[level] + around[level + 2]
                total = total + (
                    current_ref[level, at - 1 : at + 7, :] + current_ref[level, at + 1 : at + 9, :]
                )
                total = total + (roll(value, 1) + roll(value, -1))
                weight = full_weight if (pk.blocks - 1) * pk.depth + level < pk.rows else part_weight
                following = coef_ref[level, at - 8 : at, :] * value - weight * total
                if order == 0:
                    following = 0.5 * following
                else:
                    following = following - other_ref[level, at : at + 8, :]
                other_ref[level, at : at + 8, :] = following
        current_ref, other_ref = other_ref, current_ref
    return current_ref


def clear_margins(pk, ref):
    zeros = jnp.zeros((pk.depth, 8, 128), jnp.float32)
    ref[:, 0:8, :] = zeros
    ref[:, 8 + pk.side : 16 + pk.side, :] = zeros


def first_kernel(
    pk, bands, slab_ref, start_ref, halo_ref, coef_ref, filt_ref, edge_ref, dens_ref, one_ref, two_ref, lines_ref
):
    side, span = pk.side, pk.span
    slab = slab_ref[0]
    is_lower = slab == 0
    clear_margins(pk, one_ref)
    clear_margins(pk, two_ref)
    one_ref[:, 8 : 8 + side, :] = start_ref[...]
    halo = halo_ref[:, 0, :]
    lines_ref[...] = jnp.zeros(lines_ref.shape, jnp.float32)
    for y in range(side):
        lines_ref[y * DEG : (y + 1) * DEG, 0:side] = halo[:, y * side : (y + 1) * side]
    for row in range(DEG):
        line = lines_ref[pl.ds(row, side, stride=DEG), :]
        low_block, low_level = pk.where(pk.half + row)
        high_block, high_level = pk.where(row)
        if low_level == high_level:
            line = jnp.where(is_lower, roll(line, low_block * span), roll(line, high_block * span))
            one_ref[low_level, 8 : 8 + side, :] = one_ref[low_level, 8 : 8 + side, :] + line
        else:
            low_line = jnp.where(is_lower, roll(line, low_block * span), 0.0)
            high_line = jnp.where(is_lower, 0.0, roll(line, high_block * span))
            one_ref[low_level, 8 : 8 + side, :] = one_ref[low_level, 8 : 8 + side, :] + low_line
            one_ref[high_level, 8 : 8 + side, :] = one_ref[high_level, 8 : 8 + side, :] + high_line

    result_ref = filtered_field(pk, one_ref, two_ref, coef_ref)
    filt_ref[...] = result_ref[:, 8 : 8 + side, :]

    lane = lanes_of((side, 128))
    for group in range(pk.edge_groups):
        total = jnp.zeros((side, 128), jnp.float32)
        for slot in range(min(pk.blocks, DEG - group * pk.blocks)):
            row = group * pk.blocks + slot + jnp.where(is_lower, pk.half - DEG, DEG)
            shift = slot * span - row // pk.depth * span + 128 * pk.blocks
            line = pltpu.roll(result_ref[row % pk.depth, 8 : 8 + side, :], shift % 128, 1)
            total = jnp.where((lane >= slot * span) & (lane < slot * span + side), line, total)
        edge_ref[group * side : (group + 1) * side] = total

    lane = lanes_of((8, 128))
    lines = 128 // CORE
    for cell in range(CORE // 2):
        row = cell + jnp.where(is_lower, BUF, DEG)
        block, level = row // pk.depth, row % pk.depth
        total = jnp.zeros((8, 128), jnp.float32)
        for line in range(lines):
            value = result_ref[level, 8 + BUF + 8 * line : 16 + BUF + 8 * line, :]
            shift = line * CORE - BUF - block * span + 128 * pk.blocks
            total = jnp.where(lane // CORE == line, pltpu.roll(value, shift % 128, 1), total)
        dens_ref[cell * 8 : (cell + 1) * 8] = total * total * (1.0 / bands)


def split2(values):
    high = values.astype(jnp.bfloat16)
    return high, (values - high.astype(jnp.float32)).astype(jnp.bfloat16)


def split3(values):
    high = values.astype(jnp.bfloat16)
    rest = values - high.astype(jnp.float32)
    middle = rest.astype(jnp.bfloat16)
    return high, middle, (rest - middle.astype(jnp.float32)).astype(jnp.bfloat16)


def dot(left, right):
    return jnp.dot(left, right, preferred_element_type=jnp.float32)


def table_parts(table):
    high = table.astype(ml_dtypes.bfloat16)
    return high, (table - high.astype(np.float64)).astype(ml_dtypes.bfloat16)


def left_table(table):
    high, low = table_parts(table)
    return np.concatenate([high, low, high], -1)


def stacked(values):
    high, low = split2(values)
    return jnp.concatenate([high, high, low], 0)


@functools.lru_cache(maxsize=None)
def solver_tables(side, grid_z):
    pk = Packing(side)
    blocks_z = grid_z // CORE
    lanes = 4 * grid_z
    basis, waves = parity_basis()
    z_basis, z_waves = wave_basis(grid_z)
    lines = 128 // CORE
    into = []
    for place_z in range(blocks_z):
        along_z = z_basis[:, place_z * CORE : (place_z + 1) * CORE].T
        for place_y in range(2):
            for place_x in range(2):
                signs = [(-1.0) ** (px * place_x + py * place_y) for px in range(2) for py in range(2)]
                table = np.kron(np.eye(lines), np.concatenate([sign * along_z for sign in signs], 1))
                high, low = table_parts(table)
                into += [high, high, low]
    into = np.concatenate(into, 0)
    region = np.arange(side) - BUF
    outer = basis[:, :, region % (2 * CORE)]
    small = [left_table(np.concatenate([basis[0, :, :CORE], basis[1, :, :CORE]], 0))]
    small.append(left_table(np.concatenate([outer[0].T, outer[1].T], 0)))
    for first_row in (0, side - pk.rows):
        rows = outer[:, :, first_row : first_row + pk.rows]
        rows = np.pad(rows, ((0, 0), (0, 0), (0, padded(pk.rows, 8) - pk.rows)))
        small.append(left_table(np.concatenate([rows[0].T, rows[1].T], 0)))
    small = np.concatenate(small, 0)
    back_z = []
    spread = np.zeros((blocks_z, 3, 128, 128))
    for block in range(pk.blocks):
        start = block * pk.span
        table = np.zeros((4, grid_z, 128))
        table[:, :, start : start + side] = z_basis[:, region % grid_z]
        high, low = table_parts(table.reshape(lanes, 128))
        back_z.append(np.block([[high, low], [high, np.zeros_like(low)]]))
        for cell, pos in enumerate(region % grid_z):
            spread[pos // CORE, :, block * CORE + pos % CORE, start + cell] = 1.0
    back_z = np.concatenate(back_z, 0)
    spread = spread.reshape(blocks_z * 3 * 128, 128).astype(ml_dtypes.bfloat16)
    eigen = eigenvalue(waves, 2 * CORE)
    lam = (
        eigen.T[:, None, None, :, None]
        + eigen.T[None, :, :, None, None]
        + eigenvalue(z_waves, grid_z)[None, None, None, None, :]
    )
    lam[0, 0, 0, 0, 0] = np.inf
    factor = (FOUR_PI / lam).reshape(CORE * CORE, lanes).astype(np.float32)
    return dict(into=into, small=small, back_z=back_z, factor=factor, spread=spread)


def cube_root(values):
    positive = values > 0.0
    safe = jnp.where(positive, values, 1.0)
    root = jnp.exp(jnp.log(safe) * (1.0 / 3.0))
    root = root - (root - safe / (root * root)) * (1.0 / 3.0)
    return jnp.where(positive, root, 0.0)


def second_kernel(
    pk, masks, info_ref, near_ref, across_ref, filt_ref, beside_ref, start_coef_ref,
    into_ref, small_ref, back_z_ref, factor_ref, spread_ref,
    out_ref, cubes_ref, one_ref, two_ref, coef_ref, left_ref, rows_ref, waves_ref, mixed_ref, flat_ref,
    near_dens_ref, own_ref, lined_ref,
):
    side, half, span = pk.side, pk.half, pk.span
    slab, dom = info_ref[0], info_ref[1]
    is_lower = slab == 0
    dom_count = len(masks)
    blocks_z = dom_count // 4
    grid_z = CORE * blocks_z
    lanes = 4 * grid_z
    columns = lanes // 128
    lines = 128 // CORE
    pitch = CORE + 8
    kept = padded(pk.rows, 8)

    def offset(which, axis):
        return info_ref[2 + 3 * which + axis]

    place_of = []
    for mask in masks:
        other = dom ^ mask
        at_x = (offset(other, 0) != offset(dom, 0)).astype(jnp.int32)
        at_y = (offset(other, 1) != offset(dom, 1)).astype(jnp.int32)
        at_z = (offset(other, 2) - offset(dom, 2)) // CORE
        at_z = jnp.where(at_z < 0, at_z + blocks_z, at_z)
        place_of.append((at_z * 2 + at_y) * 2 + at_x)
    cube_at = []
    for where in range(dom_count):
        found = jnp.int32(0)
        for idx in range(dom_count):
            found = found + jnp.where(place_of[idx] == where, idx, 0)
        cube_at.append(found)

    cubes_ref[0 : dom_count // 2] = near_ref[...]
    cubes_ref[dom_count // 2 : dom_count] = across_ref[...]
    mean = jnp.sum(cubes_ref[...]) * (1.0 / (dom_count * CORE * CORE * CORE))

    for where in range(dom_count):
        high, low = split2(cubes_ref[cube_at[where]] - mean)
        for idx, piece in enumerate((high, low, high)):
            left_ref[:, (where * 3 + idx) * 128 : (where * 3 + idx + 1) * 128] = piece
    product = dot(left_ref[...], into_ref[...])
    for x in range(CORE):
        for line in range(lines):
            for col in range(columns):
                start = line * lanes + col * 128
                rows_ref[col, x * pitch + line * 8 : x * pitch + line * 8 + 8, :] = product[
                    x * 8 : (x + 1) * 8, start : start + 128
                ]

    lane = lanes_of((8, 128))
    for at_z in range(blocks_z):
        for level in range(pk.depth):
            inner, low_wrap, high_wrap = [], None, None
            for block in range(pk.blocks):
                row = block * pk.depth + level
                if row >= pk.rows:
                    continue
                x = row - BUF + jnp.where(is_lower, 0, side - pk.rows)
                inside = (x >= 0) & (x < CORE)
                cell = pl.multiple_of((x + CORE) % CORE * 8, 8)

                def source(at_y):
                    place = (at_z * 2 + at_y) * 2
                    cube = jnp.where(inside, cube_at[place], cube_at[place + 1])
                    return cubes_ref[cube, pl.ds(cell, 8), :]

                def put(value, line, total):
                    value = roll(value, (block - line) * CORE)
                    return jnp.where((lane >= block * CORE) & (lane < (block + 1) * CORE), value, total)

                own, beside = source(0), source(1)
                zeros = jnp.zeros((8, 128), jnp.float32)
                inner = inner or [zeros] * lines
                inner = [put(own, line, total) for line, total in enumerate(inner)]
                low_wrap = put(beside, lines - 1, zeros if low_wrap is None else low_wrap)
                high_wrap = put(beside, 0, zeros if high_wrap is None else high_wrap)
            base = level * side
            near_dens_ref[at_z, base : base + BUF, :] = low_wrap[8 - BUF :]
            for line in range(lines):
                near_dens_ref[at_z, base + BUF + 8 * line : base + BUF + 8 * line + 8, :] = inner[line]
            near_dens_ref[at_z, base + BUF + CORE : base + side, :] = high_wrap[:BUF]

    group = max(1, 256 // lanes)
    lane_id = lanes_of((1, group * lanes)) % lanes
    even_x = lane_id < 2 * grid_z
    even_y = (lane_id // grid_z) % 2 == 0

    def side_by_side(ref, starts, stride, count):
        pieces = []
        for start in starts:
            for col in range(columns):
                if stride == 1:
                    pieces.append(ref[col, pl.ds(start, count), :])
                else:
                    pieces.append(ref[col, pl.ds(start, count, stride=stride), :])
        return jnp.concatenate(pieces, 1)

    def scatter(ref, starts, values, count):
        for idx, start in enumerate(starts):
            for col in range(columns):
                at = (idx * columns + col) * 128
                ref[col, start : start + count, :] = values[:, at : at + 128]

    forward = small_ref[0 : 2 * CORE]
    back_y = small_ref[2 * CORE : 2 * CORE + 2 * side]
    first = 2 * CORE + 2 * side
    back_x = jnp.where(is_lower, small_ref[first : first + 2 * kept], small_ref[first + 2 * kept : first + 4 * kept])
    for first in range(0, CORE, group):
        starts = [x * pitch for x in range(first, first + group)]
        both = dot(forward, stacked(side_by_side(rows_ref, starts, 1, CORE)))
        scatter(waves_ref, starts, jnp.where(even_y, both[:CORE], both[CORE:]), CORE)

    for first in range(0, CORE, group):
        waves_y = list(range(first, first + group))
        both = dot(forward, stacked(side_by_side(waves_ref, waves_y, pitch, CORE)))
        modes = jnp.where(even_x, both[:CORE], both[CORE:])
        scale = jnp.concatenate([factor_ref[wave * CORE : (wave + 1) * CORE] for wave in waves_y], 1)
        both = dot(back_x, stacked(modes * scale))
        scatter(mixed_ref, [wave * pitch for wave in waves_y], jnp.where(even_x, both[:kept], both[kept:]), kept)

    for level in range(pk.depth):
        rows = [block * pk.depth + level for block in range(pk.blocks)]
        rows = [row for row in rows if row < pk.rows]
        for first in range(0, len(rows), group):
            taken = rows[first : first + group]
            both = dot(back_y, stacked(side_by_side(mixed_ref, taken, pitch, CORE)))
            width = both.shape[1]
            field = jnp.where(even_y[:, :width], both[:side], both[side:])
            for idx in range(len(taken)):
                flat_ref[first + idx, level * side : (level + 1) * side, :] = field[:, idx * lanes : (idx + 1) * lanes]
        for block in range(len(rows), pk.blocks):
            flat_ref[block, level * side : (level + 1) * side, :] = jnp.zeros((side, lanes), jnp.float32)

    pieces = []
    for block in range(pk.blocks):
        pieces += split2(flat_ref[block])
    product = dot(jnp.concatenate(pieces, 1), back_z_ref[...])
    hartree = product[:, 0:128] + product[:, 128:256]
    pieces = []
    for at_z in range(blocks_z):
        pieces += split3(near_dens_ref[at_z])
    density = dot(jnp.concatenate(pieces, 1), spread_ref[...])
    added = (hartree + EXCHANGE_COEF * cube_root(density)) * (2.0 / HALF_WIDTH)
    for level in range(pk.depth):
        coef_ref[level] = start_coef_ref[level] + added[level * side : (level + 1) * side]

    clear_margins(pk, one_ref)
    clear_margins(pk, two_ref)
    one_ref[:, 8 : 8 + side, :] = filt_ref[...]
    lane = lanes_of((side, 128))
    base = CORE // 2 * 8
    for row in range(DEG):
        group_at, slot = row // pk.blocks, row % pk.blocks
        line = beside_ref[base + group_at * side : base + (group_at + 1) * side, :]
        for wanted, (block, level) in ((True, pk.where(half + row)), (False, pk.where(row))):
            here = (lane >= block * span) & (lane < block * span + side) & (is_lower == wanted)
            old = one_ref[level, 8 : 8 + side, :]
            one_ref[level, 8 : 8 + side, :] = jnp.where(here, roll(line, (block - slot) * span), old)
    result_ref = filtered_field(pk, one_ref, two_ref, coef_ref)

    for row in range(half):
        at = row + jnp.where(is_lower, 0, DEG)
        shift = 128 * pk.blocks - at // pk.depth * span
        own_ref[row * side : (row + 1) * side, :] = pltpu.roll(
            result_ref[at % pk.depth, 8 : 8 + side, :], shift % 128, 1
        )
    for y in range(side):
        lined_ref[:, y * side : (y + 1) * side] = own_ref[pl.ds(y, half, stride=side), :][:, 0:side]
    out_ref[:, 0, :] = lined_ref[...]


SMEM = pl.BlockSpec(memory_space=pltpu.SMEM)
VMEM = pl.BlockSpec(memory_space=pltpu.VMEM)
params = pltpu.CompilerParams(vmem_limit_bytes=32 * 1024 * 1024)


def local(psi_in, v_in, offsets):
    band_count = lax.axis_size("band")
    dom_count = lax.axis_size("dom")
    dom_idx = lax.axis_index("dom")
    slab_idx = lax.axis_index("band") % 2
    is_lower = slab_idx == 0
    slab_scalar = slab_idx.astype(jnp.int32).reshape(1)
    side = v_in.shape[1]
    pk = Packing(side)
    half = side // 2
    cells = side * side
    bands = band_count // 2
    grid_z = CORE * dom_count // 4
    lanes = 4 * grid_z
    slab_rows = CORE // 2 * 8

    f32, bf16 = jnp.float32, jnp.bfloat16
    field_type = jax.ShapeDtypeStruct(pk.shape, f32)
    padded_field = pltpu.VMEM(pk.padded_shape, f32)

    rows = psi_in.reshape(half, 1, cells)
    halo = swapped(lax.dynamic_slice_in_dim(rows, jnp.where(is_lower, half - DEG, 0), DEG, 0), "band", 1)
    start, coef = pl.pallas_call(
        functools.partial(start_kernel, pk),
        out_shape=(field_type, field_type),
        in_specs=[SMEM, VMEM, VMEM],
        out_specs=(VMEM, VMEM),
        scratch_shapes=[pltpu.VMEM((pk.rows, cells), f32), pltpu.VMEM((side * pk.pitch, 128), f32)],
        compiler_params=params,
    )(slab_scalar, rows, v_in[0])

    filt, edge, dens = pl.pallas_call(
        functools.partial(first_kernel, pk, bands),
        out_shape=(
            field_type,
            jax.ShapeDtypeStruct((pk.edge_groups * side, 128), f32),
            jax.ShapeDtypeStruct((slab_rows, 128), f32),
        ),
        in_specs=[SMEM, VMEM, VMEM, VMEM],
        out_specs=(VMEM, VMEM, VMEM),
        scratch_shapes=[padded_field, padded_field, pltpu.VMEM((side * DEG, 128), f32)],
        compiler_params=params,
    )(slab_scalar, start, halo, coef)

    mask = 2
    while mask < band_count:
        dens = dens + swapped(dens, "band", mask)
        mask *= 2

    far = dom_count // 2
    both = ("dom", "band")
    count = dom_count * band_count

    def crossed(value, mask):
        return lax.ppermute(value, both, [(source, source ^ mask) for source in range(count)])

    beside_all = crossed(jnp.concatenate([dens, edge], 0), 1)
    beside = beside_all[:slab_rows]
    across = crossed(dens, far * band_count)
    diagonal = crossed(dens, far * band_count + 1)

    def cube_of(own, other):
        return jnp.concatenate([jnp.where(is_lower, own, other), jnp.where(is_lower, other, own)], 0)

    cubes = jnp.stack([cube_of(dens, beside), cube_of(across, diagonal)])
    masks = [0, far]
    bit = far // 2
    while bit:
        if bit > 1:
            cubes = jnp.concatenate([cubes, swapped(cubes, "dom", bit)], 0)
        masks = masks + [one | bit for one in masks]
        bit //= 2
    cubes_across = swapped(cubes, "dom", 1)

    tables = solver_tables(side, grid_z)
    names = ("into", "small", "back_z", "factor", "spread")
    info = jnp.concatenate([slab_scalar, dom_idx.astype(jnp.int32).reshape(1), offsets.reshape(-1)])
    pitch = CORE + 8
    result = pl.pallas_call(
        functools.partial(second_kernel, pk, masks),
        out_shape=jax.ShapeDtypeStruct((half, 1, cells), f32),
        in_specs=[SMEM] + [VMEM] * (5 + len(names)),
        out_specs=VMEM,
        scratch_shapes=[
            pltpu.VMEM((dom_count, CORE * 8, 128), f32),
            padded_field,
            padded_field,
            pltpu.VMEM(pk.shape, f32),
            pltpu.VMEM((CORE * 8, dom_count * 3 * 128), bf16),
            pltpu.VMEM((lanes // 128, CORE * pitch, 128), f32),
            pltpu.VMEM((lanes // 128, CORE * pitch, 128), f32),
            pltpu.VMEM((lanes // 128, CORE * pitch, 128), f32),
            pltpu.VMEM((pk.blocks, pk.depth * side, lanes), f32),
            pltpu.VMEM((dom_count // 4, pk.depth * side, 128), f32),
            pltpu.VMEM((half * side, 128), f32),
            pltpu.VMEM((half, cells), f32),
        ],
        compiler_params=params,
    )(info, cubes, cubes_across, filt, beside_all, coef, *[jnp.asarray(tables[name]) for name in names])
    return result.reshape(1, 1, half, cells)


def solution(mesh):
    in_specs = (P("dom", "band", None, None), P("dom", None, None), P())
    out_specs = P("dom", "band", None, None)
    return jax.shard_map(local, mesh=mesh, in_specs=in_specs, out_specs=out_specs, check_vma=False)
```

time: 36.8 us -> 34.2 us (0.929)
  Pallas kernels: 9.32 us -> 7.24 us
  waiting for transfers between devices: 10.8 us -> 9.65 us
  starting transfers between devices: 12 us -> 11 us
  local copies, waits for them, and re-layouts: 4.11 us -> 5.07 us
  other arithmetic: 0.17 us -> 0.83 us
    pallas_call x3, Pallas kernels: 9.32 us -> 7.24 us  [the longest x1 4.79 us: local(): pl.pallas_call(functools.partial(second_kernel, pk, masks), out_shape=jax...]
    ppermute x4, starting transfers between devices: 8.34 us -> 7.37 us  [swapped(): return lax.ppermute(value, axis, pairs)]
    concatenate x0 -> x1, other arithmetic: none -> 0.73 us  [local(): jnp.concatenate([slab_scalar, dom_idx.astype(jnp.int32).reshape(1), offse...]
    ppermute x4, waiting for transfers between devices: 6.1 us -> 5.45 us  [swapped(): return lax.ppermute(value, axis, pairs)]
    reshape x0 -> x1, local copies, waits for them, and re-layouts: none -> 0.59 us  [local(): offsets.reshape(-1)]
    ppermute x3, waiting for transfers between devices: 4.73 us -> 4.2 us  [crossed(): lax.ppermute(value, both, [(source, source ^ mask) for source in range(co...]
    unnamed x20 -> x16, local copies, waits for them, and re-layouts: 3.28 us -> 3.65 us
  transfers between devices with their start and end apart: 7 -> 7, of which waited for: 7 -> 6; matrix products, arithmetic and copies ran while one was open for 0% -> 4% of each run, Pallas kernels for 0% -> 3%
where the time goes in v5:
time: 34.2 us; the launch traced here: 33.9 us
  starting transfers between devices  11 us (32%)
  waiting for transfers between devices  9.65 us (28%)
  Pallas kernels  7.24 us (21%)
  local copies, waits for them, and re-layouts  5.07 us (15%)
  other arithmetic  0.83 us (2%)
    ppermute x4, starting transfers between devices, swapped(): return lax.ppermute(value, axis, pairs)  7.37 us
    ppermute x4, waiting for transfers between devices, swapped(): return lax.ppermute(value, axis, pairs)  5.45 us
    pallas_call x1, Pallas kernels, local(): pl.pallas_call(functools.partial(second_kernel, pk, masks), out_shape=jax...  4.79 us
    ppermute x3, waiting for transfers between devices, crossed(): lax.ppermute(value, both, [(source, source ^ mask) for source in range(co...  4.2 us
    unnamed x16, local copies, waits for them, and re-layouts  3.65 us
    ppermute x3, starting transfers between devices, crossed(): lax.ppermute(value, both, [(source, source ^ mask) for source in range(co...  3.62 us
    pallas_call x1, Pallas kernels, local(): pl.pallas_call(functools.partial(first_kernel, pk, bands), out_shape=(fie...  1.53 us
    pallas_call x1, Pallas kernels, local(): pl.pallas_call(functools.partial(start_kernel, pk), out_shape=(field_type...  0.92 us
  transfers between devices with their start and end apart: 7, of which 6 were waited for; matrix products, arithmetic and copies ran while one was open for 4% of the time, Pallas kernels for 3%

profile of v5, /device:TPU:0, one launch (start us, length us, event | category | flops | bytes accessed | tf_op | source)
XLA Modules:
  0.0 33.9 jit_solution(7092906635577828455)
XLA Ops:
  0.0 0.8 %dynamic-slice_bitcast_fusion = f32[8,1,1600]{2,1,0:T(1,128)S(1)} fusion(f32[1,1,20,1600]{3,1,2,0:T(1,128)} %param.8, s32[]{:T(128)S(6)} %select_n.34), kind=kLoop, calls=%fused_computation.6 | loop fusion | bytes 102404 | tf_op jit(solution)/shard_map/dynamic_slice | solution.py:506
  0.9 0.0 copy-start.2
  0.9 3.0 %collective-permute-start = (f32[8,1,1600]{2,1,0:T(1,128)S(1)}, f32[8,1,1600]{2,1,0:T(1,128)S(1)}, u32[]{:S(2)}, u32[]{:S(2)}) collective-permute-start(f32[8,1,1600]{2,1,0:T(1,128)S(1)} %dynamic-slice_bitcast_fusion), channel_id=1, source_target_pairs={{0,1},{1,0},{2,3},{3,2},{4,5},{5,4},{6,7},{7,6},{8,9},{9,8},{10,11... | collective-permute-start | bytes 153608 | tf_op jit(solution)/shard_map/ppermute | solution.py:24
  3.9 0.9 %copy-done.3 = f32[1,40,1600]{2,1,0:T(8,128)S(1)} copy-done((f32[1,40,1600]{2,1,0:T(8,128)S(1)}, f32[1,40,1600]{2,1,0:T(8,128)}, u32[]{:S(2)}) %copy-start.3) | copy-done | bytes 256024
  4.8 0.9 %copy-done.4 = f32[1,1,20,1600]{3,1,2,0:T(1,128)S(1)} copy-done((f32[1,1,20,1600]{3,1,2,0:T(1,128)S(1)}, f32[1,1,20,1600]{3,1,2,0:T(1,128)}, u32[]{:S(2)}) %copy-start.4) | copy-done | bytes 128024
  5.7 0.9 %shard_map.82 = (f32[10,40,128]{2,1,0:T(8,128)S(1)}, f32[10,40,128]{2,1,0:T(8,128)S(1)}) custom-call(s32[1]{0:T(128)} %bitcast.slab_ref, f32[20,1,1600]{2,1,0:T(1,128)S(1)} %bitcast.14, f32[40,1600]{1,0:T(8,128)S(1)} %bitcast.13), custom_call_target="tpu_custom_call" | custom-call | tf_op jit(solution)/shard_map/pallas_call | solution.py:507
  6.7 1.5 %shard_map.83 = (f32[10,40,128]{2,1,0:T(8,128)S(1)}, f32[120,128]{1,0:T(8,128)S(1)}, f32[128,128]{1,0:T(8,128)S(1)}) custom-call(s32[1]{0:T(128)} %bitcast.slab_ref, f32[10,40,128]{2,1,0:T(8,128)S(1)} %get-tuple-element.10.start_ref, f32[8,1,1600]{2,1,0:T(1,128)S(1)} %collective-permute-done.halo_ref, ...), custom_call_target="tpu_custom_call" | custom-call | tf_op jit(solution)/shard_map/pallas_call | solution.py:516
  8.2 1.6 %collective-permute-start.1 = (f32[128,128]{1,0:T(8,128)S(1)}, f32[128,128]{1,0:T(8,128)S(1)}, u32[]{:S(2)}, u32[]{:S(2)}) collective-permute-start(f32[128,128]{1,0:T(8,128)S(1)} %get-tuple-element.12), channel_id=1, source_target_pairs={{0,2},{1,3},{2,0},{3,1},{4,6},{5,7},{6,4},{7,5},{8,10},{9,11},{10,... | collective-permute-start | bytes 196616 | tf_op jit(solution)/shard_map/ppermute | solution.py:24
  9.8 2.7 %collective-permute-done.1 = f32[128,128]{1,0:T(8,128)S(1)} collective-permute-done((f32[128,128]{1,0:T(8,128)S(1)}, f32[128,128]{1,0:T(8,128)S(1)}, u32[]{:S(2)}, u32[]{:S(2)}) %collective-permute-start.1) | collective-permute-done | bytes 65568 | tf_op jit(solution)/shard_map/ppermute | solution.py:24
  12.5 2.7 %collective-permute-start.2 = (f32[128,128]{1,0:T(8,128)S(1)}, f32[128,128]{1,0:T(8,128)S(1)}, u32[]{:S(2)}, u32[]{:S(2)}) collective-permute-start(f32[128,128]{1,0:T(8,128)S(1)} %add.12), channel_id=1, source_target_pairs={{0,4},{1,5},{2,6},{3,7},{4,0},{5,1},{6,2},{7,3},{8,12},{9,13},{10,... | collective-permute-start | bytes 196616 | tf_op jit(solution)/shard_map/ppermute | solution.py:24
  15.2 2.6 %collective-permute-done.2 = f32[128,128]{1,0:T(8,128)S(1)} collective-permute-done((f32[128,128]{1,0:T(8,128)S(1)}, f32[128,128]{1,0:T(8,128)S(1)}, u32[]{:S(2)}, u32[]{:S(2)}) %collective-permute-start.2) | collective-permute-done | bytes 65568 | tf_op jit(solution)/shard_map/ppermute | solution.py:24
  17.8 1.6 %collective-permute-start.4 = (f32[128,128]{1,0:T(8,128)S(1)}, f32[128,128]{1,0:T(8,128)S(1)}, u32[]{:S(2)}, u32[]{:S(2)}) collective-permute-start(f32[128,128]{1,0:T(8,128)S(1)} %add.13), channel_id=1, source_target_pairs={{0,16},{1,17},{2,18},{3,19},{4,20},{5,21},{6,22},{7,23},{8,24},{9,... | collective-permute-start | bytes 196616 | tf_op jit(solution)/shard_map/ppermute | solution.py:539
  19.4 1.3 %collective-permute-start.5 = (f32[128,128]{1,0:T(8,128)S(1)}, f32[128,128]{1,0:T(8,128)S(1)}, u32[]{:S(2)}, u32[]{:S(2)}) collective-permute-start(f32[128,128]{1,0:T(8,128)S(1)} %add.13), channel_id=1, source_target_pairs={{0,17},{1,16},{2,19},{3,18},{4,21},{5,20},{6,23},{7,22},{8,25},{9,... | collective-permute-start | bytes 196616 | tf_op jit(solution)/shard_map/ppermute | solution.py:539
  20.7 0.8 %collective-permute-start.3 = (f32[248,128]{1,0:T(8,128)S(1)}, f32[248,128]{1,0:T(8,128)S(1)}, u32[]{:S(2)}, u32[]{:S(2)}) collective-permute-start(f32[248,128]{1,0:T(8,128)S(1)} %pad_maximum_fusion.1), channel_id=1, source_target_pairs={{0,1},{1,0},{2,3},{3,2},{4,5},{5,4},{6,7},{7,6},{8,9},{9,8},{10,11... | collective-permute-start | bytes 380936 | tf_op jit(solution)/shard_map/ppermute | solution.py:539
  21.4 0.7 %collective-permute-done.4 = f32[128,128]{1,0:T(8,128)S(1)} collective-permute-done((f32[128,128]{1,0:T(8,128)S(1)}, f32[128,128]{1,0:T(8,128)S(1)}, u32[]{:S(2)}, u32[]{:S(2)}) %collective-permute-start.4) | collective-permute-done | bytes 65568 | tf_op jit(solution)/shard_map/ppermute | solution.py:539
  22.1 2.4 %collective-permute-done.5 = f32[128,128]{1,0:T(8,128)S(1)} collective-permute-done((f32[128,128]{1,0:T(8,128)S(1)}, f32[128,128]{1,0:T(8,128)S(1)}, u32[]{:S(2)}, u32[]{:S(2)}) %collective-permute-start.5) | collective-permute-done | bytes 65568 | tf_op jit(solution)/shard_map/ppermute | solution.py:539
  24.6 1.1 %collective-permute-done.3.beside_ref = f32[248,128]{1,0:T(8,128)S(1)} collective-permute-done((f32[248,128]{1,0:T(8,128)S(1)}, f32[248,128]{1,0:T(8,128)S(1)}, u32[]{:S(2)}, u32[]{:S(2)}) %collective-permute-start.3) | collective-permute-done | bytes 127008 | tf_op jit(solution)/shard_map/ppermute | solution.py:539
  25.7 0.1 collective-permute-start.6
  25.8 0.6 %reshape.18 = s32[12]{0:T(128)} reshape(s32[4,3]{1,0:T(4,128)S(1)} %copy-done.7) | data formatting | bytes 96 | tf_op jit(solution)/shard_map/reshape | solution.py:561
  26.4 0.7 %pad_add_fusion.info_ref = s32[14]{0:T(128)S(1)} fusion(s32[12]{0:T(128)} %reshape.18, s32[1]{0:T(128)} %bitcast.1, s32[1]{0:T(128)} %bitcast.slab_ref), kind=kLoop, calls=%fused_computation.9 | loop fusion | flops 28 | bytes 112 | tf_op jit(solution)/shard_map/concatenate | solution.py:561
  27.1 0.2 collective-permute-done.6.across_ref
  27.3 0.9 %copy-done.5 = bf16[384,128]{1,0:T(8,128)(2,1)S(1)} copy-done((bf16[384,128]{1,0:T(8,128)(2,1)S(1)}, bf16[384,128]{1,0:T(8,128)(2,1)}, u32[]{:S(2)}) %copy-start.5) | copy-done | bytes 98328
  28.2 0.9 %copy-done.6 = bf16[272,96]{1,0:T(8,128)(2,1)S(1)} copy-done((bf16[272,96]{1,0:T(8,128)(2,1)S(1)}, bf16[272,96]{1,0:T(8,128)(2,1)}, u32[]{:S(2)}) %copy-start.6) | copy-done | bytes 52248
  29.1 4.8 %shard_map.84 = f32[20,1,1600]{2,1,0:T(1,128)} custom-call(s32[14]{0:T(128)S(1)} %pad_add_fusion.info_ref, f32[2,256,128]{2,1,0:T(8,128)S(1)} %pad_maximum_fusion.near_ref, f32[2,256,128]{2,1,0:T(8,128)S(1)} %collective-permute-done.6.across_ref, f32[10,40,128]{2,1,0:T(8,128)S(1)} %get-tuple-element.14.filt_ref, ...), custom_call_target="tpu_custom_call" | custom-call | tf_op jit(solution)/shard_map/pallas_call | solution.py:563
  (20 shorter events, 0.1 us)
Async XLA Ops:
  0.0 25.8 %copy-start.7 = (s32[4,3]{1,0:T(4,128)S(1)}, s32[4,3]{1,0:T(4,128)}, u32[]{:S(2)}) copy-start(s32[4,3]{1,0:T(4,128)} %param.10) | copy-start | bytes 148
  0.8 26.5 %copy-start = (bf16[1536,512]{1,0:T(8,128)(2,1)S(1)}, bf16[1536,512]{1,0:T(8,128)(2,1)}, u32[]{:S(2)}) copy-start(bf16[1536,512]{1,0:T(8,128)(2,1)} %constant.37.clone.into_ref) | copy-start | bytes 4718596
  0.8 26.5 %copy-start.1 = (f32[1024,128]{1,0:T(8,128)S(1)}, f32[1024,128]{1,0:T(8,128)}, u32[]{:S(2)}) copy-start(f32[1024,128]{1,0:T(8,128)} %constant.40.clone.factor_ref) | copy-start | bytes 1572868
  0.9 26.5 %copy-start.2 = (bf16[768,256]{1,0:T(8,128)(2,1)S(1)}, bf16[768,256]{1,0:T(8,128)(2,1)}, u32[]{:S(2)}) copy-start(bf16[768,256]{1,0:T(8,128)(2,1)} %constant.39.clone.back_z_ref) | copy-start | bytes 1179652
  0.9 5.8 %collective-permute-start = (f32[8,1,1600]{2,1,0:T(1,128)S(1)}, f32[8,1,1600]{2,1,0:T(1,128)S(1)}, u32[]{:S(2)}, u32[]{:S(2)}) collective-permute-start(f32[8,1,1600]{2,1,0:T(1,128)S(1)} %dynamic-slice_bitcast_fusion), channel_id=1, source_target_pairs={{0,1},{1,0},{2,3},{3,2},{4,5},{5,4},{6,7},{7,6},{8,9},{9,8},{10,11... | collective-permute-start | bytes 153608 | tf_op jit(solution)/shard_map/ppermute | solution.py:24
  3.9 1.0 %copy-start.3 = (f32[1,40,1600]{2,1,0:T(8,128)S(1)}, f32[1,40,1600]{2,1,0:T(8,128)}, u32[]{:S(2)}) copy-start(f32[1,40,1600]{2,1,0:T(8,128)} %param.9) | copy-start | bytes 768004
  4.8 0.9 %copy-start.4 = (f32[1,1,20,1600]{3,1,2,0:T(1,128)S(1)}, f32[1,1,20,1600]{3,1,2,0:T(1,128)}, u32[]{:S(2)}) copy-start(f32[1,1,20,1600]{3,1,2,0:T(1,128)} %param.8) | copy-start | bytes 384004
  8.2 4.3 %collective-permute-start.1 = (f32[128,128]{1,0:T(8,128)S(1)}, f32[128,128]{1,0:T(8,128)S(1)}, u32[]{:S(2)}, u32[]{:S(2)}) collective-permute-start(f32[128,128]{1,0:T(8,128)S(1)} %get-tuple-element.12), channel_id=1, source_target_pairs={{0,2},{1,3},{2,0},{3,1},{4,6},{5,7},{6,4},{7,5},{8,10},{9,11},{10,... | collective-permute-start | bytes 196616 | tf_op jit(solution)/shard_map/ppermute | solution.py:24
  12.5 5.2 %collective-permute-start.2 = (f32[128,128]{1,0:T(8,128)S(1)}, f32[128,128]{1,0:T(8,128)S(1)}, u32[]{:S(2)}, u32[]{:S(2)}) collective-permute-start(f32[128,128]{1,0:T(8,128)S(1)} %add.12), channel_id=1, source_target_pairs={{0,4},{1,5},{2,6},{3,7},{4,0},{5,1},{6,2},{7,3},{8,12},{9,13},{10,... | collective-permute-start | bytes 196616 | tf_op jit(solution)/shard_map/ppermute | solution.py:24
  17.8 4.3 %collective-permute-start.4 = (f32[128,128]{1,0:T(8,128)S(1)}, f32[128,128]{1,0:T(8,128)S(1)}, u32[]{:S(2)}, u32[]{:S(2)}) collective-permute-start(f32[128,128]{1,0:T(8,128)S(1)} %add.13), channel_id=1, source_target_pairs={{0,16},{1,17},{2,18},{3,19},{4,20},{5,21},{6,22},{7,23},{8,24},{9,... | collective-permute-start | bytes 196616 | tf_op jit(solution)/shard_map/ppermute | solution.py:539
  19.4 5.2 %collective-permute-start.5 = (f32[128,128]{1,0:T(8,128)S(1)}, f32[128,128]{1,0:T(8,128)S(1)}, u32[]{:S(2)}, u32[]{:S(2)}) collective-permute-start(f32[128,128]{1,0:T(8,128)S(1)} %add.13), channel_id=1, source_target_pairs={{0,17},{1,16},{2,19},{3,18},{4,21},{5,20},{6,23},{7,22},{8,25},{9,... | collective-permute-start | bytes 196616 | tf_op jit(solution)/shard_map/ppermute | solution.py:539
  20.7 5.0 %collective-permute-start.3 = (f32[248,128]{1,0:T(8,128)S(1)}, f32[248,128]{1,0:T(8,128)S(1)}, u32[]{:S(2)}, u32[]{:S(2)}) collective-permute-start(f32[248,128]{1,0:T(8,128)S(1)} %pad_maximum_fusion.1), channel_id=1, source_target_pairs={{0,1},{1,0},{2,3},{3,2},{4,5},{5,4},{6,7},{7,6},{8,9},{9,8},{10,11... | collective-permute-start | bytes 380936 | tf_op jit(solution)/shard_map/ppermute | solution.py:539
  25.7 1.6 %collective-permute-start.6 = (f32[2,256,128]{2,1,0:T(8,128)S(1)}, f32[2,256,128]{2,1,0:T(8,128)S(1)}, u32[]{:S(2)}, u32[]{:S(2)}) collective-permute-start(f32[2,256,128]{2,1,0:T(8,128)S(1)} %pad_maximum_fusion.near_ref), channel_id=1, source_target_pairs={{0,8},{8,0},{16,24},{24,16},{1,9},{9,1},{17,25},{25,17},{2,10},{10... | collective-permute-start | bytes 786440 | tf_op jit(solution)/shard_map/ppermute | solution.py:24
  27.3 0.9 %copy-start.5 = (bf16[384,128]{1,0:T(8,128)(2,1)S(1)}, bf16[384,128]{1,0:T(8,128)(2,1)}, u32[]{:S(2)}) copy-start(bf16[384,128]{1,0:T(8,128)(2,1)} %constant.41.clone.spread_ref) | copy-start | bytes 294916
  28.2 0.9 %copy-start.6 = (bf16[272,96]{1,0:T(8,128)(2,1)S(1)}, bf16[272,96]{1,0:T(8,128)(2,1)}, u32[]{:S(2)}) copy-start(bf16[272,96]{1,0:T(8,128)(2,1)} %constant.38.clone.small_ref) | copy-start | bytes 156676

commit v6 on v5

--- a/solution.py
+++ b/solution.py
@@ -81,7 +81,6 @@
 
 def pack(pk, flat, pitched_ref, field_ref):
     count = flat.shape[0]
-    pitched_ref[...] = jnp.zeros(pitched_ref.shape, jnp.float32)
     for y in range(pk.side):
         pitched_ref[y * pk.pitch : y * pk.pitch + count, 0 : pk.side] = flat[:, y * pk.side : (y + 1) * pk.side]
     for level in range(pk.depth):
@@ -94,11 +93,17 @@
         field_ref[level] = total
 
 
+def edge_kernel(pk, slab_ref, psi_ref, edge_ref):
+    first = jnp.where(slab_ref[0] == 0, pk.half - DEG, 0)
+    edge_ref[...] = psi_ref[pl.ds(first, DEG)]
+
+
 def start_kernel(pk, slab_ref, psi_ref, pot_ref, field_ref, coef_ref, flat_ref, pitched_ref):
     half, side = pk.half, pk.side
     cells = side * side
     is_lower = slab_ref[0] == 0
     flat_ref[...] = jnp.zeros(flat_ref.shape, jnp.float32)
+    pitched_ref[...] = jnp.zeros(pitched_ref.shape, jnp.float32)
     own = psi_ref[:, 0, :]
 
     @pl.when(is_lower)
@@ -291,7 +296,11 @@
     )
     lam[0, 0, 0, 0, 0] = np.inf
     factor = (FOUR_PI / lam).reshape(CORE * CORE, lanes).astype(np.float32)
-    return dict(into=into, small=small, back_z=back_z, factor=factor, spread=spread)
+    rest = np.zeros((max(len(back_z), len(spread), len(small)), into.shape[1]), ml_dtypes.bfloat16)
+    rest[: len(back_z), 0:256] = back_z
+    rest[: len(spread), 256:384] = spread
+    rest[: len(small), 384 : 384 + small.shape[1]] = small
+    return np.concatenate([into, rest], 0), factor
 
 
 def cube_root(values):
@@ -303,13 +312,13 @@
 
 
 def second_kernel(
-    pk, masks, info_ref, near_ref, across_ref, filt_ref, beside_ref, start_coef_ref,
-    into_ref, small_ref, back_z_ref, factor_ref, spread_ref,
+    pk, masks, slab_ref, dom_ref, info_in_ref, near_ref, across_ref, filt_ref, beside_ref, start_coef_ref,
+    table_ref, factor_ref,
     out_ref, cubes_ref, one_ref, two_ref, coef_ref, left_ref, rows_ref, waves_ref, mixed_ref, flat_ref,
-    near_dens_ref, own_ref, lined_ref,
+    near_dens_ref, own_ref, lined_ref, info_ref, sem,
 ):
     side, half, span = pk.side, pk.half, pk.span
-    slab, dom = info_ref[0], info_ref[1]
+    slab, dom = slab_ref[0], dom_ref[0]
     is_lower = slab == 0
     dom_count = len(masks)
     blocks_z = dom_count // 4
@@ -320,8 +329,28 @@
     pitch = CORE + 8
     kept = padded(pk.rows, 8)
 
+    copy = pltpu.make_async_copy(info_in_ref, info_ref, sem)
+    copy.start()
+    cubes_ref[0 : dom_count // 2] = near_ref[...]
+    cubes_ref[dom_count // 2 : dom_count] = across_ref[...]
+    mean = jnp.sum(cubes_ref[...]) * (1.0 / (dom_count * CORE * CORE * CORE))
+
+    clear_margins(pk, one_ref)
+    clear_margins(pk, two_ref)
+    one_ref[:, 8 : 8 + side, :] = filt_ref[...]
+    lane = lanes_of((side, 128))
+    base = CORE // 2 * 8
+    for row in range(DEG):
+        group_at, slot = row // pk.blocks, row % pk.blocks
+        line = beside_ref[base + group_at * side : base + (group_at + 1) * side, :]
+        for wanted, (block, level) in ((True, pk.where(half + row)), (False, pk.where(row))):
+            here = (lane >= block * span) & (lane < block * span + side) & (is_lower == wanted)
+            old = one_ref[level, 8 : 8 + side, :]
+            one_ref[level, 8 : 8 + side, :] = jnp.where(here, roll(line, (block - slot) * span), old)
+    copy.wait()
+
     def offset(which, axis):
-        return info_ref[2 + 3 * which + axis]
+        return info_ref[3 * which + axis]
 
     place_of = []
     for mask in masks:
@@ -338,15 +367,11 @@
             found = found + jnp.where(place_of[idx] == where, idx, 0)
         cube_at.append(found)
 
-    cubes_ref[0 : dom_count // 2] = near_ref[...]
-    cubes_ref[dom_count // 2 : dom_count] = across_ref[...]
-    mean = jnp.sum(cubes_ref[...]) * (1.0 / (dom_count * CORE * CORE * CORE))
-
     for where in range(dom_count):
         high, low = split2(cubes_ref[cube_at[where]] - mean)
         for idx, piece in enumerate((high, low, high)):
             left_ref[:, (where * 3 + idx) * 128 : (where * 3 + idx + 1) * 128] = piece
-    product = dot(left_ref[...], into_ref[...])
+    product = dot(left_ref[...], table_ref[0 : dom_count * 3 * 128])
     for x in range(CORE):
         for line in range(lines):
             for col in range(columns):
@@ -409,10 +434,15 @@
                 at = (idx * columns + col) * 128
                 ref[col, start : start + count, :] = values[:, at : at + 128]
 
-    forward = small_ref[0 : 2 * CORE]
-    back_y = small_ref[2 * CORE : 2 * CORE + 2 * side]
+    base = dom_count * 3 * 128
+
+    def small(first, count):
+        return table_ref[base + first : base + first + count, 384 : 384 + 3 * CORE]
+
+    forward = small(0, 2 * CORE)
+    back_y = small(2 * CORE, 2 * side)
     first = 2 * CORE + 2 * side
-    back_x = jnp.where(is_lower, small_ref[first : first + 2 * kept], small_ref[first + 2 * kept : first + 4 * kept])
+    back_x = jnp.where(is_lower, small(first, 2 * kept), small(first + 2 * kept, 2 * kept))
     for first in range(0, CORE, group):
         starts = [x * pitch for x in range(first, first + group)]
         both = dot(forward, stacked(side_by_side(rows_ref, starts, 1, CORE)))
@@ -442,28 +472,16 @@
     pieces = []
     for block in range(pk.blocks):
         pieces += split2(flat_ref[block])
-    product = dot(jnp.concatenate(pieces, 1), back_z_ref[...])
+    product = dot(jnp.concatenate(pieces, 1), table_ref[base : base + pk.blocks * 2 * lanes, 0:256])
     hartree = product[:, 0:128] + product[:, 128:256]
     pieces = []
     for at_z in range(blocks_z):
         pieces += split3(near_dens_ref[at_z])
-    density = dot(jnp.concatenate(pieces, 1), spread_ref[...])
+    density = dot(jnp.concatenate(pieces, 1), table_ref[base : base + blocks_z * 3 * 128, 256:384])
     added = (hartree + EXCHANGE_COEF * cube_root(density)) * (2.0 / HALF_WIDTH)
     for level in range(pk.depth):
         coef_ref[level] = start_coef_ref[level] + added[level * side : (level + 1) * side]
 
-    clear_margins(pk, one_ref)
-    clear_margins(pk, two_ref)
-    one_ref[:, 8 : 8 + side, :] = filt_ref[...]
-    lane = lanes_of((side, 128))
-    base = CORE // 2 * 8
-    for row in range(DEG):
-        group_at, slot = row // pk.blocks, row % pk.blocks
-        line = beside_ref[base + group_at * side : base + (group_at + 1) * side, :]
-        for wanted, (block, level) in ((True, pk.where(half + row)), (False, pk.where(row))):
-            here = (lane >= block * span) & (lane < block * span + side) & (is_lower == wanted)
-            old = one_ref[level, 8 : 8 + side, :]
-            one_ref[level, 8 : 8 + side, :] = jnp.where(here, roll(line, (block - slot) * span), old)
     result_ref = filtered_field(pk, one_ref, two_ref, coef_ref)
 
     for row in range(half):
@@ -503,7 +521,14 @@
     padded_field = pltpu.VMEM(pk.padded_shape, f32)
 
     rows = psi_in.reshape(half, 1, cells)
-    halo = swapped(lax.dynamic_slice_in_dim(rows, jnp.where(is_lower, half - DEG, 0), DEG, 0), "band", 1)
+    edge = pl.pallas_call(
+        functools.partial(edge_kernel, pk),
+        out_shape=jax.ShapeDtypeStruct((DEG, 1, cells), f32),
+        in_specs=[SMEM, VMEM],
+        out_specs=VMEM,
+        compiler_params=params,
+    )(slab_scalar, rows)
+    halo = swapped(edge, "band", 1)
     start, coef = pl.pallas_call(
         functools.partial(start_kernel, pk),
         out_shape=(field_type, field_type),
@@ -556,14 +581,13 @@
         bit //= 2
     cubes_across = swapped(cubes, "dom", 1)
 
-    tables = solver_tables(side, grid_z)
-    names = ("into", "small", "back_z", "factor", "spread")
-    info = jnp.concatenate([slab_scalar, dom_idx.astype(jnp.int32).reshape(1), offsets.reshape(-1)])
+    table, factor = solver_tables(side, grid_z)
+    dom_scalar = dom_idx.astype(jnp.int32).reshape(1)
     pitch = CORE + 8
     result = pl.pallas_call(
         functools.partial(second_kernel, pk, masks),
         out_shape=jax.ShapeDtypeStruct((half, 1, cells), f32),
-        in_specs=[SMEM] + [VMEM] * (5 + len(names)),
+        in_specs=[SMEM, SMEM] + [VMEM] * 8,
         out_specs=VMEM,
         scratch_shapes=[
             pltpu.VMEM((dom_count, CORE * 8, 128), f32),
@@ -578,9 +602,14 @@
             pltpu.VMEM((dom_count // 4, pk.depth * side, 128), f32),
             pltpu.VMEM((half * side, 128), f32),
             pltpu.VMEM((half, cells), f32),
+            pltpu.SMEM((3 * dom_count,), jnp.int32),
+            pltpu.SemaphoreType.DMA,
         ],
         compiler_params=params,
-    )(info, cubes, cubes_across, filt, beside_all, coef, *[jnp.asarray(tables[name]) for name in names])
+    )(
+        slab_scalar, dom_scalar, offsets.reshape(-1), cubes, cubes_across, filt, beside_all, coef,
+        jnp.asarray(table), jnp.asarray(factor),
+    )
     return result.reshape(1, 1, half, cells)
 
 

time: 34.2 us -> 35 us (1.023)
  local copies, waits for them, and re-layouts: 5.07 us -> 3.69 us
  waiting for transfers between devices: 9.65 us -> 10.9 us
  starting transfers between devices: 11 us -> 11.9 us
  Pallas kernels: 7.24 us -> 8.1 us
  other arithmetic: 0.83 us -> 0.1 us
    ppermute x4, starting transfers between devices: 7.37 us -> 8.28 us  [swapped(): return lax.ppermute(value, axis, pairs)]
    dynamic_slice x1 -> x0, local copies, waits for them, and re-layouts: 0.83 us -> none  [local(): lax.dynamic_slice_in_dim(rows, jnp.where(is_lower, half - DEG, 0), DEG, 0)]
    pallas_call x1, Pallas kernels: 4.79 us -> 5.61 us  [local(): pl.pallas_call(functools.partial(second_kernel, pk, masks), out_shape=jax...]
    ppermute x4, waiting for transfers between devices: 5.45 us -> 6.24 us  [swapped(): return lax.ppermute(value, axis, pairs)]
    concatenate x1 -> x0, other arithmetic: 0.73 us -> none  [local(): jnp.concatenate([slab_scalar, dom_idx.astype(jnp.int32).reshape(1), offse...]
    reshape x1, local copies, waits for them, and re-layouts: 0.59 us -> 0.08 us  [local(): offsets.reshape(-1)]
    ppermute x3, waiting for transfers between devices: 4.2 us -> 4.68 us  [crossed(): lax.ppermute(value, both, [(source, source ^ mask) for source in range(co...]
    unnamed x16 -> x14, local copies, waits for them, and re-layouts: 3.65 us -> 3.61 us
  transfers between devices with their start and end apart: 7 -> 7, of which waited for: 6 -> 7; matrix products, arithmetic and copies ran while one was open for 4% -> 0% of each run, Pallas kernels for 3% -> 3%
where the time goes in v6:
time: 35 us; the launch traced here: 34.8 us
  starting transfers between devices  11.9 us (34%)
  waiting for transfers between devices  10.9 us (31%)
  Pallas kernels  8.1 us (23%)
  local copies, waits for them, and re-layouts  3.69 us (11%)
    ppermute x4, starting transfers between devices, swapped(): return lax.ppermute(value, axis, pairs)  8.28 us
    ppermute x4, waiting for transfers between devices, swapped(): return lax.ppermute(value, axis, pairs)  6.24 us
    pallas_call x1, Pallas kernels, local(): pl.pallas_call(functools.partial(second_kernel, pk, masks), out_shape=jax...  5.61 us
    ppermute x3, waiting for transfers between devices, crossed(): lax.ppermute(value, both, [(source, source ^ mask) for source in range(co...  4.68 us
    ppermute x3, starting transfers between devices, crossed(): lax.ppermute(value, both, [(source, source ^ mask) for source in range(co...  3.62 us
    unnamed x14, local copies, waits for them, and re-layouts  3.61 us
    pallas_call x1, Pallas kernels, local(): pl.pallas_call(functools.partial(first_kernel, pk, bands), out_shape=(fie...  1.53 us
    pallas_call x1, Pallas kernels, local(): pl.pallas_call(functools.partial(start_kernel, pk), out_shape=(field_type...  0.96 us
  transfers between devices with their start and end apart: 7, of which 7 were waited for; matrix products, arithmetic and copies ran while one was open for 0% of the time, Pallas kernels for 3%

profile of v6, /device:TPU:0, one launch (start us, length us, event | category | flops | bytes accessed | tf_op | source)
XLA Modules:
  0.0 34.8 jit_solution(2060470948712420539)
XLA Ops:
  0.0 1.1 %copy-done.1 = f32[1,1,20,1600]{3,1,2,0:T(1,128)S(1)} copy-done((f32[1,1,20,1600]{3,1,2,0:T(1,128)S(1)}, f32[1,1,20,1600]{3,1,2,0:T(1,128)}, u32[]{:S(2)}) %copy-start.1) | copy-done | bytes 128024
  1.1 3.0 %collective-permute-start = (f32[8,1,1600]{2,1,0:T(1,128)S(1)}, f32[8,1,1600]{2,1,0:T(1,128)S(1)}, u32[]{:S(2)}, u32[]{:S(2)}) collective-permute-start(f32[8,1,1600]{2,1,0:T(1,128)S(1)} %shard_map.56), channel_id=1, source_target_pairs={{0,1},{1,0},{2,3},{3,2},{4,5},{5,4},{6,7},{7,6},{8,9},{9,8},{10,11... | collective-permute-start | bytes 153608 | tf_op jit(solution)/shard_map/ppermute | solution.py:24
  4.1 0.9 %copy-done.3 = f32[1,40,1600]{2,1,0:T(8,128)S(1)} copy-done((f32[1,40,1600]{2,1,0:T(8,128)S(1)}, f32[1,40,1600]{2,1,0:T(8,128)}, u32[]{:S(2)}) %copy-start.3) | copy-done | bytes 256024
  5.0 1.0 %shard_map.55 = (f32[10,40,128]{2,1,0:T(8,128)S(1)}, f32[10,40,128]{2,1,0:T(8,128)S(1)}) custom-call(s32[1]{0:T(128)} %bitcast.slab_ref, f32[20,1,1600]{2,1,0:T(1,128)S(1)} %bitcast.12, f32[40,1600]{1,0:T(8,128)S(1)} %bitcast.13), custom_call_target="tpu_custom_call" | custom-call | tf_op jit(solution)/shard_map/pallas_call | solution.py:532
  6.0 0.2 collective-permute-done.halo_ref
  6.2 1.5 %shard_map.57 = (f32[10,40,128]{2,1,0:T(8,128)S(1)}, f32[120,128]{1,0:T(8,128)S(1)}, f32[128,128]{1,0:T(8,128)S(1)}) custom-call(s32[1]{0:T(128)} %bitcast.slab_ref, f32[10,40,128]{2,1,0:T(8,128)S(1)} %get-tuple-element.10.start_ref, f32[8,1,1600]{2,1,0:T(1,128)S(1)} %collective-permute-done.halo_ref, ...), custom_call_target="tpu_custom_call" | custom-call | tf_op jit(solution)/shard_map/pallas_call | solution.py:541
  7.7 0.0 copy-start.4
  7.7 0.7 %copy-done.4 = f32[10,40,128]{2,1,0:T(8,128)} copy-done((f32[10,40,128]{2,1,0:T(8,128)}, f32[10,40,128]{2,1,0:T(8,128)S(1)}, u32[]{:S(2)}) %copy-start.4) | copy-done | bytes 204824
  8.4 2.1 %collective-permute-start.1 = (f32[128,128]{1,0:T(8,128)S(1)}, f32[128,128]{1,0:T(8,128)S(1)}, u32[]{:S(2)}, u32[]{:S(2)}) collective-permute-start(f32[128,128]{1,0:T(8,128)S(1)} %get-tuple-element.12), channel_id=1, source_target_pairs={{0,2},{1,3},{2,0},{3,1},{4,6},{5,7},{6,4},{7,5},{8,10},{9,11},{10,... | collective-permute-start | bytes 196616 | tf_op jit(solution)/shard_map/ppermute | solution.py:24
  10.5 2.2 %collective-permute-done.1 = f32[128,128]{1,0:T(8,128)S(1)} collective-permute-done((f32[128,128]{1,0:T(8,128)S(1)}, f32[128,128]{1,0:T(8,128)S(1)}, u32[]{:S(2)}, u32[]{:S(2)}) %collective-permute-start.1) | collective-permute-done | bytes 65568 | tf_op jit(solution)/shard_map/ppermute | solution.py:24
  12.8 3.1 %collective-permute-start.2 = (f32[128,128]{1,0:T(8,128)S(1)}, f32[128,128]{1,0:T(8,128)S(1)}, u32[]{:S(2)}, u32[]{:S(2)}) collective-permute-start(f32[128,128]{1,0:T(8,128)S(1)} %add.11), channel_id=1, source_target_pairs={{0,4},{1,5},{2,6},{3,7},{4,0},{5,1},{6,2},{7,3},{8,12},{9,13},{10,... | collective-permute-start | bytes 196616 | tf_op jit(solution)/shard_map/ppermute | solution.py:24
  15.9 2.2 %collective-permute-done.2 = f32[128,128]{1,0:T(8,128)S(1)} collective-permute-done((f32[128,128]{1,0:T(8,128)S(1)}, f32[128,128]{1,0:T(8,128)S(1)}, u32[]{:S(2)}, u32[]{:S(2)}) %collective-permute-start.2) | collective-permute-done | bytes 65568 | tf_op jit(solution)/shard_map/ppermute | solution.py:24
  18.1 1.9 %collective-permute-start.4 = (f32[128,128]{1,0:T(8,128)S(1)}, f32[128,128]{1,0:T(8,128)S(1)}, u32[]{:S(2)}, u32[]{:S(2)}) collective-permute-start(f32[128,128]{1,0:T(8,128)S(1)} %add.12), channel_id=1, source_target_pairs={{0,16},{1,17},{2,18},{3,19},{4,20},{5,21},{6,22},{7,23},{8,24},{9,... | collective-permute-start | bytes 196616 | tf_op jit(solution)/shard_map/ppermute | solution.py:564
  20.0 1.4 %collective-permute-start.5 = (f32[128,128]{1,0:T(8,128)S(1)}, f32[128,128]{1,0:T(8,128)S(1)}, u32[]{:S(2)}, u32[]{:S(2)}) collective-permute-start(f32[128,128]{1,0:T(8,128)S(1)} %add.12), channel_id=1, source_target_pairs={{0,17},{1,16},{2,19},{3,18},{4,21},{5,20},{6,23},{7,22},{8,25},{9,... | collective-permute-start | bytes 196616 | tf_op jit(solution)/shard_map/ppermute | solution.py:564
  21.5 0.3 collective-permute-start.3
  21.7 0.7 %collective-permute-done.4 = f32[128,128]{1,0:T(8,128)S(1)} collective-permute-done((f32[128,128]{1,0:T(8,128)S(1)}, f32[128,128]{1,0:T(8,128)S(1)}, u32[]{:S(2)}, u32[]{:S(2)}) %collective-permute-start.4) | collective-permute-done | bytes 65568 | tf_op jit(solution)/shard_map/ppermute | solution.py:564
  22.4 2.7 %collective-permute-done.5 = f32[128,128]{1,0:T(8,128)S(1)} collective-permute-done((f32[128,128]{1,0:T(8,128)S(1)}, f32[128,128]{1,0:T(8,128)S(1)}, u32[]{:S(2)}, u32[]{:S(2)}) %collective-permute-start.5) | collective-permute-done | bytes 65568 | tf_op jit(solution)/shard_map/ppermute | solution.py:564
  25.2 1.2 %collective-permute-done.3.beside_ref = f32[248,128]{1,0:T(8,128)S(1)} collective-permute-done((f32[248,128]{1,0:T(8,128)S(1)}, f32[248,128]{1,0:T(8,128)S(1)}, u32[]{:S(2)}, u32[]{:S(2)}) %collective-permute-start.3) | collective-permute-done | bytes 127008 | tf_op jit(solution)/shard_map/ppermute | solution.py:564
  26.5 0.1 collective-permute-start.6
  26.6 0.1 reshape.17.info_in_ref
  26.7 1.6 %collective-permute-done.6.across_ref = f32[2,256,128]{2,1,0:T(8,128)} collective-permute-done((f32[2,256,128]{2,1,0:T(8,128)S(1)}, f32[2,256,128]{2,1,0:T(8,128)}, u32[]{:S(2)}, u32[]{:S(2)}) %collective-permute-start.6) | collective-permute-done | bytes 262176 | tf_op jit(solution)/shard_map/ppermute | solution.py:24
  28.3 0.0 copy-done.2
  28.3 0.9 %copy-done.5 = f32[10,40,128]{2,1,0:T(8,128)S(1)} copy-done((f32[10,40,128]{2,1,0:T(8,128)S(1)}, f32[10,40,128]{2,1,0:T(8,128)}, u32[]{:S(2)}) %copy-start.5) | copy-done | bytes 204824
  29.2 5.6 %shard_map.58 = f32[20,1,1600]{2,1,0:T(1,128)} custom-call(s32[1]{0:T(128)} %bitcast.slab_ref, s32[1]{0:T(128)} %bitcast.1.dom_ref, s32[12]{0:T(128)S(1)} %reshape.17.info_in_ref, f32[2,256,128]{2,1,0:T(8,128)S(1)} %pad_maximum_fusion.near_ref, f32[2,256,128]{2,1,0:T(8,128)} %collective-permute-done.6.across_ref, f32[10,40,128]{2,1,0:T(8,128)S(1)} %copy-done.5, ...), custom_call_target="tpu_custom_call" | custom-call | tf_op jit(solution)/shard_map/pallas_call | solution.py:587
  (17 shorter events, 0.1 us)
Async XLA Ops:
  0.0 28.3 %copy-start = (bf16[2304,512]{1,0:T(8,128)(2,1)S(1)}, bf16[2304,512]{1,0:T(8,128)(2,1)}, u32[]{:S(2)}) copy-start(bf16[2304,512]{1,0:T(8,128)(2,1)} %constant.26.clone.table_ref) | copy-start | bytes 7077892
  0.0 1.1 %copy-start.1 = (f32[1,1,20,1600]{3,1,2,0:T(1,128)S(1)}, f32[1,1,20,1600]{3,1,2,0:T(1,128)}, u32[]{:S(2)}) copy-start(f32[1,1,20,1600]{3,1,2,0:T(1,128)} %param.5) | copy-start | bytes 384004
  1.1 27.2 %copy-start.2 = (f32[1024,128]{1,0:T(8,128)S(1)}, f32[1024,128]{1,0:T(8,128)}, u32[]{:S(2)}) copy-start(f32[1024,128]{1,0:T(8,128)} %constant.27.clone.factor_ref) | copy-start | bytes 1572868
  1.1 5.1 %collective-permute-start = (f32[8,1,1600]{2,1,0:T(1,128)S(1)}, f32[8,1,1600]{2,1,0:T(1,128)S(1)}, u32[]{:S(2)}, u32[]{:S(2)}) collective-permute-start(f32[8,1,1600]{2,1,0:T(1,128)S(1)} %shard_map.56), channel_id=1, source_target_pairs={{0,1},{1,0},{2,3},{3,2},{4,5},{5,4},{6,7},{7,6},{8,9},{9,8},{10,11... | collective-permute-start | bytes 153608 | tf_op jit(solution)/shard_map/ppermute | solution.py:24
  4.1 1.0 %copy-start.3 = (f32[1,40,1600]{2,1,0:T(8,128)S(1)}, f32[1,40,1600]{2,1,0:T(8,128)}, u32[]{:S(2)}) copy-start(f32[1,40,1600]{2,1,0:T(8,128)} %param.6) | copy-start | bytes 768004
  5.0 21.6 %copy-start.6 = (s32[4,3]{1,0:T(4,128)S(1)}, s32[4,3]{1,0:T(4,128)}, u32[]{:S(2)}) copy-start(s32[4,3]{1,0:T(4,128)} %param.7) | copy-start | bytes 148
  7.7 0.7 %copy-start.4 = (f32[10,40,128]{2,1,0:T(8,128)}, f32[10,40,128]{2,1,0:T(8,128)S(1)}, u32[]{:S(2)}) copy-start(f32[10,40,128]{2,1,0:T(8,128)S(1)} %get-tuple-element.14.filt_ref) | copy-start | bytes 614404
  8.4 4.3 %collective-permute-start.1 = (f32[128,128]{1,0:T(8,128)S(1)}, f32[128,128]{1,0:T(8,128)S(1)}, u32[]{:S(2)}, u32[]{:S(2)}) collective-permute-start(f32[128,128]{1,0:T(8,128)S(1)} %get-tuple-element.12), channel_id=1, source_target_pairs={{0,2},{1,3},{2,0},{3,1},{4,6},{5,7},{6,4},{7,5},{8,10},{9,11},{10,... | collective-permute-start | bytes 196616 | tf_op jit(solution)/shard_map/ppermute | solution.py:24
  12.8 5.3 %collective-permute-start.2 = (f32[128,128]{1,0:T(8,128)S(1)}, f32[128,128]{1,0:T(8,128)S(1)}, u32[]{:S(2)}, u32[]{:S(2)}) collective-permute-start(f32[128,128]{1,0:T(8,128)S(1)} %add.11), channel_id=1, source_target_pairs={{0,4},{1,5},{2,6},{3,7},{4,0},{5,1},{6,2},{7,3},{8,12},{9,13},{10,... | collective-permute-start | bytes 196616 | tf_op jit(solution)/shard_map/ppermute | solution.py:24
  18.1 4.3 %collective-permute-start.4 = (f32[128,128]{1,0:T(8,128)S(1)}, f32[128,128]{1,0:T(8,128)S(1)}, u32[]{:S(2)}, u32[]{:S(2)}) collective-permute-start(f32[128,128]{1,0:T(8,128)S(1)} %add.12), channel_id=1, source_target_pairs={{0,16},{1,17},{2,18},{3,19},{4,20},{5,21},{6,22},{7,23},{8,24},{9,... | collective-permute-start | bytes 196616 | tf_op jit(solution)/shard_map/ppermute | solution.py:564
  20.0 5.2 %collective-permute-start.5 = (f32[128,128]{1,0:T(8,128)S(1)}, f32[128,128]{1,0:T(8,128)S(1)}, u32[]{:S(2)}, u32[]{:S(2)}) collective-permute-start(f32[128,128]{1,0:T(8,128)S(1)} %add.12), channel_id=1, source_target_pairs={{0,17},{1,16},{2,19},{3,18},{4,21},{5,20},{6,23},{7,22},{8,25},{9,... | collective-permute-start | bytes 196616 | tf_op jit(solution)/shard_map/ppermute | solution.py:564
  21.5 5.0 %collective-permute-start.3 = (f32[248,128]{1,0:T(8,128)S(1)}, f32[248,128]{1,0:T(8,128)S(1)}, u32[]{:S(2)}, u32[]{:S(2)}) collective-permute-start(f32[248,128]{1,0:T(8,128)S(1)} %pad_maximum_fusion.1), channel_id=1, source_target_pairs={{0,1},{1,0},{2,3},{3,2},{4,5},{5,4},{6,7},{7,6},{8,9},{9,8},{10,11... | collective-permute-start | bytes 380936 | tf_op jit(solution)/shard_map/ppermute | solution.py:564
  26.5 1.7 %collective-permute-start.6 = (f32[2,256,128]{2,1,0:T(8,128)S(1)}, f32[2,256,128]{2,1,0:T(8,128)}, u32[]{:S(2)}, u32[]{:S(2)}) collective-permute-start(f32[2,256,128]{2,1,0:T(8,128)S(1)} %pad_maximum_fusion.near_ref), channel_id=1, source_target_pairs={{0,8},{8,0},{16,24},{24,16},{1,9},{9,1},{17,25},{25,17},{2,10},{10... | collective-permute-start | bytes 786440 | tf_op jit(solution)/shard_map/ppermute | solution.py:24
  28.3 0.9 %copy-start.5 = (f32[10,40,128]{2,1,0:T(8,128)S(1)}, f32[10,40,128]{2,1,0:T(8,128)}, u32[]{:S(2)}) copy-start(f32[10,40,128]{2,1,0:T(8,128)} %copy-done.4) | copy-start | bytes 614404

commit v7 on v6

--- a/solution.py
+++ b/solution.py
@@ -93,12 +93,17 @@
         field_ref[level] = total
 
 
-def edge_kernel(pk, slab_ref, psi_ref, edge_ref):
+def edge_kernel(pk, slab_ref, psi_ref, edge_ref, own_ref, sem):
+    copy = pltpu.make_async_copy(psi_ref, own_ref, sem)
+    copy.start()
     first = jnp.where(slab_ref[0] == 0, pk.half - DEG, 0)
-    edge_ref[...] = psi_ref[pl.ds(first, DEG)]
-
-
-def start_kernel(pk, slab_ref, psi_ref, pot_ref, field_ref, coef_ref, flat_ref, pitched_ref):
+    copy.wait()
+    edge_ref[...] = own_ref[pl.ds(first, DEG)]
+
+
+def start_kernel(pk, slab_ref, psi_ref, pot_in_ref, field_ref, coef_ref, flat_ref, pitched_ref, pot_ref, sem):
+    copy = pltpu.make_async_copy(pot_in_ref, pot_ref, sem)
+    copy.start()
     half, side = pk.half, pk.side
     cells = side * side
     is_lower = slab_ref[0] == 0
@@ -115,6 +120,7 @@
         flat_ref[DEG : DEG + half] = own
 
     pack(pk, flat_ref[...], pitched_ref, field_ref)
+    copy.wait()
 
     @pl.when(is_lower)
     def _():
@@ -260,12 +266,8 @@
     into = []
     for place_z in range(blocks_z):
         along_z = z_basis[:, place_z * CORE : (place_z + 1) * CORE].T
-        for place_y in range(2):
-            for place_x in range(2):
-                signs = [(-1.0) ** (px * place_x + py * place_y) for px in range(2) for py in range(2)]
-                table = np.kron(np.eye(lines), np.concatenate([sign * along_z for sign in signs], 1))
-                high, low = table_parts(table)
-                into += [high, high, low]
+        high, low = table_parts(np.kron(np.eye(lines), along_z))
+        into += [high, high, low]
     into = np.concatenate(into, 0)
     region = np.arange(side) - BUF
     outer = basis[:, :, region % (2 * CORE)]
@@ -296,11 +298,10 @@
     )
     lam[0, 0, 0, 0, 0] = np.inf
     factor = (FOUR_PI / lam).reshape(CORE * CORE, lanes).astype(np.float32)
-    rest = np.zeros((max(len(back_z), len(spread), len(small)), into.shape[1]), ml_dtypes.bfloat16)
-    rest[: len(back_z), 0:256] = back_z
-    rest[: len(spread), 256:384] = spread
-    rest[: len(small), 384 : 384 + small.shape[1]] = small
-    return np.concatenate([into, rest], 0), factor
+    pieces = [back_z, np.concatenate([into, np.pad(spread, ((0, 0), (0, lanes - 128)))], 0), small]
+    height = max(len(piece) for piece in pieces)
+    pieces = [np.pad(piece, ((0, height - len(piece)), (0, -piece.shape[1] % 128))) for piece in pieces]
+    return np.concatenate(pieces, 1), factor
 
 
 def cube_root(values):
@@ -367,18 +368,30 @@
             found = found + jnp.where(place_of[idx] == where, idx, 0)
         cube_at.append(found)
 
-    for where in range(dom_count):
-        high, low = split2(cubes_ref[cube_at[where]] - mean)
-        for idx, piece in enumerate((high, low, high)):
-            left_ref[:, (where * 3 + idx) * 128 : (where * 3 + idx + 1) * 128] = piece
-    product = dot(left_ref[...], table_ref[0 : dom_count * 3 * 128])
+    for at_z in range(blocks_z):
+        near, at_x, at_y, at_xy = [cubes_ref[cube_at[at_z * 4 + place]] for place in range(4)]
+        sums, others = near + at_x, at_y + at_xy
+        diffs, other_diffs = near - at_x, at_y - at_xy
+        parities = (sums + others - 4.0 * mean, sums - others, diffs + other_diffs, diffs - other_diffs)
+        for parity, value in enumerate(parities):
+            high, low = split2(value)
+            for idx, piece in enumerate((high, low, high)):
+                cols = slice((at_z * 3 + idx) * 128, (at_z * 3 + idx + 1) * 128)
+                left_ref[parity * CORE * 8 : (parity + 1) * CORE * 8, cols] = piece
+    product = dot(left_ref[...], table_ref[0 : blocks_z * 3 * 128, 256 : 256 + lanes])
+    lane = lanes_of((8, 128))
     for x in range(CORE):
         for line in range(lines):
             for col in range(columns):
-                start = line * lanes + col * 128
-                rows_ref[col, x * pitch + line * 8 : x * pitch + line * 8 + 8, :] = product[
-                    x * 8 : (x + 1) * 8, start : start + 128
-                ]
+                total = None
+                for parity in range(4):
+                    into = parity * grid_z - col * 128
+                    if 0 <= into < 128:
+                        at = line * grid_z
+                        part = product[(parity * CORE + x) * 8 : (parity * CORE + x + 1) * 8, at // 128 * 128 : at // 128 * 128 + 128]
+                        part = roll(part, into - at % 128)
+                        total = part if total is None else jnp.where(lane >= into, part, total)
+                rows_ref[col, x * pitch + line * 8 : x * pitch + line * 8 + 8, :] = total
 
     lane = lanes_of((8, 128))
     for at_z in range(blocks_z):
@@ -434,10 +447,8 @@
                 at = (idx * columns + col) * 128
                 ref[col, start : start + count, :] = values[:, at : at + 128]
 
-    base = dom_count * 3 * 128
-
     def small(first, count):
-        return table_ref[base + first : base + first + count, 384 : 384 + 3 * CORE]
+        return table_ref[first : first + count, 256 + lanes : 256 + lanes + 3 * CORE]
 
     forward = small(0, 2 * CORE)
     back_y = small(2 * CORE, 2 * side)
@@ -472,12 +483,12 @@
     pieces = []
     for block in range(pk.blocks):
         pieces += split2(flat_ref[block])
-    product = dot(jnp.concatenate(pieces, 1), table_ref[base : base + pk.blocks * 2 * lanes, 0:256])
+    product = dot(jnp.concatenate(pieces, 1), table_ref[0 : pk.blocks * 2 * lanes, 0:256])
     hartree = product[:, 0:128] + product[:, 128:256]
     pieces = []
     for at_z in range(blocks_z):
         pieces += split3(near_dens_ref[at_z])
-    density = dot(jnp.concatenate(pieces, 1), table_ref[base : base + blocks_z * 3 * 128, 256:384])
+    density = dot(jnp.concatenate(pieces, 1), table_ref[blocks_z * 3 * 128 : blocks_z * 6 * 128, 256:384])
     added = (hartree + EXCHANGE_COEF * cube_root(density)) * (2.0 / HALF_WIDTH)
     for level in range(pk.depth):
         coef_ref[level] = start_coef_ref[level] + added[level * side : (level + 1) * side]
@@ -497,7 +508,16 @@
 
 SMEM = pl.BlockSpec(memory_space=pltpu.SMEM)
 VMEM = pl.BlockSpec(memory_space=pltpu.VMEM)
+HBM = pl.BlockSpec(memory_space=pltpu.HBM)
 params = pltpu.CompilerParams(vmem_limit_bytes=32 * 1024 * 1024)
+
+
+def in_vmem(*shape):
+    return pltpu.VMEM(shape, jnp.float32)
+
+
+def in_hbm(value):
+    return pltpu.with_memory_space_constraint(value, pltpu.HBM)
 
 
 def local(psi_in, v_in, offsets):
@@ -517,33 +537,39 @@
     slab_rows = CORE // 2 * 8
 
     f32, bf16 = jnp.float32, jnp.bfloat16
-    field_type = jax.ShapeDtypeStruct(pk.shape, f32)
+    field_type = in_vmem(*pk.shape)
     padded_field = pltpu.VMEM(pk.padded_shape, f32)
 
     rows = psi_in.reshape(half, 1, cells)
-    edge = pl.pallas_call(
+    edge, rows = pl.pallas_call(
         functools.partial(edge_kernel, pk),
-        out_shape=jax.ShapeDtypeStruct((DEG, 1, cells), f32),
-        in_specs=[SMEM, VMEM],
-        out_specs=VMEM,
+        out_shape=(in_vmem(DEG, 1, cells), in_vmem(half, 1, cells)),
+        in_specs=[SMEM, HBM],
+        out_specs=(VMEM, VMEM),
+        scratch_shapes=[pltpu.SemaphoreType.DMA],
         compiler_params=params,
-    )(slab_scalar, rows)
+    )(slab_scalar, in_hbm(rows))
     halo = swapped(edge, "band", 1)
     start, coef = pl.pallas_call(
         functools.partial(start_kernel, pk),
         out_shape=(field_type, field_type),
-        in_specs=[SMEM, VMEM, VMEM],
+        in_specs=[SMEM, VMEM, HBM],
         out_specs=(VMEM, VMEM),
-        scratch_shapes=[pltpu.VMEM((pk.rows, cells), f32), pltpu.VMEM((side * pk.pitch, 128), f32)],
+        scratch_shapes=[
+            pltpu.VMEM((pk.rows, cells), f32),
+            pltpu.VMEM((side * pk.pitch, 128), f32),
+            pltpu.VMEM((side, cells), f32),
+            pltpu.SemaphoreType.DMA,
+        ],
         compiler_params=params,
-    )(slab_scalar, rows, v_in[0])
+    )(slab_scalar, rows, in_hbm(v_in[0]))
 
     filt, edge, dens = pl.pallas_call(
         functools.partial(first_kernel, pk, bands),
         out_shape=(
             field_type,
-            jax.ShapeDtypeStruct((pk.edge_groups * side, 128), f32),
-            jax.ShapeDtypeStruct((slab_rows, 128), f32),
+            in_vmem(pk.edge_groups * side, 128),
+            in_vmem(slab_rows, 128),
         ),
         in_specs=[SMEM, VMEM, VMEM, VMEM],
         out_specs=(VMEM, VMEM, VMEM),
@@ -594,7 +620,7 @@
             padded_field,
             padded_field,
             pltpu.VMEM(pk.shape, f32),
-            pltpu.VMEM((CORE * 8, dom_count * 3 * 128), bf16),
+            pltpu.VMEM((4 * CORE * 8, dom_count // 4 * 3 * 128), bf16),
             pltpu.VMEM((lanes // 128, CORE * pitch, 128), f32),
             pltpu.VMEM((lanes // 128, CORE * pitch, 128), f32),
             pltpu.VMEM((lanes // 128, CORE * pitch, 128), f32),

time: 35 us -> 32.3 us (0.923)
  local copies, waits for them, and re-layouts: 3.69 us -> 0.77 us
  Pallas kernels: 8.1 us -> 8.62 us
    unnamed x14 -> x6, local copies, waits for them, and re-layouts: 3.61 us -> 0.69 us
    pallas_call x1, Pallas kernels: 0.01 us -> 0.92 us  [local(): pl.pallas_call(functools.partial(edge_kernel, pk), out_shape=(in_vmem(DEG...]
    pallas_call x1, Pallas kernels: 5.61 us -> 4.75 us  [local(): pl.pallas_call(functools.partial(second_kernel, pk, masks), out_shape=jax...]
    pallas_call x1, Pallas kernels: 0.96 us -> 1.42 us  [local(): pl.pallas_call(functools.partial(start_kernel, pk), out_shape=(field_type...]
  transfers between devices with their start and end apart: 7 -> 7, of which waited for: 7 -> 7; matrix products, arithmetic and copies ran while one was open for 0% -> 0% of each run, Pallas kernels for 3% -> 4%
where the time goes in v7:
time: 32.3 us; the launch traced here: 32.1 us
  starting transfers between devices  12 us (37%)
  waiting for transfers between devices  10.6 us (33%)
  Pallas kernels  8.62 us (27%)
  local copies, waits for them, and re-layouts  0.77 us (2%)
    ppermute x4, starting transfers between devices, swapped(): return lax.ppermute(value, axis, pairs)  8.34 us
    ppermute x4, waiting for transfers between devices, swapped(): return lax.ppermute(value, axis, pairs)  5.93 us
    pallas_call x1, Pallas kernels, local(): pl.pallas_call(functools.partial(second_kernel, pk, masks), out_shape=jax...  4.75 us
    ppermute x3, waiting for transfers between devices, crossed(): lax.ppermute(value, both, [(source, source ^ mask) for source in range(co...  4.67 us
    ppermute x3, starting transfers between devices, crossed(): lax.ppermute(value, both, [(source, source ^ mask) for source in range(co...  3.62 us
    pallas_call x1, Pallas kernels, local(): pl.pallas_call(functools.partial(first_kernel, pk, bands), out_shape=(fie...  1.53 us
    pallas_call x1, Pallas kernels, local(): pl.pallas_call(functools.partial(start_kernel, pk), out_shape=(field_type...  1.42 us
    pallas_call x1, Pallas kernels, local(): pl.pallas_call(functools.partial(edge_kernel, pk), out_shape=(in_vmem(DEG...  0.92 us
  transfers between devices with their start and end apart: 7, of which 7 were waited for; matrix products, arithmetic and copies ran while one was open for 0% of the time, Pallas kernels for 4%

profile of v7, /device:TPU:0, one launch (start us, length us, event | category | flops | bytes accessed | tf_op | source)
XLA Modules:
  0.0 32.1 jit_solution(7670316283437627048)
XLA Ops:
  0.0 0.9 %shard_map.55 = (f32[8,1,1600]{2,1,0:T(1,128)S(1)}, f32[20,1,1600]{2,1,0:T(1,128)S(1)}) custom-call(s32[1]{0:T(128)} %bitcast.slab_ref, f32[20,1,1600]{2,1,0:T(1,128)} %bitcast.12), custom_call_target="tpu_custom_call" | custom-call | tf_op jit(solution)/shard_map/pallas_call | solution.py:544
  0.9 3.0 %collective-permute-start = (f32[8,1,1600]{2,1,0:T(1,128)S(1)}, f32[8,1,1600]{2,1,0:T(1,128)S(1)}, u32[]{:S(2)}, u32[]{:S(2)}) collective-permute-start(f32[8,1,1600]{2,1,0:T(1,128)S(1)} %get-tuple-element.14), channel_id=1, source_target_pairs={{0,1},{1,0},{2,3},{3,2},{4,5},{5,4},{6,7},{7,6},{8,9},{9,8},{10,11... | collective-permute-start | bytes 153608 | tf_op jit(solution)/shard_map/ppermute | solution.py:24
  3.9 1.4 %shard_map.56 = (f32[10,40,128]{2,1,0:T(8,128)S(1)}, f32[10,40,128]{2,1,0:T(8,128)S(1)}) custom-call(s32[1]{0:T(128)} %bitcast.slab_ref, f32[20,1,1600]{2,1,0:T(1,128)S(1)} %get-tuple-element.12.psi_ref, f32[40,1600]{1,0:T(8,128)} %bitcast.11), custom_call_target="tpu_custom_call" | custom-call | tf_op jit(solution)/shard_map/pallas_call | solution.py:553
  5.4 0.7 %collective-permute-done.halo_ref = f32[8,1,1600]{2,1,0:T(1,128)S(1)} collective-permute-done((f32[8,1,1600]{2,1,0:T(1,128)S(1)}, f32[8,1,1600]{2,1,0:T(1,128)S(1)}, u32[]{:S(2)}, u32[]{:S(2)}) %collective-permute-start) | collective-permute-done | bytes 51232 | tf_op jit(solution)/shard_map/ppermute | solution.py:24
  6.0 1.5 %shard_map.57 = (f32[10,40,128]{2,1,0:T(8,128)S(1)}, f32[120,128]{1,0:T(8,128)S(1)}, f32[128,128]{1,0:T(8,128)S(1)}) custom-call(s32[1]{0:T(128)} %bitcast.slab_ref, f32[10,40,128]{2,1,0:T(8,128)S(1)} %get-tuple-element.13.start_ref, f32[8,1,1600]{2,1,0:T(1,128)S(1)} %collective-permute-done.halo_ref, ...), custom_call_target="tpu_custom_call" | custom-call | tf_op jit(solution)/shard_map/pallas_call | solution.py:567
  7.6 2.2 %collective-permute-start.1 = (f32[128,128]{1,0:T(8,128)S(1)}, f32[128,128]{1,0:T(8,128)S(1)}, u32[]{:S(2)}, u32[]{:S(2)}) collective-permute-start(f32[128,128]{1,0:T(8,128)S(1)} %get-tuple-element.16), channel_id=1, source_target_pairs={{0,2},{1,3},{2,0},{3,1},{4,6},{5,7},{6,4},{7,5},{8,10},{9,11},{10,... | collective-permute-start | bytes 196616 | tf_op jit(solution)/shard_map/ppermute | solution.py:24
  9.8 2.2 %collective-permute-done.1 = f32[128,128]{1,0:T(8,128)S(1)} collective-permute-done((f32[128,128]{1,0:T(8,128)S(1)}, f32[128,128]{1,0:T(8,128)S(1)}, u32[]{:S(2)}, u32[]{:S(2)}) %collective-permute-start.1) | collective-permute-done | bytes 65568 | tf_op jit(solution)/shard_map/ppermute | solution.py:24
  12.0 3.1 %collective-permute-start.2 = (f32[128,128]{1,0:T(8,128)S(1)}, f32[128,128]{1,0:T(8,128)S(1)}, u32[]{:S(2)}, u32[]{:S(2)}) collective-permute-start(f32[128,128]{1,0:T(8,128)S(1)} %add.11), channel_id=1, source_target_pairs={{0,4},{1,5},{2,6},{3,7},{4,0},{5,1},{6,2},{7,3},{8,12},{9,13},{10,... | collective-permute-start | bytes 196616 | tf_op jit(solution)/shard_map/ppermute | solution.py:24
  15.1 2.2 %collective-permute-done.2 = f32[128,128]{1,0:T(8,128)S(1)} collective-permute-done((f32[128,128]{1,0:T(8,128)S(1)}, f32[128,128]{1,0:T(8,128)S(1)}, u32[]{:S(2)}, u32[]{:S(2)}) %collective-permute-start.2) | collective-permute-done | bytes 65568 | tf_op jit(solution)/shard_map/ppermute | solution.py:24
  17.4 1.9 %collective-permute-start.4 = (f32[128,128]{1,0:T(8,128)S(1)}, f32[128,128]{1,0:T(8,128)S(1)}, u32[]{:S(2)}, u32[]{:S(2)}) collective-permute-start(f32[128,128]{1,0:T(8,128)S(1)} %add.12), channel_id=1, source_target_pairs={{0,16},{1,17},{2,18},{3,19},{4,20},{5,21},{6,22},{7,23},{8,24},{9,... | collective-permute-start | bytes 196616 | tf_op jit(solution)/shard_map/ppermute | solution.py:590
  19.3 1.4 %collective-permute-start.5 = (f32[128,128]{1,0:T(8,128)S(1)}, f32[128,128]{1,0:T(8,128)S(1)}, u32[]{:S(2)}, u32[]{:S(2)}) collective-permute-start(f32[128,128]{1,0:T(8,128)S(1)} %add.12), channel_id=1, source_target_pairs={{0,17},{1,16},{2,19},{3,18},{4,21},{5,20},{6,23},{7,22},{8,25},{9,... | collective-permute-start | bytes 196616 | tf_op jit(solution)/shard_map/ppermute | solution.py:590
  20.7 0.0 copy-start
  20.7 0.3 collective-permute-start.3
  21.0 0.7 %collective-permute-done.4 = f32[128,128]{1,0:T(8,128)S(1)} collective-permute-done((f32[128,128]{1,0:T(8,128)S(1)}, f32[128,128]{1,0:T(8,128)S(1)}, u32[]{:S(2)}, u32[]{:S(2)}) %collective-permute-start.4) | collective-permute-done | bytes 65568 | tf_op jit(solution)/shard_map/ppermute | solution.py:590
  21.7 2.7 %collective-permute-done.5 = f32[128,128]{1,0:T(8,128)S(1)} collective-permute-done((f32[128,128]{1,0:T(8,128)S(1)}, f32[128,128]{1,0:T(8,128)S(1)}, u32[]{:S(2)}, u32[]{:S(2)}) %collective-permute-start.5) | collective-permute-done | bytes 65568 | tf_op jit(solution)/shard_map/ppermute | solution.py:590
  24.5 0.0 copy-start.1
  24.5 1.2 %collective-permute-done.3.beside_ref = f32[248,128]{1,0:T(8,128)S(1)} collective-permute-done((f32[248,128]{1,0:T(8,128)S(1)}, f32[248,128]{1,0:T(8,128)S(1)}, u32[]{:S(2)}, u32[]{:S(2)}) %collective-permute-start.3) | collective-permute-done | bytes 127008 | tf_op jit(solution)/shard_map/ppermute | solution.py:590
  25.8 0.1 collective-permute-start.6
  25.9 0.0 copy-start.2
  25.9 0.7 %copy-done.2 = s32[4,3]{1,0:T(4,128)S(1)} copy-done((s32[4,3]{1,0:T(4,128)S(1)}, s32[4,3]{1,0:T(4,128)}, u32[]{:S(2)}) %copy-start.2) | copy-done | bytes 72
  26.6 0.1 reshape.17.info_in_ref
  26.6 0.8 %collective-permute-done.6.across_ref = f32[2,256,128]{2,1,0:T(8,128)S(1)} collective-permute-done((f32[2,256,128]{2,1,0:T(8,128)S(1)}, f32[2,256,128]{2,1,0:T(8,128)S(1)}, u32[]{:S(2)}, u32[]{:S(2)}) %collective-permute-start.6) | collective-permute-done | bytes 262176 | tf_op jit(solution)/shard_map/ppermute | solution.py:24
  27.4 0.0 copy-done
  27.4 4.7 %shard_map.58 = f32[20,1,1600]{2,1,0:T(1,128)} custom-call(s32[1]{0:T(128)} %bitcast.slab_ref, s32[1]{0:T(128)} %bitcast.1.dom_ref, s32[12]{0:T(128)S(1)} %reshape.17.info_in_ref, f32[2,256,128]{2,1,0:T(8,128)S(1)} %pad_maximum_fusion.near_ref, f32[2,256,128]{2,1,0:T(8,128)S(1)} %collective-permute-done.6.across_ref, ...), custom_call_target="tpu_custom_call" | custom-call | tf_op jit(solution)/shard_map/pallas_call | solution.py:613
  (9 shorter events, 0.1 us)
Async XLA Ops:
  0.9 5.1 %collective-permute-start = (f32[8,1,1600]{2,1,0:T(1,128)S(1)}, f32[8,1,1600]{2,1,0:T(1,128)S(1)}, u32[]{:S(2)}, u32[]{:S(2)}) collective-permute-start(f32[8,1,1600]{2,1,0:T(1,128)S(1)} %get-tuple-element.14), channel_id=1, source_target_pairs={{0,1},{1,0},{2,3},{3,2},{4,5},{5,4},{6,7},{7,6},{8,9},{9,8},{10,11... | collective-permute-start | bytes 153608 | tf_op jit(solution)/shard_map/ppermute | solution.py:24
  7.6 4.4 %collective-permute-start.1 = (f32[128,128]{1,0:T(8,128)S(1)}, f32[128,128]{1,0:T(8,128)S(1)}, u32[]{:S(2)}, u32[]{:S(2)}) collective-permute-start(f32[128,128]{1,0:T(8,128)S(1)} %get-tuple-element.16), channel_id=1, source_target_pairs={{0,2},{1,3},{2,0},{3,1},{4,6},{5,7},{6,4},{7,5},{8,10},{9,11},{10,... | collective-permute-start | bytes 196616 | tf_op jit(solution)/shard_map/ppermute | solution.py:24
  12.0 5.3 %collective-permute-start.2 = (f32[128,128]{1,0:T(8,128)S(1)}, f32[128,128]{1,0:T(8,128)S(1)}, u32[]{:S(2)}, u32[]{:S(2)}) collective-permute-start(f32[128,128]{1,0:T(8,128)S(1)} %add.11), channel_id=1, source_target_pairs={{0,4},{1,5},{2,6},{3,7},{4,0},{5,1},{6,2},{7,3},{8,12},{9,13},{10,... | collective-permute-start | bytes 196616 | tf_op jit(solution)/shard_map/ppermute | solution.py:24
  17.4 4.3 %collective-permute-start.4 = (f32[128,128]{1,0:T(8,128)S(1)}, f32[128,128]{1,0:T(8,128)S(1)}, u32[]{:S(2)}, u32[]{:S(2)}) collective-permute-start(f32[128,128]{1,0:T(8,128)S(1)} %add.12), channel_id=1, source_target_pairs={{0,16},{1,17},{2,18},{3,19},{4,20},{5,21},{6,22},{7,23},{8,24},{9,... | collective-permute-start | bytes 196616 | tf_op jit(solution)/shard_map/ppermute | solution.py:590
  19.3 5.2 %collective-permute-start.5 = (f32[128,128]{1,0:T(8,128)S(1)}, f32[128,128]{1,0:T(8,128)S(1)}, u32[]{:S(2)}, u32[]{:S(2)}) collective-permute-start(f32[128,128]{1,0:T(8,128)S(1)} %add.12), channel_id=1, source_target_pairs={{0,17},{1,16},{2,19},{3,18},{4,21},{5,20},{6,23},{7,22},{8,25},{9,... | collective-permute-start | bytes 196616 | tf_op jit(solution)/shard_map/ppermute | solution.py:590
  20.7 6.7 %copy-start = (bf16[768,512]{1,0:T(8,128)(2,1)S(1)}, bf16[768,512]{1,0:T(8,128)(2,1)}, u32[]{:S(2)}) copy-start(bf16[768,512]{1,0:T(8,128)(2,1)} %constant.26.clone.table_ref) | copy-start | bytes 2359300
  20.7 5.0 %collective-permute-start.3 = (f32[248,128]{1,0:T(8,128)S(1)}, f32[248,128]{1,0:T(8,128)S(1)}, u32[]{:S(2)}, u32[]{:S(2)}) collective-permute-start(f32[248,128]{1,0:T(8,128)S(1)} %pad_maximum_fusion.1), channel_id=1, source_target_pairs={{0,1},{1,0},{2,3},{3,2},{4,5},{5,4},{6,7},{7,6},{8,9},{9,8},{10,11... | collective-permute-start | bytes 380936 | tf_op jit(solution)/shard_map/ppermute | solution.py:590
  24.5 2.9 %copy-start.1 = (f32[1024,128]{1,0:T(8,128)S(1)}, f32[1024,128]{1,0:T(8,128)}, u32[]{:S(2)}) copy-start(f32[1024,128]{1,0:T(8,128)} %constant.27.clone.factor_ref) | copy-start | bytes 1572868
  25.8 1.6 %collective-permute-start.6 = (f32[2,256,128]{2,1,0:T(8,128)S(1)}, f32[2,256,128]{2,1,0:T(8,128)S(1)}, u32[]{:S(2)}, u32[]{:S(2)}) collective-permute-start(f32[2,256,128]{2,1,0:T(8,128)S(1)} %pad_maximum_fusion.near_ref), channel_id=1, source_target_pairs={{0,8},{8,0},{16,24},{24,16},{1,9},{9,1},{17,25},{25,17},{2,10},{10... | collective-permute-start | bytes 786440 | tf_op jit(solution)/shard_map/ppermute | solution.py:24
  25.9 0.7 %copy-start.2 = (s32[4,3]{1,0:T(4,128)S(1)}, s32[4,3]{1,0:T(4,128)}, u32[]{:S(2)}) copy-start(s32[4,3]{1,0:T(4,128)} %param.7) | copy-start | bytes 148

commit v8 on v7

--- a/solution.py
+++ b/solution.py
@@ -101,9 +101,14 @@
     edge_ref[...] = own_ref[pl.ds(first, DEG)]
 
 
-def start_kernel(pk, slab_ref, psi_ref, pot_in_ref, field_ref, coef_ref, flat_ref, pitched_ref, pot_ref, sem):
-    copy = pltpu.make_async_copy(pot_in_ref, pot_ref, sem)
+def start_kernel(
+    pk, masks, slab_ref, dom_ref, psi_ref, pot_in_ref, offsets_in_ref,
+    field_ref, coef_ref, code_ref, flat_ref, pitched_ref, pot_ref, offsets_ref, sems,
+):
+    copy = pltpu.make_async_copy(pot_in_ref, pot_ref, sems.at[0])
+    offsets_copy = pltpu.make_async_copy(offsets_in_ref, offsets_ref, sems.at[1])
     copy.start()
+    offsets_copy.start()
     half, side = pk.half, pk.side
     cells = side * side
     is_lower = slab_ref[0] == 0
@@ -132,16 +137,32 @@
 
     pack(pk, flat_ref[...], pitched_ref, coef_ref)
 
-
-def filtered_field(pk, first_ref, second_ref, coef_ref):
+    offsets_copy.wait()
+    dom, dom_count = dom_ref[0], len(masks)
+    blocks_z = dom_count // 4
+    code = jnp.int32(0)
+    for idx, mask in enumerate(masks):
+        other = dom ^ mask
+        at_x = (offsets_ref[other, 0] != offsets_ref[dom, 0]).astype(jnp.int32)
+        at_y = (offsets_ref[other, 1] != offsets_ref[dom, 1]).astype(jnp.int32)
+        at_z = (offsets_ref[other, 2] - offsets_ref[dom, 2]) // CORE
+        at_z = jnp.where(at_z < 0, at_z + blocks_z, at_z)
+        place = (at_z * 2 + at_y) * 2 + at_x
+        for where in range(dom_count):
+            code = code + jnp.where(place == where, idx * dom_count**where, 0)
+    code_ref[...] = jnp.full(code_ref.shape, code.astype(jnp.float32))
+
+
+def filtered_field(pk, start_ref, one_ref, two_ref, coef_ref):
     lane = lanes_of((8, 128))
     is_cell = (lane % pk.span < pk.side) & (lane < pk.blocks * pk.span)
     full_weight = jnp.where(is_cell, 1.0 / HALF_WIDTH, 0.0)
     part_weight = jnp.where(is_cell & (lane < (pk.blocks - 1) * pk.span), 1.0 / HALF_WIDTH, 0.0)
     after_first = lane >= pk.span
     before_last = lane < (pk.blocks - 1) * pk.span
-    current_ref, other_ref = first_ref, second_ref
+    previous_ref, current_ref = None, start_ref
     for order in range(DEG):
+        target_ref = (one_ref, two_ref)[order % 2]
         for tile in range(pk.side // 8):
             at = 8 + 8 * tile
             values = [current_ref[level, at : at + 8, :] for level in range(pk.depth)]
@@ -160,10 +181,9 @@
                 if order == 0:
                     following = 0.5 * following
                 else:
-                    following = following - other_ref[level, at : at + 8, :]
-                other_ref[level, at : at + 8, :] = following
-        current_ref, other_ref = other_ref, current_ref
-    return current_ref
+                    following = following - previous_ref[level, at : at + 8, :]
+                target_ref[level, at : at + 8, :] = following
+        previous_ref, current_ref = current_ref, target_ref
 
 
 def clear_margins(pk, ref):
@@ -173,14 +193,15 @@
 
 
 def first_kernel(
-    pk, bands, slab_ref, start_ref, halo_ref, coef_ref, filt_ref, edge_ref, dens_ref, one_ref, two_ref, lines_ref
+    pk, bands, slab_ref, start_ref, halo_ref, coef_ref, filt_ref, dens_ref, field_ref, one_ref, lines_ref
 ):
     side, span = pk.side, pk.span
     slab = slab_ref[0]
     is_lower = slab == 0
+    clear_margins(pk, field_ref)
     clear_margins(pk, one_ref)
-    clear_margins(pk, two_ref)
-    one_ref[:, 8 : 8 + side, :] = start_ref[...]
+    clear_margins(pk, filt_ref)
+    field_ref[:, 8 : 8 + side, :] = start_ref[...]
     halo = halo_ref[:, 0, :]
     lines_ref[...] = jnp.zeros(lines_ref.shape, jnp.float32)
     for y in range(side):
@@ -191,25 +212,15 @@
         high_block, high_level = pk.where(row)
         if low_level == high_level:
             line = jnp.where(is_lower, roll(line, low_block * span), roll(line, high_block * span))
-            one_ref[low_level, 8 : 8 + side, :] = one_ref[low_level, 8 : 8 + side, :] + line
+            field_ref[low_level, 8 : 8 + side, :] = field_ref[low_level, 8 : 8 + side, :] + line
         else:
             low_line = jnp.where(is_lower, roll(line, low_block * span), 0.0)
             high_line = jnp.where(is_lower, 0.0, roll(line, high_block * span))
-            one_ref[low_level, 8 : 8 + side, :] = one_ref[low_level, 8 : 8 + side, :] + low_line
-            one_ref[high_level, 8 : 8 + side, :] = one_ref[high_level, 8 : 8 + side, :] + high_line
-
-    result_ref = filtered_field(pk, one_ref, two_ref, coef_ref)
-    filt_ref[...] = result_ref[:, 8 : 8 + side, :]
-
-    lane = lanes_of((side, 128))
-    for group in range(pk.edge_groups):
-        total = jnp.zeros((side, 128), jnp.float32)
-        for slot in range(min(pk.blocks, DEG - group * pk.blocks)):
-            row = group * pk.blocks + slot + jnp.where(is_lower, pk.half - DEG, DEG)
-            shift = slot * span - row // pk.depth * span + 128 * pk.blocks
-            line = pltpu.roll(result_ref[row % pk.depth, 8 : 8 + side, :], shift % 128, 1)
-            total = jnp.where((lane >= slot * span) & (lane < slot * span + side), line, total)
-        edge_ref[group * side : (group + 1) * side] = total
+            field_ref[low_level, 8 : 8 + side, :] = field_ref[low_level, 8 : 8 + side, :] + low_line
+            field_ref[high_level, 8 : 8 + side, :] = field_ref[high_level, 8 : 8 + side, :] + high_line
+
+    filtered_field(pk, field_ref, one_ref, filt_ref, coef_ref)
+    result_ref = filt_ref
 
     lane = lanes_of((8, 128))
     lines = 128 // CORE
@@ -222,6 +233,35 @@
             shift = line * CORE - BUF - block * span + 128 * pk.blocks
             total = jnp.where(lane // CORE == line, pltpu.roll(value, shift % 128, 1), total)
         dens_ref[cell * 8 : (cell + 1) * 8] = total * total * (1.0 / bands)
+
+
+def send_kernel(pk, slab_ref, result_ref, edge_ref):
+    side, span = pk.side, pk.span
+    is_lower = slab_ref[0] == 0
+    lane = lanes_of((side, 128))
+    for group in range(pk.edge_groups):
+        total = jnp.zeros((side, 128), jnp.float32)
+        for slot in range(min(pk.blocks, DEG - group * pk.blocks)):
+            row = group * pk.blocks + slot + jnp.where(is_lower, pk.half - DEG, DEG)
+            shift = slot * span - row // pk.depth * span + 128 * pk.blocks
+            line = pltpu.roll(result_ref[row % pk.depth, 8 : 8 + side, :], shift % 128, 1)
+            total = jnp.where((lane >= slot * span) & (lane < slot * span + side), line, total)
+        edge_ref[group * side : (group + 1) * side] = total
+
+
+def take_kernel(pk, slab_ref, filt_ref, beside_ref, field_ref):
+    side, span, half = pk.side, pk.span, pk.half
+    is_lower = slab_ref[0] == 0
+    field_ref[...] = filt_ref[...]
+    lane = lanes_of((side, 128))
+    base = CORE // 2 * 8
+    for row in range(DEG):
+        group_at, slot = row // pk.blocks, row % pk.blocks
+        line = beside_ref[base + group_at * side : base + (group_at + 1) * side, :]
+        for wanted, (block, level) in ((True, pk.where(half + row)), (False, pk.where(row))):
+            here = (lane >= block * span) & (lane < block * span + side) & (is_lower == wanted)
+            old = field_ref[level, 8 : 8 + side, :]
+            field_ref[level, 8 : 8 + side, :] = jnp.where(here, roll(line, (block - slot) * span), old)
 
 
 def split2(values):
@@ -313,15 +353,13 @@
 
 
 def second_kernel(
-    pk, masks, slab_ref, dom_ref, info_in_ref, near_ref, across_ref, filt_ref, beside_ref, start_coef_ref,
+    pk, dom_count, slab_ref, code_ref, near_ref, across_ref, field_ref, start_coef_ref,
     table_ref, factor_ref,
     out_ref, cubes_ref, one_ref, two_ref, coef_ref, left_ref, rows_ref, waves_ref, mixed_ref, flat_ref,
-    near_dens_ref, own_ref, lined_ref, info_ref, sem,
+    near_dens_ref, own_ref,
 ):
     side, half, span = pk.side, pk.half, pk.span
-    slab, dom = slab_ref[0], dom_ref[0]
-    is_lower = slab == 0
-    dom_count = len(masks)
+    is_lower = slab_ref[0] == 0
     blocks_z = dom_count // 4
     grid_z = CORE * blocks_z
     lanes = 4 * grid_z
@@ -330,43 +368,12 @@
     pitch = CORE + 8
     kept = padded(pk.rows, 8)
 
-    copy = pltpu.make_async_copy(info_in_ref, info_ref, sem)
-    copy.start()
     cubes_ref[0 : dom_count // 2] = near_ref[...]
     cubes_ref[dom_count // 2 : dom_count] = across_ref[...]
     mean = jnp.sum(cubes_ref[...]) * (1.0 / (dom_count * CORE * CORE * CORE))
 
-    clear_margins(pk, one_ref)
-    clear_margins(pk, two_ref)
-    one_ref[:, 8 : 8 + side, :] = filt_ref[...]
-    lane = lanes_of((side, 128))
-    base = CORE // 2 * 8
-    for row in range(DEG):
-        group_at, slot = row // pk.blocks, row % pk.blocks
-        line = beside_ref[base + group_at * side : base + (group_at + 1) * side, :]
-        for wanted, (block, level) in ((True, pk.where(half + row)), (False, pk.where(row))):
-            here = (lane >= block * span) & (lane < block * span + side) & (is_lower == wanted)
-            old = one_ref[level, 8 : 8 + side, :]
-            one_ref[level, 8 : 8 + side, :] = jnp.where(here, roll(line, (block - slot) * span), old)
-    copy.wait()
-
-    def offset(which, axis):
-        return info_ref[3 * which + axis]
-
-    place_of = []
-    for mask in masks:
-        other = dom ^ mask
-        at_x = (offset(other, 0) != offset(dom, 0)).astype(jnp.int32)
-        at_y = (offset(other, 1) != offset(dom, 1)).astype(jnp.int32)
-        at_z = (offset(other, 2) - offset(dom, 2)) // CORE
-        at_z = jnp.where(at_z < 0, at_z + blocks_z, at_z)
-        place_of.append((at_z * 2 + at_y) * 2 + at_x)
-    cube_at = []
-    for where in range(dom_count):
-        found = jnp.int32(0)
-        for idx in range(dom_count):
-            found = found + jnp.where(place_of[idx] == where, idx, 0)
-        cube_at.append(found)
+    code = jnp.max(code_ref[...]).astype(jnp.int32)
+    cube_at = [code // dom_count**where % dom_count for where in range(dom_count)]
 
     for at_z in range(blocks_z):
         near, at_x, at_y, at_xy = [cubes_ref[cube_at[at_z * 4 + place]] for place in range(4)]
@@ -493,17 +500,26 @@
     for level in range(pk.depth):
         coef_ref[level] = start_coef_ref[level] + added[level * side : (level + 1) * side]
 
-    result_ref = filtered_field(pk, one_ref, two_ref, coef_ref)
+    clear_margins(pk, one_ref)
+    clear_margins(pk, two_ref)
+    filtered_field(pk, field_ref, one_ref, two_ref, coef_ref)
 
     for row in range(half):
         at = row + jnp.where(is_lower, 0, DEG)
         shift = 128 * pk.blocks - at // pk.depth * span
         own_ref[row * side : (row + 1) * side, :] = pltpu.roll(
-            result_ref[at % pk.depth, 8 : 8 + side, :], shift % 128, 1
+            two_ref[at % pk.depth, 8 : 8 + side, :], shift % 128, 1
         )
-    for y in range(side):
-        lined_ref[:, y * side : (y + 1) * side] = own_ref[pl.ds(y, half, stride=side), :][:, 0:side]
-    out_ref[:, 0, :] = lined_ref[...]
+    cells = side * side
+    parts = [roll(own_ref[pl.ds(y, half, stride=side), :], y * side) for y in range(side)]
+    for tile in range(-(-cells // 128)):
+        first, last = tile * 128 // side, min(side - 1, (tile * 128 + 127) // side)
+        lane = lanes_of((half, 128)) + tile * 128
+        total = None
+        for y in range(first, last + 1):
+            total = parts[y] if total is None else jnp.where(lane >= y * side, parts[y], total)
+        width = min(128, cells - tile * 128)
+        out_ref[:, 0, tile * 128 : tile * 128 + width] = total[:, :width]
 
 
 SMEM = pl.BlockSpec(memory_space=pltpu.SMEM)
@@ -550,32 +566,43 @@
         compiler_params=params,
     )(slab_scalar, in_hbm(rows))
     halo = swapped(edge, "band", 1)
-    start, coef = pl.pallas_call(
-        functools.partial(start_kernel, pk),
-        out_shape=(field_type, field_type),
-        in_specs=[SMEM, VMEM, HBM],
-        out_specs=(VMEM, VMEM),
+    masks = [0]
+    bit = dom_count // 2
+    while bit:
+        masks = masks + [one | bit for one in masks]
+        bit //= 2
+    dom_scalar = dom_idx.astype(jnp.int32).reshape(1)
+    start, coef, code = pl.pallas_call(
+        functools.partial(start_kernel, pk, masks),
+        out_shape=(field_type, field_type, in_vmem(8, 128)),
+        in_specs=[SMEM, SMEM, VMEM, HBM, HBM],
+        out_specs=(VMEM, VMEM, VMEM),
         scratch_shapes=[
             pltpu.VMEM((pk.rows, cells), f32),
             pltpu.VMEM((side * pk.pitch, 128), f32),
             pltpu.VMEM((side, cells), f32),
-            pltpu.SemaphoreType.DMA,
+            pltpu.SMEM((dom_count, 3), jnp.int32),
+            pltpu.SemaphoreType.DMA((2,)),
         ],
         compiler_params=params,
-    )(slab_scalar, rows, in_hbm(v_in[0]))
-
-    filt, edge, dens = pl.pallas_call(
+    )(slab_scalar, dom_scalar, rows, in_hbm(v_in[0]), in_hbm(offsets))
+
+    padded_type = in_vmem(*pk.padded_shape)
+    filt, dens = pl.pallas_call(
         functools.partial(first_kernel, pk, bands),
-        out_shape=(
-            field_type,
-            in_vmem(pk.edge_groups * side, 128),
-            in_vmem(slab_rows, 128),
-        ),
+        out_shape=(padded_type, in_vmem(slab_rows, 128)),
         in_specs=[SMEM, VMEM, VMEM, VMEM],
-        out_specs=(VMEM, VMEM, VMEM),
+        out_specs=(VMEM, VMEM),
         scratch_shapes=[padded_field, padded_field, pltpu.VMEM((side * DEG, 128), f32)],
         compiler_params=params,
     )(slab_scalar, start, halo, coef)
+    edge = pl.pallas_call(
+        functools.partial(send_kernel, pk),
+        out_shape=in_vmem(pk.edge_groups * side, 128),
+        in_specs=[SMEM, VMEM],
+        out_specs=VMEM,
+        compiler_params=params,
+    )(slab_scalar, filt)
 
     mask = 2
     while mask < band_count:
@@ -598,22 +625,26 @@
         return jnp.concatenate([jnp.where(is_lower, own, other), jnp.where(is_lower, other, own)], 0)
 
     cubes = jnp.stack([cube_of(dens, beside), cube_of(across, diagonal)])
-    masks = [0, far]
     bit = far // 2
     while bit:
         if bit > 1:
             cubes = jnp.concatenate([cubes, swapped(cubes, "dom", bit)], 0)
-        masks = masks + [one | bit for one in masks]
         bit //= 2
     cubes_across = swapped(cubes, "dom", 1)
 
+    field = pl.pallas_call(
+        functools.partial(take_kernel, pk),
+        out_shape=padded_type,
+        in_specs=[SMEM, VMEM, VMEM],
+        out_specs=VMEM,
+        compiler_params=params,
+    )(slab_scalar, filt, beside_all)
     table, factor = solver_tables(side, grid_z)
-    dom_scalar = dom_idx.astype(jnp.int32).reshape(1)
     pitch = CORE + 8
     result = pl.pallas_call(
-        functools.partial(second_kernel, pk, masks),
+        functools.partial(second_kernel, pk, dom_count),
         out_shape=jax.ShapeDtypeStruct((half, 1, cells), f32),
-        in_specs=[SMEM, SMEM] + [VMEM] * 8,
+        in_specs=[SMEM] + [VMEM] * 7,
         out_specs=VMEM,
         scratch_shapes=[
             pltpu.VMEM((dom_count, CORE * 8, 128), f32),
@@ -627,13 +658,10 @@
             pltpu.VMEM((pk.blocks, pk.depth * side, lanes), f32),
             pltpu.VMEM((dom_count // 4, pk.depth * side, 128), f32),
             pltpu.VMEM((half * side, 128), f32),
-            pltpu.VMEM((half, cells), f32),
-            pltpu.SMEM((3 * dom_count,), jnp.int32),
-            pltpu.SemaphoreType.DMA,
         ],
         compiler_params=params,
     )(
-        slab_scalar, dom_scalar, offsets.reshape(-1), cubes, cubes_across, filt, beside_all, coef,
+        slab_scalar, code, cubes, cubes_across, field, coef,
         jnp.asarray(table), jnp.asarray(factor),
     )
     return result.reshape(1, 1, half, cells)

time: 32.3 us -> 32 us (level)
  local copies, waits for them, and re-layouts: 0.77 us -> 0.01 us
  waiting for transfers between devices: 10.6 us -> 11.1 us
    unnamed x6 -> x4, local copies, waits for them, and re-layouts: 0.69 us -> 0.01 us
    ppermute x4, waiting for transfers between devices: 5.93 us -> 6.39 us  [swapped(): return lax.ppermute(value, axis, pairs)]
    pallas_call x3 -> x5, Pallas kernels: 7.7 us -> 7.64 us  [the longest x1 4.41 us: local(): pl.pallas_call(functools.partial(second_kernel, pk, dom_count), out_shape...]
  transfers between devices with their start and end apart: 7 -> 7, of which waited for: 7 -> 7; matrix products, arithmetic and copies ran while one was open for 0% -> 0% of each run, Pallas kernels for 4% -> 5%
where the time goes in v8:
time: 32 us; the launch traced here: 31.8 us
  starting transfers between devices  12 us (38%)
  waiting for transfers between devices  11.1 us (35%)
  Pallas kernels  8.56 us (27%)
    ppermute x4, starting transfers between devices, swapped(): return lax.ppermute(value, axis, pairs)  8.34 us
    ppermute x4, waiting for transfers between devices, swapped(): return lax.ppermute(value, axis, pairs)  6.39 us
    ppermute x3, waiting for transfers between devices, crossed(): lax.ppermute(value, both, [(source, source ^ mask) for source in range(co...  4.69 us
    pallas_call x1, Pallas kernels, local(): pl.pallas_call(functools.partial(second_kernel, pk, dom_count), out_shape...  4.41 us
    ppermute x3, starting transfers between devices, crossed(): lax.ppermute(value, both, [(source, source ^ mask) for source in range(co...  3.62 us
    pallas_call x1, Pallas kernels, local(): pl.pallas_call(functools.partial(first_kernel, pk, bands), out_shape=(pad...  1.51 us
    pallas_call x1, Pallas kernels, local(): pl.pallas_call(functools.partial(start_kernel, pk, masks), out_shape=(fie...  1.49 us
    pallas_call x1, Pallas kernels, local(): pl.pallas_call(functools.partial(edge_kernel, pk), out_shape=(in_vmem(DEG...  0.92 us
  transfers between devices with their start and end apart: 7, of which 7 were waited for; matrix products, arithmetic and copies ran while one was open for 0% of the time, Pallas kernels for 5%

profile of v8, /device:TPU:0, one launch (start us, length us, event | category | flops | bytes accessed | tf_op | source)
XLA Modules:
  0.0 31.8 jit_solution(16362507742335126598)
XLA Ops:
  0.0 0.9 %shard_map.55 = (f32[8,1,1600]{2,1,0:T(1,128)S(1)}, f32[20,1,1600]{2,1,0:T(1,128)S(1)}) custom-call(s32[1]{0:T(128)} %bitcast.slab_ref, f32[20,1,1600]{2,1,0:T(1,128)} %bitcast.12), custom_call_target="tpu_custom_call" | custom-call | tf_op jit(solution)/shard_map/pallas_call | solution.py:560
  0.9 3.0 %collective-permute-start = (f32[8,1,1600]{2,1,0:T(1,128)S(1)}, f32[8,1,1600]{2,1,0:T(1,128)S(1)}, u32[]{:S(2)}, u32[]{:S(2)}) collective-permute-start(f32[8,1,1600]{2,1,0:T(1,128)S(1)} %get-tuple-element.15), channel_id=1, source_target_pairs={{0,1},{1,0},{2,3},{3,2},{4,5},{5,4},{6,7},{7,6},{8,9},{9,8},{10,11... | collective-permute-start | bytes 153608 | tf_op jit(solution)/shard_map/ppermute | solution.py:24
  3.9 1.5 %shard_map.56 = (f32[10,40,128]{2,1,0:T(8,128)S(1)}, f32[10,40,128]{2,1,0:T(8,128)S(1)}, f32[8,128]{1,0:T(8,128)S(1)}) custom-call(s32[1]{0:T(128)} %bitcast.slab_ref, s32[1]{0:T(128)} %bitcast.1.dom_ref, f32[20,1,1600]{2,1,0:T(1,128)S(1)} %get-tuple-element.12.psi_ref, f32[40,1600]{1,0:T(8,128)} %bitcast.11, s32[4,3]{1,0:T(4,128)} %offsets_in_ref.1), custom_call_target="tpu_custom_call" | custom-call | tf_op jit(solution)/shard_map/pallas_call | solution.py:575
  5.4 0.6 %collective-permute-done.halo_ref = f32[8,1,1600]{2,1,0:T(1,128)S(1)} collective-permute-done((f32[8,1,1600]{2,1,0:T(1,128)S(1)}, f32[8,1,1600]{2,1,0:T(1,128)S(1)}, u32[]{:S(2)}, u32[]{:S(2)}) %collective-permute-start) | collective-permute-done | bytes 51232 | tf_op jit(solution)/shard_map/ppermute | solution.py:24
  6.0 1.5 %shard_map.57 = (f32[10,56,128]{2,1,0:T(8,128)S(1)}, f32[128,128]{1,0:T(8,128)S(1)}) custom-call(s32[1]{0:T(128)} %bitcast.slab_ref, f32[10,40,128]{2,1,0:T(8,128)S(1)} %get-tuple-element.14.start_ref, f32[8,1,1600]{2,1,0:T(1,128)S(1)} %collective-permute-done.halo_ref, f32[10,40,128]{2,1,0:T(8,128)S(1)} %get-tuple-element.16.coef_ref.start_coef_ref), custom_call_target="tpu_custom_call" | custom-call | tf_op jit(solution)/shard_map/pallas_call | solution.py:591
  7.6 2.2 %collective-permute-start.1 = (f32[128,128]{1,0:T(8,128)S(1)}, f32[128,128]{1,0:T(8,128)S(1)}, u32[]{:S(2)}, u32[]{:S(2)}) collective-permute-start(f32[128,128]{1,0:T(8,128)S(1)} %get-tuple-element.17), channel_id=1, source_target_pairs={{0,2},{1,3},{2,0},{3,1},{4,6},{5,7},{6,4},{7,5},{8,10},{9,11},{10,... | collective-permute-start | bytes 196616 | tf_op jit(solution)/shard_map/ppermute | solution.py:24
  9.7 2.2 %collective-permute-done.1 = f32[128,128]{1,0:T(8,128)S(1)} collective-permute-done((f32[128,128]{1,0:T(8,128)S(1)}, f32[128,128]{1,0:T(8,128)S(1)}, u32[]{:S(2)}, u32[]{:S(2)}) %collective-permute-start.1) | collective-permute-done | bytes 65568 | tf_op jit(solution)/shard_map/ppermute | solution.py:24
  12.0 3.1 %collective-permute-start.2 = (f32[128,128]{1,0:T(8,128)S(1)}, f32[128,128]{1,0:T(8,128)S(1)}, u32[]{:S(2)}, u32[]{:S(2)}) collective-permute-start(f32[128,128]{1,0:T(8,128)S(1)} %add.11), channel_id=1, source_target_pairs={{0,4},{1,5},{2,6},{3,7},{4,0},{5,1},{6,2},{7,3},{8,12},{9,13},{10,... | collective-permute-start | bytes 196616 | tf_op jit(solution)/shard_map/ppermute | solution.py:24
  15.1 0.1 shard_map.58
  15.2 2.1 %collective-permute-done.2 = f32[128,128]{1,0:T(8,128)S(1)} collective-permute-done((f32[128,128]{1,0:T(8,128)S(1)}, f32[128,128]{1,0:T(8,128)S(1)}, u32[]{:S(2)}, u32[]{:S(2)}) %collective-permute-start.2) | collective-permute-done | bytes 65568 | tf_op jit(solution)/shard_map/ppermute | solution.py:24
  17.3 1.9 %collective-permute-start.4 = (f32[128,128]{1,0:T(8,128)S(1)}, f32[128,128]{1,0:T(8,128)S(1)}, u32[]{:S(2)}, u32[]{:S(2)}) collective-permute-start(f32[128,128]{1,0:T(8,128)S(1)} %add.12), channel_id=1, source_target_pairs={{0,16},{1,17},{2,18},{3,19},{4,20},{5,21},{6,22},{7,23},{8,24},{9,... | collective-permute-start | bytes 196616 | tf_op jit(solution)/shard_map/ppermute | solution.py:617
  19.3 1.4 %collective-permute-start.5 = (f32[128,128]{1,0:T(8,128)S(1)}, f32[128,128]{1,0:T(8,128)S(1)}, u32[]{:S(2)}, u32[]{:S(2)}) collective-permute-start(f32[128,128]{1,0:T(8,128)S(1)} %add.12), channel_id=1, source_target_pairs={{0,17},{1,16},{2,19},{3,18},{4,21},{5,20},{6,23},{7,22},{8,25},{9,... | collective-permute-start | bytes 196616 | tf_op jit(solution)/shard_map/ppermute | solution.py:617
  20.7 0.3 collective-permute-start.3
  21.0 0.7 %collective-permute-done.4 = f32[128,128]{1,0:T(8,128)S(1)} collective-permute-done((f32[128,128]{1,0:T(8,128)S(1)}, f32[128,128]{1,0:T(8,128)S(1)}, u32[]{:S(2)}, u32[]{:S(2)}) %collective-permute-start.4) | collective-permute-done | bytes 65568 | tf_op jit(solution)/shard_map/ppermute | solution.py:617
  21.7 2.7 %collective-permute-done.5 = f32[128,128]{1,0:T(8,128)S(1)} collective-permute-done((f32[128,128]{1,0:T(8,128)S(1)}, f32[128,128]{1,0:T(8,128)S(1)}, u32[]{:S(2)}, u32[]{:S(2)}) %collective-permute-start.5) | collective-permute-done | bytes 65568 | tf_op jit(solution)/shard_map/ppermute | solution.py:617
  24.5 1.2 %collective-permute-done.3.beside_ref = f32[248,128]{1,0:T(8,128)S(1)} collective-permute-done((f32[248,128]{1,0:T(8,128)S(1)}, f32[248,128]{1,0:T(8,128)S(1)}, u32[]{:S(2)}, u32[]{:S(2)}) %collective-permute-start.3) | collective-permute-done | bytes 127008 | tf_op jit(solution)/shard_map/ppermute | solution.py:617
  25.7 0.0 copy-start
  25.7 0.0 copy-start.1
  25.8 0.1 collective-permute-start.6
  25.9 0.1 shard_map.59.field_ref
  26.0 1.4 %collective-permute-done.6.across_ref = f32[2,256,128]{2,1,0:T(8,128)S(1)} collective-permute-done((f32[2,256,128]{2,1,0:T(8,128)S(1)}, f32[2,256,128]{2,1,0:T(8,128)S(1)}, u32[]{:S(2)}, u32[]{:S(2)}) %collective-permute-start.6) | collective-permute-done | bytes 262176 | tf_op jit(solution)/shard_map/ppermute | solution.py:24
  27.4 0.0 copy-done
  27.4 0.0 copy-done.1
  27.4 4.4 %shard_map.60 = f32[20,1,1600]{2,1,0:T(1,128)} custom-call(s32[1]{0:T(128)} %bitcast.slab_ref, f32[8,128]{1,0:T(8,128)S(1)} %get-tuple-element.13.code_ref, f32[2,256,128]{2,1,0:T(8,128)S(1)} %pad_maximum_fusion.near_ref, f32[2,256,128]{2,1,0:T(8,128)S(1)} %collective-permute-done.6.across_ref, f32[10,56,128]{2,1,0:T(8,128)S(1)} %shard_map.59.field_ref, ...), custom_call_target="tpu_custom_call" | custom-call | tf_op jit(solution)/shard_map/pallas_call | solution.py:644
  (8 shorter events, 0.1 us)
Async XLA Ops:
  0.9 5.1 %collective-permute-start = (f32[8,1,1600]{2,1,0:T(1,128)S(1)}, f32[8,1,1600]{2,1,0:T(1,128)S(1)}, u32[]{:S(2)}, u32[]{:S(2)}) collective-permute-start(f32[8,1,1600]{2,1,0:T(1,128)S(1)} %get-tuple-element.15), channel_id=1, source_target_pairs={{0,1},{1,0},{2,3},{3,2},{4,5},{5,4},{6,7},{7,6},{8,9},{9,8},{10,11... | collective-permute-start | bytes 153608 | tf_op jit(solution)/shard_map/ppermute | solution.py:24
  7.6 4.4 %collective-permute-start.1 = (f32[128,128]{1,0:T(8,128)S(1)}, f32[128,128]{1,0:T(8,128)S(1)}, u32[]{:S(2)}, u32[]{:S(2)}) collective-permute-start(f32[128,128]{1,0:T(8,128)S(1)} %get-tuple-element.17), channel_id=1, source_target_pairs={{0,2},{1,3},{2,0},{3,1},{4,6},{5,7},{6,4},{7,5},{8,10},{9,11},{10,... | collective-permute-start | bytes 196616 | tf_op jit(solution)/shard_map/ppermute | solution.py:24
  12.0 5.3 %collective-permute-start.2 = (f32[128,128]{1,0:T(8,128)S(1)}, f32[128,128]{1,0:T(8,128)S(1)}, u32[]{:S(2)}, u32[]{:S(2)}) collective-permute-start(f32[128,128]{1,0:T(8,128)S(1)} %add.11), channel_id=1, source_target_pairs={{0,4},{1,5},{2,6},{3,7},{4,0},{5,1},{6,2},{7,3},{8,12},{9,13},{10,... | collective-permute-start | bytes 196616 | tf_op jit(solution)/shard_map/ppermute | solution.py:24
  17.3 4.3 %collective-permute-start.4 = (f32[128,128]{1,0:T(8,128)S(1)}, f32[128,128]{1,0:T(8,128)S(1)}, u32[]{:S(2)}, u32[]{:S(2)}) collective-permute-start(f32[128,128]{1,0:T(8,128)S(1)} %add.12), channel_id=1, source_target_pairs={{0,16},{1,17},{2,18},{3,19},{4,20},{5,21},{6,22},{7,23},{8,24},{9,... | collective-permute-start | bytes 196616 | tf_op jit(solution)/shard_map/ppermute | solution.py:617
  19.3 5.2 %collective-permute-start.5 = (f32[128,128]{1,0:T(8,128)S(1)}, f32[128,128]{1,0:T(8,128)S(1)}, u32[]{:S(2)}, u32[]{:S(2)}) collective-permute-start(f32[128,128]{1,0:T(8,128)S(1)} %add.12), channel_id=1, source_target_pairs={{0,17},{1,16},{2,19},{3,18},{4,21},{5,20},{6,23},{7,22},{8,25},{9,... | collective-permute-start | bytes 196616 | tf_op jit(solution)/shard_map/ppermute | solution.py:617
  20.7 5.0 %collective-permute-start.3 = (f32[248,128]{1,0:T(8,128)S(1)}, f32[248,128]{1,0:T(8,128)S(1)}, u32[]{:S(2)}, u32[]{:S(2)}) collective-permute-start(f32[248,128]{1,0:T(8,128)S(1)} %pad_maximum_fusion.1), channel_id=1, source_target_pairs={{0,1},{1,0},{2,3},{3,2},{4,5},{5,4},{6,7},{7,6},{8,9},{9,8},{10,11... | collective-permute-start | bytes 380936 | tf_op jit(solution)/shard_map/ppermute | solution.py:617
  25.7 1.7 %copy-start = (bf16[768,512]{1,0:T(8,128)(2,1)S(1)}, bf16[768,512]{1,0:T(8,128)(2,1)}, u32[]{:S(2)}) copy-start(bf16[768,512]{1,0:T(8,128)(2,1)} %constant.26.clone.table_ref) | copy-start | bytes 2359300
  25.7 1.6 %copy-start.1 = (f32[1024,128]{1,0:T(8,128)S(1)}, f32[1024,128]{1,0:T(8,128)}, u32[]{:S(2)}) copy-start(f32[1024,128]{1,0:T(8,128)} %constant.27.clone.factor_ref) | copy-start | bytes 1572868
  25.8 1.6 %collective-permute-start.6 = (f32[2,256,128]{2,1,0:T(8,128)S(1)}, f32[2,256,128]{2,1,0:T(8,128)S(1)}, u32[]{:S(2)}, u32[]{:S(2)}) collective-permute-start(f32[2,256,128]{2,1,0:T(8,128)S(1)} %pad_maximum_fusion.near_ref), channel_id=1, source_target_pairs={{0,8},{8,0},{16,24},{24,16},{1,9},{9,1},{17,25},{25,17},{2,10},{10... | collective-permute-start | bytes 786440 | tf_op jit(solution)/shard_map/ppermute | solution.py:24

commit v9 on v8

--- a/solution.py
+++ b/solution.py
@@ -93,19 +93,20 @@
         field_ref[level] = total
 
 
-def edge_kernel(pk, slab_ref, psi_ref, edge_ref, own_ref, sem):
-    copy = pltpu.make_async_copy(psi_ref, own_ref, sem)
+def edge_kernel(pk, slab_ref, psi_ref, edge_ref, sem):
+    first = jnp.where(slab_ref[0] == 0, pk.half - DEG, 0)
+    copy = pltpu.make_async_copy(psi_ref.at[pl.ds(first, DEG)], edge_ref, sem)
     copy.start()
-    first = jnp.where(slab_ref[0] == 0, pk.half - DEG, 0)
     copy.wait()
-    edge_ref[...] = own_ref[pl.ds(first, DEG)]
 
 
 def start_kernel(
-    pk, masks, slab_ref, dom_ref, psi_ref, pot_in_ref, offsets_in_ref,
-    field_ref, coef_ref, code_ref, flat_ref, pitched_ref, pot_ref, offsets_ref, sems,
+    pk, masks, slab_ref, dom_ref, psi_in_ref, pot_in_ref, offsets_in_ref,
+    field_ref, coef_ref, code_ref, flat_ref, pitched_ref, psi_ref, pot_ref, offsets_ref, sems,
 ):
+    psi_copy = pltpu.make_async_copy(psi_in_ref, psi_ref, sems.at[2])
     copy = pltpu.make_async_copy(pot_in_ref, pot_ref, sems.at[0])
+    psi_copy.start()
     offsets_copy = pltpu.make_async_copy(offsets_in_ref, offsets_ref, sems.at[1])
     copy.start()
     offsets_copy.start()
@@ -114,6 +115,7 @@
     is_lower = slab_ref[0] == 0
     flat_ref[...] = jnp.zeros(flat_ref.shape, jnp.float32)
     pitched_ref[...] = jnp.zeros(pitched_ref.shape, jnp.float32)
+    psi_copy.wait()
     own = psi_ref[:, 0, :]
 
     @pl.when(is_lower)
@@ -202,22 +204,27 @@
     clear_margins(pk, one_ref)
     clear_margins(pk, filt_ref)
     field_ref[:, 8 : 8 + side, :] = start_ref[...]
-    halo = halo_ref[:, 0, :]
-    lines_ref[...] = jnp.zeros(lines_ref.shape, jnp.float32)
+    low_block, low_level = pk.where(pk.half)
+    high_block, high_level = pk.where(0)
+    shift = jnp.where(is_lower, low_block * span, high_block * span)
+    past = lanes_of((DEG, 128)) - shift
+    is_line = (past >= 0) & (past < side)
+    cells = side * side
+    tiles = []
+    for tile in range(-(-cells // 128)):
+        width = min(128, cells - tile * 128)
+        part = halo_ref[:, 0, tile * 128 : tile * 128 + width]
+        tiles.append(part if width == 128 else jnp.concatenate([part, jnp.zeros((DEG, 128 - width), jnp.float32)], 1))
     for y in range(side):
-        lines_ref[y * DEG : (y + 1) * DEG, 0:side] = halo[:, y * side : (y + 1) * side]
+        tile, start = y * side // 128, y * side % 128
+        line = pltpu.roll(tiles[tile], shift + (128 - start), 1)
+        if start + side > 128:
+            line = jnp.where(past < 128 - start, line, pltpu.roll(tiles[tile + 1], shift + (128 - start), 1))
+        lines_ref[y * DEG : (y + 1) * DEG, :] = jnp.where(is_line, line, 0.0)
     for row in range(DEG):
+        level = jnp.where(is_lower, low_level, high_level) + row
         line = lines_ref[pl.ds(row, side, stride=DEG), :]
-        low_block, low_level = pk.where(pk.half + row)
-        high_block, high_level = pk.where(row)
-        if low_level == high_level:
-            line = jnp.where(is_lower, roll(line, low_block * span), roll(line, high_block * span))
-            field_ref[low_level, 8 : 8 + side, :] = field_ref[low_level, 8 : 8 + side, :] + line
-        else:
-            low_line = jnp.where(is_lower, roll(line, low_block * span), 0.0)
-            high_line = jnp.where(is_lower, 0.0, roll(line, high_block * span))
-            field_ref[low_level, 8 : 8 + side, :] = field_ref[low_level, 8 : 8 + side, :] + low_line
-            field_ref[high_level, 8 : 8 + side, :] = field_ref[high_level, 8 : 8 + side, :] + high_line
+        field_ref[level, 8 : 8 + side, :] = field_ref[level, 8 : 8 + side, :] + line
 
     filtered_field(pk, field_ref, one_ref, filt_ref, coef_ref)
     result_ref = filt_ref
@@ -557,14 +564,15 @@
     padded_field = pltpu.VMEM(pk.padded_shape, f32)
 
     rows = psi_in.reshape(half, 1, cells)
-    edge, rows = pl.pallas_call(
+    rows = in_hbm(rows)
+    edge = pl.pallas_call(
         functools.partial(edge_kernel, pk),
-        out_shape=(in_vmem(DEG, 1, cells), in_vmem(half, 1, cells)),
+        out_shape=in_vmem(DEG, 1, cells),
         in_specs=[SMEM, HBM],
-        out_specs=(VMEM, VMEM),
+        out_specs=VMEM,
         scratch_shapes=[pltpu.SemaphoreType.DMA],
         compiler_params=params,
-    )(slab_scalar, in_hbm(rows))
+    )(slab_scalar, rows)
     halo = swapped(edge, "band", 1)
     masks = [0]
     bit = dom_count // 2
@@ -575,14 +583,15 @@
     start, coef, code = pl.pallas_call(
         functools.partial(start_kernel, pk, masks),
         out_shape=(field_type, field_type, in_vmem(8, 128)),
-        in_specs=[SMEM, SMEM, VMEM, HBM, HBM],
+        in_specs=[SMEM, SMEM, HBM, HBM, HBM],
         out_specs=(VMEM, VMEM, VMEM),
         scratch_shapes=[
             pltpu.VMEM((pk.rows, cells), f32),
             pltpu.VMEM((side * pk.pitch, 128), f32),
+            pltpu.VMEM((half, 1, cells), f32),
             pltpu.VMEM((side, cells), f32),
             pltpu.SMEM((dom_count, 3), jnp.int32),
-            pltpu.SemaphoreType.DMA((2,)),
+            pltpu.SemaphoreType.DMA((3,)),
         ],
         compiler_params=params,
     )(slab_scalar, dom_scalar, rows, in_hbm(v_in[0]), in_hbm(offsets))

time: 32 us -> 31.8 us (level)
  waiting for transfers between devices: 11.1 us -> 10.6 us
    ppermute x4, waiting for transfers between devices: 6.39 us -> 5.96 us  [swapped(): return lax.ppermute(value, axis, pairs)]
    pallas_call x1, Pallas kernels: 1.49 us -> 1.92 us  [local(): pl.pallas_call(functools.partial(start_kernel, pk, masks), out_shape=(fie...]
  transfers between devices with their start and end apart: 7 -> 7, of which waited for: 7 -> 7; matrix products, arithmetic and copies ran while one was open for 0% -> 0% of each run, Pallas kernels for 5% -> 7%
where the time goes in v9:
time: 31.8 us; the launch traced here: 31.6 us
  starting transfers between devices  12 us (38%)
  waiting for transfers between devices  10.6 us (33%)
  Pallas kernels  8.77 us (28%)
    ppermute x4, starting transfers between devices, swapped(): return lax.ppermute(value, axis, pairs)  8.34 us
    ppermute x4, waiting for transfers between devices, swapped(): return lax.ppermute(value, axis, pairs)  5.96 us
    ppermute x3, waiting for transfers between devices, crossed(): lax.ppermute(value, both, [(source, source ^ mask) for source in range(co...  4.69 us
    pallas_call x1, Pallas kernels, local(): pl.pallas_call(functools.partial(second_kernel, pk, dom_count), out_shape...  4.41 us
    ppermute x3, starting transfers between devices, crossed(): lax.ppermute(value, both, [(source, source ^ mask) for source in range(co...  3.62 us
    pallas_call x1, Pallas kernels, local(): pl.pallas_call(functools.partial(start_kernel, pk, masks), out_shape=(fie...  1.92 us
    pallas_call x1, Pallas kernels, local(): pl.pallas_call(functools.partial(first_kernel, pk, bands), out_shape=(pad...  1.4 us
    pallas_call x1, Pallas kernels, local(): pl.pallas_call(functools.partial(edge_kernel, pk), out_shape=in_vmem(DEG,...  0.82 us
  transfers between devices with their start and end apart: 7, of which 7 were waited for; matrix products, arithmetic and copies ran while one was open for 0% of the time, Pallas kernels for 7%

profile of v9, /device:TPU:0, one launch (start us, length us, event | category | flops | bytes accessed | tf_op | source)
XLA Modules:
  0.0 31.6 jit_solution(13399035745262951399)
XLA Ops:
  0.0 0.8 %shard_map.56 = f32[8,1,1600]{2,1,0:T(1,128)S(1)} custom-call(s32[1]{0:T(128)} %bitcast.slab_ref, f32[20,1,1600]{2,1,0:T(1,128)} %bitcast.11), custom_call_target="tpu_custom_call" | custom-call | tf_op jit(solution)/shard_map/pallas_call | solution.py:568
  0.8 3.0 %collective-permute-start = (f32[8,1,1600]{2,1,0:T(1,128)S(1)}, f32[8,1,1600]{2,1,0:T(1,128)S(1)}, u32[]{:S(2)}, u32[]{:S(2)}) collective-permute-start(f32[8,1,1600]{2,1,0:T(1,128)S(1)} %shard_map.56), channel_id=1, source_target_pairs={{0,1},{1,0},{2,3},{3,2},{4,5},{5,4},{6,7},{7,6},{8,9},{9,8},{10,11... | collective-permute-start | bytes 153608 | tf_op jit(solution)/shard_map/ppermute | solution.py:24
  3.8 1.9 %shard_map.55 = (f32[10,40,128]{2,1,0:T(8,128)S(1)}, f32[10,40,128]{2,1,0:T(8,128)S(1)}, f32[8,128]{1,0:T(8,128)S(1)}) custom-call(s32[1]{0:T(128)} %bitcast.slab_ref, s32[1]{0:T(128)} %bitcast.1.dom_ref, f32[20,1,1600]{2,1,0:T(1,128)} %bitcast.12, f32[40,1600]{1,0:T(8,128)} %bitcast.13, s32[4,3]{1,0:T(4,128)} %offsets_in_ref.1), custom_call_target="tpu_custom_call" | custom-call | tf_op jit(solution)/shard_map/pallas_call | solution.py:583
  5.8 0.2 collective-permute-done.halo_ref
  5.9 1.4 %shard_map.57 = (f32[10,56,128]{2,1,0:T(8,128)S(1)}, f32[128,128]{1,0:T(8,128)S(1)}) custom-call(s32[1]{0:T(128)} %bitcast.slab_ref, f32[10,40,128]{2,1,0:T(8,128)S(1)} %get-tuple-element.11.start_ref, f32[8,1,1600]{2,1,0:T(1,128)S(1)} %collective-permute-done.halo_ref, f32[10,40,128]{2,1,0:T(8,128)S(1)} %get-tuple-element.12.coef_ref.start_coef_ref), custom_call_target="tpu_custom_call" | custom-call | tf_op jit(solution)/shard_map/pallas_call | solution.py:600
  7.3 2.2 %collective-permute-start.1 = (f32[128,128]{1,0:T(8,128)S(1)}, f32[128,128]{1,0:T(8,128)S(1)}, u32[]{:S(2)}, u32[]{:S(2)}) collective-permute-start(f32[128,128]{1,0:T(8,128)S(1)} %get-tuple-element.13), channel_id=1, source_target_pairs={{0,2},{1,3},{2,0},{3,1},{4,6},{5,7},{6,4},{7,5},{8,10},{9,11},{10,... | collective-permute-start | bytes 196616 | tf_op jit(solution)/shard_map/ppermute | solution.py:24
  9.5 2.2 %collective-permute-done.1 = f32[128,128]{1,0:T(8,128)S(1)} collective-permute-done((f32[128,128]{1,0:T(8,128)S(1)}, f32[128,128]{1,0:T(8,128)S(1)}, u32[]{:S(2)}, u32[]{:S(2)}) %collective-permute-start.1) | collective-permute-done | bytes 65568 | tf_op jit(solution)/shard_map/ppermute | solution.py:24
  11.8 3.1 %collective-permute-start.2 = (f32[128,128]{1,0:T(8,128)S(1)}, f32[128,128]{1,0:T(8,128)S(1)}, u32[]{:S(2)}, u32[]{:S(2)}) collective-permute-start(f32[128,128]{1,0:T(8,128)S(1)} %add.11), channel_id=1, source_target_pairs={{0,4},{1,5},{2,6},{3,7},{4,0},{5,1},{6,2},{7,3},{8,12},{9,13},{10,... | collective-permute-start | bytes 196616 | tf_op jit(solution)/shard_map/ppermute | solution.py:24
  14.9 0.1 shard_map.58
  15.0 2.1 %collective-permute-done.2 = f32[128,128]{1,0:T(8,128)S(1)} collective-permute-done((f32[128,128]{1,0:T(8,128)S(1)}, f32[128,128]{1,0:T(8,128)S(1)}, u32[]{:S(2)}, u32[]{:S(2)}) %collective-permute-start.2) | collective-permute-done | bytes 65568 | tf_op jit(solution)/shard_map/ppermute | solution.py:24
  17.1 1.9 %collective-permute-start.4 = (f32[128,128]{1,0:T(8,128)S(1)}, f32[128,128]{1,0:T(8,128)S(1)}, u32[]{:S(2)}, u32[]{:S(2)}) collective-permute-start(f32[128,128]{1,0:T(8,128)S(1)} %add.12), channel_id=1, source_target_pairs={{0,16},{1,17},{2,18},{3,19},{4,20},{5,21},{6,22},{7,23},{8,24},{9,... | collective-permute-start | bytes 196616 | tf_op jit(solution)/shard_map/ppermute | solution.py:626
  19.1 1.4 %collective-permute-start.5 = (f32[128,128]{1,0:T(8,128)S(1)}, f32[128,128]{1,0:T(8,128)S(1)}, u32[]{:S(2)}, u32[]{:S(2)}) collective-permute-start(f32[128,128]{1,0:T(8,128)S(1)} %add.12), channel_id=1, source_target_pairs={{0,17},{1,16},{2,19},{3,18},{4,21},{5,20},{6,23},{7,22},{8,25},{9,... | collective-permute-start | bytes 196616 | tf_op jit(solution)/shard_map/ppermute | solution.py:626
  20.5 0.3 collective-permute-start.3
  20.8 0.7 %collective-permute-done.4 = f32[128,128]{1,0:T(8,128)S(1)} collective-permute-done((f32[128,128]{1,0:T(8,128)S(1)}, f32[128,128]{1,0:T(8,128)S(1)}, u32[]{:S(2)}, u32[]{:S(2)}) %collective-permute-start.4) | collective-permute-done | bytes 65568 | tf_op jit(solution)/shard_map/ppermute | solution.py:626
  21.5 2.7 %collective-permute-done.5 = f32[128,128]{1,0:T(8,128)S(1)} collective-permute-done((f32[128,128]{1,0:T(8,128)S(1)}, f32[128,128]{1,0:T(8,128)S(1)}, u32[]{:S(2)}, u32[]{:S(2)}) %collective-permute-start.5) | collective-permute-done | bytes 65568 | tf_op jit(solution)/shard_map/ppermute | solution.py:626
  24.3 1.2 %collective-permute-done.3.beside_ref = f32[248,128]{1,0:T(8,128)S(1)} collective-permute-done((f32[248,128]{1,0:T(8,128)S(1)}, f32[248,128]{1,0:T(8,128)S(1)}, u32[]{:S(2)}, u32[]{:S(2)}) %collective-permute-start.3) | collective-permute-done | bytes 127008 | tf_op jit(solution)/shard_map/ppermute | solution.py:626
  25.5 0.0 copy-start
  25.5 0.0 copy-start.1
  25.6 0.1 collective-permute-start.6
  25.7 0.1 shard_map.59.field_ref
  25.8 1.4 %collective-permute-done.6.across_ref = f32[2,256,128]{2,1,0:T(8,128)S(1)} collective-permute-done((f32[2,256,128]{2,1,0:T(8,128)S(1)}, f32[2,256,128]{2,1,0:T(8,128)S(1)}, u32[]{:S(2)}, u32[]{:S(2)}) %collective-permute-start.6) | collective-permute-done | bytes 262176 | tf_op jit(solution)/shard_map/ppermute | solution.py:24
  27.2 0.0 copy-done
  27.2 0.0 copy-done.1
  27.2 4.4 %shard_map.60 = f32[20,1,1600]{2,1,0:T(1,128)} custom-call(s32[1]{0:T(128)} %bitcast.slab_ref, f32[8,128]{1,0:T(8,128)S(1)} %get-tuple-element.10.code_ref, f32[2,256,128]{2,1,0:T(8,128)S(1)} %pad_maximum_fusion.near_ref, f32[2,256,128]{2,1,0:T(8,128)S(1)} %collective-permute-done.6.across_ref, f32[10,56,128]{2,1,0:T(8,128)S(1)} %shard_map.59.field_ref, ...), custom_call_target="tpu_custom_call" | custom-call | tf_op jit(solution)/shard_map/pallas_call | solution.py:653
  (8 shorter events, 0.1 us)
Async XLA Ops:
  0.8 5.1 %collective-permute-start = (f32[8,1,1600]{2,1,0:T(1,128)S(1)}, f32[8,1,1600]{2,1,0:T(1,128)S(1)}, u32[]{:S(2)}, u32[]{:S(2)}) collective-permute-start(f32[8,1,1600]{2,1,0:T(1,128)S(1)} %shard_map.56), channel_id=1, source_target_pairs={{0,1},{1,0},{2,3},{3,2},{4,5},{5,4},{6,7},{7,6},{8,9},{9,8},{10,11... | collective-permute-start | bytes 153608 | tf_op jit(solution)/shard_map/ppermute | solution.py:24
  7.3 4.4 %collective-permute-start.1 = (f32[128,128]{1,0:T(8,128)S(1)}, f32[128,128]{1,0:T(8,128)S(1)}, u32[]{:S(2)}, u32[]{:S(2)}) collective-permute-start(f32[128,128]{1,0:T(8,128)S(1)} %get-tuple-element.13), channel_id=1, source_target_pairs={{0,2},{1,3},{2,0},{3,1},{4,6},{5,7},{6,4},{7,5},{8,10},{9,11},{10,... | collective-permute-start | bytes 196616 | tf_op jit(solution)/shard_map/ppermute | solution.py:24
  11.8 5.3 %collective-permute-start.2 = (f32[128,128]{1,0:T(8,128)S(1)}, f32[128,128]{1,0:T(8,128)S(1)}, u32[]{:S(2)}, u32[]{:S(2)}) collective-permute-start(f32[128,128]{1,0:T(8,128)S(1)} %add.11), channel_id=1, source_target_pairs={{0,4},{1,5},{2,6},{3,7},{4,0},{5,1},{6,2},{7,3},{8,12},{9,13},{10,... | collective-permute-start | bytes 196616 | tf_op jit(solution)/shard_map/ppermute | solution.py:24
  17.1 4.3 %collective-permute-start.4 = (f32[128,128]{1,0:T(8,128)S(1)}, f32[128,128]{1,0:T(8,128)S(1)}, u32[]{:S(2)}, u32[]{:S(2)}) collective-permute-start(f32[128,128]{1,0:T(8,128)S(1)} %add.12), channel_id=1, source_target_pairs={{0,16},{1,17},{2,18},{3,19},{4,20},{5,21},{6,22},{7,23},{8,24},{9,... | collective-permute-start | bytes 196616 | tf_op jit(solution)/shard_map/ppermute | solution.py:626
  19.1 5.2 %collective-permute-start.5 = (f32[128,128]{1,0:T(8,128)S(1)}, f32[128,128]{1,0:T(8,128)S(1)}, u32[]{:S(2)}, u32[]{:S(2)}) collective-permute-start(f32[128,128]{1,0:T(8,128)S(1)} %add.12), channel_id=1, source_target_pairs={{0,17},{1,16},{2,19},{3,18},{4,21},{5,20},{6,23},{7,22},{8,25},{9,... | collective-permute-start | bytes 196616 | tf_op jit(solution)/shard_map/ppermute | solution.py:626
  20.5 5.0 %collective-permute-start.3 = (f32[248,128]{1,0:T(8,128)S(1)}, f32[248,128]{1,0:T(8,128)S(1)}, u32[]{:S(2)}, u32[]{:S(2)}) collective-permute-start(f32[248,128]{1,0:T(8,128)S(1)} %pad_maximum_fusion.1), channel_id=1, source_target_pairs={{0,1},{1,0},{2,3},{3,2},{4,5},{5,4},{6,7},{7,6},{8,9},{9,8},{10,11... | collective-permute-start | bytes 380936 | tf_op jit(solution)/shard_map/ppermute | solution.py:626
  25.5 1.7 %copy-start = (bf16[768,512]{1,0:T(8,128)(2,1)S(1)}, bf16[768,512]{1,0:T(8,128)(2,1)}, u32[]{:S(2)}) copy-start(bf16[768,512]{1,0:T(8,128)(2,1)} %constant.26.clone.table_ref) | copy-start | bytes 2359300
  25.5 1.6 %copy-start.1 = (f32[1024,128]{1,0:T(8,128)S(1)}, f32[1024,128]{1,0:T(8,128)}, u32[]{:S(2)}) copy-start(f32[1024,128]{1,0:T(8,128)} %constant.27.clone.factor_ref) | copy-start | bytes 1572868
  25.6 1.6 %collective-permute-start.6 = (f32[2,256,128]{2,1,0:T(8,128)S(1)}, f32[2,256,128]{2,1,0:T(8,128)S(1)}, u32[]{:S(2)}, u32[]{:S(2)}) collective-permute-start(f32[2,256,128]{2,1,0:T(8,128)S(1)} %pad_maximum_fusion.near_ref), channel_id=1, source_target_pairs={{0,8},{8,0},{16,24},{24,16},{1,9},{9,1},{17,25},{25,17},{2,10},{10... | collective-permute-start | bytes 786440 | tf_op jit(solution)/shard_map/ppermute | solution.py:24

commit v10 on v9

--- a/solution.py
+++ b/solution.py
@@ -256,7 +256,8 @@
         edge_ref[group * side : (group + 1) * side] = total
 
 
-def take_kernel(pk, slab_ref, filt_ref, beside_ref, field_ref):
+def take_kernel(pk, slab_ref, filt_ref, beside_ref, near_ref, field_ref, mean_ref):
+    mean_ref[...] = jnp.full(mean_ref.shape, jnp.mean(near_ref[...]))
     side, span, half = pk.side, pk.span, pk.half
     is_lower = slab_ref[0] == 0
     field_ref[...] = filt_ref[...]
@@ -360,7 +361,7 @@
 
 
 def second_kernel(
-    pk, dom_count, slab_ref, code_ref, near_ref, across_ref, field_ref, start_coef_ref,
+    pk, dom_count, slab_ref, code_ref, mean_ref, near_ref, across_ref, field_ref, start_coef_ref,
     table_ref, factor_ref,
     out_ref, cubes_ref, one_ref, two_ref, coef_ref, left_ref, rows_ref, waves_ref, mixed_ref, flat_ref,
     near_dens_ref, own_ref,
@@ -377,8 +378,7 @@
 
     cubes_ref[0 : dom_count // 2] = near_ref[...]
     cubes_ref[dom_count // 2 : dom_count] = across_ref[...]
-    mean = jnp.sum(cubes_ref[...]) * (1.0 / (dom_count * CORE * CORE * CORE))
-
+    mean = 4.0 * jnp.concatenate([mean_ref[...]] * CORE, 0)
     code = jnp.max(code_ref[...]).astype(jnp.int32)
     cube_at = [code // dom_count**where % dom_count for where in range(dom_count)]
 
@@ -386,7 +386,7 @@
         near, at_x, at_y, at_xy = [cubes_ref[cube_at[at_z * 4 + place]] for place in range(4)]
         sums, others = near + at_x, at_y + at_xy
         diffs, other_diffs = near - at_x, at_y - at_xy
-        parities = (sums + others - 4.0 * mean, sums - others, diffs + other_diffs, diffs - other_diffs)
+        parities = (sums + others - mean, sums - others, diffs + other_diffs, diffs - other_diffs)
         for parity, value in enumerate(parities):
             high, low = split2(value)
             for idx, piece in enumerate((high, low, high)):
@@ -641,19 +641,19 @@
         bit //= 2
     cubes_across = swapped(cubes, "dom", 1)
 
-    field = pl.pallas_call(
+    field, mean = pl.pallas_call(
         functools.partial(take_kernel, pk),
-        out_shape=padded_type,
-        in_specs=[SMEM, VMEM, VMEM],
-        out_specs=VMEM,
+        out_shape=(padded_type, in_vmem(8, 128)),
+        in_specs=[SMEM, VMEM, VMEM, VMEM],
+        out_specs=(VMEM, VMEM),
         compiler_params=params,
-    )(slab_scalar, filt, beside_all)
+    )(slab_scalar, filt, beside_all, cubes)
     table, factor = solver_tables(side, grid_z)
     pitch = CORE + 8
     result = pl.pallas_call(
         functools.partial(second_kernel, pk, dom_count),
         out_shape=jax.ShapeDtypeStruct((half, 1, cells), f32),
-        in_specs=[SMEM] + [VMEM] * 7,
+        in_specs=[SMEM] + [VMEM] * 8,
         out_specs=VMEM,
         scratch_shapes=[
             pltpu.VMEM((dom_count, CORE * 8, 128), f32),
@@ -670,7 +670,7 @@
         ],
         compiler_params=params,
     )(
-        slab_scalar, code, cubes, cubes_across, field, coef,
+        slab_scalar, code, mean, cubes, cubes_across, field, coef,
         jnp.asarray(table), jnp.asarray(factor),
     )
     return result.reshape(1, 1, half, cells)

time: 31.8 us -> 31.6 us (level)
  no operation moved by 1% of the time
where the time goes in v10:
time: 31.6 us; the launch traced here: 31.4 us
  starting transfers between devices  12 us (38%)
  waiting for transfers between devices  10.6 us (34%)
  Pallas kernels  8.67 us (27%)
    ppermute x4, starting transfers between devices, swapped(): return lax.ppermute(value, axis, pairs)  8.34 us
    ppermute x4, waiting for transfers between devices, swapped(): return lax.ppermute(value, axis, pairs)  5.89 us
    ppermute x3, waiting for transfers between devices, crossed(): lax.ppermute(value, both, [(source, source ^ mask) for source in range(co...  4.69 us
    pallas_call x1, Pallas kernels, local(): pl.pallas_call(functools.partial(second_kernel, pk, dom_count), out_shape...  4.25 us
    ppermute x3, starting transfers between devices, crossed(): lax.ppermute(value, both, [(source, source ^ mask) for source in range(co...  3.62 us
    pallas_call x1, Pallas kernels, local(): pl.pallas_call(functools.partial(start_kernel, pk, masks), out_shape=(fie...  1.92 us
    pallas_call x1, Pallas kernels, local(): pl.pallas_call(functools.partial(first_kernel, pk, bands), out_shape=(pad...  1.4 us
    pallas_call x1, Pallas kernels, local(): pl.pallas_call(functools.partial(edge_kernel, pk), out_shape=in_vmem(DEG,...  0.82 us
  transfers between devices with their start and end apart: 7, of which 7 were waited for; matrix products, arithmetic and copies ran while one was open for 0% of the time, Pallas kernels for 7%

profile of v10, /device:TPU:0, one launch (start us, length us, event | category | flops | bytes accessed | tf_op | source)
XLA Modules:
  0.0 31.4 jit_solution(17258984927836389849)
XLA Ops:
  0.0 0.8 %shard_map.56 = f32[8,1,1600]{2,1,0:T(1,128)S(1)} custom-call(s32[1]{0:T(128)} %bitcast.slab_ref, f32[20,1,1600]{2,1,0:T(1,128)} %bitcast.11), custom_call_target="tpu_custom_call" | custom-call | tf_op jit(solution)/shard_map/pallas_call | solution.py:568
  0.8 3.0 %collective-permute-start = (f32[8,1,1600]{2,1,0:T(1,128)S(1)}, f32[8,1,1600]{2,1,0:T(1,128)S(1)}, u32[]{:S(2)}, u32[]{:S(2)}) collective-permute-start(f32[8,1,1600]{2,1,0:T(1,128)S(1)} %shard_map.56), channel_id=1, source_target_pairs={{0,1},{1,0},{2,3},{3,2},{4,5},{5,4},{6,7},{7,6},{8,9},{9,8},{10,11... | collective-permute-start | bytes 153608 | tf_op jit(solution)/shard_map/ppermute | solution.py:24
  3.8 1.9 %shard_map.55 = (f32[10,40,128]{2,1,0:T(8,128)S(1)}, f32[10,40,128]{2,1,0:T(8,128)S(1)}, f32[8,128]{1,0:T(8,128)S(1)}) custom-call(s32[1]{0:T(128)} %bitcast.slab_ref, s32[1]{0:T(128)} %bitcast.1.dom_ref, f32[20,1,1600]{2,1,0:T(1,128)} %bitcast.12, f32[40,1600]{1,0:T(8,128)} %bitcast.13, s32[4,3]{1,0:T(4,128)} %offsets_in_ref.1), custom_call_target="tpu_custom_call" | custom-call | tf_op jit(solution)/shard_map/pallas_call | solution.py:583
  5.8 0.2 collective-permute-done.halo_ref
  5.9 1.4 %shard_map.57 = (f32[10,56,128]{2,1,0:T(8,128)S(1)}, f32[128,128]{1,0:T(8,128)S(1)}) custom-call(s32[1]{0:T(128)} %bitcast.slab_ref, f32[10,40,128]{2,1,0:T(8,128)S(1)} %get-tuple-element.13.start_ref, f32[8,1,1600]{2,1,0:T(1,128)S(1)} %collective-permute-done.halo_ref, f32[10,40,128]{2,1,0:T(8,128)S(1)} %get-tuple-element.14.coef_ref.start_coef_ref), custom_call_target="tpu_custom_call" | custom-call | tf_op jit(solution)/shard_map/pallas_call | solution.py:600
  7.3 2.2 %collective-permute-start.1 = (f32[128,128]{1,0:T(8,128)S(1)}, f32[128,128]{1,0:T(8,128)S(1)}, u32[]{:S(2)}, u32[]{:S(2)}) collective-permute-start(f32[128,128]{1,0:T(8,128)S(1)} %get-tuple-element.16), channel_id=1, source_target_pairs={{0,2},{1,3},{2,0},{3,1},{4,6},{5,7},{6,4},{7,5},{8,10},{9,11},{10,... | collective-permute-start | bytes 196616 | tf_op jit(solution)/shard_map/ppermute | solution.py:24
  9.5 2.2 %collective-permute-done.1 = f32[128,128]{1,0:T(8,128)S(1)} collective-permute-done((f32[128,128]{1,0:T(8,128)S(1)}, f32[128,128]{1,0:T(8,128)S(1)}, u32[]{:S(2)}, u32[]{:S(2)}) %collective-permute-start.1) | collective-permute-done | bytes 65568 | tf_op jit(solution)/shard_map/ppermute | solution.py:24
  11.8 3.1 %collective-permute-start.2 = (f32[128,128]{1,0:T(8,128)S(1)}, f32[128,128]{1,0:T(8,128)S(1)}, u32[]{:S(2)}, u32[]{:S(2)}) collective-permute-start(f32[128,128]{1,0:T(8,128)S(1)} %add.11), channel_id=1, source_target_pairs={{0,4},{1,5},{2,6},{3,7},{4,0},{5,1},{6,2},{7,3},{8,12},{9,13},{10,... | collective-permute-start | bytes 196616 | tf_op jit(solution)/shard_map/ppermute | solution.py:24
  14.9 0.1 shard_map.58
  15.0 2.1 %collective-permute-done.2 = f32[128,128]{1,0:T(8,128)S(1)} collective-permute-done((f32[128,128]{1,0:T(8,128)S(1)}, f32[128,128]{1,0:T(8,128)S(1)}, u32[]{:S(2)}, u32[]{:S(2)}) %collective-permute-start.2) | collective-permute-done | bytes 65568 | tf_op jit(solution)/shard_map/ppermute | solution.py:24
  17.1 1.9 %collective-permute-start.4 = (f32[128,128]{1,0:T(8,128)S(1)}, f32[128,128]{1,0:T(8,128)S(1)}, u32[]{:S(2)}, u32[]{:S(2)}) collective-permute-start(f32[128,128]{1,0:T(8,128)S(1)} %add.12), channel_id=1, source_target_pairs={{0,16},{1,17},{2,18},{3,19},{4,20},{5,21},{6,22},{7,23},{8,24},{9,... | collective-permute-start | bytes 196616 | tf_op jit(solution)/shard_map/ppermute | solution.py:626
  19.1 1.4 %collective-permute-start.5 = (f32[128,128]{1,0:T(8,128)S(1)}, f32[128,128]{1,0:T(8,128)S(1)}, u32[]{:S(2)}, u32[]{:S(2)}) collective-permute-start(f32[128,128]{1,0:T(8,128)S(1)} %add.12), channel_id=1, source_target_pairs={{0,17},{1,16},{2,19},{3,18},{4,21},{5,20},{6,23},{7,22},{8,25},{9,... | collective-permute-start | bytes 196616 | tf_op jit(solution)/shard_map/ppermute | solution.py:626
  20.5 0.3 collective-permute-start.3
  20.8 0.7 %collective-permute-done.4 = f32[128,128]{1,0:T(8,128)S(1)} collective-permute-done((f32[128,128]{1,0:T(8,128)S(1)}, f32[128,128]{1,0:T(8,128)S(1)}, u32[]{:S(2)}, u32[]{:S(2)}) %collective-permute-start.4) | collective-permute-done | bytes 65568 | tf_op jit(solution)/shard_map/ppermute | solution.py:626
  21.5 2.7 %collective-permute-done.5 = f32[128,128]{1,0:T(8,128)S(1)} collective-permute-done((f32[128,128]{1,0:T(8,128)S(1)}, f32[128,128]{1,0:T(8,128)S(1)}, u32[]{:S(2)}, u32[]{:S(2)}) %collective-permute-start.5) | collective-permute-done | bytes 65568 | tf_op jit(solution)/shard_map/ppermute | solution.py:626
  24.3 1.2 %collective-permute-done.3.beside_ref = f32[248,128]{1,0:T(8,128)S(1)} collective-permute-done((f32[248,128]{1,0:T(8,128)S(1)}, f32[248,128]{1,0:T(8,128)S(1)}, u32[]{:S(2)}, u32[]{:S(2)}) %collective-permute-start.3) | collective-permute-done | bytes 127008 | tf_op jit(solution)/shard_map/ppermute | solution.py:626
  25.5 0.0 copy-start
  25.5 0.0 copy-start.1
  25.6 0.1 collective-permute-start.6
  25.7 0.2 shard_map.59
  25.9 1.3 %collective-permute-done.6.across_ref = f32[2,256,128]{2,1,0:T(8,128)S(1)} collective-permute-done((f32[2,256,128]{2,1,0:T(8,128)S(1)}, f32[2,256,128]{2,1,0:T(8,128)S(1)}, u32[]{:S(2)}, u32[]{:S(2)}) %collective-permute-start.6) | collective-permute-done | bytes 262176 | tf_op jit(solution)/shard_map/ppermute | solution.py:24
  27.2 0.0 copy-done
  27.2 0.0 copy-done.1
  27.2 4.2 %shard_map.60 = f32[20,1,1600]{2,1,0:T(1,128)} custom-call(s32[1]{0:T(128)} %bitcast.slab_ref, f32[8,128]{1,0:T(8,128)S(1)} %get-tuple-element.12.code_ref, f32[8,128]{1,0:T(8,128)S(1)} %get-tuple-element.17.mean_ref, f32[2,256,128]{2,1,0:T(8,128)S(1)} %pad_maximum_fusion.near_ref, f32[2,256,128]{2,1,0:T(8,128)S(1)} %collective-permute-done.6.across_ref, ...), custom_call_target="tpu_custom_call" | custom-call | tf_op jit(solution)/shard_map/pallas_call | solution.py:653
  (8 shorter events, 0.1 us)
Async XLA Ops:
  0.8 5.1 %collective-permute-start = (f32[8,1,1600]{2,1,0:T(1,128)S(1)}, f32[8,1,1600]{2,1,0:T(1,128)S(1)}, u32[]{:S(2)}, u32[]{:S(2)}) collective-permute-start(f32[8,1,1600]{2,1,0:T(1,128)S(1)} %shard_map.56), channel_id=1, source_target_pairs={{0,1},{1,0},{2,3},{3,2},{4,5},{5,4},{6,7},{7,6},{8,9},{9,8},{10,11... | collective-permute-start | bytes 153608 | tf_op jit(solution)/shard_map/ppermute | solution.py:24
  7.3 4.4 %collective-permute-start.1 = (f32[128,128]{1,0:T(8,128)S(1)}, f32[128,128]{1,0:T(8,128)S(1)}, u32[]{:S(2)}, u32[]{:S(2)}) collective-permute-start(f32[128,128]{1,0:T(8,128)S(1)} %get-tuple-element.16), channel_id=1, source_target_pairs={{0,2},{1,3},{2,0},{3,1},{4,6},{5,7},{6,4},{7,5},{8,10},{9,11},{10,... | collective-permute-start | bytes 196616 | tf_op jit(solution)/shard_map/ppermute | solution.py:24
  11.8 5.3 %collective-permute-start.2 = (f32[128,128]{1,0:T(8,128)S(1)}, f32[128,128]{1,0:T(8,128)S(1)}, u32[]{:S(2)}, u32[]{:S(2)}) collective-permute-start(f32[128,128]{1,0:T(8,128)S(1)} %add.11), channel_id=1, source_target_pairs={{0,4},{1,5},{2,6},{3,7},{4,0},{5,1},{6,2},{7,3},{8,12},{9,13},{10,... | collective-permute-start | bytes 196616 | tf_op jit(solution)/shard_map/ppermute | solution.py:24
  17.1 4.3 %collective-permute-start.4 = (f32[128,128]{1,0:T(8,128)S(1)}, f32[128,128]{1,0:T(8,128)S(1)}, u32[]{:S(2)}, u32[]{:S(2)}) collective-permute-start(f32[128,128]{1,0:T(8,128)S(1)} %add.12), channel_id=1, source_target_pairs={{0,16},{1,17},{2,18},{3,19},{4,20},{5,21},{6,22},{7,23},{8,24},{9,... | collective-permute-start | bytes 196616 | tf_op jit(solution)/shard_map/ppermute | solution.py:626
  19.1 5.2 %collective-permute-start.5 = (f32[128,128]{1,0:T(8,128)S(1)}, f32[128,128]{1,0:T(8,128)S(1)}, u32[]{:S(2)}, u32[]{:S(2)}) collective-permute-start(f32[128,128]{1,0:T(8,128)S(1)} %add.12), channel_id=1, source_target_pairs={{0,17},{1,16},{2,19},{3,18},{4,21},{5,20},{6,23},{7,22},{8,25},{9,... | collective-permute-start | bytes 196616 | tf_op jit(solution)/shard_map/ppermute | solution.py:626
  20.5 5.0 %collective-permute-start.3 = (f32[248,128]{1,0:T(8,128)S(1)}, f32[248,128]{1,0:T(8,128)S(1)}, u32[]{:S(2)}, u32[]{:S(2)}) collective-permute-start(f32[248,128]{1,0:T(8,128)S(1)} %pad_maximum_fusion.1), channel_id=1, source_target_pairs={{0,1},{1,0},{2,3},{3,2},{4,5},{5,4},{6,7},{7,6},{8,9},{9,8},{10,11... | collective-permute-start | bytes 380936 | tf_op jit(solution)/shard_map/ppermute | solution.py:626
  25.5 1.7 %copy-start = (bf16[768,512]{1,0:T(8,128)(2,1)S(1)}, bf16[768,512]{1,0:T(8,128)(2,1)}, u32[]{:S(2)}) copy-start(bf16[768,512]{1,0:T(8,128)(2,1)} %constant.26.clone.table_ref) | copy-start | bytes 2359300
  25.5 1.6 %copy-start.1 = (f32[1024,128]{1,0:T(8,128)S(1)}, f32[1024,128]{1,0:T(8,128)}, u32[]{:S(2)}) copy-start(f32[1024,128]{1,0:T(8,128)} %constant.27.clone.factor_ref) | copy-start | bytes 1572868
  25.6 1.6 %collective-permute-start.6 = (f32[2,256,128]{2,1,0:T(8,128)S(1)}, f32[2,256,128]{2,1,0:T(8,128)S(1)}, u32[]{:S(2)}, u32[]{:S(2)}) collective-permute-start(f32[2,256,128]{2,1,0:T(8,128)S(1)} %pad_maximum_fusion.near_ref), channel_id=1, source_target_pairs={{0,8},{8,0},{16,24},{24,16},{1,9},{9,1},{17,25},{25,17},{2,10},{10... | collective-permute-start | bytes 786440 | tf_op jit(solution)/shard_map/ppermute | solution.py:24

commit v11 on v10

--- a/solution.py
+++ b/solution.py
@@ -361,11 +361,13 @@
 
 
 def second_kernel(
-    pk, dom_count, slab_ref, code_ref, mean_ref, near_ref, across_ref, field_ref, start_coef_ref,
-    table_ref, factor_ref,
-    out_ref, cubes_ref, one_ref, two_ref, coef_ref, left_ref, rows_ref, waves_ref, mixed_ref, flat_ref,
-    near_dens_ref, own_ref,
+    pk, dom_count, slab_ref, code_ref, mean_ref, field_ref, start_coef_ref, table_ref, factor_ref, *refs
 ):
+    gathered_refs, refs = refs[:dom_count], refs[dom_count:]
+    (
+        out_ref, cubes_ref, one_ref, two_ref, coef_ref, left_ref, rows_ref, waves_ref, mixed_ref, flat_ref,
+        near_dens_ref, own_ref,
+    ) = refs
     side, half, span = pk.side, pk.half, pk.span
     is_lower = slab_ref[0] == 0
     blocks_z = dom_count // 4
@@ -376,8 +378,16 @@
     pitch = CORE + 8
     kept = padded(pk.rows, 8)
 
-    cubes_ref[0 : dom_count // 2] = near_ref[...]
-    cubes_ref[dom_count // 2 : dom_count] = across_ref[...]
+    near_count = dom_count // 2
+    early_ref, late_ref = gathered_refs[near_count : near_count + 2]
+    whole, part = CORE * 8, CORE * 4
+    for idx, ref in enumerate(gathered_refs):
+        if idx not in (near_count, near_count + 1):
+            cubes_ref[idx] = ref[...]
+    cubes_ref[near_count] = early_ref[0:whole]
+    own_part, other_part = early_ref[whole : whole + part], late_ref[...]
+    cubes_ref[near_count + 1, 0:part] = jnp.where(is_lower, own_part, other_part)
+    cubes_ref[near_count + 1, part:whole] = jnp.where(is_lower, other_part, own_part)
     mean = 4.0 * jnp.concatenate([mean_ref[...]] * CORE, 0)
     code = jnp.max(code_ref[...]).astype(jnp.int32)
     cube_at = [code // dom_count**where % dom_count for where in range(dom_count)]
@@ -574,8 +584,8 @@
         compiler_params=params,
     )(slab_scalar, rows)
     halo = swapped(edge, "band", 1)
-    masks = [0]
-    bit = dom_count // 2
+    masks = [dom_count // 2, 0]
+    bit = dom_count // 4
     while bit:
         masks = masks + [one | bit for one in masks]
         bit //= 2
@@ -633,13 +643,14 @@
     def cube_of(own, other):
         return jnp.concatenate([jnp.where(is_lower, own, other), jnp.where(is_lower, other, own)], 0)
 
-    cubes = jnp.stack([cube_of(dens, beside), cube_of(across, diagonal)])
+    cubes = [cube_of(across, diagonal), cube_of(dens, beside)]
     bit = far // 2
-    while bit:
-        if bit > 1:
-            cubes = jnp.concatenate([cubes, swapped(cubes, "dom", bit)], 0)
+    while bit > 1:
+        cubes = cubes + [swapped(cube, "dom", bit) for cube in cubes]
         bit //= 2
-    cubes_across = swapped(cubes, "dom", 1)
+    early = swapped(jnp.concatenate([cubes[0], dens], 0), "dom", 1)
+    late = swapped(beside, "dom", 1)
+    cubes_across = [early, late] + [swapped(cube, "dom", 1) for cube in cubes[2:]]
 
     field, mean = pl.pallas_call(
         functools.partial(take_kernel, pk),
@@ -647,13 +658,13 @@
         in_specs=[SMEM, VMEM, VMEM, VMEM],
         out_specs=(VMEM, VMEM),
         compiler_params=params,
-    )(slab_scalar, filt, beside_all, cubes)
+    )(slab_scalar, filt, beside_all, cubes[1])
     table, factor = solver_tables(side, grid_z)
     pitch = CORE + 8
     result = pl.pallas_call(
         functools.partial(second_kernel, pk, dom_count),
         out_shape=jax.ShapeDtypeStruct((half, 1, cells), f32),
-        in_specs=[SMEM] + [VMEM] * 8,
+        in_specs=[SMEM] + [VMEM] * (6 + dom_count),
         out_specs=VMEM,
         scratch_shapes=[
             pltpu.VMEM((dom_count, CORE * 8, 128), f32),
@@ -670,8 +681,7 @@
         ],
         compiler_params=params,
     )(
-        slab_scalar, code, mean, cubes, cubes_across, field, coef,
-        jnp.asarray(table), jnp.asarray(factor),
+        slab_scalar, code, mean, field, coef, jnp.asarray(table), jnp.asarray(factor), *cubes, *cubes_across
     )
     return result.reshape(1, 1, half, cells)
 

time: 31.6 us -> 31.3 us (level)
  waiting for transfers between devices: 10.6 us -> 10.2 us
    ppermute x4 -> x5, waiting for transfers between devices: 5.89 us -> 5.64 us  [swapped(): return lax.ppermute(value, axis, pairs)]
    ppermute x4 -> x5, starting transfers between devices: 8.34 us -> 8.41 us  [swapped(): return lax.ppermute(value, axis, pairs)]
  transfers between devices with their start and end apart: 7 -> 8, of which waited for: 7 -> 7; matrix products, arithmetic and copies ran while one was open for 0% -> 0% of each run, Pallas kernels for 7% -> 7%
where the time goes in v11:
time: 31.3 us; the launch traced here: 31.1 us
  starting transfers between devices  12 us (38%)
  waiting for transfers between devices  10.2 us (33%)
  Pallas kernels  8.67 us (28%)
    ppermute x5, starting transfers between devices, swapped(): return lax.ppermute(value, axis, pairs)  8.41 us
    ppermute x5, waiting for transfers between devices, swapped(): return lax.ppermute(value, axis, pairs)  5.64 us
    ppermute x3, waiting for transfers between devices, crossed(): lax.ppermute(value, both, [(source, source ^ mask) for source in range(co...  4.56 us
    pallas_call x1, Pallas kernels, local(): pl.pallas_call(functools.partial(second_kernel, pk, dom_count), out_shape...  4.28 us
    ppermute x3, starting transfers between devices, crossed(): lax.ppermute(value, both, [(source, source ^ mask) for source in range(co...  3.62 us
    pallas_call x1, Pallas kernels, local(): pl.pallas_call(functools.partial(start_kernel, pk, masks), out_shape=(fie...  1.9 us
    pallas_call x1, Pallas kernels, local(): pl.pallas_call(functools.partial(first_kernel, pk, bands), out_shape=(pad...  1.4 us
    pallas_call x1, Pallas kernels, local(): pl.pallas_call(functools.partial(edge_kernel, pk), out_shape=in_vmem(DEG,...  0.82 us
  transfers between devices with their start and end apart: 8, of which 7 were waited for; matrix products, arithmetic and copies ran while one was open for 0% of the time, Pallas kernels for 7%

profile of v11, /device:TPU:0, one launch (start us, length us, event | category | flops | bytes accessed | tf_op | source)
XLA Modules:
  0.0 31.1 jit_solution(15558616747427779394)
XLA Ops:
  0.0 0.8 %shard_map.56 = f32[8,1,1600]{2,1,0:T(1,128)S(1)} custom-call(s32[1]{0:T(128)} %bitcast.slab_ref, f32[20,1,1600]{2,1,0:T(1,128)} %bitcast.7), custom_call_target="tpu_custom_call" | custom-call | tf_op jit(solution)/shard_map/pallas_call | solution.py:578
  0.8 3.0 %collective-permute-start = (f32[8,1,1600]{2,1,0:T(1,128)S(1)}, f32[8,1,1600]{2,1,0:T(1,128)S(1)}, u32[]{:S(2)}, u32[]{:S(2)}) collective-permute-start(f32[8,1,1600]{2,1,0:T(1,128)S(1)} %shard_map.56), channel_id=1, source_target_pairs={{0,1},{1,0},{2,3},{3,2},{4,5},{5,4},{6,7},{7,6},{8,9},{9,8},{10,11... | collective-permute-start | bytes 153608 | tf_op jit(solution)/shard_map/ppermute | solution.py:24
  3.8 1.9 %shard_map.55 = (f32[10,40,128]{2,1,0:T(8,128)S(1)}, f32[10,40,128]{2,1,0:T(8,128)S(1)}, f32[8,128]{1,0:T(8,128)S(1)}) custom-call(s32[1]{0:T(128)} %bitcast.slab_ref, s32[1]{0:T(128)} %bitcast.1.dom_ref, f32[20,1,1600]{2,1,0:T(1,128)} %bitcast.8, f32[40,1600]{1,0:T(8,128)} %bitcast.9, s32[4,3]{1,0:T(4,128)} %offsets_in_ref.1), custom_call_target="tpu_custom_call" | custom-call | tf_op jit(solution)/shard_map/pallas_call | solution.py:593
  5.7 0.2 collective-permute-done.halo_ref
  5.9 1.4 %shard_map.57 = (f32[10,56,128]{2,1,0:T(8,128)S(1)}, f32[128,128]{1,0:T(8,128)S(1)}) custom-call(s32[1]{0:T(128)} %bitcast.slab_ref, f32[10,40,128]{2,1,0:T(8,128)S(1)} %get-tuple-element.13.start_ref, f32[8,1,1600]{2,1,0:T(1,128)S(1)} %collective-permute-done.halo_ref, f32[10,40,128]{2,1,0:T(8,128)S(1)} %get-tuple-element.14.coef_ref.start_coef_ref), custom_call_target="tpu_custom_call" | custom-call | tf_op jit(solution)/shard_map/pallas_call | solution.py:610
  7.3 2.2 %collective-permute-start.1 = (f32[128,128]{1,0:T(8,128)S(1)}, f32[128,128]{1,0:T(8,128)S(1)}, u32[]{:S(2)}, u32[]{:S(2)}) collective-permute-start(f32[128,128]{1,0:T(8,128)S(1)} %get-tuple-element.16), channel_id=1, source_target_pairs={{0,2},{1,3},{2,0},{3,1},{4,6},{5,7},{6,4},{7,5},{8,10},{9,11},{10,... | collective-permute-start | bytes 196616 | tf_op jit(solution)/shard_map/ppermute | solution.py:24
  9.5 2.2 %collective-permute-done.1 = f32[128,128]{1,0:T(8,128)S(1)} collective-permute-done((f32[128,128]{1,0:T(8,128)S(1)}, f32[128,128]{1,0:T(8,128)S(1)}, u32[]{:S(2)}, u32[]{:S(2)}) %collective-permute-start.1) | collective-permute-done | bytes 65568 | tf_op jit(solution)/shard_map/ppermute | solution.py:24
  11.8 3.1 %collective-permute-start.2 = (f32[128,128]{1,0:T(8,128)S(1)}, f32[128,128]{1,0:T(8,128)S(1)}, u32[]{:S(2)}, u32[]{:S(2)}) collective-permute-start(f32[128,128]{1,0:T(8,128)S(1)} %add.11), channel_id=1, source_target_pairs={{0,4},{1,5},{2,6},{3,7},{4,0},{5,1},{6,2},{7,3},{8,12},{9,13},{10,... | collective-permute-start | bytes 196616 | tf_op jit(solution)/shard_map/ppermute | solution.py:24
  14.9 0.1 shard_map.58
  15.0 2.1 %collective-permute-done.2 = f32[128,128]{1,0:T(8,128)S(1)} collective-permute-done((f32[128,128]{1,0:T(8,128)S(1)}, f32[128,128]{1,0:T(8,128)S(1)}, u32[]{:S(2)}, u32[]{:S(2)}) %collective-permute-start.2) | collective-permute-done | bytes 65568 | tf_op jit(solution)/shard_map/ppermute | solution.py:24
  17.1 1.9 %collective-permute-start.4 = (f32[128,128]{1,0:T(8,128)S(1)}, f32[128,128]{1,0:T(8,128)S(1)}, u32[]{:S(2)}, u32[]{:S(2)}) collective-permute-start(f32[128,128]{1,0:T(8,128)S(1)} %add.12), channel_id=1, source_target_pairs={{0,16},{1,17},{2,18},{3,19},{4,20},{5,21},{6,22},{7,23},{8,24},{9,... | collective-permute-start | bytes 196616 | tf_op jit(solution)/shard_map/ppermute | solution.py:636
  19.1 1.4 %collective-permute-start.5 = (f32[128,128]{1,0:T(8,128)S(1)}, f32[128,128]{1,0:T(8,128)S(1)}, u32[]{:S(2)}, u32[]{:S(2)}) collective-permute-start(f32[128,128]{1,0:T(8,128)S(1)} %add.12), channel_id=1, source_target_pairs={{0,17},{1,16},{2,19},{3,18},{4,21},{5,20},{6,23},{7,22},{8,25},{9,... | collective-permute-start | bytes 196616 | tf_op jit(solution)/shard_map/ppermute | solution.py:636
  20.5 0.3 collective-permute-start.3
  20.8 0.7 %collective-permute-done.4 = f32[128,128]{1,0:T(8,128)S(1)} collective-permute-done((f32[128,128]{1,0:T(8,128)S(1)}, f32[128,128]{1,0:T(8,128)S(1)}, u32[]{:S(2)}, u32[]{:S(2)}) %collective-permute-start.4) | collective-permute-done | bytes 65568 | tf_op jit(solution)/shard_map/ppermute | solution.py:636
  21.5 2.7 %collective-permute-done.5 = f32[128,128]{1,0:T(8,128)S(1)} collective-permute-done((f32[128,128]{1,0:T(8,128)S(1)}, f32[128,128]{1,0:T(8,128)S(1)}, u32[]{:S(2)}, u32[]{:S(2)}) %collective-permute-start.5) | collective-permute-done | bytes 65568 | tf_op jit(solution)/shard_map/ppermute | solution.py:636
  24.3 0.0 copy-start
  24.3 0.1 collective-permute-start.6
  24.4 0.0 copy-start.1
  24.4 1.1 %collective-permute-done.3.beside_ref = f32[248,128]{1,0:T(8,128)S(1)} collective-permute-done((f32[248,128]{1,0:T(8,128)S(1)}, f32[248,128]{1,0:T(8,128)S(1)}, u32[]{:S(2)}, u32[]{:S(2)}) %collective-permute-start.3) | collective-permute-done | bytes 127008 | tf_op jit(solution)/shard_map/ppermute | solution.py:636
  25.5 0.1 collective-permute-start.7
  25.6 0.2 shard_map.59
  25.8 1.1 %collective-permute-done.7.refs_3_ = f32[128,128]{1,0:T(8,128)S(1)} collective-permute-done((f32[128,128]{1,0:T(8,128)S(1)}, f32[128,128]{1,0:T(8,128)S(1)}, u32[]{:S(2)}, u32[]{:S(2)}) %collective-permute-start.7) | collective-permute-done | bytes 65568 | tf_op jit(solution)/shard_map/ppermute | solution.py:24
  26.8 0.0 collective-permute-done.6.refs_2_
  26.8 4.3 %shard_map.60 = f32[20,1,1600]{2,1,0:T(1,128)} custom-call(s32[1]{0:T(128)} %bitcast.slab_ref, f32[8,128]{1,0:T(8,128)S(1)} %get-tuple-element.12.code_ref, f32[8,128]{1,0:T(8,128)S(1)} %get-tuple-element.17.mean_ref, f32[10,56,128]{2,1,0:T(8,128)S(1)} %get-tuple-element.18.field_ref, f32[10,40,128]{2,1,0:T(8,128)S(1)} %get-tuple-element.14.coef_ref.start_coef_ref, ...), custom_call_target="tpu_custom_call" | custom-call | tf_op jit(solution)/shard_map/pallas_call | solution.py:664
  (10 shorter events, 0.1 us)
Async XLA Ops:
  0.8 5.1 %collective-permute-start = (f32[8,1,1600]{2,1,0:T(1,128)S(1)}, f32[8,1,1600]{2,1,0:T(1,128)S(1)}, u32[]{:S(2)}, u32[]{:S(2)}) collective-permute-start(f32[8,1,1600]{2,1,0:T(1,128)S(1)} %shard_map.56), channel_id=1, source_target_pairs={{0,1},{1,0},{2,3},{3,2},{4,5},{5,4},{6,7},{7,6},{8,9},{9,8},{10,11... | collective-permute-start | bytes 153608 | tf_op jit(solution)/shard_map/ppermute | solution.py:24
  7.3 4.4 %collective-permute-start.1 = (f32[128,128]{1,0:T(8,128)S(1)}, f32[128,128]{1,0:T(8,128)S(1)}, u32[]{:S(2)}, u32[]{:S(2)}) collective-permute-start(f32[128,128]{1,0:T(8,128)S(1)} %get-tuple-element.16), channel_id=1, source_target_pairs={{0,2},{1,3},{2,0},{3,1},{4,6},{5,7},{6,4},{7,5},{8,10},{9,11},{10,... | collective-permute-start | bytes 196616 | tf_op jit(solution)/shard_map/ppermute | solution.py:24
  11.8 5.3 %collective-permute-start.2 = (f32[128,128]{1,0:T(8,128)S(1)}, f32[128,128]{1,0:T(8,128)S(1)}, u32[]{:S(2)}, u32[]{:S(2)}) collective-permute-start(f32[128,128]{1,0:T(8,128)S(1)} %add.11), channel_id=1, source_target_pairs={{0,4},{1,5},{2,6},{3,7},{4,0},{5,1},{6,2},{7,3},{8,12},{9,13},{10,... | collective-permute-start | bytes 196616 | tf_op jit(solution)/shard_map/ppermute | solution.py:24
  17.1 4.3 %collective-permute-start.4 = (f32[128,128]{1,0:T(8,128)S(1)}, f32[128,128]{1,0:T(8,128)S(1)}, u32[]{:S(2)}, u32[]{:S(2)}) collective-permute-start(f32[128,128]{1,0:T(8,128)S(1)} %add.12), channel_id=1, source_target_pairs={{0,16},{1,17},{2,18},{3,19},{4,20},{5,21},{6,22},{7,23},{8,24},{9,... | collective-permute-start | bytes 196616 | tf_op jit(solution)/shard_map/ppermute | solution.py:636
  19.1 5.2 %collective-permute-start.5 = (f32[128,128]{1,0:T(8,128)S(1)}, f32[128,128]{1,0:T(8,128)S(1)}, u32[]{:S(2)}, u32[]{:S(2)}) collective-permute-start(f32[128,128]{1,0:T(8,128)S(1)} %add.12), channel_id=1, source_target_pairs={{0,17},{1,16},{2,19},{3,18},{4,21},{5,20},{6,23},{7,22},{8,25},{9,... | collective-permute-start | bytes 196616 | tf_op jit(solution)/shard_map/ppermute | solution.py:636
  20.5 5.0 %collective-permute-start.3 = (f32[248,128]{1,0:T(8,128)S(1)}, f32[248,128]{1,0:T(8,128)S(1)}, u32[]{:S(2)}, u32[]{:S(2)}) collective-permute-start(f32[248,128]{1,0:T(8,128)S(1)} %pad_maximum_fusion.3), channel_id=1, source_target_pairs={{0,1},{1,0},{2,3},{3,2},{4,5},{5,4},{6,7},{7,6},{8,9},{9,8},{10,11... | collective-permute-start | bytes 380936 | tf_op jit(solution)/shard_map/ppermute | solution.py:636
  24.3 2.6 %copy-start = (bf16[768,512]{1,0:T(8,128)(2,1)S(1)}, bf16[768,512]{1,0:T(8,128)(2,1)}, u32[]{:S(2)}) copy-start(bf16[768,512]{1,0:T(8,128)(2,1)} %constant.26.clone.table_ref) | copy-start | bytes 2359300
  24.3 2.6 %collective-permute-start.6 = (f32[384,128]{1,0:T(8,128)S(1)}, f32[384,128]{1,0:T(8,128)S(1)}, u32[]{:S(2)}, u32[]{:S(2)}) collective-permute-start(f32[384,128]{1,0:T(8,128)S(1)} %pad_maximum_fusion), channel_id=1, source_target_pairs={{0,8},{8,0},{16,24},{24,16},{1,9},{9,1},{17,25},{25,17},{2,10},{10... | collective-permute-start | bytes 589832 | tf_op jit(solution)/shard_map/ppermute | solution.py:24
  24.4 2.5 %copy-start.1 = (f32[1024,128]{1,0:T(8,128)S(1)}, f32[1024,128]{1,0:T(8,128)}, u32[]{:S(2)}) copy-start(f32[1024,128]{1,0:T(8,128)} %constant.27.clone.factor_ref) | copy-start | bytes 1572868
  25.5 1.3 %collective-permute-start.7 = (f32[128,128]{1,0:T(8,128)S(1)}, f32[128,128]{1,0:T(8,128)S(1)}, u32[]{:S(2)}, u32[]{:S(2)}) collective-permute-start(f32[128,128]{1,0:T(8,128)S(1)} %get-tuple-element.23), channel_id=1, source_target_pairs={{0,8},{8,0},{16,24},{24,16},{1,9},{9,1},{17,25},{25,17},{2,10},{10... | collective-permute-start | bytes 196616 | tf_op jit(solution)/shard_map/ppermute | solution.py:24

commit v12 on v11

--- a/solution.py
+++ b/solution.py
@@ -231,15 +231,18 @@
 
     lane = lanes_of((8, 128))
     lines = 128 // CORE
-    for cell in range(CORE // 2):
-        row = cell + jnp.where(is_lower, BUF, DEG)
-        block, level = row // pk.depth, row % pk.depth
-        total = jnp.zeros((8, 128), jnp.float32)
-        for line in range(lines):
-            value = result_ref[level, 8 + BUF + 8 * line : 16 + BUF + 8 * line, :]
-            shift = line * CORE - BUF - block * span + 128 * pk.blocks
-            total = jnp.where(lane // CORE == line, pltpu.roll(value, shift % 128, 1), total)
-        dens_ref[cell * 8 : (cell + 1) * 8] = total * total * (1.0 / bands)
+    for lower, offset in ((True, BUF), (False, DEG)):
+
+        @pl.when(is_lower == lower)
+        def _(offset=offset):
+            for cell in range(CORE // 2):
+                block, level = pk.where(cell + offset)
+                total = None
+                for line in range(lines):
+                    value = result_ref[level, 8 + BUF + 8 * line : 16 + BUF + 8 * line, :]
+                    value = roll(value, line * CORE - BUF - block * span)
+                    total = value if total is None else jnp.where(lane >= line * CORE, value, total)
+                dens_ref[cell * 8 : (cell + 1) * 8] = total * total * (1.0 / bands)
 
 
 def send_kernel(pk, slab_ref, result_ref, edge_ref):
@@ -392,6 +395,7 @@
     code = jnp.max(code_ref[...]).astype(jnp.int32)
     cube_at = [code // dom_count**where % dom_count for where in range(dom_count)]
 
+    stacks = [[] for _ in range(4)]
     for at_z in range(blocks_z):
         near, at_x, at_y, at_xy = [cubes_ref[cube_at[at_z * 4 + place]] for place in range(4)]
         sums, others = near + at_x, at_y + at_xy
@@ -399,10 +403,9 @@
         parities = (sums + others - mean, sums - others, diffs + other_diffs, diffs - other_diffs)
         for parity, value in enumerate(parities):
             high, low = split2(value)
-            for idx, piece in enumerate((high, low, high)):
-                cols = slice((at_z * 3 + idx) * 128, (at_z * 3 + idx + 1) * 128)
-                left_ref[parity * CORE * 8 : (parity + 1) * CORE * 8, cols] = piece
-    product = dot(left_ref[...], table_ref[0 : blocks_z * 3 * 128, 256 : 256 + lanes])
+            stacks[parity] += [high, low, high]
+    z_table = table_ref[0 : blocks_z * 3 * 128, 256 : 256 + lanes]
+    product = jnp.concatenate([dot(jnp.concatenate(stack, 1), z_table) for stack in stacks], 0)
     lane = lanes_of((8, 128))
     for x in range(CORE):
         for line in range(lines):
@@ -521,12 +524,14 @@
     clear_margins(pk, two_ref)
     filtered_field(pk, field_ref, one_ref, two_ref, coef_ref)
 
-    for row in range(half):
-        at = row + jnp.where(is_lower, 0, DEG)
-        shift = 128 * pk.blocks - at // pk.depth * span
-        own_ref[row * side : (row + 1) * side, :] = pltpu.roll(
-            two_ref[at % pk.depth, 8 : 8 + side, :], shift % 128, 1
-        )
+    for lower, offset in ((True, 0), (False, DEG)):
+
+        @pl.when(is_lower == lower)
+        def _(offset=offset):
+            for row in range(half):
+                block, level = pk.where(row + offset)
+                own_ref[row * side : (row + 1) * side, :] = roll(two_ref[level, 8 : 8 + side, :], -block * span)
+
     cells = side * side
     parts = [roll(own_ref[pl.ds(y, half, stride=side), :], y * side) for y in range(side)]
     for tile in range(-(-cells // 128)):

time: 31.3 us -> 31 us (level)
  no operation moved by 1% of the time
where the time goes in v12:
time: 31 us; the launch traced here: 30.8 us
  starting transfers between devices  12 us (39%)
  waiting for transfers between devices  10.2 us (33%)
  Pallas kernels  8.37 us (27%)
    ppermute x5, starting transfers between devices, swapped(): return lax.ppermute(value, axis, pairs)  8.41 us
    ppermute x5, waiting for transfers between devices, swapped(): return lax.ppermute(value, axis, pairs)  5.64 us
    ppermute x3, waiting for transfers between devices, crossed(): lax.ppermute(value, both, [(source, source ^ mask) for source in range(co...  4.56 us
    pallas_call x1, Pallas kernels, local(): pl.pallas_call(functools.partial(second_kernel, pk, dom_count), out_shape...  4.1 us
    ppermute x3, starting transfers between devices, crossed(): lax.ppermute(value, both, [(source, source ^ mask) for source in range(co...  3.62 us
    pallas_call x1, Pallas kernels, local(): pl.pallas_call(functools.partial(start_kernel, pk, masks), out_shape=(fie...  1.9 us
    pallas_call x1, Pallas kernels, local(): pl.pallas_call(functools.partial(first_kernel, pk, bands), out_shape=(pad...  1.29 us
    pallas_call x1, Pallas kernels, local(): pl.pallas_call(functools.partial(edge_kernel, pk), out_shape=in_vmem(DEG,...  0.82 us
  transfers between devices with their start and end apart: 8, of which 7 were waited for; matrix products, arithmetic and copies ran while one was open for 0% of the time, Pallas kernels for 7%

profile of v12, /device:TPU:0, one launch (start us, length us, event | category | flops | bytes accessed | tf_op | source)
XLA Modules:
  0.0 30.8 jit_solution(2622563748872330298)
XLA Ops:
  0.0 0.8 %shard_map.56 = f32[8,1,1600]{2,1,0:T(1,128)S(1)} custom-call(s32[1]{0:T(128)} %bitcast.slab_ref, f32[20,1,1600]{2,1,0:T(1,128)} %bitcast.7), custom_call_target="tpu_custom_call" | custom-call | tf_op jit(solution)/shard_map/pallas_call | solution.py:583
  0.8 3.0 %collective-permute-start = (f32[8,1,1600]{2,1,0:T(1,128)S(1)}, f32[8,1,1600]{2,1,0:T(1,128)S(1)}, u32[]{:S(2)}, u32[]{:S(2)}) collective-permute-start(f32[8,1,1600]{2,1,0:T(1,128)S(1)} %shard_map.56), channel_id=1, source_target_pairs={{0,1},{1,0},{2,3},{3,2},{4,5},{5,4},{6,7},{7,6},{8,9},{9,8},{10,11... | collective-permute-start | bytes 153608 | tf_op jit(solution)/shard_map/ppermute | solution.py:24
  3.8 1.9 %shard_map.55 = (f32[10,40,128]{2,1,0:T(8,128)S(1)}, f32[10,40,128]{2,1,0:T(8,128)S(1)}, f32[8,128]{1,0:T(8,128)S(1)}) custom-call(s32[1]{0:T(128)} %bitcast.slab_ref, s32[1]{0:T(128)} %bitcast.1.dom_ref, f32[20,1,1600]{2,1,0:T(1,128)} %bitcast.8, f32[40,1600]{1,0:T(8,128)} %bitcast.9, s32[4,3]{1,0:T(4,128)} %offsets_in_ref.1), custom_call_target="tpu_custom_call" | custom-call | tf_op jit(solution)/shard_map/pallas_call | solution.py:598
  5.7 0.2 collective-permute-done.halo_ref
  5.9 1.3 %shard_map.57 = (f32[10,56,128]{2,1,0:T(8,128)S(1)}, f32[128,128]{1,0:T(8,128)S(1)}) custom-call(s32[1]{0:T(128)} %bitcast.slab_ref, f32[10,40,128]{2,1,0:T(8,128)S(1)} %get-tuple-element.13.start_ref, f32[8,1,1600]{2,1,0:T(1,128)S(1)} %collective-permute-done.halo_ref, f32[10,40,128]{2,1,0:T(8,128)S(1)} %get-tuple-element.14.coef_ref.start_coef_ref), custom_call_target="tpu_custom_call" | custom-call | tf_op jit(solution)/shard_map/pallas_call | solution.py:615
  7.2 2.2 %collective-permute-start.1 = (f32[128,128]{1,0:T(8,128)S(1)}, f32[128,128]{1,0:T(8,128)S(1)}, u32[]{:S(2)}, u32[]{:S(2)}) collective-permute-start(f32[128,128]{1,0:T(8,128)S(1)} %get-tuple-element.16), channel_id=1, source_target_pairs={{0,2},{1,3},{2,0},{3,1},{4,6},{5,7},{6,4},{7,5},{8,10},{9,11},{10,... | collective-permute-start | bytes 196616 | tf_op jit(solution)/shard_map/ppermute | solution.py:24
  9.4 2.2 %collective-permute-done.1 = f32[128,128]{1,0:T(8,128)S(1)} collective-permute-done((f32[128,128]{1,0:T(8,128)S(1)}, f32[128,128]{1,0:T(8,128)S(1)}, u32[]{:S(2)}, u32[]{:S(2)}) %collective-permute-start.1) | collective-permute-done | bytes 65568 | tf_op jit(solution)/shard_map/ppermute | solution.py:24
  11.7 3.1 %collective-permute-start.2 = (f32[128,128]{1,0:T(8,128)S(1)}, f32[128,128]{1,0:T(8,128)S(1)}, u32[]{:S(2)}, u32[]{:S(2)}) collective-permute-start(f32[128,128]{1,0:T(8,128)S(1)} %add.11), channel_id=1, source_target_pairs={{0,4},{1,5},{2,6},{3,7},{4,0},{5,1},{6,2},{7,3},{8,12},{9,13},{10,... | collective-permute-start | bytes 196616 | tf_op jit(solution)/shard_map/ppermute | solution.py:24
  14.8 0.1 shard_map.58
  14.9 2.1 %collective-permute-done.2 = f32[128,128]{1,0:T(8,128)S(1)} collective-permute-done((f32[128,128]{1,0:T(8,128)S(1)}, f32[128,128]{1,0:T(8,128)S(1)}, u32[]{:S(2)}, u32[]{:S(2)}) %collective-permute-start.2) | collective-permute-done | bytes 65568 | tf_op jit(solution)/shard_map/ppermute | solution.py:24
  17.0 1.9 %collective-permute-start.4 = (f32[128,128]{1,0:T(8,128)S(1)}, f32[128,128]{1,0:T(8,128)S(1)}, u32[]{:S(2)}, u32[]{:S(2)}) collective-permute-start(f32[128,128]{1,0:T(8,128)S(1)} %add.12), channel_id=1, source_target_pairs={{0,16},{1,17},{2,18},{3,19},{4,20},{5,21},{6,22},{7,23},{8,24},{9,... | collective-permute-start | bytes 196616 | tf_op jit(solution)/shard_map/ppermute | solution.py:641
  18.9 1.4 %collective-permute-start.5 = (f32[128,128]{1,0:T(8,128)S(1)}, f32[128,128]{1,0:T(8,128)S(1)}, u32[]{:S(2)}, u32[]{:S(2)}) collective-permute-start(f32[128,128]{1,0:T(8,128)S(1)} %add.12), channel_id=1, source_target_pairs={{0,17},{1,16},{2,19},{3,18},{4,21},{5,20},{6,23},{7,22},{8,25},{9,... | collective-permute-start | bytes 196616 | tf_op jit(solution)/shard_map/ppermute | solution.py:641
  20.4 0.3 collective-permute-start.3
  20.7 0.7 %collective-permute-done.4 = f32[128,128]{1,0:T(8,128)S(1)} collective-permute-done((f32[128,128]{1,0:T(8,128)S(1)}, f32[128,128]{1,0:T(8,128)S(1)}, u32[]{:S(2)}, u32[]{:S(2)}) %collective-permute-start.4) | collective-permute-done | bytes 65568 | tf_op jit(solution)/shard_map/ppermute | solution.py:641
  21.4 2.7 %collective-permute-done.5 = f32[128,128]{1,0:T(8,128)S(1)} collective-permute-done((f32[128,128]{1,0:T(8,128)S(1)}, f32[128,128]{1,0:T(8,128)S(1)}, u32[]{:S(2)}, u32[]{:S(2)}) %collective-permute-start.5) | collective-permute-done | bytes 65568 | tf_op jit(solution)/shard_map/ppermute | solution.py:641
  24.1 0.0 copy-start
  24.2 0.1 collective-permute-start.6
  24.3 0.0 copy-start.1
  24.3 1.1 %collective-permute-done.3.beside_ref = f32[248,128]{1,0:T(8,128)S(1)} collective-permute-done((f32[248,128]{1,0:T(8,128)S(1)}, f32[248,128]{1,0:T(8,128)S(1)}, u32[]{:S(2)}, u32[]{:S(2)}) %collective-permute-start.3) | collective-permute-done | bytes 127008 | tf_op jit(solution)/shard_map/ppermute | solution.py:641
  25.4 0.1 collective-permute-start.7
  25.5 0.2 shard_map.59
  25.7 1.1 %collective-permute-done.7.refs_3_ = f32[128,128]{1,0:T(8,128)S(1)} collective-permute-done((f32[128,128]{1,0:T(8,128)S(1)}, f32[128,128]{1,0:T(8,128)S(1)}, u32[]{:S(2)}, u32[]{:S(2)}) %collective-permute-start.7) | collective-permute-done | bytes 65568 | tf_op jit(solution)/shard_map/ppermute | solution.py:24
  26.7 0.0 collective-permute-done.6.refs_2_
  26.7 4.1 %shard_map.60 = f32[20,1,1600]{2,1,0:T(1,128)} custom-call(s32[1]{0:T(128)} %bitcast.slab_ref, f32[8,128]{1,0:T(8,128)S(1)} %get-tuple-element.12.code_ref, f32[8,128]{1,0:T(8,128)S(1)} %get-tuple-element.17.mean_ref, f32[10,56,128]{2,1,0:T(8,128)S(1)} %get-tuple-element.18.field_ref, f32[10,40,128]{2,1,0:T(8,128)S(1)} %get-tuple-element.14.coef_ref.start_coef_ref, ...), custom_call_target="tpu_custom_call" | custom-call | tf_op jit(solution)/shard_map/pallas_call | solution.py:669
  (10 shorter events, 0.1 us)
Async XLA Ops:
  0.8 5.1 %collective-permute-start = (f32[8,1,1600]{2,1,0:T(1,128)S(1)}, f32[8,1,1600]{2,1,0:T(1,128)S(1)}, u32[]{:S(2)}, u32[]{:S(2)}) collective-permute-start(f32[8,1,1600]{2,1,0:T(1,128)S(1)} %shard_map.56), channel_id=1, source_target_pairs={{0,1},{1,0},{2,3},{3,2},{4,5},{5,4},{6,7},{7,6},{8,9},{9,8},{10,11... | collective-permute-start | bytes 153608 | tf_op jit(solution)/shard_map/ppermute | solution.py:24
  7.2 4.4 %collective-permute-start.1 = (f32[128,128]{1,0:T(8,128)S(1)}, f32[128,128]{1,0:T(8,128)S(1)}, u32[]{:S(2)}, u32[]{:S(2)}) collective-permute-start(f32[128,128]{1,0:T(8,128)S(1)} %get-tuple-element.16), channel_id=1, source_target_pairs={{0,2},{1,3},{2,0},{3,1},{4,6},{5,7},{6,4},{7,5},{8,10},{9,11},{10,... | collective-permute-start | bytes 196616 | tf_op jit(solution)/shard_map/ppermute | solution.py:24
  11.7 5.3 %collective-permute-start.2 = (f32[128,128]{1,0:T(8,128)S(1)}, f32[128,128]{1,0:T(8,128)S(1)}, u32[]{:S(2)}, u32[]{:S(2)}) collective-permute-start(f32[128,128]{1,0:T(8,128)S(1)} %add.11), channel_id=1, source_target_pairs={{0,4},{1,5},{2,6},{3,7},{4,0},{5,1},{6,2},{7,3},{8,12},{9,13},{10,... | collective-permute-start | bytes 196616 | tf_op jit(solution)/shard_map/ppermute | solution.py:24
  17.0 4.3 %collective-permute-start.4 = (f32[128,128]{1,0:T(8,128)S(1)}, f32[128,128]{1,0:T(8,128)S(1)}, u32[]{:S(2)}, u32[]{:S(2)}) collective-permute-start(f32[128,128]{1,0:T(8,128)S(1)} %add.12), channel_id=1, source_target_pairs={{0,16},{1,17},{2,18},{3,19},{4,20},{5,21},{6,22},{7,23},{8,24},{9,... | collective-permute-start | bytes 196616 | tf_op jit(solution)/shard_map/ppermute | solution.py:641
  18.9 5.2 %collective-permute-start.5 = (f32[128,128]{1,0:T(8,128)S(1)}, f32[128,128]{1,0:T(8,128)S(1)}, u32[]{:S(2)}, u32[]{:S(2)}) collective-permute-start(f32[128,128]{1,0:T(8,128)S(1)} %add.12), channel_id=1, source_target_pairs={{0,17},{1,16},{2,19},{3,18},{4,21},{5,20},{6,23},{7,22},{8,25},{9,... | collective-permute-start | bytes 196616 | tf_op jit(solution)/shard_map/ppermute | solution.py:641
  20.4 5.0 %collective-permute-start.3 = (f32[248,128]{1,0:T(8,128)S(1)}, f32[248,128]{1,0:T(8,128)S(1)}, u32[]{:S(2)}, u32[]{:S(2)}) collective-permute-start(f32[248,128]{1,0:T(8,128)S(1)} %pad_maximum_fusion.3), channel_id=1, source_target_pairs={{0,1},{1,0},{2,3},{3,2},{4,5},{5,4},{6,7},{7,6},{8,9},{9,8},{10,11... | collective-permute-start | bytes 380936 | tf_op jit(solution)/shard_map/ppermute | solution.py:641
  24.1 2.6 %copy-start = (bf16[768,512]{1,0:T(8,128)(2,1)S(1)}, bf16[768,512]{1,0:T(8,128)(2,1)}, u32[]{:S(2)}) copy-start(bf16[768,512]{1,0:T(8,128)(2,1)} %constant.26.clone.table_ref) | copy-start | bytes 2359300
  24.2 2.6 %collective-permute-start.6 = (f32[384,128]{1,0:T(8,128)S(1)}, f32[384,128]{1,0:T(8,128)S(1)}, u32[]{:S(2)}, u32[]{:S(2)}) collective-permute-start(f32[384,128]{1,0:T(8,128)S(1)} %pad_maximum_fusion), channel_id=1, source_target_pairs={{0,8},{8,0},{16,24},{24,16},{1,9},{9,1},{17,25},{25,17},{2,10},{10... | collective-permute-start | bytes 589832 | tf_op jit(solution)/shard_map/ppermute | solution.py:24
  24.3 2.5 %copy-start.1 = (f32[1024,128]{1,0:T(8,128)S(1)}, f32[1024,128]{1,0:T(8,128)}, u32[]{:S(2)}) copy-start(f32[1024,128]{1,0:T(8,128)} %constant.27.clone.factor_ref) | copy-start | bytes 1572868
  25.4 1.3 %collective-permute-start.7 = (f32[128,128]{1,0:T(8,128)S(1)}, f32[128,128]{1,0:T(8,128)S(1)}, u32[]{:S(2)}, u32[]{:S(2)}) collective-permute-start(f32[128,128]{1,0:T(8,128)S(1)} %get-tuple-element.23), channel_id=1, source_target_pairs={{0,8},{8,0},{16,24},{24,16},{1,9},{9,1},{17,25},{25,17},{2,10},{10... | collective-permute-start | bytes 196616 | tf_op jit(solution)/shard_map/ppermute | solution.py:24

commit v13 on v12

--- a/solution.py
+++ b/solution.py
@@ -368,7 +368,7 @@
 ):
     gathered_refs, refs = refs[:dom_count], refs[dom_count:]
     (
-        out_ref, cubes_ref, one_ref, two_ref, coef_ref, left_ref, rows_ref, waves_ref, mixed_ref, flat_ref,
+        out_ref, cubes_ref, one_ref, two_ref, coef_ref, rows_ref, waves_ref, mixed_ref, flat_ref,
         near_dens_ref, own_ref,
     ) = refs
     side, half, span = pk.side, pk.half, pk.span
@@ -676,13 +676,12 @@
             padded_field,
             padded_field,
             pltpu.VMEM(pk.shape, f32),
-            pltpu.VMEM((4 * CORE * 8, dom_count // 4 * 3 * 128), bf16),
             pltpu.VMEM((lanes // 128, CORE * pitch, 128), f32),
             pltpu.VMEM((lanes // 128, CORE * pitch, 128), f32),
             pltpu.VMEM((lanes // 128, CORE * pitch, 128), f32),
             pltpu.VMEM((pk.blocks, pk.depth * side, lanes), f32),
             pltpu.VMEM((dom_count // 4, pk.depth * side, 128), f32),
-            pltpu.VMEM((half * side, 128), f32),
+            pltpu.VMEM((padded(half, 8) * side, 128), f32),
         ],
         compiler_params=params,
     )(

time: 31 us -> 31 us (level)
  no operation moved by 1% of the time
where the time goes in v13:
time: 31 us; the launch traced here: 30.8 us
  starting transfers between devices  12 us (39%)
  waiting for transfers between devices  10.2 us (33%)
  Pallas kernels  8.37 us (27%)
    ppermute x5, starting transfers between devices, swapped(): return lax.ppermute(value, axis, pairs)  8.41 us
    ppermute x5, waiting for transfers between devices, swapped(): return lax.ppermute(value, axis, pairs)  5.64 us
    ppermute x3, waiting for transfers between devices, crossed(): lax.ppermute(value, both, [(source, source ^ mask) for source in range(co...  4.56 us
    pallas_call x1, Pallas kernels, local(): pl.pallas_call(functools.partial(second_kernel, pk, dom_count), out_shape...  4.1 us
    ppermute x3, starting transfers between devices, crossed(): lax.ppermute(value, both, [(source, source ^ mask) for source in range(co...  3.62 us
    pallas_call x1, Pallas kernels, local(): pl.pallas_call(functools.partial(start_kernel, pk, masks), out_shape=(fie...  1.9 us
    pallas_call x1, Pallas kernels, local(): pl.pallas_call(functools.partial(first_kernel, pk, bands), out_shape=(pad...  1.29 us
    pallas_call x1, Pallas kernels, local(): pl.pallas_call(functools.partial(edge_kernel, pk), out_shape=in_vmem(DEG,...  0.82 us
  transfers between devices with their start and end apart: 8, of which 7 were waited for; matrix products, arithmetic and copies ran while one was open for 0% of the time, Pallas kernels for 7%

profile of v13, /device:TPU:0, one launch (start us, length us, event | category | flops | bytes accessed | tf_op | source)
XLA Modules:
  0.0 30.8 jit_solution(5658329852624602873)
XLA Ops:
  0.0 0.8 %shard_map.56 = f32[8,1,1600]{2,1,0:T(1,128)S(1)} custom-call(s32[1]{0:T(128)} %bitcast.slab_ref, f32[20,1,1600]{2,1,0:T(1,128)} %bitcast.7), custom_call_target="tpu_custom_call" | custom-call | tf_op jit(solution)/shard_map/pallas_call | solution.py:583
  0.8 3.0 %collective-permute-start = (f32[8,1,1600]{2,1,0:T(1,128)S(1)}, f32[8,1,1600]{2,1,0:T(1,128)S(1)}, u32[]{:S(2)}, u32[]{:S(2)}) collective-permute-start(f32[8,1,1600]{2,1,0:T(1,128)S(1)} %shard_map.56), channel_id=1, source_target_pairs={{0,1},{1,0},{2,3},{3,2},{4,5},{5,4},{6,7},{7,6},{8,9},{9,8},{10,11... | collective-permute-start | bytes 153608 | tf_op jit(solution)/shard_map/ppermute | solution.py:24
  3.8 1.9 %shard_map.55 = (f32[10,40,128]{2,1,0:T(8,128)S(1)}, f32[10,40,128]{2,1,0:T(8,128)S(1)}, f32[8,128]{1,0:T(8,128)S(1)}) custom-call(s32[1]{0:T(128)} %bitcast.slab_ref, s32[1]{0:T(128)} %bitcast.1.dom_ref, f32[20,1,1600]{2,1,0:T(1,128)} %bitcast.8, f32[40,1600]{1,0:T(8,128)} %bitcast.9, s32[4,3]{1,0:T(4,128)} %offsets_in_ref.1), custom_call_target="tpu_custom_call" | custom-call | tf_op jit(solution)/shard_map/pallas_call | solution.py:598
  5.7 0.2 collective-permute-done.halo_ref
  5.9 1.3 %shard_map.57 = (f32[10,56,128]{2,1,0:T(8,128)S(1)}, f32[128,128]{1,0:T(8,128)S(1)}) custom-call(s32[1]{0:T(128)} %bitcast.slab_ref, f32[10,40,128]{2,1,0:T(8,128)S(1)} %get-tuple-element.13.start_ref, f32[8,1,1600]{2,1,0:T(1,128)S(1)} %collective-permute-done.halo_ref, f32[10,40,128]{2,1,0:T(8,128)S(1)} %get-tuple-element.14.coef_ref.start_coef_ref), custom_call_target="tpu_custom_call" | custom-call | tf_op jit(solution)/shard_map/pallas_call | solution.py:615
  7.2 2.2 %collective-permute-start.1 = (f32[128,128]{1,0:T(8,128)S(1)}, f32[128,128]{1,0:T(8,128)S(1)}, u32[]{:S(2)}, u32[]{:S(2)}) collective-permute-start(f32[128,128]{1,0:T(8,128)S(1)} %get-tuple-element.16), channel_id=1, source_target_pairs={{0,2},{1,3},{2,0},{3,1},{4,6},{5,7},{6,4},{7,5},{8,10},{9,11},{10,... | collective-permute-start | bytes 196616 | tf_op jit(solution)/shard_map/ppermute | solution.py:24
  9.4 2.2 %collective-permute-done.1 = f32[128,128]{1,0:T(8,128)S(1)} collective-permute-done((f32[128,128]{1,0:T(8,128)S(1)}, f32[128,128]{1,0:T(8,128)S(1)}, u32[]{:S(2)}, u32[]{:S(2)}) %collective-permute-start.1) | collective-permute-done | bytes 65568 | tf_op jit(solution)/shard_map/ppermute | solution.py:24
  11.7 3.1 %collective-permute-start.2 = (f32[128,128]{1,0:T(8,128)S(1)}, f32[128,128]{1,0:T(8,128)S(1)}, u32[]{:S(2)}, u32[]{:S(2)}) collective-permute-start(f32[128,128]{1,0:T(8,128)S(1)} %add.11), channel_id=1, source_target_pairs={{0,4},{1,5},{2,6},{3,7},{4,0},{5,1},{6,2},{7,3},{8,12},{9,13},{10,... | collective-permute-start | bytes 196616 | tf_op jit(solution)/shard_map/ppermute | solution.py:24
  14.8 0.1 shard_map.58
  14.9 2.1 %collective-permute-done.2 = f32[128,128]{1,0:T(8,128)S(1)} collective-permute-done((f32[128,128]{1,0:T(8,128)S(1)}, f32[128,128]{1,0:T(8,128)S(1)}, u32[]{:S(2)}, u32[]{:S(2)}) %collective-permute-start.2) | collective-permute-done | bytes 65568 | tf_op jit(solution)/shard_map/ppermute | solution.py:24
  17.0 1.9 %collective-permute-start.4 = (f32[128,128]{1,0:T(8,128)S(1)}, f32[128,128]{1,0:T(8,128)S(1)}, u32[]{:S(2)}, u32[]{:S(2)}) collective-permute-start(f32[128,128]{1,0:T(8,128)S(1)} %add.12), channel_id=1, source_target_pairs={{0,16},{1,17},{2,18},{3,19},{4,20},{5,21},{6,22},{7,23},{8,24},{9,... | collective-permute-start | bytes 196616 | tf_op jit(solution)/shard_map/ppermute | solution.py:641
  18.9 1.4 %collective-permute-start.5 = (f32[128,128]{1,0:T(8,128)S(1)}, f32[128,128]{1,0:T(8,128)S(1)}, u32[]{:S(2)}, u32[]{:S(2)}) collective-permute-start(f32[128,128]{1,0:T(8,128)S(1)} %add.12), channel_id=1, source_target_pairs={{0,17},{1,16},{2,19},{3,18},{4,21},{5,20},{6,23},{7,22},{8,25},{9,... | collective-permute-start | bytes 196616 | tf_op jit(solution)/shard_map/ppermute | solution.py:641
  20.4 0.3 collective-permute-start.3
  20.7 0.7 %collective-permute-done.4 = f32[128,128]{1,0:T(8,128)S(1)} collective-permute-done((f32[128,128]{1,0:T(8,128)S(1)}, f32[128,128]{1,0:T(8,128)S(1)}, u32[]{:S(2)}, u32[]{:S(2)}) %collective-permute-start.4) | collective-permute-done | bytes 65568 | tf_op jit(solution)/shard_map/ppermute | solution.py:641
  21.4 2.7 %collective-permute-done.5 = f32[128,128]{1,0:T(8,128)S(1)} collective-permute-done((f32[128,128]{1,0:T(8,128)S(1)}, f32[128,128]{1,0:T(8,128)S(1)}, u32[]{:S(2)}, u32[]{:S(2)}) %collective-permute-start.5) | collective-permute-done | bytes 65568 | tf_op jit(solution)/shard_map/ppermute | solution.py:641
  24.1 0.0 copy-start
  24.2 0.1 collective-permute-start.6
  24.3 0.0 copy-start.1
  24.3 1.1 %collective-permute-done.3.beside_ref = f32[248,128]{1,0:T(8,128)S(1)} collective-permute-done((f32[248,128]{1,0:T(8,128)S(1)}, f32[248,128]{1,0:T(8,128)S(1)}, u32[]{:S(2)}, u32[]{:S(2)}) %collective-permute-start.3) | collective-permute-done | bytes 127008 | tf_op jit(solution)/shard_map/ppermute | solution.py:641
  25.4 0.1 collective-permute-start.7
  25.5 0.2 shard_map.59
  25.7 1.1 %collective-permute-done.7.refs_3_ = f32[128,128]{1,0:T(8,128)S(1)} collective-permute-done((f32[128,128]{1,0:T(8,128)S(1)}, f32[128,128]{1,0:T(8,128)S(1)}, u32[]{:S(2)}, u32[]{:S(2)}) %collective-permute-start.7) | collective-permute-done | bytes 65568 | tf_op jit(solution)/shard_map/ppermute | solution.py:24
  26.7 0.0 collective-permute-done.6.refs_2_
  26.7 4.1 %shard_map.60 = f32[20,1,1600]{2,1,0:T(1,128)} custom-call(s32[1]{0:T(128)} %bitcast.slab_ref, f32[8,128]{1,0:T(8,128)S(1)} %get-tuple-element.12.code_ref, f32[8,128]{1,0:T(8,128)S(1)} %get-tuple-element.17.mean_ref, f32[10,56,128]{2,1,0:T(8,128)S(1)} %get-tuple-element.18.field_ref, f32[10,40,128]{2,1,0:T(8,128)S(1)} %get-tuple-element.14.coef_ref.start_coef_ref, ...), custom_call_target="tpu_custom_call" | custom-call | tf_op jit(solution)/shard_map/pallas_call | solution.py:669
  (10 shorter events, 0.1 us)
Async XLA Ops:
  0.8 5.1 %collective-permute-start = (f32[8,1,1600]{2,1,0:T(1,128)S(1)}, f32[8,1,1600]{2,1,0:T(1,128)S(1)}, u32[]{:S(2)}, u32[]{:S(2)}) collective-permute-start(f32[8,1,1600]{2,1,0:T(1,128)S(1)} %shard_map.56), channel_id=1, source_target_pairs={{0,1},{1,0},{2,3},{3,2},{4,5},{5,4},{6,7},{7,6},{8,9},{9,8},{10,11... | collective-permute-start | bytes 153608 | tf_op jit(solution)/shard_map/ppermute | solution.py:24
  7.2 4.4 %collective-permute-start.1 = (f32[128,128]{1,0:T(8,128)S(1)}, f32[128,128]{1,0:T(8,128)S(1)}, u32[]{:S(2)}, u32[]{:S(2)}) collective-permute-start(f32[128,128]{1,0:T(8,128)S(1)} %get-tuple-element.16), channel_id=1, source_target_pairs={{0,2},{1,3},{2,0},{3,1},{4,6},{5,7},{6,4},{7,5},{8,10},{9,11},{10,... | collective-permute-start | bytes 196616 | tf_op jit(solution)/shard_map/ppermute | solution.py:24
  11.7 5.3 %collective-permute-start.2 = (f32[128,128]{1,0:T(8,128)S(1)}, f32[128,128]{1,0:T(8,128)S(1)}, u32[]{:S(2)}, u32[]{:S(2)}) collective-permute-start(f32[128,128]{1,0:T(8,128)S(1)} %add.11), channel_id=1, source_target_pairs={{0,4},{1,5},{2,6},{3,7},{4,0},{5,1},{6,2},{7,3},{8,12},{9,13},{10,... | collective-permute-start | bytes 196616 | tf_op jit(solution)/shard_map/ppermute | solution.py:24
  17.0 4.3 %collective-permute-start.4 = (f32[128,128]{1,0:T(8,128)S(1)}, f32[128,128]{1,0:T(8,128)S(1)}, u32[]{:S(2)}, u32[]{:S(2)}) collective-permute-start(f32[128,128]{1,0:T(8,128)S(1)} %add.12), channel_id=1, source_target_pairs={{0,16},{1,17},{2,18},{3,19},{4,20},{5,21},{6,22},{7,23},{8,24},{9,... | collective-permute-start | bytes 196616 | tf_op jit(solution)/shard_map/ppermute | solution.py:641
  18.9 5.2 %collective-permute-start.5 = (f32[128,128]{1,0:T(8,128)S(1)}, f32[128,128]{1,0:T(8,128)S(1)}, u32[]{:S(2)}, u32[]{:S(2)}) collective-permute-start(f32[128,128]{1,0:T(8,128)S(1)} %add.12), channel_id=1, source_target_pairs={{0,17},{1,16},{2,19},{3,18},{4,21},{5,20},{6,23},{7,22},{8,25},{9,... | collective-permute-start | bytes 196616 | tf_op jit(solution)/shard_map/ppermute | solution.py:641
  20.4 5.0 %collective-permute-start.3 = (f32[248,128]{1,0:T(8,128)S(1)}, f32[248,128]{1,0:T(8,128)S(1)}, u32[]{:S(2)}, u32[]{:S(2)}) collective-permute-start(f32[248,128]{1,0:T(8,128)S(1)} %pad_maximum_fusion.3), channel_id=1, source_target_pairs={{0,1},{1,0},{2,3},{3,2},{4,5},{5,4},{6,7},{7,6},{8,9},{9,8},{10,11... | collective-permute-start | bytes 380936 | tf_op jit(solution)/shard_map/ppermute | solution.py:641
  24.1 2.6 %copy-start = (bf16[768,512]{1,0:T(8,128)(2,1)S(1)}, bf16[768,512]{1,0:T(8,128)(2,1)}, u32[]{:S(2)}) copy-start(bf16[768,512]{1,0:T(8,128)(2,1)} %constant.26.clone.table_ref) | copy-start | bytes 2359300
  24.2 2.6 %collective-permute-start.6 = (f32[384,128]{1,0:T(8,128)S(1)}, f32[384,128]{1,0:T(8,128)S(1)}, u32[]{:S(2)}, u32[]{:S(2)}) collective-permute-start(f32[384,128]{1,0:T(8,128)S(1)} %pad_maximum_fusion), channel_id=1, source_target_pairs={{0,8},{8,0},{16,24},{24,16},{1,9},{9,1},{17,25},{25,17},{2,10},{10... | collective-permute-start | bytes 589832 | tf_op jit(solution)/shard_map/ppermute | solution.py:24
  24.3 2.5 %copy-start.1 = (f32[1024,128]{1,0:T(8,128)S(1)}, f32[1024,128]{1,0:T(8,128)}, u32[]{:S(2)}) copy-start(f32[1024,128]{1,0:T(8,128)} %constant.27.clone.factor_ref) | copy-start | bytes 1572868
  25.4 1.3 %collective-permute-start.7 = (f32[128,128]{1,0:T(8,128)S(1)}, f32[128,128]{1,0:T(8,128)S(1)}, u32[]{:S(2)}, u32[]{:S(2)}) collective-permute-start(f32[128,128]{1,0:T(8,128)S(1)} %get-tuple-element.23), channel_id=1, source_target_pairs={{0,8},{8,0},{16,24},{24,16},{1,9},{9,1},{17,25},{25,17},{2,10},{10... | collective-permute-start | bytes 196616 | tf_op jit(solution)/shard_map/ppermute | solution.py:24

commit v14 on v13

--- a/solution.py
+++ b/solution.py
@@ -126,7 +126,7 @@
     def _():
         flat_ref[DEG : DEG + half] = own
 
-    pack(pk, flat_ref[...], pitched_ref, field_ref)
+    pack(pk, flat_ref[0 : pk.rows], pitched_ref, field_ref)
     copy.wait()
 
     @pl.when(is_lower)
@@ -137,7 +137,7 @@
     def _():
         flat_ref[0 : pk.rows] = pot_ref[side - pk.rows : side] * (2.0 / HALF_WIDTH)
 
-    pack(pk, flat_ref[...], pitched_ref, coef_ref)
+    pack(pk, flat_ref[0 : pk.rows], pitched_ref, coef_ref)
 
     offsets_copy.wait()
     dom, dom_count = dom_ref[0], len(masks)
@@ -514,7 +514,7 @@
     hartree = product[:, 0:128] + product[:, 128:256]
     pieces = []
     for at_z in range(blocks_z):
-        pieces += split3(near_dens_ref[at_z])
+        pieces += split3(near_dens_ref[at_z, 0 : pk.depth * side])
     density = dot(jnp.concatenate(pieces, 1), table_ref[blocks_z * 3 * 128 : blocks_z * 6 * 128, 256:384])
     added = (hartree + EXCHANGE_COEF * cube_root(density)) * (2.0 / HALF_WIDTH)
     for level in range(pk.depth):
@@ -601,7 +601,7 @@
         in_specs=[SMEM, SMEM, HBM, HBM, HBM],
         out_specs=(VMEM, VMEM, VMEM),
         scratch_shapes=[
-            pltpu.VMEM((pk.rows, cells), f32),
+            pltpu.VMEM((padded(pk.rows, 8), cells), f32),
             pltpu.VMEM((side * pk.pitch, 128), f32),
             pltpu.VMEM((half, 1, cells), f32),
             pltpu.VMEM((side, cells), f32),
@@ -680,7 +680,7 @@
             pltpu.VMEM((lanes // 128, CORE * pitch, 128), f32),
             pltpu.VMEM((lanes // 128, CORE * pitch, 128), f32),
             pltpu.VMEM((pk.blocks, pk.depth * side, lanes), f32),
-            pltpu.VMEM((dom_count // 4, pk.depth * side, 128), f32),
+            pltpu.VMEM((dom_count // 4, pk.depth * side + 8, 128), f32),
             pltpu.VMEM((padded(half, 8) * side, 128), f32),
         ],
         compiler_params=params,

time: 31 us -> 31 us (level)
  no operation moved by 1% of the time
where the time goes in v14:
time: 31 us; the launch traced here: 30.8 us
  starting transfers between devices  12 us (39%)
  waiting for transfers between devices  10.2 us (33%)
  Pallas kernels  8.37 us (27%)
    ppermute x5, starting transfers between devices, swapped(): return lax.ppermute(value, axis, pairs)  8.41 us
    ppermute x5, waiting for transfers between devices, swapped(): return lax.ppermute(value, axis, pairs)  5.64 us
    ppermute x3, waiting for transfers between devices, crossed(): lax.ppermute(value, both, [(source, source ^ mask) for source in range(co...  4.56 us
    pallas_call x1, Pallas kernels, local(): pl.pallas_call(functools.partial(second_kernel, pk, dom_count), out_shape...  4.11 us
    ppermute x3, starting transfers between devices, crossed(): lax.ppermute(value, both, [(source, source ^ mask) for source in range(co...  3.62 us
    pallas_call x1, Pallas kernels, local(): pl.pallas_call(functools.partial(start_kernel, pk, masks), out_shape=(fie...  1.9 us
    pallas_call x1, Pallas kernels, local(): pl.pallas_call(functools.partial(first_kernel, pk, bands), out_shape=(pad...  1.29 us
    pallas_call x1, Pallas kernels, local(): pl.pallas_call(functools.partial(edge_kernel, pk), out_shape=in_vmem(DEG,...  0.82 us
  transfers between devices with their start and end apart: 8, of which 7 were waited for; matrix products, arithmetic and copies ran while one was open for 0% of the time, Pallas kernels for 7%

profile of v14, /device:TPU:0, one launch (start us, length us, event | category | flops | bytes accessed | tf_op | source)
XLA Modules:
  0.0 30.8 jit_solution(14737651920467129475)
XLA Ops:
  0.0 0.8 %shard_map.56 = f32[8,1,1600]{2,1,0:T(1,128)S(1)} custom-call(s32[1]{0:T(128)} %bitcast.slab_ref, f32[20,1,1600]{2,1,0:T(1,128)} %bitcast.7), custom_call_target="tpu_custom_call" | custom-call | tf_op jit(solution)/shard_map/pallas_call | solution.py:583
  0.8 3.0 %collective-permute-start = (f32[8,1,1600]{2,1,0:T(1,128)S(1)}, f32[8,1,1600]{2,1,0:T(1,128)S(1)}, u32[]{:S(2)}, u32[]{:S(2)}) collective-permute-start(f32[8,1,1600]{2,1,0:T(1,128)S(1)} %shard_map.56), channel_id=1, source_target_pairs={{0,1},{1,0},{2,3},{3,2},{4,5},{5,4},{6,7},{7,6},{8,9},{9,8},{10,11... | collective-permute-start | bytes 153608 | tf_op jit(solution)/shard_map/ppermute | solution.py:24
  3.8 1.9 %shard_map.55 = (f32[10,40,128]{2,1,0:T(8,128)S(1)}, f32[10,40,128]{2,1,0:T(8,128)S(1)}, f32[8,128]{1,0:T(8,128)S(1)}) custom-call(s32[1]{0:T(128)} %bitcast.slab_ref, s32[1]{0:T(128)} %bitcast.1.dom_ref, f32[20,1,1600]{2,1,0:T(1,128)} %bitcast.8, f32[40,1600]{1,0:T(8,128)} %bitcast.9, s32[4,3]{1,0:T(4,128)} %offsets_in_ref.1), custom_call_target="tpu_custom_call" | custom-call | tf_op jit(solution)/shard_map/pallas_call | solution.py:598
  5.7 0.2 collective-permute-done.halo_ref
  5.9 1.3 %shard_map.57 = (f32[10,56,128]{2,1,0:T(8,128)S(1)}, f32[128,128]{1,0:T(8,128)S(1)}) custom-call(s32[1]{0:T(128)} %bitcast.slab_ref, f32[10,40,128]{2,1,0:T(8,128)S(1)} %get-tuple-element.13.start_ref, f32[8,1,1600]{2,1,0:T(1,128)S(1)} %collective-permute-done.halo_ref, f32[10,40,128]{2,1,0:T(8,128)S(1)} %get-tuple-element.14.coef_ref.start_coef_ref), custom_call_target="tpu_custom_call" | custom-call | tf_op jit(solution)/shard_map/pallas_call | solution.py:615
  7.2 2.2 %collective-permute-start.1 = (f32[128,128]{1,0:T(8,128)S(1)}, f32[128,128]{1,0:T(8,128)S(1)}, u32[]{:S(2)}, u32[]{:S(2)}) collective-permute-start(f32[128,128]{1,0:T(8,128)S(1)} %get-tuple-element.16), channel_id=1, source_target_pairs={{0,2},{1,3},{2,0},{3,1},{4,6},{5,7},{6,4},{7,5},{8,10},{9,11},{10,... | collective-permute-start | bytes 196616 | tf_op jit(solution)/shard_map/ppermute | solution.py:24
  9.4 2.2 %collective-permute-done.1 = f32[128,128]{1,0:T(8,128)S(1)} collective-permute-done((f32[128,128]{1,0:T(8,128)S(1)}, f32[128,128]{1,0:T(8,128)S(1)}, u32[]{:S(2)}, u32[]{:S(2)}) %collective-permute-start.1) | collective-permute-done | bytes 65568 | tf_op jit(solution)/shard_map/ppermute | solution.py:24
  11.7 3.1 %collective-permute-start.2 = (f32[128,128]{1,0:T(8,128)S(1)}, f32[128,128]{1,0:T(8,128)S(1)}, u32[]{:S(2)}, u32[]{:S(2)}) collective-permute-start(f32[128,128]{1,0:T(8,128)S(1)} %add.11), channel_id=1, source_target_pairs={{0,4},{1,5},{2,6},{3,7},{4,0},{5,1},{6,2},{7,3},{8,12},{9,13},{10,... | collective-permute-start | bytes 196616 | tf_op jit(solution)/shard_map/ppermute | solution.py:24
  14.8 0.1 shard_map.58
  14.9 2.1 %collective-permute-done.2 = f32[128,128]{1,0:T(8,128)S(1)} collective-permute-done((f32[128,128]{1,0:T(8,128)S(1)}, f32[128,128]{1,0:T(8,128)S(1)}, u32[]{:S(2)}, u32[]{:S(2)}) %collective-permute-start.2) | collective-permute-done | bytes 65568 | tf_op jit(solution)/shard_map/ppermute | solution.py:24
  17.0 1.9 %collective-permute-start.4 = (f32[128,128]{1,0:T(8,128)S(1)}, f32[128,128]{1,0:T(8,128)S(1)}, u32[]{:S(2)}, u32[]{:S(2)}) collective-permute-start(f32[128,128]{1,0:T(8,128)S(1)} %add.12), channel_id=1, source_target_pairs={{0,16},{1,17},{2,18},{3,19},{4,20},{5,21},{6,22},{7,23},{8,24},{9,... | collective-permute-start | bytes 196616 | tf_op jit(solution)/shard_map/ppermute | solution.py:641
  18.9 1.4 %collective-permute-start.5 = (f32[128,128]{1,0:T(8,128)S(1)}, f32[128,128]{1,0:T(8,128)S(1)}, u32[]{:S(2)}, u32[]{:S(2)}) collective-permute-start(f32[128,128]{1,0:T(8,128)S(1)} %add.12), channel_id=1, source_target_pairs={{0,17},{1,16},{2,19},{3,18},{4,21},{5,20},{6,23},{7,22},{8,25},{9,... | collective-permute-start | bytes 196616 | tf_op jit(solution)/shard_map/ppermute | solution.py:641
  20.4 0.3 collective-permute-start.3
  20.7 0.7 %collective-permute-done.4 = f32[128,128]{1,0:T(8,128)S(1)} collective-permute-done((f32[128,128]{1,0:T(8,128)S(1)}, f32[128,128]{1,0:T(8,128)S(1)}, u32[]{:S(2)}, u32[]{:S(2)}) %collective-permute-start.4) | collective-permute-done | bytes 65568 | tf_op jit(solution)/shard_map/ppermute | solution.py:641
  21.4 2.7 %collective-permute-done.5 = f32[128,128]{1,0:T(8,128)S(1)} collective-permute-done((f32[128,128]{1,0:T(8,128)S(1)}, f32[128,128]{1,0:T(8,128)S(1)}, u32[]{:S(2)}, u32[]{:S(2)}) %collective-permute-start.5) | collective-permute-done | bytes 65568 | tf_op jit(solution)/shard_map/ppermute | solution.py:641
  24.1 0.0 copy-start
  24.2 0.1 collective-permute-start.6
  24.3 0.0 copy-start.1
  24.3 1.1 %collective-permute-done.3.beside_ref = f32[248,128]{1,0:T(8,128)S(1)} collective-permute-done((f32[248,128]{1,0:T(8,128)S(1)}, f32[248,128]{1,0:T(8,128)S(1)}, u32[]{:S(2)}, u32[]{:S(2)}) %collective-permute-start.3) | collective-permute-done | bytes 127008 | tf_op jit(solution)/shard_map/ppermute | solution.py:641
  25.4 0.1 collective-permute-start.7
  25.5 0.2 shard_map.59
  25.7 1.1 %collective-permute-done.7.refs_3_ = f32[128,128]{1,0:T(8,128)S(1)} collective-permute-done((f32[128,128]{1,0:T(8,128)S(1)}, f32[128,128]{1,0:T(8,128)S(1)}, u32[]{:S(2)}, u32[]{:S(2)}) %collective-permute-start.7) | collective-permute-done | bytes 65568 | tf_op jit(solution)/shard_map/ppermute | solution.py:24
  26.7 0.0 collective-permute-done.6.refs_2_
  26.7 4.1 %shard_map.60 = f32[20,1,1600]{2,1,0:T(1,128)} custom-call(s32[1]{0:T(128)} %bitcast.slab_ref, f32[8,128]{1,0:T(8,128)S(1)} %get-tuple-element.12.code_ref, f32[8,128]{1,0:T(8,128)S(1)} %get-tuple-element.17.mean_ref, f32[10,56,128]{2,1,0:T(8,128)S(1)} %get-tuple-element.18.field_ref, f32[10,40,128]{2,1,0:T(8,128)S(1)} %get-tuple-element.14.coef_ref.start_coef_ref, ...), custom_call_target="tpu_custom_call" | custom-call | tf_op jit(solution)/shard_map/pallas_call | solution.py:669
  (10 shorter events, 0.1 us)
Async XLA Ops:
  0.8 5.1 %collective-permute-start = (f32[8,1,1600]{2,1,0:T(1,128)S(1)}, f32[8,1,1600]{2,1,0:T(1,128)S(1)}, u32[]{:S(2)}, u32[]{:S(2)}) collective-permute-start(f32[8,1,1600]{2,1,0:T(1,128)S(1)} %shard_map.56), channel_id=1, source_target_pairs={{0,1},{1,0},{2,3},{3,2},{4,5},{5,4},{6,7},{7,6},{8,9},{9,8},{10,11... | collective-permute-start | bytes 153608 | tf_op jit(solution)/shard_map/ppermute | solution.py:24
  7.2 4.4 %collective-permute-start.1 = (f32[128,128]{1,0:T(8,128)S(1)}, f32[128,128]{1,0:T(8,128)S(1)}, u32[]{:S(2)}, u32[]{:S(2)}) collective-permute-start(f32[128,128]{1,0:T(8,128)S(1)} %get-tuple-element.16), channel_id=1, source_target_pairs={{0,2},{1,3},{2,0},{3,1},{4,6},{5,7},{6,4},{7,5},{8,10},{9,11},{10,... | collective-permute-start | bytes 196616 | tf_op jit(solution)/shard_map/ppermute | solution.py:24
  11.7 5.3 %collective-permute-start.2 = (f32[128,128]{1,0:T(8,128)S(1)}, f32[128,128]{1,0:T(8,128)S(1)}, u32[]{:S(2)}, u32[]{:S(2)}) collective-permute-start(f32[128,128]{1,0:T(8,128)S(1)} %add.11), channel_id=1, source_target_pairs={{0,4},{1,5},{2,6},{3,7},{4,0},{5,1},{6,2},{7,3},{8,12},{9,13},{10,... | collective-permute-start | bytes 196616 | tf_op jit(solution)/shard_map/ppermute | solution.py:24
  17.0 4.3 %collective-permute-start.4 = (f32[128,128]{1,0:T(8,128)S(1)}, f32[128,128]{1,0:T(8,128)S(1)}, u32[]{:S(2)}, u32[]{:S(2)}) collective-permute-start(f32[128,128]{1,0:T(8,128)S(1)} %add.12), channel_id=1, source_target_pairs={{0,16},{1,17},{2,18},{3,19},{4,20},{5,21},{6,22},{7,23},{8,24},{9,... | collective-permute-start | bytes 196616 | tf_op jit(solution)/shard_map/ppermute | solution.py:641
  18.9 5.2 %collective-permute-start.5 = (f32[128,128]{1,0:T(8,128)S(1)}, f32[128,128]{1,0:T(8,128)S(1)}, u32[]{:S(2)}, u32[]{:S(2)}) collective-permute-start(f32[128,128]{1,0:T(8,128)S(1)} %add.12), channel_id=1, source_target_pairs={{0,17},{1,16},{2,19},{3,18},{4,21},{5,20},{6,23},{7,22},{8,25},{9,... | collective-permute-start | bytes 196616 | tf_op jit(solution)/shard_map/ppermute | solution.py:641
  20.4 5.0 %collective-permute-start.3 = (f32[248,128]{1,0:T(8,128)S(1)}, f32[248,128]{1,0:T(8,128)S(1)}, u32[]{:S(2)}, u32[]{:S(2)}) collective-permute-start(f32[248,128]{1,0:T(8,128)S(1)} %pad_maximum_fusion.3), channel_id=1, source_target_pairs={{0,1},{1,0},{2,3},{3,2},{4,5},{5,4},{6,7},{7,6},{8,9},{9,8},{10,11... | collective-permute-start | bytes 380936 | tf_op jit(solution)/shard_map/ppermute | solution.py:641
  24.1 2.6 %copy-start = (bf16[768,512]{1,0:T(8,128)(2,1)S(1)}, bf16[768,512]{1,0:T(8,128)(2,1)}, u32[]{:S(2)}) copy-start(bf16[768,512]{1,0:T(8,128)(2,1)} %constant.26.clone.table_ref) | copy-start | bytes 2359300
  24.2 2.6 %collective-permute-start.6 = (f32[384,128]{1,0:T(8,128)S(1)}, f32[384,128]{1,0:T(8,128)S(1)}, u32[]{:S(2)}, u32[]{:S(2)}) collective-permute-start(f32[384,128]{1,0:T(8,128)S(1)} %pad_maximum_fusion), channel_id=1, source_target_pairs={{0,8},{8,0},{16,24},{24,16},{1,9},{9,1},{17,25},{25,17},{2,10},{10... | collective-permute-start | bytes 589832 | tf_op jit(solution)/shard_map/ppermute | solution.py:24
  24.3 2.5 %copy-start.1 = (f32[1024,128]{1,0:T(8,128)S(1)}, f32[1024,128]{1,0:T(8,128)}, u32[]{:S(2)}) copy-start(f32[1024,128]{1,0:T(8,128)} %constant.27.clone.factor_ref) | copy-start | bytes 1572868
  25.4 1.3 %collective-permute-start.7 = (f32[128,128]{1,0:T(8,128)S(1)}, f32[128,128]{1,0:T(8,128)S(1)}, u32[]{:S(2)}, u32[]{:S(2)}) collective-permute-start(f32[128,128]{1,0:T(8,128)S(1)} %get-tuple-element.23), channel_id=1, source_target_pairs={{0,8},{8,0},{16,24},{24,16},{1,9},{9,1},{17,25},{25,17},{2,10},{10... | collective-permute-start | bytes 196616 | tf_op jit(solution)/shard_map/ppermute | solution.py:24

commit v15 on v14

--- a/solution.py
+++ b/solution.py
@@ -356,7 +356,7 @@
 
 
 def cube_root(values):
-    positive = values > 0.0
+    positive = values >= np.finfo(np.float32).tiny
     safe = jnp.where(positive, values, 1.0)
     root = jnp.exp(jnp.log(safe) * (1.0 / 3.0))
     root = root - (root - safe / (root * root)) * (1.0 / 3.0)

time: 31 us -> 31 us (level)
  no operation moved by 1% of the time
where the time goes in v15:
time: 31 us; the launch traced here: 30.8 us
  starting transfers between devices  12 us (39%)
  waiting for transfers between devices  10.2 us (33%)
  Pallas kernels  8.37 us (27%)
    ppermute x5, starting transfers between devices, swapped(): return lax.ppermute(value, axis, pairs)  8.41 us
    ppermute x5, waiting for transfers between devices, swapped(): return lax.ppermute(value, axis, pairs)  5.64 us
    ppermute x3, waiting for transfers between devices, crossed(): lax.ppermute(value, both, [(source, source ^ mask) for source in range(co...  4.56 us
    pallas_call x1, Pallas kernels, local(): pl.pallas_call(functools.partial(second_kernel, pk, dom_count), out_shape...  4.11 us
    ppermute x3, starting transfers between devices, crossed(): lax.ppermute(value, both, [(source, source ^ mask) for source in range(co...  3.62 us
    pallas_call x1, Pallas kernels, local(): pl.pallas_call(functools.partial(start_kernel, pk, masks), out_shape=(fie...  1.9 us
    pallas_call x1, Pallas kernels, local(): pl.pallas_call(functools.partial(first_kernel, pk, bands), out_shape=(pad...  1.29 us
    pallas_call x1, Pallas kernels, local(): pl.pallas_call(functools.partial(edge_kernel, pk), out_shape=in_vmem(DEG,...  0.82 us
  transfers between devices with their start and end apart: 8, of which 7 were waited for; matrix products, arithmetic and copies ran while one was open for 0% of the time, Pallas kernels for 7%

profile of v15, /device:TPU:0, one launch (start us, length us, event | category | flops | bytes accessed | tf_op | source)
XLA Modules:
  0.0 30.8 jit_solution(10661189213164784310)
XLA Ops:
  0.0 0.8 %shard_map.56 = f32[8,1,1600]{2,1,0:T(1,128)S(1)} custom-call(s32[1]{0:T(128)} %bitcast.slab_ref, f32[20,1,1600]{2,1,0:T(1,128)} %bitcast.7), custom_call_target="tpu_custom_call" | custom-call | tf_op jit(solution)/shard_map/pallas_call | solution.py:583
  0.8 3.0 %collective-permute-start = (f32[8,1,1600]{2,1,0:T(1,128)S(1)}, f32[8,1,1600]{2,1,0:T(1,128)S(1)}, u32[]{:S(2)}, u32[]{:S(2)}) collective-permute-start(f32[8,1,1600]{2,1,0:T(1,128)S(1)} %shard_map.56), channel_id=1, source_target_pairs={{0,1},{1,0},{2,3},{3,2},{4,5},{5,4},{6,7},{7,6},{8,9},{9,8},{10,11... | collective-permute-start | bytes 153608 | tf_op jit(solution)/shard_map/ppermute | solution.py:24
  3.8 1.9 %shard_map.55 = (f32[10,40,128]{2,1,0:T(8,128)S(1)}, f32[10,40,128]{2,1,0:T(8,128)S(1)}, f32[8,128]{1,0:T(8,128)S(1)}) custom-call(s32[1]{0:T(128)} %bitcast.slab_ref, s32[1]{0:T(128)} %bitcast.1.dom_ref, f32[20,1,1600]{2,1,0:T(1,128)} %bitcast.8, f32[40,1600]{1,0:T(8,128)} %bitcast.9, s32[4,3]{1,0:T(4,128)} %offsets_in_ref.1), custom_call_target="tpu_custom_call" | custom-call | tf_op jit(solution)/shard_map/pallas_call | solution.py:598
  5.7 0.2 collective-permute-done.halo_ref
  5.9 1.3 %shard_map.57 = (f32[10,56,128]{2,1,0:T(8,128)S(1)}, f32[128,128]{1,0:T(8,128)S(1)}) custom-call(s32[1]{0:T(128)} %bitcast.slab_ref, f32[10,40,128]{2,1,0:T(8,128)S(1)} %get-tuple-element.13.start_ref, f32[8,1,1600]{2,1,0:T(1,128)S(1)} %collective-permute-done.halo_ref, f32[10,40,128]{2,1,0:T(8,128)S(1)} %get-tuple-element.14.coef_ref.start_coef_ref), custom_call_target="tpu_custom_call" | custom-call | tf_op jit(solution)/shard_map/pallas_call | solution.py:615
  7.2 2.2 %collective-permute-start.1 = (f32[128,128]{1,0:T(8,128)S(1)}, f32[128,128]{1,0:T(8,128)S(1)}, u32[]{:S(2)}, u32[]{:S(2)}) collective-permute-start(f32[128,128]{1,0:T(8,128)S(1)} %get-tuple-element.16), channel_id=1, source_target_pairs={{0,2},{1,3},{2,0},{3,1},{4,6},{5,7},{6,4},{7,5},{8,10},{9,11},{10,... | collective-permute-start | bytes 196616 | tf_op jit(solution)/shard_map/ppermute | solution.py:24
  9.4 2.2 %collective-permute-done.1 = f32[128,128]{1,0:T(8,128)S(1)} collective-permute-done((f32[128,128]{1,0:T(8,128)S(1)}, f32[128,128]{1,0:T(8,128)S(1)}, u32[]{:S(2)}, u32[]{:S(2)}) %collective-permute-start.1) | collective-permute-done | bytes 65568 | tf_op jit(solution)/shard_map/ppermute | solution.py:24
  11.7 3.1 %collective-permute-start.2 = (f32[128,128]{1,0:T(8,128)S(1)}, f32[128,128]{1,0:T(8,128)S(1)}, u32[]{:S(2)}, u32[]{:S(2)}) collective-permute-start(f32[128,128]{1,0:T(8,128)S(1)} %add.11), channel_id=1, source_target_pairs={{0,4},{1,5},{2,6},{3,7},{4,0},{5,1},{6,2},{7,3},{8,12},{9,13},{10,... | collective-permute-start | bytes 196616 | tf_op jit(solution)/shard_map/ppermute | solution.py:24
  14.8 0.1 shard_map.58
  14.9 2.1 %collective-permute-done.2 = f32[128,128]{1,0:T(8,128)S(1)} collective-permute-done((f32[128,128]{1,0:T(8,128)S(1)}, f32[128,128]{1,0:T(8,128)S(1)}, u32[]{:S(2)}, u32[]{:S(2)}) %collective-permute-start.2) | collective-permute-done | bytes 65568 | tf_op jit(solution)/shard_map/ppermute | solution.py:24
  17.0 1.9 %collective-permute-start.4 = (f32[128,128]{1,0:T(8,128)S(1)}, f32[128,128]{1,0:T(8,128)S(1)}, u32[]{:S(2)}, u32[]{:S(2)}) collective-permute-start(f32[128,128]{1,0:T(8,128)S(1)} %add.12), channel_id=1, source_target_pairs={{0,16},{1,17},{2,18},{3,19},{4,20},{5,21},{6,22},{7,23},{8,24},{9,... | collective-permute-start | bytes 196616 | tf_op jit(solution)/shard_map/ppermute | solution.py:641
  18.9 1.4 %collective-permute-start.5 = (f32[128,128]{1,0:T(8,128)S(1)}, f32[128,128]{1,0:T(8,128)S(1)}, u32[]{:S(2)}, u32[]{:S(2)}) collective-permute-start(f32[128,128]{1,0:T(8,128)S(1)} %add.12), channel_id=1, source_target_pairs={{0,17},{1,16},{2,19},{3,18},{4,21},{5,20},{6,23},{7,22},{8,25},{9,... | collective-permute-start | bytes 196616 | tf_op jit(solution)/shard_map/ppermute | solution.py:641
  20.4 0.3 collective-permute-start.3
  20.7 0.7 %collective-permute-done.4 = f32[128,128]{1,0:T(8,128)S(1)} collective-permute-done((f32[128,128]{1,0:T(8,128)S(1)}, f32[128,128]{1,0:T(8,128)S(1)}, u32[]{:S(2)}, u32[]{:S(2)}) %collective-permute-start.4) | collective-permute-done | bytes 65568 | tf_op jit(solution)/shard_map/ppermute | solution.py:641
  21.4 2.7 %collective-permute-done.5 = f32[128,128]{1,0:T(8,128)S(1)} collective-permute-done((f32[128,128]{1,0:T(8,128)S(1)}, f32[128,128]{1,0:T(8,128)S(1)}, u32[]{:S(2)}, u32[]{:S(2)}) %collective-permute-start.5) | collective-permute-done | bytes 65568 | tf_op jit(solution)/shard_map/ppermute | solution.py:641
  24.1 0.0 copy-start
  24.2 0.1 collective-permute-start.6
  24.3 0.0 copy-start.1
  24.3 1.1 %collective-permute-done.3.beside_ref = f32[248,128]{1,0:T(8,128)S(1)} collective-permute-done((f32[248,128]{1,0:T(8,128)S(1)}, f32[248,128]{1,0:T(8,128)S(1)}, u32[]{:S(2)}, u32[]{:S(2)}) %collective-permute-start.3) | collective-permute-done | bytes 127008 | tf_op jit(solution)/shard_map/ppermute | solution.py:641
  25.4 0.1 collective-permute-start.7
  25.5 0.2 shard_map.59
  25.7 1.1 %collective-permute-done.7.refs_3_ = f32[128,128]{1,0:T(8,128)S(1)} collective-permute-done((f32[128,128]{1,0:T(8,128)S(1)}, f32[128,128]{1,0:T(8,128)S(1)}, u32[]{:S(2)}, u32[]{:S(2)}) %collective-permute-start.7) | collective-permute-done | bytes 65568 | tf_op jit(solution)/shard_map/ppermute | solution.py:24
  26.7 0.0 collective-permute-done.6.refs_2_
  26.7 4.1 %shard_map.60 = f32[20,1,1600]{2,1,0:T(1,128)} custom-call(s32[1]{0:T(128)} %bitcast.slab_ref, f32[8,128]{1,0:T(8,128)S(1)} %get-tuple-element.12.code_ref, f32[8,128]{1,0:T(8,128)S(1)} %get-tuple-element.17.mean_ref, f32[10,56,128]{2,1,0:T(8,128)S(1)} %get-tuple-element.18.field_ref, f32[10,40,128]{2,1,0:T(8,128)S(1)} %get-tuple-element.14.coef_ref.start_coef_ref, ...), custom_call_target="tpu_custom_call" | custom-call | tf_op jit(solution)/shard_map/pallas_call | solution.py:669
  (10 shorter events, 0.1 us)
Async XLA Ops:
  0.8 5.1 %collective-permute-start = (f32[8,1,1600]{2,1,0:T(1,128)S(1)}, f32[8,1,1600]{2,1,0:T(1,128)S(1)}, u32[]{:S(2)}, u32[]{:S(2)}) collective-permute-start(f32[8,1,1600]{2,1,0:T(1,128)S(1)} %shard_map.56), channel_id=1, source_target_pairs={{0,1},{1,0},{2,3},{3,2},{4,5},{5,4},{6,7},{7,6},{8,9},{9,8},{10,11... | collective-permute-start | bytes 153608 | tf_op jit(solution)/shard_map/ppermute | solution.py:24
  7.2 4.4 %collective-permute-start.1 = (f32[128,128]{1,0:T(8,128)S(1)}, f32[128,128]{1,0:T(8,128)S(1)}, u32[]{:S(2)}, u32[]{:S(2)}) collective-permute-start(f32[128,128]{1,0:T(8,128)S(1)} %get-tuple-element.16), channel_id=1, source_target_pairs={{0,2},{1,3},{2,0},{3,1},{4,6},{5,7},{6,4},{7,5},{8,10},{9,11},{10,... | collective-permute-start | bytes 196616 | tf_op jit(solution)/shard_map/ppermute | solution.py:24
  11.7 5.3 %collective-permute-start.2 = (f32[128,128]{1,0:T(8,128)S(1)}, f32[128,128]{1,0:T(8,128)S(1)}, u32[]{:S(2)}, u32[]{:S(2)}) collective-permute-start(f32[128,128]{1,0:T(8,128)S(1)} %add.11), channel_id=1, source_target_pairs={{0,4},{1,5},{2,6},{3,7},{4,0},{5,1},{6,2},{7,3},{8,12},{9,13},{10,... | collective-permute-start | bytes 196616 | tf_op jit(solution)/shard_map/ppermute | solution.py:24
  17.0 4.3 %collective-permute-start.4 = (f32[128,128]{1,0:T(8,128)S(1)}, f32[128,128]{1,0:T(8,128)S(1)}, u32[]{:S(2)}, u32[]{:S(2)}) collective-permute-start(f32[128,128]{1,0:T(8,128)S(1)} %add.12), channel_id=1, source_target_pairs={{0,16},{1,17},{2,18},{3,19},{4,20},{5,21},{6,22},{7,23},{8,24},{9,... | collective-permute-start | bytes 196616 | tf_op jit(solution)/shard_map/ppermute | solution.py:641
  18.9 5.2 %collective-permute-start.5 = (f32[128,128]{1,0:T(8,128)S(1)}, f32[128,128]{1,0:T(8,128)S(1)}, u32[]{:S(2)}, u32[]{:S(2)}) collective-permute-start(f32[128,128]{1,0:T(8,128)S(1)} %add.12), channel_id=1, source_target_pairs={{0,17},{1,16},{2,19},{3,18},{4,21},{5,20},{6,23},{7,22},{8,25},{9,... | collective-permute-start | bytes 196616 | tf_op jit(solution)/shard_map/ppermute | solution.py:641
  20.4 5.0 %collective-permute-start.3 = (f32[248,128]{1,0:T(8,128)S(1)}, f32[248,128]{1,0:T(8,128)S(1)}, u32[]{:S(2)}, u32[]{:S(2)}) collective-permute-start(f32[248,128]{1,0:T(8,128)S(1)} %pad_maximum_fusion.3), channel_id=1, source_target_pairs={{0,1},{1,0},{2,3},{3,2},{4,5},{5,4},{6,7},{7,6},{8,9},{9,8},{10,11... | collective-permute-start | bytes 380936 | tf_op jit(solution)/shard_map/ppermute | solution.py:641
  24.1 2.6 %copy-start = (bf16[768,512]{1,0:T(8,128)(2,1)S(1)}, bf16[768,512]{1,0:T(8,128)(2,1)}, u32[]{:S(2)}) copy-start(bf16[768,512]{1,0:T(8,128)(2,1)} %constant.26.clone.table_ref) | copy-start | bytes 2359300
  24.2 2.6 %collective-permute-start.6 = (f32[384,128]{1,0:T(8,128)S(1)}, f32[384,128]{1,0:T(8,128)S(1)}, u32[]{:S(2)}, u32[]{:S(2)}) collective-permute-start(f32[384,128]{1,0:T(8,128)S(1)} %pad_maximum_fusion), channel_id=1, source_target_pairs={{0,8},{8,0},{16,24},{24,16},{1,9},{9,1},{17,25},{25,17},{2,10},{10... | collective-permute-start | bytes 589832 | tf_op jit(solution)/shard_map/ppermute | solution.py:24
  24.3 2.5 %copy-start.1 = (f32[1024,128]{1,0:T(8,128)S(1)}, f32[1024,128]{1,0:T(8,128)}, u32[]{:S(2)}) copy-start(f32[1024,128]{1,0:T(8,128)} %constant.27.clone.factor_ref) | copy-start | bytes 1572868
  25.4 1.3 %collective-permute-start.7 = (f32[128,128]{1,0:T(8,128)S(1)}, f32[128,128]{1,0:T(8,128)S(1)}, u32[]{:S(2)}, u32[]{:S(2)}) collective-permute-start(f32[128,128]{1,0:T(8,128)S(1)} %get-tuple-element.23), channel_id=1, source_target_pairs={{0,8},{8,0},{16,24},{24,16},{1,9},{9,1},{17,25},{25,17},{2,10},{10... | collective-permute-start | bytes 196616 | tf_op jit(solution)/shard_map/ppermute | solution.py:24
